TPU v7x, 32 devices: a whole 2x2x4 slice. The times are simulated.
32 devices in a mesh: shard: 4 (over x, core), ctx: 4 (over z), tp: 2 (over y).
Axes of the slice: x: 2, y: 2, z: 4, core: 2. Of those that a mesh axis runs over, the one named last changes fastest.
Arguments:
- tokens: bfloat16 [16384, 1536], P(('shard', 'ctx')), may hold values from -6 to 6
- cotangent: bfloat16 [16384, 1536], P(('shard', 'ctx')), may hold values from -6 to 6
- segment: int32 [4, 4096], P('shard'), may hold values from 0 to 16, as said below
- parent: int32 [4, 17], P('shard'), may hold values from -1 to 16, as said below
- gain_attn: bfloat16 [1536], replicated, may hold values from 0.5 to 1.5
- qkv_weight: bfloat16 [1536, 2048], P('shard', 'tp'), may hold values from -0.15625 to 0.15625
- qkv_bias: bfloat16 [2048], P('tp'), may hold values from -0.59765625 to 0.59765625
- out_weight: bfloat16 [1536, 1536], P('shard', 'tp'), may hold values from -2.5 to 2.5
- gain_ffn: bfloat16 [1536], replicated, may hold values from 0.5 to 1.5
- gate_weight: bfloat16 [1536, 8960], P('shard', 'tp'), may hold values from -0.15625 to 0.15625
- up_weight: bfloat16 [1536, 8960], P('shard', 'tp'), may hold values from -0.15625 to 0.15625
- down_weight: bfloat16 [1536, 8960], P('shard', 'tp'), may hold values from -0.125 to 0.125
Outputs:
- output: bfloat16 [16384, 1536], P(('shard', 'ctx'))
- input_grad: float32 [16384, 1536], P(('shard', 'ctx'))
- grad_gain_attn: float32 [1536], replicated
- grad_qkv: float32 [1536, 2048], P('shard', 'tp')
- grad_bias: float32 [2048], P('tp')
- grad_out: float32 [1536, 1536], P('shard', 'tp')
- grad_gain_ffn: float32 [1536], replicated
- grad_gate: float32 [1536, 8960], P('shard', 'tp')
- grad_up: float32 [1536, 8960], P('shard', 'tp')
- grad_down: float32 [1536, 8960], P('shard', 'tp')
- clip: float32 [12], P('tp')
Inputs may be any that keep to these rules, and one draw needn't show every extreme that they name: `segment`: in each row ids never fall, and every id of 0 to 16 occurs in one run. parent[s] is -1 for a root, s for a padding segment, or an id below s that is not a padding segment; a parent's parent is a root or -1 is reached within two steps.
All inputs are finite; a program needn't handle non-finite values.
Results may differ from a plain program's by a relative error of at most 0.019.
Values may be sent and summed in bfloat16 or wider, within the bound.
A program may use at most 320 MiB of HBM per device.

v0:
```python
import math

import jax
import jax.numpy as jnp
from jax import lax
from jax.sharding import PartitionSpec as P

HEAD = 128


EPSILON = 1e-06
THETA = 1000000.0
CLIP_BOUND = 4.0
NEG_FILL = -1e30


def tree_tables(seg_row, parent_row):
    seg_count = parent_row.shape[0]
    seg_ids = jnp.arange(seg_count, dtype=jnp.int32)
    slot_ids = jnp.arange(seg_row.shape[0], dtype=jnp.int32)
    one_hot = (seg_row[:, None] == seg_ids[None, :]).astype(jnp.int32)
    lengths = jnp.sum(one_hot, axis=0, dtype=jnp.int32)
    starts = jnp.cumsum(lengths, dtype=jnp.int32) - lengths
    parent_link = (
        (parent_row[:, None] == seg_ids[None, :]) & (parent_row[:, None] != seg_ids[:, None])
    ).astype(jnp.int32)
    padding = (parent_row == seg_ids).astype(jnp.int32)
    strict = jnp.minimum(parent_link + jnp.dot(parent_link, parent_link), 1)
    reachable = jnp.minimum(strict + jnp.diag(1 - padding), 1)
    offsets = jnp.dot(strict, lengths) - starts
    positions = jnp.dot(one_hot, offsets) + slot_ids
    return (one_hot, reachable, positions)


def visible(reach_rows, row_ids, hot_cols, col_ids):
    linked = jnp.dot(reach_rows, hot_cols.T) > 0
    before = col_ids[None, :] <= row_ids[:, None]
    diagonal = col_ids[None, :] == row_ids[:, None]
    return linked & before | diagonal


def rotate(values_in, positions, direction):
    head_dim = values_in.shape[-1]
    half_dim = head_dim // 2
    frequency = THETA ** (-2.0 * jnp.arange(half_dim, dtype=jnp.float32) / head_dim)
    angles = positions.astype(jnp.float32)[:, None] * frequency[None, :]
    view_shape = (angles.shape[0],) + (1,) * (values_in.ndim - 2) + (half_dim,)
    cosine = jnp.cos(angles).reshape(view_shape)
    sine_part = direction * jnp.sin(angles).reshape(view_shape)
    first_half = values_in[..., :half_dim]
    second = values_in[..., half_dim:]
    return jnp.concatenate(
        [first_half * cosine - second * sine_part, second * cosine + first_half * sine_part],
        axis=-1,
    )


def norm_back(grad_hidden, gain_vec, normed, inv_rms):
    scaled = grad_hidden * gain_vec
    return inv_rms * (scaled - normed * jnp.mean(scaled * normed, axis=-1, keepdims=True))


def contract_rows(left, right):
    return lax.dot_general(
        left, right, (((0,), (0,)), ((), ())), preferred_element_type=jnp.float32
    )


def contract_cols(left, right):
    return lax.dot_general(
        left, right, (((1,), (1,)), ((), ())), preferred_element_type=jnp.float32
    )


def local(
    tokens,
    cotangent,
    segment,
    parent,
    gain_attn,
    qkv_weight,
    qkv_bias,
    out_weight,
    gain_ffn,
    gate_weight,
    up_weight,
    down_weight,
):
    row_count = tokens.shape[0]
    slot_count = segment.shape[1]
    per_group = out_weight.shape[1] // HEAD
    score_scale = HEAD ** (-0.5)
    first_row = lax.axis_index("ctx") * row_count
    one_hot, reachable, positions = tree_tables(segment[0], parent[0])
    row_ids = first_row + jnp.arange(row_count, dtype=jnp.int32)
    reach_rows = jnp.dot(lax.dynamic_slice_in_dim(one_hot, first_row, row_count, 0), reachable)
    own_pos = lax.dynamic_slice_in_dim(positions, first_row, row_count, 0)
    full_qkv, full_out, full_gate, full_up, full_down = (
        lax.all_gather(qkv_weight, "shard", axis=0, tiled=True),
        lax.all_gather(out_weight, "shard", axis=0, tiled=True),
        lax.all_gather(gate_weight, "shard", axis=0, tiled=True),
        lax.all_gather(up_weight, "shard", axis=0, tiled=True),
        lax.all_gather(down_weight, "shard", axis=0, tiled=True),
    )
    inputs = tokens.astype(jnp.float32)
    inv_one = lax.rsqrt(jnp.mean(inputs * inputs, axis=-1, keepdims=True) + EPSILON)
    norm_one = inputs * inv_one
    gain_one = gain_attn.astype(jnp.float32)
    hidden_one = (norm_one * gain_one).astype(jnp.bfloat16)
    mixed = jnp.dot(hidden_one, full_qkv, preferred_element_type=jnp.float32) + qkv_bias.astype(
        jnp.float32
    )
    split_q = per_group * HEAD
    queries = rotate(mixed[:, :split_q].reshape(row_count, per_group, HEAD), own_pos, 1.0).astype(
        jnp.bfloat16
    )
    keys_own = rotate(mixed[:, split_q : split_q + HEAD], own_pos, 1.0).astype(jnp.bfloat16)
    values_own = mixed[:, split_q + HEAD :].astype(jnp.bfloat16)
    keys_all, values_all = (
        lax.all_gather(keys_own, "ctx", axis=0, tiled=True),
        lax.all_gather(values_own, "ctx", axis=0, tiled=True),
    )
    block_len = math.gcd(slot_count, 1024)
    block_count = slot_count // block_len

    def block_scores(begin_at):
        hot_cols = lax.dynamic_slice_in_dim(one_hot, begin_at, block_len, 0)
        col_ids = begin_at + jnp.arange(block_len, dtype=jnp.int32)
        seen_mask = visible(reach_rows, row_ids, hot_cols, col_ids)
        key_blk = lax.dynamic_slice_in_dim(keys_all, begin_at, block_len, 0)
        value_blk = lax.dynamic_slice_in_dim(values_all, begin_at, block_len, 0)
        scores = (
            jnp.einsum("igd,jd->gij", queries, key_blk, preferred_element_type=jnp.float32)
            * score_scale
        )
        return (jnp.where(seen_mask[None], scores, NEG_FILL), seen_mask, key_blk, value_blk)

    def first_pass(blk_index, running):
        row_max, row_total = running
        masked, seen_mask, key_blk, value_blk = block_scores(blk_index * block_len)
        new_max = jnp.maximum(row_max, jnp.max(masked, axis=-1))
        fresh = jnp.where(seen_mask[None], jnp.exp(masked - new_max[..., None]), 0.0)
        row_total = row_total * jnp.exp(row_max - new_max) + jnp.sum(fresh, axis=-1)
        return (new_max, row_total)

    start_max = jnp.full((per_group, row_count), NEG_FILL, jnp.float32)
    start_total = jnp.zeros((per_group, row_count), jnp.float32)
    row_max, row_total = lax.fori_loop(0, block_count, first_pass, (start_max, start_total))
    log_total = row_max + jnp.log(row_total)
    peak_row = jnp.max(row_max, axis=1)

    def second_pass(blk_index, summed_av):
        masked, seen_mask, key_blk, value_blk = block_scores(blk_index * block_len)
        softmax_w = jnp.exp(masked - log_total[..., None]).astype(jnp.bfloat16)
        return summed_av + jnp.einsum(
            "gij,jd->igd", softmax_w, value_blk, preferred_element_type=jnp.float32
        )

    attended_f = lax.fori_loop(
        0, block_count, second_pass, jnp.zeros((row_count, per_group, HEAD), jnp.float32)
    )
    attended_b = attended_f.reshape(row_count, per_group * HEAD).astype(jnp.bfloat16)
    branch = lax.psum(contract_cols(attended_b, full_out).astype(jnp.bfloat16), "tp").astype(
        jnp.float32
    )
    mid = inputs + branch
    inv_two = lax.rsqrt(jnp.mean(mid * mid, axis=-1, keepdims=True) + EPSILON)
    norm_two = mid * inv_two
    gain_two = gain_ffn.astype(jnp.float32)
    hidden_two = (norm_two * gain_two).astype(jnp.bfloat16)
    gate_pre = jnp.dot(hidden_two, full_gate, preferred_element_type=jnp.float32)
    up_pre = jnp.dot(hidden_two, full_up, preferred_element_type=jnp.float32)
    sigmoid_g = jax.nn.sigmoid(gate_pre)
    silu_val = gate_pre * sigmoid_g
    inner_act = (silu_val * up_pre).astype(jnp.bfloat16)
    ffn_out = lax.psum(contract_cols(inner_act, full_down).astype(jnp.bfloat16), "tp").astype(
        jnp.float32
    )
    output = (mid + ffn_out).astype(jnp.bfloat16)
    grad_top = cotangent.astype(jnp.float32)
    grad_down = contract_rows(cotangent, inner_act)
    d_inner = jnp.dot(cotangent, full_down, preferred_element_type=jnp.float32)
    d_gate = (d_inner * up_pre * sigmoid_g * (1.0 + gate_pre * (1.0 - sigmoid_g))).astype(
        jnp.bfloat16
    )
    d_up = (d_inner * silu_val).astype(jnp.bfloat16)
    grad_gate = contract_rows(hidden_two, d_gate)
    grad_up = contract_rows(hidden_two, d_up)
    d_hidden_two = contract_cols(d_gate, full_gate) + contract_cols(d_up, full_up)
    gain_two_part = jnp.sum(d_hidden_two * norm_two, axis=0)
    back_two = norm_back(d_hidden_two, gain_two, norm_two, inv_two)
    back_two, gain_two_grad = (
        lax.psum(back_two.astype(jnp.bfloat16), "tp").astype(jnp.float32),
        lax.psum(gain_two_part.astype(jnp.bfloat16), "tp").astype(jnp.float32),
    )
    d_mid = grad_top + back_two
    d_branch = d_mid.astype(jnp.bfloat16)
    grad_outw = contract_rows(d_branch, attended_b)
    d_att = (
        jnp.dot(d_branch, full_out, preferred_element_type=jnp.float32)
        .reshape(row_count, per_group, HEAD)
        .astype(jnp.bfloat16)
    )
    row_dot = jnp.einsum("igd,igd->gi", d_att.astype(jnp.float32), attended_f)

    def back_step(grad_query, blk_index):
        masked, seen_mask, key_blk, value_blk = block_scores(blk_index * block_len)
        softmax_f = jnp.exp(masked - log_total[..., None])
        grad_prob = jnp.einsum("igd,jd->gij", d_att, value_blk, preferred_element_type=jnp.float32)
        grad_score = (softmax_f * (grad_prob - row_dot[..., None])).astype(jnp.bfloat16)
        grad_query = (
            grad_query
            + jnp.einsum("gij,jd->igd", grad_score, key_blk, preferred_element_type=jnp.float32)
            * score_scale
        )
        grad_key = (
            jnp.einsum("gij,igd->jd", grad_score, queries, preferred_element_type=jnp.float32)
            * score_scale
        )
        grad_value = jnp.einsum(
            "gij,igd->jd", softmax_f.astype(jnp.bfloat16), d_att, preferred_element_type=jnp.float32
        )
        return (grad_query, (grad_key, grad_value))

    grad_query, (key_parts, value_parts) = lax.scan(
        back_step,
        jnp.zeros((row_count, per_group, HEAD), jnp.float32),
        jnp.arange(block_count, dtype=jnp.int32),
    )
    key_grads = key_parts.reshape(slot_count, HEAD)
    value_grads = value_parts.reshape(slot_count, HEAD)
    key_grad_own, value_grad_own = (
        lax.psum_scatter(
            key_grads.astype(jnp.bfloat16), "ctx", scatter_dimension=0, tiled=True
        ).astype(jnp.float32),
        lax.psum_scatter(
            value_grads.astype(jnp.bfloat16), "ctx", scatter_dimension=0, tiled=True
        ).astype(jnp.float32),
    )
    query_back = rotate(grad_query, own_pos, -1.0).reshape(row_count, per_group * HEAD)
    key_back = rotate(key_grad_own, own_pos, -1.0)
    d_mixed = jnp.concatenate([query_back, key_back, value_grad_own], axis=1).astype(jnp.bfloat16)
    grad_qkv = contract_rows(hidden_one, d_mixed)
    bias_part = jnp.sum(d_mixed.astype(jnp.float32), axis=0)
    d_hidden_one = contract_cols(d_mixed, full_qkv)
    gain_one_part = jnp.sum(d_hidden_one * norm_one, axis=0)
    back_one = norm_back(d_hidden_one, gain_one, norm_one, inv_one)
    back_one, gain_one_grad = (
        lax.psum(back_one.astype(jnp.bfloat16), "tp").astype(jnp.float32),
        lax.psum(gain_one_part.astype(jnp.bfloat16), "tp").astype(jnp.float32),
    )
    input_grad = d_mid + back_one
    peak_all = lax.pmax(peak_row, ("shard", "ctx"))
    clip_out = CLIP_BOUND / jnp.maximum(peak_all, CLIP_BOUND)
    gain_one_grad, gain_two_grad, bias_grad = lax.psum(
        (gain_one_grad, gain_two_grad, bias_part), ("shard", "ctx")
    )
    grad_parts = (
        lax.psum_scatter(grad_qkv, ("shard", "ctx"), scatter_dimension=0, tiled=True),
        lax.psum_scatter(grad_outw, ("shard", "ctx"), scatter_dimension=0, tiled=True),
        lax.psum_scatter(grad_gate, ("shard", "ctx"), scatter_dimension=0, tiled=True),
        lax.psum_scatter(grad_up, ("shard", "ctx"), scatter_dimension=0, tiled=True),
        lax.psum_scatter(grad_down, ("shard", "ctx"), scatter_dimension=0, tiled=True),
    )
    summed = (
        lax.all_gather(grad_parts[0].astype(jnp.bfloat16), "ctx", axis=0, tiled=True).astype(
            jnp.float32
        ),
        lax.all_gather(grad_parts[1].astype(jnp.bfloat16), "ctx", axis=0, tiled=True).astype(
            jnp.float32
        ),
        lax.all_gather(grad_parts[2].astype(jnp.bfloat16), "ctx", axis=0, tiled=True).astype(
            jnp.float32
        ),
        lax.all_gather(grad_parts[3].astype(jnp.bfloat16), "ctx", axis=0, tiled=True).astype(
            jnp.float32
        ),
        lax.all_gather(grad_parts[4].astype(jnp.bfloat16), "ctx", axis=0, tiled=True).astype(
            jnp.float32
        ),
    )
    qkv_total, out_total, gate_total, up_total, down_total = summed
    return (
        output,
        input_grad,
        gain_one_grad,
        qkv_total,
        bias_grad,
        out_total,
        gain_two_grad,
        gate_total,
        up_total,
        down_total,
        clip_out,
    )


def solution(mesh):
    placed = (
        P(("shard", "ctx"), None),
        P(("shard", "ctx"), None),
        P("shard", None),
        P("shard", None),
        P(),
        P("shard", "tp"),
        P("tp"),
        P("shard", "tp"),
        P(),
        P("shard", "tp"),
        P("shard", "tp"),
        P("shard", "tp"),
    )
    return jax.shard_map(
        local,
        mesh=mesh,
        in_specs=placed,
        out_specs=(
            P(("shard", "ctx"), None),
            P(("shard", "ctx"), None),
            P(),
            P("shard", "tp"),
            P("tp"),
            P("shard", "tp"),
            P(),
            P("shard", "tp"),
            P("shard", "tp"),
            P("shard", "tp"),
            P("tp"),
        ),
        check_vma=False,
    )
```

profile of v0, /device:TPU:0, one launch (start us, length us, event | category | flops | bytes accessed | tf_op | source)
XLA Modules:
  0.0 2481.0 jit_solution(15337620005727726702)
XLA Ops:
  16.0 24.8 all-gather.11.cloned.1.call-done
  58.6 20.7 all-gather.15.cloned.1.call-done
  81.6 122.9 %while.45 = (s32[]{:T(128)}, f32[6,1024]{1,0:T(8,128)S(1)}, f32[6,1024]{1,0:T(8,128)S(1)}, s32[4096,17]{0,1:T(8,128)}, s32[1024,17]{0,1:T(8,128)S(1)}, /*index=5...) while((s32[]{:T(128)}, f32[6,1024]{1,0:T(8,128)S(1)}, ...), condition=%wide.region_6.7_spmd.clone, body=%wide.region_3.6_spmd.clone.sunk | while | flops 1701871616 | bytes 55816380 | solution.py:148
  89.0 11.6 fusion.209
  100.6 11.7 select_reduce_fusion.2
  119.8 11.6 fusion.209
  131.5 11.7 select_reduce_fusion.2
  150.6 11.5 fusion.209
  162.2 11.6 select_reduce_fusion.2
  181.3 11.5 fusion.209
  192.8 11.6 select_reduce_fusion.2
  205.2 74.9 %while.46 = (s32[]{:T(128)}, f32[1024,6,128]{0,2,1:T(8,128)}, bf16[4096,128]{0,1:T(8,128)(2,1)}, s32[4096,17]{0,1:T(8,128)}, s32[1024,17]{0,1:T(8,128)S(1)}, /*i...) while((s32[]{:T(128)}, f32[1024,6,128]{0,2,1:T(8,128)}, ...), condition=%wide.region_8.9_spmd.clone, body=%wide.region_7.8_spmd.clone.sunk | while | flops 3288860672 | bytes 10696384 | solution.py:159
  212.7 11.0 bitcast_add_fusion.4
  231.1 11.4 bitcast_add_fusion.4
  249.9 11.4 bitcast_add_fusion.4
  268.7 11.4 bitcast_add_fusion.4
  291.4 83.2 %all-reduce.7.cloned.1.call-done = bf16[1024,1536]{1,0:T(8,128)(2,1)} async-done(((bf16[1024,1536]{1,0:T(8,128)(2,1)}), bf16[1024,1536]{1,0:T(8,128)(2,1)}) %all-reduce.7.cloned.1.call-update) | async-done | bytes 3145744 | tf_op jit(solution)/shard_map/psum | solution.py:163
  381.2 83.8 %all-gather.19.cloned.1.call-done = bf16[1536,4480]{1,0:T(8,128)(2,1)} async-done(((bf16[384,4480]{1,0:T(8,128)(2,1)}), bf16[1536,4480]{1,0:T(8,128)(2,1)}) %all-gather.19.cloned.1.call-update) | async-done | bytes 13762576 | tf_op jit(solution)/shard_map/all_gather | solution.py:101
  465.0 21.3 fusion.134
  486.3 69.2 %all-gather.21.cloned.1.call-done = bf16[1536,4480]{1,0:T(8,128)(2,1)} async-done(((bf16[384,4480]{1,0:T(8,128)(2,1)}), bf16[1536,4480]{1,0:T(8,128)(2,1)}) %all-gather.21.cloned.1.call-update) | async-done | bytes 13762576 | tf_op jit(solution)/shard_map/all_gather | solution.py:102
  555.5 21.1 fusion.135
  576.5 69.4 %all-gather.23.cloned.1.call-done = bf16[1536,4480]{1,0:T(8,128)(2,1)} async-done(((bf16[384,4480]{1,0:T(8,128)(2,1)}), bf16[1536,4480]{1,0:T(8,128)(2,1)}) %all-gather.23.cloned.1.call-update) | async-done | bytes 13762576 | tf_op jit(solution)/shard_map/all_gather | solution.py:103
  645.9 31.6 %multiply_convert_fusion = (bf16[1024,4480]{1,0:T(8,128)(2,1)}, bf16[1024,4480]{1,0:T(8,128)(2,1)}, bf16[1024,4480]{1,0:T(8,128)(2,1)}) fusion(f32[1024,4480]{1,0:T(8,128)} %fusion.134, f32[1024,4480]{1,0:T(8,128)} %fusion.135, bf16[1024,1536]{1,0:T(8,128)(2,1)S(1)} %copy-done.14, bf16[1536,4480]{1,0:T(8,128)(2,1)} %all-gather.23.cloned.1.call-done), kind=kOutput, calls=%fused_computation.75 | convolution fusion | flops 14161674240 | bytes 81133568 | tf_op jit(solution)/shard_map/dot_general | solution.py:182
  677.6 21.7 fusion.136
  699.3 23.2 multiply_reduce_fusion
  725.7 85.9 %all-reduce.9.cloned.1.call-done = bf16[1024,1536]{1,0:T(8,128)(2,1)} async-done(((bf16[1024,1536]{1,0:T(8,128)(2,1)}), bf16[1024,1536]{1,0:T(8,128)(2,1)}) %all-reduce.9.cloned.1.call-update) | async-done | bytes 3145744 | tf_op jit(solution)/shard_map/psum | solution.py:193
  822.0 252.9 %while.47 = (s32[]{:T(128)}, f32[1024,6,128]{0,2,1:T(8,128)}, bf16[4,1024,128]{2,1,0:T(8,128)(2,1)}, bf16[4,1024,128]{2,1,0:T(8,128)(2,1)}, s32[4]{0:T(128)S(1)}...) while((s32[]{:T(128)}, f32[1024,6,128]{0,2,1:T(8,128)}, ...), condition=%wide.region_15.16_spmd.clone, body=%wide.region_14.15_spmd.clone.sunk | while | flops 8159365120 | bytes 200274848 | solution.py:225
  831.6 11.7 fusion.230
  843.3 15.6 fusion.232
  858.9 8.7 bitcast_add_fusion.5
  872.8 11.7 fusion.234
  885.8 8.2 fusion.231
  894.0 11.7 fusion.230
  905.7 15.6 fusion.232
  921.3 9.6 bitcast_add_fusion.5
  936.1 11.7 fusion.234
  949.1 8.2 fusion.231
  957.3 11.7 fusion.230
  969.0 15.6 fusion.232
  984.6 9.6 bitcast_add_fusion.5
  999.5 11.7 fusion.234
  1012.5 8.2 fusion.231
  1020.6 11.7 fusion.230
  1032.4 15.6 fusion.232
  1047.9 9.6 bitcast_add_fusion.5
  1062.8 11.7 fusion.234
  1078.1 20.7 fusion.137
  1098.9 20.7 fusion.138
  1121.5 21.3 convolution_bitcast_fusion.1
  1142.8 30.5 %copy.93 = f32[1536,4480]{1,0:T(8,128)} copy(f32[1536,4480]{0,1:T(8,128)} %convolution_bitcast_fusion.1) | data formatting | bytes 55050240
  1180.7 22.6 convolution_convert_fusion
  1229.7 168.8 %reduce-scatter.18.cloned.1.call-done = f32[96,4480]{1,0:T(8,128)} async-done(((f32[1536,4480]{1,0:T(8,128)}), f32[96,4480]{1,0:T(8,128)}) %reduce-scatter.18.cloned.1.call-update) | async-done | bytes 1720336 | tf_op jit(solution)/shard_map/reduce_scatter | solution.py:261
  1401.0 264.2 %reduce-scatter.20.cloned.1.call-done = f32[96,4480]{1,0:T(8,128)} async-done(((f32[1536,4480]{1,0:T(8,128)}), f32[96,4480]{1,0:T(8,128)}) %reduce-scatter.20.cloned.1.call-update) | async-done | bytes 1720336 | tf_op jit(solution)/shard_map/reduce_scatter | solution.py:262
  1667.7 263.5 %reduce-scatter.22.cloned.1.call-done = f32[96,4480]{1,0:T(8,128)} async-done(((f32[1536,4480]{1,0:T(8,128)}), f32[96,4480]{1,0:T(8,128)}) %reduce-scatter.22.cloned.1.call-update) | async-done | bytes 1720336 | tf_op jit(solution)/shard_map/reduce_scatter | solution.py:263
  1933.7 31.7 %pmax.7 = f32[6]{0:T(128)S(1)} all-reduce(f32[6]{0:T(128)S(1)} %copy-done.46), channel_id=1, replica_groups=mesh['shard'=4,'ctx'=4,'tp'=2] {'shard','ctx'}, use_global_device_ids=true, to_apply=%region_34.35 | all-reduce | flops 6 | bytes 48 | tf_op jit(solution)/shard_map/pmax | solution.py:253
  1972.8 59.3 %all-reduce = (f32[1536]{0:T(1024)}, f32[1024]{0:T(1024)}, f32[1536]{0:T(1024)}) all-reduce(bf16[1536]{0:T(1024)(128)(2,1)S(1)} %get-tuple-element.711, f32[1024]{0:T(1024)S(1)} %convert_reduce_fusion, bf16[1536]{0:T(1024)(128)(2,1)S(1)} %get-tuple-element.712), channel_id=1, replica_groups=mesh['shard'=4,'ctx'=4,'tp'=2] {'shard','ctx'}, use_global_device_ids=true, to_apply=%region_22.23 | all-reduce | flops 4096 | bytes 26624 | tf_op jit(solution)/shard_map/psum | solution.py:255
  2033.1 16.4 all_gather.44
  2050.6 116.8 %all-reduce.11.cloned.1.call-done = (bf16[1024,1536]{1,0:T(8,128)(2,1)}, bf16[1024,1536]{1,0:T(8,128)(2,1)}) async-done(((bf16[1024,1536]{1,0:T(8,128)(2,1)}, bf16[1024,1536]{1,0:T(8,128)(2,1)}), (bf16[1024,1536]{1,0:T(8,128)(2,1)}, bf16[1024,1536]{1,0:T(8,128)(2,1)})) %all-reduce.11.cloned.1.call-update) | async-done | bytes 6291472 | tf_op jit(solution)/shard_map/psum | solution.py:176
  2167.4 9.0 convert_add_fusion.1
  2176.4 81.2 %reduce-scatter.14.cloned.1.call-done = f32[96,1024]{1,0:T(8,128)} async-done(((f32[1536,1024]{1,0:T(8,128)}), f32[96,1024]{1,0:T(8,128)}) %reduce-scatter.14.cloned.1.call-update) | async-done | bytes 393232 | tf_op jit(solution)/shard_map/reduce_scatter | solution.py:259
  2258.6 21.6 all_gather.43
  2281.5 49.2 %all-gather.25.cloned.1.call-done = bf16[384,4480]{1,0:T(8,128)(2,1)} async-done(((bf16[96,4480]{1,0:T(8,128)(2,1)}), bf16[384,4480]{1,0:T(8,128)(2,1)}) %all-gather.25.cloned.1.call-update) | async-done | bytes 3440656 | tf_op jit(solution)/shard_map/all_gather | solution.py:272
  2336.0 64.2 %all-gather.27.cloned.1.call-done = bf16[384,4480]{1,0:T(8,128)(2,1)} async-done(((bf16[96,4480]{1,0:T(8,128)(2,1)}), bf16[384,4480]{1,0:T(8,128)(2,1)}) %all-gather.27.cloned.1.call-update) | async-done | bytes 3440656 | tf_op jit(solution)/shard_map/all_gather | solution.py:275
  2405.6 63.1 %all-gather.29.cloned.1.call-done = bf16[384,4480]{1,0:T(8,128)(2,1)} async-done(((bf16[96,4480]{1,0:T(8,128)(2,1)}), bf16[384,4480]{1,0:T(8,128)(2,1)}) %all-gather.29.cloned.1.call-update) | async-done | bytes 3440656 | tf_op jit(solution)/shard_map/all_gather | solution.py:278
  (283 shorter events, 225.3 us)
Async XLA Ops:
  7.2 33.7 %copy-start.4 = (bf16[1024,1536]{1,0:T(8,128)(2,1)S(1)}, bf16[1024,1536]{1,0:T(8,128)(2,1)}, u32[]{:S(2)}) copy-start(bf16[1024,1536]{1,0:T(8,128)(2,1)} %param.18) | copy-start | bytes 9437188
  7.2 33.7 %all-gather.11.cloned.1.call-start = ((), (), s32[]{:S(2)}) async-start(), calls=%async_computation.7 | async-start | bytes 3932160 | tf_op jit(solution)/shard_map/all_gather | solution.py:99
  7.9 71.4 %all-gather.15.cloned.1.call-start = ((), (), s32[]{:S(2)}) async-start(), calls=%async_computation.9 | async-start | bytes 1310720 | tf_op jit(solution)/shard_map/all_gather | solution.py:120
  9.9 36.6 %copy-start.36 = (f32[1536]{0:T(1024)}, f32[1536]{0:T(1024)S(1)}, u32[]{:S(2)}) copy-start(f32[1536]{0:T(1024)S(1)} %convert_element_type.171) | copy-start | bytes 18436
  10.6 35.9 %copy-start.45 = (f32[64]{0:T(128)}, f32[64]{0:T(128)S(1)}, u32[]{:S(2)}) copy-start(f32[64]{0:T(128)S(1)} %multiply_power_fusion) | copy-start | bytes 772
  13.4 33.2 %copy-start.34 = (f32[1024]{0:T(1024)}, f32[1024]{0:T(1024)S(1)}, u32[]{:S(2)}) copy-start(f32[1024]{0:T(1024)S(1)} %fusion.125) | copy-start | bytes 12292
  16.0 30.6 %copy-start.40 = (f32[1024]{0:T(1024)}, f32[1024]{0:T(1024)S(1)}, u32[]{:S(2)}) copy-start(f32[1024]{0:T(1024)S(1)} %add_rsqrt_fusion.1) | copy-start | bytes 12292
  16.0 38.4 %copy-start.31 = (s32[1,4096]{1,0:T(1,128)S(1)}, s32[1,4096]{1,0:T(1,128)}, u32[]{:S(2)}) copy-start(s32[1,4096]{1,0:T(1,128)} %param.20) | copy-start | bytes 49156
  48.6 6.7 copy-start.47
  50.5 6.6 copy-start.17
  51.3 5.8 slice-start
  51.3 153.9 %all-gather.13.cloned.1.call-start = ((), (), s32[]{:S(2)}) async-start(), calls=%async_computation.8 | async-start | bytes 1310720 | tf_op jit(solution)/shard_map/all_gather | solution.py:121
  53.3 229.6 %all-gather.17.cloned.1.call-start = ((), (), s32[]{:S(2)}) async-start(), calls=%async_computation.10 | async-start | bytes 2949120 | tf_op jit(solution)/shard_map/all_gather | solution.py:100
  53.8 320.8 %all-reduce.7.cloned.1.call-start = ((), (), s32[]{:S(2)}) async-start(), calls=%async_computation.11 | async-start | bytes 6291456 | tf_op jit(solution)/shard_map/psum | solution.py:163
  57.6 24.0 copy-start.26
  280.1 9.1 copy-start
  280.1 9.1 copy-start.27
  280.1 9.1 copy-start.38
  282.9 6.3 copy-start.20
  289.2 175.7 %all-gather.19.cloned.1.call-start = ((), (), s32[]{:S(2)}) async-start(), calls=%async_computation.12 | async-start | bytes 17203200 | tf_op jit(solution)/shard_map/all_gather | solution.py:101
  289.8 84.8 %copy-start.5 = (bf16[1024,1536]{1,0:T(8,128)(2,1)S(1)}, bf16[1024,1536]{1,0:T(8,128)(2,1)}, u32[]{:S(2)}) copy-start(bf16[1024,1536]{1,0:T(8,128)(2,1)} %param.18) | copy-start | bytes 9437188
  289.8 265.6 %all-gather.21.cloned.1.call-start = ((), (), s32[]{:S(2)}) async-start(), calls=%async_computation.13 | async-start | bytes 17203200 | tf_op jit(solution)/shard_map/all_gather | solution.py:102
  290.6 355.3 %all-gather.23.cloned.1.call-start = ((), (), s32[]{:S(2)}) async-start(), calls=%async_computation.14 | async-start | bytes 17203200 | tf_op jit(solution)/shard_map/all_gather | solution.py:103
  291.3 520.3 %all-reduce.9.cloned.1.call-start = ((), (), s32[]{:S(2)}) async-start(), calls=%async_computation.15 | async-start | bytes 6291456 | tf_op jit(solution)/shard_map/psum | solution.py:193
  291.4 89.8 %copy-start.29 = (f32[1536]{0:T(1024)}, f32[1536]{0:T(1024)S(1)}, u32[]{:S(2)}) copy-start(f32[1536]{0:T(1024)S(1)} %convert_element_type.182) | copy-start | bytes 18436
  486.3 159.6 %copy-start.14 = (bf16[1024,1536]{1,0:T(8,128)(2,1)S(1)}, bf16[1024,1536]{1,0:T(8,128)(2,1)}, u32[]{:S(2)}) copy-start(bf16[1024,1536]{1,0:T(8,128)(2,1)} %param.19) | copy-start | bytes 9437188
  677.5 21.7 copy-start.6
  677.6 21.7 copy-start.9
  677.6 21.7 copy-start.30
  677.6 21.7 copy-start.33
  725.6 479.5 %reduce-scatter.10.cloned.1.call-start = ((), (), s32[]{:S(2)}) async-start(), calls=%async_computation.16 | async-start | bytes 1310720 | tf_op jit(solution)/shard_map/reduce_scatter | solution.py:233
  811.6 6.4 copy-start.11
  858.9 8.7 copy-start.2
  858.9 9.4 copy-start.21
  921.3 9.6 copy-start.2
  921.3 10.3 copy-start.21
  931.6 4.5 copy-start.48
  984.6 9.6 copy-start.2
  984.6 10.3 copy-start.21
  995.0 4.5 copy-start.48
  1047.9 9.6 copy-start.2
  1047.9 10.3 copy-start.21
  1058.3 4.5 copy-start.48
  1077.3 129.9 %reduce-scatter.12.cloned.1.call-start = ((), (), s32[]{:S(2)}) async-start(), calls=%async_computation.17 | async-start | bytes 1310720 | tf_op jit(solution)/shard_map/reduce_scatter | solution.py:236
  1078.1 320.3 %reduce-scatter.18.cloned.1.call-start = ((), (), s32[]{:S(2)}) async-start(), calls=%async_computation.20 | async-start | bytes 29245440 | tf_op jit(solution)/shard_map/reduce_scatter | solution.py:261
  1098.9 566.3 %reduce-scatter.20.cloned.1.call-start = ((), (), s32[]{:S(2)}) async-start(), calls=%async_computation.22 | async-start | bytes 29245440 | tf_op jit(solution)/shard_map/reduce_scatter | solution.py:262
  1119.6 811.6 %reduce-scatter.22.cloned.1.call-start = ((), (), s32[]{:S(2)}) async-start(), calls=%async_computation.25 | async-start | bytes 29245440 | tf_op jit(solution)/shard_map/reduce_scatter | solution.py:263
  1173.3 858.8 %reduce-scatter.16.cloned.1.call-start = ((), (), s32[]{:S(2)}) async-start(), calls=%async_computation.19 | async-start | bytes 5013504 | tf_op jit(solution)/shard_map/reduce_scatter | solution.py:260
  1180.6 22.7 copy-start.3
  1180.6 22.7 copy-start.18
  1180.6 986.8 %all-reduce.11.cloned.1.call-start = ((), (), s32[]{:S(2)}) async-start(), calls=%async_computation.26 | async-start | bytes 12582912 | tf_op jit(solution)/shard_map/psum | solution.py:176
  1180.7 22.6 copy-start.23
  1203.3 5.0 copy-start.35
  1203.3 7.2 copy-start.37
  1203.3 7.2 copy-start.41
  1203.9 6.7 copy-start.7
  1210.5 8.1 copy-start.25
  1221.4 1036.2 %reduce-scatter.14.cloned.1.call-start = ((), (), s32[]{:S(2)}) async-start(), calls=%async_computation.18 | async-start | bytes 6684672 | tf_op jit(solution)/shard_map/reduce_scatter | solution.py:259
  1229.6 1101.1 %all-gather.25.cloned.1.call-start = ((), (), s32[]{:S(2)}) async-start(), calls=%async_computation.21 | async-start | bytes 4300800 | tf_op jit(solution)/shard_map/all_gather | solution.py:272
  1400.9 532.8 %copy-start.46 = (f32[6]{0:T(128)S(1)}, f32[6]{0:T(128)}, u32[]{:S(2)}) copy-start(f32[6]{0:T(128)} %get-tuple-element.734) | copy-start | bytes 76
  1400.9 565.1 %copy-start.43 = (bf16[1536]{0:T(1024)(128)(2,1)S(1)}, bf16[1536]{0:T(1024)(128)(2,1)}, u32[]{:S(2)}) copy-start(bf16[1536]{0:T(1024)(128)(2,1)} %get-tuple-element.642) | copy-start | bytes 9220
  1400.9 565.1 %copy-start.44 = (bf16[1536]{0:T(1024)(128)(2,1)S(1)}, bf16[1536]{0:T(1024)(128)(2,1)}, u32[]{:S(2)}) copy-start(bf16[1536]{0:T(1024)(128)(2,1)} %get-tuple-element.644) | copy-start | bytes 9220
  1400.9 999.3 %all-gather.27.cloned.1.call-start = ((), (), s32[]{:S(2)}) async-start(), calls=%async_computation.23 | async-start | bytes 4300800 | tf_op jit(solution)/shard_map/all_gather | solution.py:275
  1667.6 801.0 %all-gather.29.cloned.1.call-start = ((), (), s32[]{:S(2)}) async-start(), calls=%async_computation.24 | async-start | bytes 4300800 | tf_op jit(solution)/shard_map/all_gather | solution.py:278
  (21 other events, 58.4 us)
Sparse Core Ops, SparseCore 0:
  9.6 31.2 all-gather.10
  51.4 27.9 all-gather.14
  81.5 27.4 all-gather.12
  110.4 23.5 all-gather.16
  289.3 85.2 all-reduce.6
  376.1 88.7 all-gather.18
  466.6 88.7 all-gather.20
  557.1 88.7 all-gather.22
  725.7 85.8 all-reduce.8
  1077.5 27.1 reduce-scatter.9
  1107.0 25.7 reduce-scatter.11
  1136.8 261.5 reduce-scatter.17
  1403.1 262.0 reduce-scatter.19
  1669.1 262.0 reduce-scatter.21
  1936.0 75.1 reduce-scatter.15
  2014.6 152.7 all-reduce.10
  2172.3 85.2 reduce-scatter.13
  2259.6 71.1 all-gather.24
  2332.3 67.9 all-gather.26
  2401.7 66.9 all-gather.28
where the time goes:
time: 2490 us; the launch traced here: 2480 us
  waiting for transfers between devices  1510 us (61%)
  matrix products  640 us (26%)
  blocking collectives  134 us (5%)
  other arithmetic  118 us (5%)
  local copies, waits for them, and re-layouts  56.4 us (2%)
    reduce_scatter x1, waiting for transfers between devices, local(): lax.psum_scatter(grad_up, ('shard', 'ctx'), scatter_dimension=0, tiled=True)  264 us
    reduce_scatter x1, waiting for transfers between devices, local(): lax.psum_scatter(grad_down, ('shard', 'ctx'), scatter_dimension=0, tiled=...  264 us
    reduce_scatter x1, waiting for transfers between devices, local(): lax.psum_scatter(grad_gate, ('shard', 'ctx'), scatter_dimension=0, tiled=...  169 us
    psum x1, waiting for transfers between devices, local(): lax.psum(contract_cols(inner_act, full_down).astype(jnp.bfloat16), 'tp')  117 us
    dot_general x8, matrix products, block_scores(): jnp.einsum('igd,jd->gij', queries, key_blk, preferred_element_type=jnp.fl...  93.3 us
    dot_general x12, matrix products, visible(): linked = jnp.dot(reach_rows, hot_cols.T) > 0  91.8 us
    psum x1, waiting for transfers between devices, local(): lax.psum(back_two.astype(jnp.bfloat16), 'tp').astype(jnp.float32)  85.9 us
    all_gather x1, waiting for transfers between devices, local(): lax.all_gather(gate_weight, 'shard', axis=0, tiled=True)  83.8 us
  transfers between devices with their start and end apart: 20, of which 15 were waited for; matrix products, arithmetic and copies ran while one was open for 18% of the time, Pallas kernels for 0%

commit v1 on v0

v1 whole, which is shorter than its diff:
```python
import functools
import math

import jax
import jax.numpy as jnp
from jax import lax
from jax.experimental import pallas as pl
from jax.experimental.pallas import tpu as pltpu
from jax.sharding import PartitionSpec as P

HEAD = 128
EPSILON = 1e-06
THETA = 1000000.0
CLIP_BOUND = 4.0
NEG_FILL = -1e30
SCALE = HEAD ** (-0.5)
SCALE_2 = SCALE * math.log2(math.e)
MIB = 1 << 20
BF16 = jnp.bfloat16
F32 = jnp.float32


def dot_nt(left, right):
    return lax.dot_general(left, right, (((1,), (1,)), ((), ())), preferred_element_type=F32)


def dot_nn(left, right):
    return jnp.dot(left, right, preferred_element_type=F32)


def seen_block(hot, reach_rows, col_at, row_at, bk, bq):
    linked = dot_nt(hot, reach_rows) > 0.5
    cols = col_at + lax.broadcasted_iota(jnp.int32, (bk, bq), 0)
    rows = row_at + lax.broadcasted_iota(jnp.int32, (bk, bq), 1)
    return (linked & (cols <= rows)) | (cols == rows)


def attention_forward_kernel(
    group, bq, bk, blocks, count, chosen, places, q_ref, kv_ref, reach_ref, hot_ref,
    out_ref, lse_ref, top_ref, max_s, sum_s, acc_s,
):
    row_block = pl.program_id(0)
    max_s[...] = jnp.full_like(max_s, NEG_FILL)
    sum_s[...] = jnp.zeros_like(sum_s)
    acc_s[...] = jnp.zeros_like(acc_s)
    row_at = places[blocks] + row_block * bq

    def body(step, carry):
        block = chosen[row_block * blocks + step]
        here = pl.ds(pl.multiple_of(block * bk, bk), bk)
        keys = kv_ref[here, :HEAD]
        values_t = kv_ref[here, HEAD:].T
        seen = seen_block(hot_ref[here, :], reach_ref[...], places[block], row_at, bk, bq)
        for h in range(group):
            score = jnp.where(seen, dot_nt(keys, q_ref[:, h * HEAD : (h + 1) * HEAD]), NEG_FILL)
            old = max_s[h : h + 1, :]
            new = jnp.maximum(old, jnp.max(score, axis=0, keepdims=True))
            prob = jnp.exp2((score - new) * SCALE_2)
            fade = jnp.exp2((old - new) * SCALE_2)
            max_s[h : h + 1, :] = new
            sum_s[h : h + 1, :] = sum_s[h : h + 1, :] * fade + jnp.sum(prob, axis=0, keepdims=True)
            acc_s[h] = acc_s[h] * fade + dot_nn(values_t, prob.astype(BF16))
        return carry

    lax.fori_loop(0, count[row_block], body, 0)
    top_ref[...] = max_s[...] * SCALE
    lse_ref[...] = max_s[...] * SCALE_2 + jnp.log2(sum_s[...])
    for h in range(group):
        out_ref[:, h * HEAD : (h + 1) * HEAD] = (acc_s[h] / sum_s[h : h + 1, :]).T.astype(BF16)


def attention_forward(lists, queries, kv, reach_rows, hot, bq, bk):
    rows, width = queries.shape
    slots = kv.shape[0]
    group = width // HEAD
    whole = lambda *_: (0, 0)
    row = lambda i, *_: (i, 0)
    col = lambda i, *_: (0, i)
    return pl.pallas_call(
        functools.partial(attention_forward_kernel, group, bq, bk, slots // bk),
        grid_spec=pltpu.PrefetchScalarGridSpec(
            num_scalar_prefetch=3,
            grid=(rows // bq,),
            in_specs=[
                pl.BlockSpec((bq, width), row),
                pl.BlockSpec((slots, 2 * HEAD), whole),
                pl.BlockSpec((bq, HEAD), row),
                pl.BlockSpec((slots, HEAD), whole),
            ],
            out_specs=[
                pl.BlockSpec((bq, width), row),
                pl.BlockSpec((group, bq), col),
                pl.BlockSpec((group, bq), col),
            ],
            scratch_shapes=[
                pltpu.VMEM((group, bq), F32),
                pltpu.VMEM((group, bq), F32),
                pltpu.VMEM((group, HEAD, bq), F32),
            ],
        ),
        out_shape=[
            jax.ShapeDtypeStruct((rows, width), BF16),
            jax.ShapeDtypeStruct((group, rows), F32),
            jax.ShapeDtypeStruct((group, rows), F32),
        ],
        compiler_params=pltpu.CompilerParams(vmem_limit_bytes=32 * MIB),
        cost_estimate=pl.CostEstimate(
            flops=18_000_000_000, bytes_accessed=8_000_000, transcendentals=0
        ),
        name="attention_forward",
    )(*lists, queries, kv, reach_rows, hot)


def attention_backward_kernel(
    group, bq, bk, blocks, count, chosen, places, q_ref, do_ref, lse_ref, delta_ref, kv_ref,
    reach_ref, hot_ref, cos_ref, sin_ref, dq_ref, dkv_ref, acc_s, dk_s, dv_s,
):
    row_block = pl.program_id(0)

    @pl.when(row_block == 0)
    def _():
        dk_s[...] = jnp.zeros_like(dk_s)
        dv_s[...] = jnp.zeros_like(dv_s)

    acc_s[...] = jnp.zeros_like(acc_s)
    row_at = places[blocks] + row_block * bq

    def body(step, carry):
        block = chosen[row_block * blocks + step]
        here = pl.ds(pl.multiple_of(block * bk, bk), bk)
        keys = kv_ref[here, :HEAD]
        values = kv_ref[here, HEAD:]
        keys_t = keys.T
        seen = seen_block(hot_ref[here, :], reach_ref[...], places[block], row_at, bk, bq)
        dk = jnp.zeros((bk, HEAD), F32)
        dv = jnp.zeros((bk, HEAD), F32)
        for h in range(group):
            qh = q_ref[:, h * HEAD : (h + 1) * HEAD]
            doh = do_ref[:, h * HEAD : (h + 1) * HEAD]
            prob = jnp.where(
                seen, jnp.exp2(dot_nt(keys, qh) * SCALE_2 - lse_ref[h : h + 1, :]), 0.0
            )
            ds = (prob * (dot_nt(values, doh) - delta_ref[h : h + 1, :])).astype(BF16)
            dv = dv + dot_nn(prob.astype(BF16), doh)
            dk = dk + dot_nn(ds, qh)
            acc_s[h] = acc_s[h] + dot_nn(keys_t, ds)
        dk_s[here, :] += dk
        dv_s[here, :] += dv
        return carry

    lax.fori_loop(0, count[row_block], body, 0)
    for h in range(group):
        d_query = (acc_s[h] * SCALE).T
        dq_ref[:, h * HEAD : (h + 1) * HEAD] = turned(
            d_query, cos_ref[...], -sin_ref[...]
        ).astype(BF16)

    @pl.when(row_block == pl.num_programs(0) - 1)
    def _():
        dkv_ref[:, :HEAD] = (dk_s[...] * SCALE).astype(BF16)
        dkv_ref[:, HEAD:] = dv_s[...].astype(BF16)


def attention_backward(
    lists, queries, d_att, lse, delta, kv, reach_rows, hot, cosine, sine, bq, bk
):
    rows, width = queries.shape
    slots = kv.shape[0]
    group = width // HEAD
    whole = lambda *_: (0, 0)
    row = lambda i, *_: (i, 0)
    col = lambda i, *_: (0, i)
    return pl.pallas_call(
        functools.partial(attention_backward_kernel, group, bq, bk, slots // bk),
        grid_spec=pltpu.PrefetchScalarGridSpec(
            num_scalar_prefetch=3,
            grid=(rows // bq,),
            in_specs=[
                pl.BlockSpec((bq, width), row),
                pl.BlockSpec((bq, width), row),
                pl.BlockSpec((group, bq), col),
                pl.BlockSpec((group, bq), col),
                pl.BlockSpec((slots, 2 * HEAD), whole),
                pl.BlockSpec((bq, HEAD), row),
                pl.BlockSpec((slots, HEAD), whole),
                pl.BlockSpec((bq, HEAD), row),
                pl.BlockSpec((bq, HEAD), row),
            ],
            out_specs=[
                pl.BlockSpec((bq, width), row),
                pl.BlockSpec((slots, 2 * HEAD), whole),
            ],
            scratch_shapes=[
                pltpu.VMEM((group, HEAD, bq), F32),
                pltpu.VMEM((slots, HEAD), F32),
                pltpu.VMEM((slots, HEAD), F32),
            ],
        ),
        out_shape=[
            jax.ShapeDtypeStruct((rows, width), BF16),
            jax.ShapeDtypeStruct((slots, 2 * HEAD), BF16),
        ],
        compiler_params=pltpu.CompilerParams(vmem_limit_bytes=40 * MIB),
        cost_estimate=pl.CostEstimate(
            flops=32_000_000_000, bytes_accessed=12_000_000, transcendentals=0
        ),
        name="attention_backward",
    )(*lists, queries, d_att, lse, delta, kv, reach_rows, hot, cosine, sine)


def join(mine, pieces, joined, at_col=None):
    depth, cols = pieces[0].shape
    where = slice(None) if at_col is None else pl.ds(pl.multiple_of(at_col, HEAD), cols)
    for j, piece in enumerate(pieces):
        joined[pl.ds(pl.multiple_of((mine ^ j) * depth, 16), depth), where] = piece[...]


def whole_block(*_):
    return (0, 0)


def row_block(i, *_):
    return (i, 0)


def col_block(i, *_):
    return (0, i)


def once(shape):
    return pl.BlockSpec(shape, whole_block, pipeline_mode=pl.Buffered(1))


def call(kernel, grid, in_specs, out_specs, out_shape, scratch, vmem, flops, size, name):
    return pl.pallas_call(
        kernel,
        grid_spec=pltpu.PrefetchScalarGridSpec(
            num_scalar_prefetch=1,
            grid=(grid,),
            in_specs=in_specs,
            out_specs=out_specs,
            scratch_shapes=scratch,
        ),
        out_shape=out_shape,
        compiler_params=pltpu.CompilerParams(vmem_limit_bytes=vmem * MIB),
        cost_estimate=pl.CostEstimate(flops=flops, bytes_accessed=size, transcendentals=0),
        name=name,
    )


def shape(dims, dtype):
    return jax.ShapeDtypeStruct(dims, dtype)


def ffn_middle_kernel(parts, tail, place, h_ref, c_ref, *refs):
    gates, ups, downs = refs[:parts], refs[parts : 2 * parts], refs[2 * parts : 3 * parts]
    act_ref, dg_ref, du_ref, dh_ref, gate_s, up_s, down_s, sum_s = refs[3 * parts :]
    step = pl.program_id(0)
    join(place[0], gates, gate_s)
    join(place[0], ups, up_s)
    join(place[0], downs, down_s)
    if tail:

        @pl.when(step == pl.num_programs(0) - 1)
        def _():
            for joined in (gate_s, up_s, down_s):
                joined[:, tail:] = jnp.zeros_like(joined[:, tail:])

    gate = dot_nn(h_ref[...], gate_s[...])
    up = dot_nn(h_ref[...], up_s[...])
    d_act = dot_nn(c_ref[...], down_s[...])
    sig = jax.nn.sigmoid(gate)
    silu = gate * sig
    act_ref[...] = (silu * up).astype(BF16)
    d_gate = (d_act * up * sig * (1.0 + gate * (1.0 - sig))).astype(BF16)
    d_up = (d_act * silu).astype(BF16)
    dg_ref[...] = d_gate
    du_ref[...] = d_up

    @pl.when(step == 0)
    def _():
        sum_s[...] = jnp.zeros_like(sum_s)

    sum_s[...] += dot_nt(d_gate, gate_s[...]) + dot_nt(d_up, up_s[...])

    @pl.when(step == pl.num_programs(0) - 1)
    def _():
        dh_ref[...] = sum_s[...].astype(BF16)


def ffn_middle(place, hidden, cotangent, gates, ups, downs, tf):
    rows, width = hidden.shape
    depth, units = gates[0].shape
    parts = len(gates)
    return call(
        functools.partial(ffn_middle_kernel, parts, units % tf),
        pl.cdiv(units, tf),
        [once((rows, width))] * 2 + [pl.BlockSpec((depth, tf), col_block)] * (3 * parts),
        [pl.BlockSpec((rows, tf), col_block)] * 3 + [once((rows, width))],
        [shape((rows, units), BF16)] * 3 + [shape((rows, width), BF16)],
        [pltpu.VMEM((width, tf), BF16)] * 3 + [pltpu.VMEM((rows, width), F32)],
        60,
        10 * rows * width * units,
        6 * width * units + 6 * rows * units,
        "ffn_middle",
    )(place, hidden, cotangent, *gates, *ups, *downs)


def weight_grad_kernel(depth, parts, place, left_ref, right_ref, keep_ref, send_ref):
    for j in range(parts):
        half = keep_ref if j % 2 == 0 else send_ref
        rows = pl.ds(pl.multiple_of((place[0] ^ j) * depth, 16), depth)
        at = (j // 2) * depth
        half[at : at + depth, :] = dot_nn(left_ref[rows, :], right_ref[...]).astype(BF16)


def weight_grad(place, left_t, right, parts, tf):
    width, rows = left_t.shape
    units = right.shape[1]
    return call(
        functools.partial(weight_grad_kernel, width // parts, parts),
        pl.cdiv(units, tf),
        [once((width, rows)), pl.BlockSpec((rows, tf), col_block)],
        [pl.BlockSpec((width // 2, tf), col_block)] * 2,
        [shape((width // 2, units), BF16)] * 2,
        [],
        48,
        2 * rows * width * units,
        2 * width * units + 2 * rows * units,
        "weight_grad",
    )(place, left_t, right)


def down_project_kernel(parts, place, act_ref, *refs):
    downs, (out_ref, down_s, sum_s) = refs[:parts], refs[parts:]
    step = pl.program_id(0)
    join(place[0], downs, down_s)

    @pl.when(step == 0)
    def _():
        sum_s[...] = jnp.zeros_like(sum_s)

    sum_s[...] += dot_nt(act_ref[...], down_s[...])

    @pl.when(step == pl.num_programs(0) - 1)
    def _():
        out_ref[...] = sum_s[...].astype(BF16)


def down_project(place, act, downs, tf):
    rows, units = act.shape
    parts = len(downs)
    depth = downs[0].shape[0]
    width = depth * parts
    return call(
        functools.partial(down_project_kernel, parts),
        units // tf,
        [pl.BlockSpec((rows, tf), col_block)] + [pl.BlockSpec((depth, tf), col_block)] * parts,
        once((rows, width)),
        shape((rows, width), BF16),
        [pltpu.VMEM((width, tf), BF16), pltpu.VMEM((rows, width), F32)],
        48,
        2 * rows * width * units,
        2 * width * units + 2 * rows * units,
        "down_project",
    )(place, act, *downs)


def inverse_rms(values):
    return lax.rsqrt(jnp.mean(values * values, axis=-1, keepdims=True) + EPSILON)


def turned(values, cosine, sine):
    return values * cosine + pltpu.roll(values, HEAD // 2, 1) * sine


def mix_kernel(parts, group, place, x_ref, gain_ref, bias_ref, cos_ref, sin_ref, *refs):
    pieces, (q_ref, kv_ref, ht_ref, weight_s) = refs[:parts], refs[parts:]

    @pl.when(pl.program_id(0) == 0)
    def _():
        join(place[0], pieces, weight_s)

    x = x_ref[...].astype(F32)
    hidden = (x * inverse_rms(x) * gain_ref[...].astype(F32)).astype(BF16)
    ht_ref[...] = hidden.T
    mixed = dot_nn(hidden, weight_s[...]) + bias_ref[...].astype(F32)
    cosine, sine = cos_ref[...], sin_ref[...]
    for h in range(group):
        at = slice(h * HEAD, (h + 1) * HEAD)
        q_ref[:, at] = turned(mixed[:, at], cosine, sine).astype(BF16)
    split = group * HEAD
    kv_ref[:, :HEAD] = turned(mixed[:, split : split + HEAD], cosine, sine).astype(BF16)
    kv_ref[:, HEAD:] = mixed[:, split + HEAD :].astype(BF16)


def mix(place, tokens, gain, bias, cosine, sine, pieces, group, bq):
    rows, width = tokens.shape
    depth, cols = pieces[0].shape
    parts = len(pieces)
    return call(
        functools.partial(mix_kernel, parts, group),
        rows // bq,
        [
            pl.BlockSpec((bq, width), row_block),
            once((1, width)),
            once((1, cols)),
            pl.BlockSpec((bq, HEAD), row_block),
            pl.BlockSpec((bq, HEAD), row_block),
        ]
        + [once((depth, cols))] * parts,
        [
            pl.BlockSpec((bq, group * HEAD), row_block),
            pl.BlockSpec((bq, 2 * HEAD), row_block),
            pl.BlockSpec((width, bq), col_block),
        ],
        [
            shape((rows, group * HEAD), BF16),
            shape((rows, 2 * HEAD), BF16),
            shape((width, rows), BF16),
        ],
        [pltpu.VMEM((width, cols), BF16)],
        32,
        2 * rows * width * cols,
        2 * width * cols + 10 * rows * width,
        "mix",
    )(place, tokens, gain[None], bias[None], cosine, sine, *pieces)


def branch_kernel(parts, place, x_ref, own_ref, other_ref, gain_ref, *refs):
    own_w, other_w = refs[:parts], refs[parts : 2 * parts]
    mid_ref, h_ref, ht_ref, weight_s, att_s = refs[2 * parts :]
    split = own_ref.shape[1]
    own_at = pl.multiple_of(place[1] * split, HEAD)
    other_at = pl.multiple_of((1 - place[1]) * split, HEAD)

    @pl.when(pl.program_id(0) == 0)
    def _():
        join(place[0], own_w, weight_s, own_at)
        join(place[0], other_w, weight_s, other_at)

    att_s[:, pl.ds(own_at, split)] = own_ref[...]
    att_s[:, pl.ds(other_at, split)] = other_ref[...]
    mid = x_ref[...].astype(F32) + dot_nt(att_s[...], weight_s[...])
    mid_ref[...] = mid
    hidden = (mid * inverse_rms(mid) * gain_ref[...].astype(F32)).astype(BF16)
    h_ref[...] = hidden
    ht_ref[...] = hidden.T


def branch(place, tokens, own, other, gain, own_pieces, other_pieces, bq):
    rows, width = tokens.shape
    depth, cols = own_pieces[0].shape
    parts = len(own_pieces)
    wide = pl.BlockSpec((bq, width), row_block)
    narrow = pl.BlockSpec((bq, cols), row_block)
    return call(
        functools.partial(branch_kernel, parts),
        rows // bq,
        [wide, narrow, narrow, once((1, width))] + [once((depth, cols))] * (2 * parts),
        [wide, wide, pl.BlockSpec((width, bq), col_block)],
        [shape((rows, width), F32), shape((rows, width), BF16), shape((width, rows), BF16)],
        [pltpu.VMEM((width, 2 * cols), BF16), pltpu.VMEM((bq, 2 * cols), BF16)],
        40,
        4 * rows * width * cols,
        4 * width * cols + 14 * rows * width,
        "branch",
    )(place, tokens, own, other, gain[None], *own_pieces, *other_pieces)


def middle_back_kernel(
    parts, group, place, own_ref, other_ref, mid_ref, c_ref, gain_ref, att_ref, *refs
):
    pieces, (dm_ref, dbt_ref, da_ref, delta_ref, dgain_ref, weight_s) = refs[:parts], refs[parts:]

    @pl.when(pl.program_id(0) == 0)
    def _():
        join(place[0], pieces, weight_s)
        dgain_ref[...] = jnp.zeros_like(dgain_ref)

    mid = mid_ref[...]
    inverse = inverse_rms(mid)
    normed = mid * inverse
    own = own_ref[...].astype(F32)
    dgain_ref[...] += jnp.sum(own * normed, axis=0, keepdims=True)
    scaled = (own + other_ref[...].astype(F32)) * gain_ref[...].astype(F32)
    d_mid = c_ref[...].astype(F32) + inverse * (
        scaled - normed * jnp.mean(scaled * normed, axis=-1, keepdims=True)
    )
    dm_ref[...] = d_mid
    d_branch = d_mid.astype(BF16)
    dbt_ref[...] = d_branch.T
    d_att = dot_nn(d_branch, weight_s[...]).astype(BF16)
    da_ref[...] = d_att
    product = d_att.astype(F32) * att_ref[...].astype(F32)
    for h in range(group):
        delta_ref[h : h + 1, :] = jnp.sum(
            product[:, h * HEAD : (h + 1) * HEAD].T, axis=0, keepdims=True
        )


def middle_back(place, own, other, mid, cotangent, gain, attended, pieces, bq):
    rows, width = mid.shape
    depth, cols = pieces[0].shape
    parts = len(pieces)
    group = cols // HEAD
    wide = pl.BlockSpec((bq, width), row_block)
    narrow = pl.BlockSpec((bq, cols), row_block)
    return call(
        functools.partial(middle_back_kernel, parts, group),
        rows // bq,
        [wide, wide, wide, wide, once((1, width)), narrow] + [once((depth, cols))] * parts,
        [
            wide,
            pl.BlockSpec((width, bq), col_block),
            narrow,
            pl.BlockSpec((group, bq), col_block),
            pl.BlockSpec((1, width), whole_block),
        ],
        [
            shape((rows, width), F32),
            shape((width, rows), BF16),
            shape((rows, cols), BF16),
            shape((group, rows), F32),
            shape((1, width), F32),
        ],
        [pltpu.VMEM((width, cols), BF16)],
        48,
        2 * rows * width * cols,
        2 * width * cols + 18 * rows * width,
        "middle_back",
    )(place, own, other, mid, cotangent, gain[None], attended, *pieces)


def mix_back_kernel(
    parts, group, place, dq_ref, dkv_ref, cos_ref, sin_ref, x_ref, *refs
):
    pieces, (dm_ref, dh_ref, dbias_ref, dgain_ref, weight_s) = refs[:parts], refs[parts:]

    @pl.when(pl.program_id(0) == 0)
    def _():
        join(place[0], pieces, weight_s)
        dgain_ref[...] = jnp.zeros_like(dgain_ref)
        dbias_ref[...] = jnp.zeros_like(dbias_ref)

    split = group * HEAD
    dm_ref[:, :split] = dq_ref[...]
    d_keys = dkv_ref[:, :HEAD].astype(F32)
    dm_ref[:, split : split + HEAD] = turned(d_keys, cos_ref[...], -sin_ref[...]).astype(BF16)
    dm_ref[:, split + HEAD :] = dkv_ref[:, HEAD:]
    d_mixed = dm_ref[...]
    dbias_ref[...] += jnp.sum(d_mixed.astype(F32), axis=0, keepdims=True)
    d_hidden = dot_nt(d_mixed, weight_s[...])
    x = x_ref[...].astype(F32)
    dgain_ref[...] += jnp.sum(d_hidden * (x * inverse_rms(x)), axis=0, keepdims=True)
    dh_ref[...] = d_hidden.astype(BF16)


def mix_back(place, dq, dkv, cosine, sine, tokens, pieces, bq):
    rows, width = tokens.shape
    depth, cols = pieces[0].shape
    parts = len(pieces)
    group = dq.shape[1] // HEAD
    wide = pl.BlockSpec((bq, width), row_block)
    return call(
        functools.partial(mix_back_kernel, parts, group),
        rows // bq,
        [
            pl.BlockSpec((bq, group * HEAD), row_block),
            pl.BlockSpec((bq, 2 * HEAD), row_block),
            pl.BlockSpec((bq, HEAD), row_block),
            pl.BlockSpec((bq, HEAD), row_block),
            wide,
        ]
        + [once((depth, cols))] * parts,
        [
            pl.BlockSpec((bq, cols), row_block),
            wide,
            pl.BlockSpec((1, cols), whole_block),
            pl.BlockSpec((1, width), whole_block),
        ],
        [
            shape((rows, cols), BF16),
            shape((rows, width), BF16),
            shape((1, cols), F32),
            shape((1, width), F32),
        ],
        [pltpu.VMEM((width, cols), BF16)],
        32,
        2 * rows * width * cols,
        2 * width * cols + 8 * rows * width,
        "mix_back",
    )(place, dq, dkv, cosine, sine, tokens, *pieces)


def input_back_kernel(place, own_ref, other_ref, x_ref, gain_ref, dm_ref, out_ref):
    x = x_ref[...].astype(F32)
    inverse = inverse_rms(x)
    normed = x * inverse
    scaled = (own_ref[...].astype(F32) + other_ref[...].astype(F32)) * gain_ref[...].astype(F32)
    out_ref[...] = dm_ref[...] + inverse * (
        scaled - normed * jnp.mean(scaled * normed, axis=-1, keepdims=True)
    )


def input_back(place, own, other, tokens, gain, d_mid, bq):
    rows, width = tokens.shape
    wide = pl.BlockSpec((bq, width), row_block)
    return call(
        input_back_kernel,
        rows // bq,
        [wide, wide, wide, once((1, width)), wide],
        wide,
        shape((rows, width), F32),
        [],
        32,
        20 * rows * width,
        14 * rows * width,
        "input_back",
    )(place, own, other, tokens, gain[None], d_mid)


def after(values, *first):
    return lax.optimization_barrier((values, first))[0]


def swap(value, axis, size, bit):
    return lax.ppermute(value, axis, [(i, i ^ bit) for i in range(size)])


def gather_pieces(own, size):
    pieces = {0: own}
    bit = size // 2
    while bit:
        pieces.update({j ^ bit: swap(p, "shard", size, bit) for j, p in pieces.items()})
        bit //= 2
    return [pieces[j] for j in range(size)]


def sum_over_ctx(value, size):
    if size != 4:
        return lax.psum(value, "ctx").astype(F32)
    place = lax.axis_index("ctx")
    inner = value + lax.ppermute(value, "ctx", [(0, 1), (3, 2)])
    total = inner + lax.ppermute(inner, "ctx", [(1, 2), (2, 1)])
    outer = lax.ppermute(total, "ctx", [(1, 0), (2, 3)])
    middle = (place == 1) | (place == 2)
    return jnp.where(middle, total, outer).astype(F32)


def reduce_rows(halves, shards, contexts):
    keep, send = halves
    held = [keep, swap(send, "shard", shards, 1)]
    bit = 2
    while bit < shards:
        count = shards // bit
        size = keep.shape[0] // (bit // 2) // count

        def pick(odd):
            return [
                sum(part[at * size : (at + 1) * size] for part in held)
                for at in range(odd, count, 2)
            ]

        away, here = pick(1), pick(0)
        away = away[0] if len(away) == 1 else jnp.concatenate(away, axis=0)
        here = here[0] if len(here) == 1 else jnp.concatenate(here, axis=0)
        held = [here, swap(away, "shard", shards, bit)]
        bit *= 2
    return sum_over_ctx(sum(held), contexts)


def sum_of_all(value, sizes):
    for axis, size in sizes.items():
        bit = 1
        while bit < size:
            value = value + swap(value, axis, size, bit)
            bit *= 2
    return value


def tree_tables(seg_row, parent_row):
    seg_count = parent_row.shape[0]
    seg_ids = jnp.arange(seg_count, dtype=jnp.int32)
    one_hot = (seg_row[:, None] == seg_ids[None, :]).astype(jnp.int32)
    lengths = jnp.sum(one_hot, axis=0, dtype=jnp.int32)
    before = seg_ids[None, :] < seg_ids[:, None]
    starts = jnp.sum(jnp.where(before, lengths[None, :], 0), axis=1, dtype=jnp.int32)
    link = (parent_row[:, None] == seg_ids[None, :]) & (parent_row[:, None] != seg_ids[:, None])
    twice = jnp.any(link[:, :, None] & link[None, :, :], axis=1)
    strict = link | twice
    padding = parent_row == seg_ids
    reach = strict | ((seg_ids[:, None] == seg_ids[None, :]) & ~padding[:, None])
    offsets = jnp.sum(jnp.where(strict, lengths[None, :], 0), axis=1, dtype=jnp.int32) - starts
    return reach, offsets


def block_lists(row_hot, col_hot, reach, col_places, row_first, bq, bk):
    segs = reach.shape[0]
    row_has = jnp.any(row_hot.reshape(-1, bq, segs), axis=1)
    col_has = jnp.any(col_hot.reshape(-1, bk, segs), axis=1)
    row_blocks, col_blocks = row_has.shape[0], col_has.shape[0]
    row_reach = jnp.any(row_has[:, :, None] & reach[None], axis=1)
    meets = jnp.any(row_reach[:, None, :] & col_has[None], axis=2)
    col_at = col_places.reshape(-1, bk)[:, 0]
    row_at = row_first + bq * jnp.arange(row_blocks, dtype=jnp.int32)
    causal = col_at[None, :] < row_at[:, None] + bq
    diagonal = causal & (col_at[None, :] + bk > row_at[:, None])
    active = ((meets & causal) | diagonal) & (col_at >= 0)[None, :]
    ids = jnp.arange(col_blocks, dtype=jnp.int32)
    rank = jnp.sum(
        (active[:, None, :] & (ids[None, :] < ids[:, None])[None]).astype(jnp.int32), axis=2
    )
    placed = active[:, :, None] & (rank[:, :, None] == ids[None, None, :])
    chosen = jnp.sum(jnp.where(placed, ids[None, :, None], 0), axis=1, dtype=jnp.int32)
    count = jnp.sum(active.astype(jnp.int32), axis=1, dtype=jnp.int32)
    places = jnp.concatenate([col_at, row_first[None]])
    return count, chosen.reshape(-1), places


def layer(
    sizes, tokens, cotangent, segment, parent, gain_attn, qkv_weight, qkv_bias,
    out_weight, gain_ffn, gate_weight, up_weight, down_weight,
):
    shards, contexts, halves = sizes["shard"], sizes["ctx"], sizes["tp"]
    rows, width = tokens.shape
    group = out_weight.shape[1] // HEAD
    shard, ctx, half = lax.axis_index("shard"), lax.axis_index("ctx"), lax.axis_index("tp")
    place = jnp.stack([shard, half]).astype(jnp.int32)
    across = [(i, i ^ 1) for i in range(halves)]

    qkv_pieces = gather_pieces(qkv_weight, shards)
    out_pieces = gather_pieces(after(out_weight, qkv_pieces[-1]), shards)
    gate_pieces = gather_pieces(after(gate_weight, qkv_pieces[-1]), shards)
    up_pieces = gather_pieces(after(up_weight, out_pieces[-1]), shards)
    down_pieces = gather_pieces(after(down_weight, gate_pieces[-1]), shards)
    out_other = [lax.ppermute(piece, "tp", across) for piece in out_pieces]

    row_first = (ctx * rows).astype(jnp.int32)
    reach, offsets = tree_tables(segment[0], parent[0])
    seg_ids = jnp.arange(reach.shape[0], dtype=jnp.int32)
    behind = [jnp.maximum(ctx - k, 0) * rows for k in range(contexts)]
    seg_back = jnp.concatenate(
        [lax.dynamic_slice_in_dim(segment[0], at, rows, 0) for at in behind]
    )
    places_back = jnp.concatenate(
        [(ctx - k) * rows + jnp.arange(rows, dtype=jnp.int32) for k in range(contexts)]
    )
    col_hot = seg_back[:, None] == seg_ids[None, :]
    row_hot = col_hot[:rows]
    own_pos = places_back[:rows] + jnp.sum(
        jnp.where(row_hot, offsets[None, :], 0), axis=1, dtype=jnp.int32
    )
    pad = ((0, 0), (0, HEAD - reach.shape[0]))
    row_reach = jnp.any(row_hot[:, :, None] & reach[None], axis=1)
    reach_rows = jnp.pad(row_reach.astype(BF16), pad)
    hot = jnp.pad(col_hot.astype(BF16), pad)
    bq = math.gcd(rows, 256)
    bk_f, bk_b = math.gcd(rows, 128), math.gcd(rows, 512)
    lists_f = block_lists(row_hot, col_hot, reach, places_back, row_first, bq, bk_f)
    lists_b = block_lists(row_hot, col_hot, reach, places_back, row_first, bq, bk_b)
    lane = jnp.arange(HEAD, dtype=jnp.int32)
    frequency = THETA ** (-2.0 * (lane % (HEAD // 2)).astype(F32) / HEAD)
    angles = own_pos.astype(F32)[:, None] * frequency[None, :]
    cosine = jnp.cos(angles)
    sine = jnp.sin(angles) * jnp.where(lane < HEAD // 2, -1.0, 1.0)

    queries, kv_own, hidden_one_t = mix(
        place, tokens, gain_attn, qkv_bias, cosine, sine, qkv_pieces, group, bq
    )
    rightward = [(i, i + 1) for i in range(contexts - 1)]
    leftward = [(i + 1, i) for i in range(contexts - 1)]
    kv_blocks = [kv_own]
    for _ in range(contexts - 1):
        kv_blocks.append(lax.ppermute(kv_blocks[-1], "ctx", rightward))
    kv_back = jnp.concatenate(kv_blocks, axis=0)
    attended, lse, tops = attention_forward(lists_f, queries, kv_back, reach_rows, hot, bq, bk_f)
    attended_other = lax.ppermute(attended, "tp", across)
    mid, hidden_two, hidden_two_t = branch(
        place, tokens, attended, attended_other, gain_ffn, out_pieces, out_other, bq
    )
    top_grad_t = cotangent.T
    act, d_gate, d_up, d_hidden_two = ffn_middle(
        place, hidden_two, cotangent, gate_pieces, up_pieces, down_pieces, 512
    )

    d_hidden_two_other = lax.ppermute(d_hidden_two, "tp", across)
    gate_halves = weight_grad(place, hidden_two_t, d_gate, shards, 512)
    up_halves = weight_grad(place, after(hidden_two_t, gate_halves), d_up, shards, 512)
    down_halves = weight_grad(place, after(top_grad_t, up_halves), act, shards, 512)
    ffn_own = down_project(place, after(act, down_halves), down_pieces, 896)
    ffn_other = lax.ppermute(ffn_own, "tp", across)
    output = (mid + (ffn_own.astype(F32) + ffn_other.astype(F32))).astype(BF16)
    gate_total = reduce_rows(gate_halves, shards, contexts)
    up_total = reduce_rows(up_halves, shards, contexts)
    down_total = reduce_rows(down_halves, shards, contexts)

    d_hidden_two_other = after(d_hidden_two_other, ffn_own)
    d_mid, d_branch_t, d_att, delta, gain_two_part = middle_back(
        place, d_hidden_two, d_hidden_two_other, mid, cotangent, gain_ffn, attended, out_pieces, bq
    )
    d_query, d_kv = attention_backward(
        lists_b, queries, d_att, lse, delta, kv_back, reach_rows, hot, cosine, sine, bq, bk_b
    )
    d_kv_own = d_kv[(contexts - 1) * rows :]
    for k in range(contexts - 2, -1, -1):
        d_kv_own = d_kv[k * rows : (k + 1) * rows] + lax.ppermute(d_kv_own, "ctx", leftward)
    out_halves = weight_grad(place, after(d_branch_t, d_kv), attended, shards, 768)
    out_total = reduce_rows(out_halves, shards, contexts)
    d_mixed, d_hidden_one, bias_part, gain_one_part = mix_back(
        place, d_query, d_kv_own, cosine, sine, tokens, qkv_pieces, bq
    )
    d_hidden_one_other = lax.ppermute(d_hidden_one, "tp", across)
    qkv_halves = weight_grad(place, hidden_one_t, d_mixed, shards, 512)
    qkv_total = reduce_rows(qkv_halves, shards, contexts)
    input_grad = input_back(place, d_hidden_one, d_hidden_one_other, tokens, gain_attn, d_mid, bq)

    peak_own = jnp.max(tops, axis=1)
    device = shard * contexts + ctx
    spread = jnp.where(
        (jnp.arange(shards * contexts)[:, None, None] == device)
        & (jnp.arange(halves)[None, :, None] == half),
        peak_own[None, None, :],
        0.0,
    )
    bias_both = jnp.where(jnp.arange(halves)[:, None] == half, bias_part, 0.0)
    vector = jnp.concatenate(
        [gain_one_part[0], gain_two_part[0], bias_both.reshape(-1), spread.reshape(-1)]
    )
    vector = sum_of_all(vector, sizes)
    bias_at = 2 * width
    spread_at = bias_at + bias_both.size
    bias_grad = lax.dynamic_slice_in_dim(
        vector[bias_at:spread_at], half * bias_part.size, bias_part.size, 0
    )
    peaks = jnp.max(vector[spread_at:].reshape(shards * contexts, halves, group), axis=0)
    peak_all = lax.dynamic_index_in_dim(peaks, half, 0, keepdims=False)
    clip_out = CLIP_BOUND / jnp.maximum(peak_all, CLIP_BOUND)
    return (
        output,
        input_grad,
        vector[:width],
        qkv_total,
        bias_grad,
        out_total,
        vector[width:bias_at],
        gate_total,
        up_total,
        down_total,
        clip_out,
    )


def solution(mesh):
    token = P(("shard", "ctx"), None)
    weight = P("shard", "tp")
    return jax.shard_map(
        functools.partial(layer, dict(mesh.shape)),
        mesh=mesh,
        in_specs=(
            token,
            token,
            P("shard", None),
            P("shard", None),
            P(),
            weight,
            P("tp"),
            weight,
            P(),
            weight,
            weight,
            weight,
        ),
        out_specs=(
            token,
            token,
            P(),
            weight,
            P("tp"),
            weight,
            P(),
            weight,
            weight,
            weight,
            P("tp"),
        ),
        check_vma=False,
    )
```

time: 2490 us -> 1340 us (0.54)
  waiting for transfers between devices: 1510 us -> 769 us
  matrix products: 640 us -> 0 us
  Pallas kernels: 0 us -> 263 us
  starting transfers between devices: 1.55 us -> 143 us
  blocking collectives: 134 us -> 0 us
    reduce_scatter x7 -> x0, waiting for transfers between devices: 778 us -> none  [the longest x1 264 us: local(): lax.psum_scatter(grad_up, ('shard', 'ctx'), scatter_dimension=0, tiled=True)]
    ppermute x0 -> x59, waiting for transfers between devices: none -> 769 us  [the longest x30 458 us: swap(): return lax.ppermute(value, axis, [(i, i ^ bit) for i in range(size)])]
    dot_general x58 -> x0, matrix products: 640 us -> none  [the longest x8 93.3 us: block_scores(): jnp.einsum('igd,jd->gij', queries, key_blk, preferred_element_type=jnp.fl...]
    all_gather x10 -> x0, waiting for transfers between devices: 444 us -> none  [the longest x1 83.8 us: local(): lax.all_gather(gate_weight, 'shard', axis=0, tiled=True)]
    psum x3 -> x0, waiting for transfers between devices: 286 us -> none  [the longest x1 117 us: local(): lax.psum(contract_cols(inner_act, full_down).astype(jnp.bfloat16), 'tp')]
    pallas_call x0 -> x14, Pallas kernels: none -> 263 us  [the longest x1 93.7 us: ffn_middle(): call(functools.partial(ffn_middle_kernel, parts, units % tf), pl.cdiv(uni...]
    ppermute x0 -> x59, starting transfers between devices: none -> 143 us  [the longest x5 67.6 us: sum_over_ctx(): inner = value + lax.ppermute(value, 'ctx', [(0, 1), (3, 2)])]
    psum x2 -> x0, blocking collectives: 64.3 us -> none  [the longest x1 59.3 us: local(): lax.psum((gain_one_grad, gain_two_grad, bias_part), ('shard', 'ctx'))]
  transfers between devices with their start and end apart: 20 -> 59, of which waited for: 15 -> 26; matrix products, arithmetic and copies ran while one was open for 18% -> 8% of each run, Pallas kernels for 0% -> 11%
where the time goes in v1:
time: 1340 us; the launch traced here: 1320 us
  waiting for transfers between devices  769 us (57%)
  Pallas kernels  263 us (20%)
  starting transfers between devices  143 us (11%)
  other arithmetic  103 us (8%)
  local copies, waits for them, and re-layouts  43.4 us (3%)
    ppermute x30, waiting for transfers between devices, swap(): return lax.ppermute(value, axis, [(i, i ^ bit) for i in range(size)])  458 us
    ppermute x5, waiting for transfers between devices, sum_over_ctx(): outer = lax.ppermute(total, 'ctx', [(1, 0), (2, 3)])  155 us
    pallas_call x1, Pallas kernels, ffn_middle(): call(functools.partial(ffn_middle_kernel, parts, units % tf), pl.cdiv(uni...  93.7 us
    ppermute x4, waiting for transfers between devices, layer(): out_other = [lax.ppermute(piece, 'tp', across) for piece in out_pieces]  73.7 us
    pallas_call x5, Pallas kernels, weight_grad(): call(functools.partial(weight_grad_kernel, width // parts, parts), pl.cdi...  70.3 us
    ppermute x5, starting transfers between devices, sum_over_ctx(): inner = value + lax.ppermute(value, 'ctx', [(0, 1), (3, 2)])  67.6 us
    unnamed x159, local copies, waits for them, and re-layouts  36.4 us
    ppermute x30, starting transfers between devices, swap(): return lax.ppermute(value, axis, [(i, i ^ bit) for i in range(size)])  32.3 us
  transfers between devices with their start and end apart: 59, of which 26 were waited for; matrix products, arithmetic and copies ran while one was open for 8% of the time, Pallas kernels for 11%

profile of v1, /device:TPU:0, one launch (start us, length us, event | category | flops | bytes accessed | tf_op | source)
XLA Modules:
  0.0 1324.3 jit_solution(14777385240021720566)
XLA Ops:
  0.6 3.0 collective-permute-start.1
  3.6 17.8 %collective-permute-done.1.refs_2_ = bf16[384,1024]{1,0:T(8,128)(2,1)S(1)} collective-permute-done((bf16[384,1024]{1,0:T(8,128)(2,1)}, bf16[384,1024]{1,0:T(8,128)(2,1)S(1)}, u32[]{:S(2)}, u32[]{:S(2)}) %collective-permute-start.1) | collective-permute-done | bytes 786464 | tf_op jit(solution)/shard_map/ppermute | solution.py:628
  36.0 64.5 %collective-permute-done.15.refs_2_ = bf16[384,4480]{1,0:T(8,128)(2,1)} collective-permute-done((bf16[384,4480]{1,0:T(8,128)(2,1)}, bf16[384,4480]{1,0:T(8,128)(2,1)}, u32[]{:S(2)}, u32[]{:S(2)}) %collective-permute-start.15) | collective-permute-done | bytes 3440672 | tf_op jit(solution)/shard_map/ppermute | solution.py:628
  108.2 6.3 mix.1
  116.2 3.7 collective-permute-start.3
  121.8 9.9 collective-permute-done.3
  131.7 5.2 collective-permute-start.4
  137.4 9.8 collective-permute-done.4
  147.1 5.6 collective-permute-start.5
  157.9 4.2 collective-permute-done.5
  163.2 12.8 attention_forward.1
  181.7 44.4 %collective-permute-done.10.refs_4_ = bf16[384,768]{1,0:T(8,128)(2,1)S(1)} collective-permute-done((bf16[384,768]{1,0:T(8,128)(2,1)S(1)}, bf16[384,768]{1,0:T(8,128)(2,1)S(1)}, u32[]{:S(2)}, u32[]{:S(2)}) %collective-permute-start.10) | collective-permute-done | bytes 589856 | tf_op jit(solution)/shard_map/ppermute | solution.py:737
  228.5 10.3 collective-permute-done.11.refs_5_
  241.1 10.3 collective-permute-done.12.refs_6_
  252.2 8.7 collective-permute-done.13.refs_7_
  263.4 42.1 %collective-permute-done.21.refs_10_.refs_2_ = bf16[384,4480]{1,0:T(8,128)(2,1)} collective-permute-done((bf16[384,4480]{1,0:T(8,128)(2,1)}, bf16[384,4480]{1,0:T(8,128)(2,1)}, u32[]{:S(2)}, u32[]{:S(2)}) %collective-permute-start.21) | collective-permute-done | bytes 3440672 | tf_op jit(solution)/shard_map/ppermute | solution.py:628
  305.4 3.2 copy.36
  321.5 10.4 branch.1
  335.2 93.7 %ffn_middle.1 = (bf16[1024,4480]{1,0:T(8,128)(2,1)}, bf16[1024,4480]{1,0:T(8,128)(2,1)}, bf16[1024,4480]{1,0:T(8,128)(2,1)}, bf16[1024,1536]{1,0:T(8,128)(2,1)}) custom-call(s32[2]{0:T(128)} %copy-done.33, bf16[1024,1536]{1,0:T(8,128)(2,1)} %copy-done.62, bf16[1024,1536]{1,0:T(8,128)(2,1)} %c_ref.3, bf16[384,4480]{1,0:T(8,128)(2,1)} %refs_0_.4, ...), custom_call_target="tpu_custom_call" | custom-call | flops 70464307200 | bytes 68812800 | tf_op jit(solution)/shard_map/ffn_middle/pallas_call | solution.py:295
  430.8 19.4 %weight_grad.5 = (bf16[768,4480]{1,0:T(8,128)(2,1)}, bf16[768,4480]{1,0:T(8,128)(2,1)}) custom-call(s32[2]{0:T(128)S(1)} %copy-done.34, bf16[1536,1024]{1,0:T(8,128)(2,1)S(1)} %copy-done.61, bf16[1024,4480]{1,0:T(8,128)(2,1)} %get-tuple-element.65.right_ref), custom_call_target="tpu_custom_call" | custom-call | flops 14092861440 | bytes 22937600 | tf_op jit(solution)/shard_map/weight_grad/pallas_call | solution.py:320
  452.3 19.2 %weight_grad.6 = (bf16[768,4480]{1,0:T(8,128)(2,1)}, bf16[768,4480]{1,0:T(8,128)(2,1)}) custom-call(s32[2]{0:T(128)S(1)} %copy-done.34, bf16[1536,1024]{1,0:T(8,128)(2,1)S(1)} %copy-done.61, bf16[1024,4480]{1,0:T(8,128)(2,1)} %get-tuple-element.69.right_ref), custom_call_target="tpu_custom_call" | custom-call | flops 14092861440 | bytes 22937600 | tf_op jit(solution)/shard_map/weight_grad/pallas_call | solution.py:320
  471.5 19.2 %weight_grad.7 = (bf16[768,4480]{1,0:T(8,128)(2,1)}, bf16[768,4480]{1,0:T(8,128)(2,1)}) custom-call(s32[2]{0:T(128)S(1)} %copy-done.34, bf16[1536,1024]{1,0:T(8,128)(2,1)S(1)} %bitcast.28, bf16[1024,4480]{1,0:T(8,128)(2,1)} %get-tuple-element.75.right_ref.act_ref), custom_call_target="tpu_custom_call" | custom-call | flops 14092861440 | bytes 22937600 | tf_op jit(solution)/shard_map/weight_grad/pallas_call | solution.py:320
  491.3 24.1 %down_project.1 = bf16[1024,1536]{1,0:T(8,128)(2,1)} custom-call(s32[2]{0:T(128)S(1)} %copy-done.34, bf16[1024,4480]{1,0:T(8,128)(2,1)} %get-tuple-element.75.right_ref.act_ref, bf16[384,4480]{1,0:T(8,128)(2,1)} %refs_0_.5, bf16[384,4480]{1,0:T(8,128)(2,1)} %collective-permute-done.20.refs_9_.refs_1_, ...), custom_call_target="tpu_custom_call" | custom-call | flops 14092861440 | bytes 22937600 | tf_op jit(solution)/shard_map/down_project/pallas_call | solution.py:355
  515.4 5.5 collective-permute-done.24.other_ref
  521.0 13.0 middle_back.1
  534.1 18.1 %attention_backward.1 = (bf16[1024,768]{1,0:T(8,128)(2,1)S(1)}, bf16[4096,256]{1,0:T(8,128)(2,1)S(1)}) custom-call(s32[4]{0:T(128)S(1)} %get-tuple-element.99.count, s32[32]{0:T(128)S(1)} %reshape.675.chosen, s32[9]{0:T(128)S(1)} %pad_add_fusion.11.places, bf16[1024,768]{1,0:T(8,128)(2,1)S(1)} %copy-done.59, bf16[1024,768]{1,0:T(8,128)(2,1)S(1)} %get-tuple-element.78.do_ref, ...), custom_call_target="tpu_custom_call" | custom-call | flops 32000000000 | bytes 12000000 | tf_op jit(solution)/shard_map/attention_backward/pallas_call | solution.py:173
  553.6 3.4 slice_add_fusion.4
  558.6 3.4 slice_add_fusion.2
  562.5 16.0 %collective-permute-done.25 = bf16[1024,256]{1,0:T(8,128)(2,1)S(1)} collective-permute-done((bf16[1024,256]{1,0:T(8,128)(2,1)S(1)}, bf16[1024,256]{1,0:T(8,128)(2,1)S(1)}, u32[]{:S(2)}, u32[]{:S(2)}) %collective-permute-start.25) | collective-permute-done | bytes 524320 | tf_op jit(solution)/shard_map/ppermute | solution.py:807
  580.2 3.7 slice_add_fusion
  585.5 8.0 collective-permute-done.26
  595.6 38.9 %collective-permute-done.45 = bf16[384,4480]{1,0:T(8,128)(2,1)} collective-permute-done((bf16[384,4480]{1,0:T(8,128)(2,1)S(1)}, bf16[384,4480]{1,0:T(8,128)(2,1)}, u32[]{:S(2)}, u32[]{:S(2)}) %collective-permute-start.45) | collective-permute-done | bytes 3440672 | tf_op jit(solution)/shard_map/ppermute | solution.py:628
  634.6 4.6 fusion.2
  639.2 17.4 %collective-permute-start.46 = (bf16[384,4480]{1,0:T(8,128)(2,1)}, bf16[384,4480]{1,0:T(8,128)(2,1)}, u32[]{:S(2)}, u32[]{:S(2)}) collective-permute-start(bf16[384,4480]{1,0:T(8,128)(2,1)} %fusion.2), channel_id=1, source_target_pairs={{0,2},{6,4},{1,3},{7,5},{8,10},{14,12},{9,11},{15,13},{16,18},{22,... | collective-permute-start | bytes 10321928 | tf_op jit(solution)/shard_map/ppermute | solution.py:644
  656.6 51.7 %collective-permute-done.50 = bf16[384,4480]{1,0:T(8,128)(2,1)} collective-permute-done((bf16[384,4480]{1,0:T(8,128)(2,1)S(1)}, bf16[384,4480]{1,0:T(8,128)(2,1)}, u32[]{:S(2)}, u32[]{:S(2)}) %collective-permute-start.50) | collective-permute-done | bytes 3440672 | tf_op jit(solution)/shard_map/ppermute | solution.py:628
  708.3 6.1 fusion.1
  714.3 17.3 %collective-permute-start.51 = (bf16[384,4480]{1,0:T(8,128)(2,1)}, bf16[384,4480]{1,0:T(8,128)(2,1)}, u32[]{:S(2)}, u32[]{:S(2)}) collective-permute-start(bf16[384,4480]{1,0:T(8,128)(2,1)} %fusion.1), channel_id=1, source_target_pairs={{0,2},{6,4},{1,3},{7,5},{8,10},{14,12},{9,11},{15,13},{16,18},{22,... | collective-permute-start | bytes 10321928 | tf_op jit(solution)/shard_map/ppermute | solution.py:644
  731.6 48.5 %collective-permute-done.55 = bf16[384,4480]{1,0:T(8,128)(2,1)S(1)} collective-permute-done((bf16[384,4480]{1,0:T(8,128)(2,1)S(1)}, bf16[384,4480]{1,0:T(8,128)(2,1)S(1)}, u32[]{:S(2)}, u32[]{:S(2)}) %collective-permute-start.55) | collective-permute-done | bytes 3440672 | tf_op jit(solution)/shard_map/ppermute | solution.py:628
  780.1 3.5 fusion
  783.6 17.6 %collective-permute-start.56 = (bf16[384,4480]{1,0:T(8,128)(2,1)}, bf16[384,4480]{1,0:T(8,128)(2,1)}, u32[]{:S(2)}, u32[]{:S(2)}) collective-permute-start(bf16[384,4480]{1,0:T(8,128)(2,1)} %fusion), channel_id=1, source_target_pairs={{0,2},{6,4},{1,3},{7,5},{8,10},{14,12},{9,11},{15,13},{16,18},{22,... | collective-permute-start | bytes 10321928 | tf_op jit(solution)/shard_map/ppermute | solution.py:644
  801.2 5.3 weight_grad.9
  808.2 6.4 mix_back.1
  814.6 7.1 weight_grad.8
  823.3 5.6 add.309
  835.7 3.8 add.314
  839.5 14.5 %collective-permute-done.30 = f32[5312]{0:T(1024)S(1)} collective-permute-done((f32[5312]{0:T(1024)S(1)}, f32[5312]{0:T(1024)S(1)}, u32[]{:S(2)}, u32[]{:S(2)}) %collective-permute-start.30) | collective-permute-done | bytes 21280 | tf_op jit(solution)/shard_map/ppermute | solution.py:628
  855.0 19.3 %collective-permute-done.56 = bf16[384,4480]{1,0:T(8,128)(2,1)} collective-permute-done((bf16[384,4480]{1,0:T(8,128)(2,1)}, bf16[384,4480]{1,0:T(8,128)(2,1)}, u32[]{:S(2)}, u32[]{:S(2)}) %collective-permute-start.56) | collective-permute-done | bytes 3440672 | tf_op jit(solution)/shard_map/ppermute | solution.py:644
  876.8 5.6 add.319
  888.7 3.8 collective-permute-done.23
  892.5 11.4 collective-permute-start.32
  903.9 13.6 %collective-permute-start.36 = (bf16[384,1024]{1,0:T(8,128)(2,1)S(1)}, bf16[384,1024]{1,0:T(8,128)(2,1)S(1)}, u32[]{:S(2)}, u32[]{:S(2)}) collective-permute-start(bf16[384,1024]{1,0:T(8,128)(2,1)S(1)} %fusion.3), channel_id=1, source_target_pairs={{0,2},{6,4},{1,3},{7,5},{8,10},{14,12},{9,11},{15,13},{16,18},{22,... | collective-permute-start | bytes 2359304 | tf_op jit(solution)/shard_map/ppermute | solution.py:644
  918.6 134.3 %collective-permute-done.32 = f32[5312]{0:T(1024)S(1)} collective-permute-done((f32[5312]{0:T(1024)S(1)}, f32[5312]{0:T(1024)S(1)}, u32[]{:S(2)}, u32[]{:S(2)}) %collective-permute-start.32) | collective-permute-done | bytes 21280 | tf_op jit(solution)/shard_map/ppermute | solution.py:628
  1055.2 5.6 add.310
  1060.8 5.8 collective-permute-done.41
  1081.1 43.3 %collective-permute-done.33 = f32[5312]{0:T(1024)S(1)} collective-permute-done((f32[5312]{0:T(1024)S(1)}, f32[5312]{0:T(1024)S(1)}, u32[]{:S(2)}, u32[]{:S(2)}) %collective-permute-start.33) | collective-permute-done | bytes 21280 | tf_op jit(solution)/shard_map/ppermute | solution.py:628
  1127.0 7.6 add_convert_fusion
  1136.5 4.1 add.320
  1140.6 91.9 %collective-permute-done.43 = bf16[384,768]{1,0:T(8,128)(2,1)} collective-permute-done((bf16[384,768]{1,0:T(8,128)(2,1)}, bf16[384,768]{1,0:T(8,128)(2,1)}, u32[]{:S(2)}, u32[]{:S(2)}) %collective-permute-start.43) | collective-permute-done | bytes 589856 | tf_op jit(solution)/shard_map/ppermute | solution.py:646
  1236.0 8.0 input_back.1
  1244.0 5.4 collective-permute-done.38
  1251.7 5.3 select_convert_fusion.2
  1257.1 5.3 select_convert_fusion.1
  1262.4 58.1 %collective-permute-done.58 = bf16[384,4480]{1,0:T(8,128)(2,1)S(1)} collective-permute-done((bf16[384,4480]{1,0:T(8,128)(2,1)S(1)}, bf16[384,4480]{1,0:T(8,128)(2,1)S(1)}, u32[]{:S(2)}, u32[]{:S(2)}) %collective-permute-start.58) | collective-permute-done | bytes 3440672 | tf_op jit(solution)/shard_map/ppermute | solution.py:646
  1320.5 3.3 select_convert_fusion
  (346 shorter events, 123.3 us)
Async XLA Ops:
  0.6 20.8 %collective-permute-start.1 = (bf16[384,1024]{1,0:T(8,128)(2,1)}, bf16[384,1024]{1,0:T(8,128)(2,1)S(1)}, u32[]{:S(2)}, u32[]{:S(2)}) collective-permute-start(bf16[384,1024]{1,0:T(8,128)(2,1)} %refs_0_.7), channel_id=1, source_target_pairs={{0,16},{8,24},{16,0},{24,8},{1,17},{9,25},{17,1},{25,9},{2,18},{10... | collective-permute-start | bytes 2359304 | tf_op jit(solution)/shard_map/ppermute | solution.py:628
  21.4 2.3 collective-permute-start.2
  23.7 76.8 %collective-permute-start.15 = (bf16[384,4480]{1,0:T(8,128)(2,1)}, bf16[384,4480]{1,0:T(8,128)(2,1)}, u32[]{:S(2)}, u32[]{:S(2)}) collective-permute-start(bf16[384,4480]{1,0:T(8,128)(2,1)} %refs_0_.4), channel_id=1, source_target_pairs={{0,16},{8,24},{16,0},{24,8},{1,17},{9,25},{17,1},{25,9},{2,18},{10... | collective-permute-start | bytes 10321928 | tf_op jit(solution)/shard_map/ppermute | solution.py:628
  25.4 77.6 %collective-permute-start = (bf16[384,1024]{1,0:T(8,128)(2,1)}, bf16[384,1024]{1,0:T(8,128)(2,1)S(1)}, u32[]{:S(2)}, u32[]{:S(2)}) collective-permute-start(bf16[384,1024]{1,0:T(8,128)(2,1)} %refs_0_.7), channel_id=1, source_target_pairs={{0,8},{8,0},{16,24},{24,16},{1,9},{9,1},{17,25},{25,17},{2,10},{10... | collective-permute-start | bytes 2359304 | tf_op jit(solution)/shard_map/ppermute | solution.py:628
  100.5 55.8 %collective-permute-start.16 = (bf16[384,4480]{1,0:T(8,128)(2,1)}, bf16[384,4480]{1,0:T(8,128)(2,1)}, u32[]{:S(2)}, u32[]{:S(2)}) collective-permute-start(bf16[384,4480]{1,0:T(8,128)(2,1)} %collective-permute-done.15.refs_2_), channel_id=1, source_target_pairs={{0,8},{8,0},{16,24},{24,16},{1,9},{9,1},{17,25},{25,17},{2,10},{10... | collective-permute-start | bytes 10321928 | tf_op jit(solution)/shard_map/ppermute | solution.py:628
  101.1 209.0 %copy-start.33 = (s32[2]{0:T(128)}, s32[2]{0:T(128)S(1)}, u32[]{:S(2)}) copy-start(s32[2]{0:T(128)S(1)} %pad_add_fusion.9.place) | copy-start | bytes 28
  116.2 15.6 %collective-permute-start.3 = (bf16[1024,256]{1,0:T(8,128)(2,1)S(1)}, bf16[1024,256]{1,0:T(8,128)(2,1)S(1)}, u32[]{:S(2)}, u32[]{:S(2)}) collective-permute-start(bf16[1024,256]{1,0:T(8,128)(2,1)S(1)} %get-tuple-element.55), channel_id=1, source_target_pairs={{0,2},{2,4},{4,6},{1,3},{3,5},{5,7},{8,10},{10,12},{12,14},{9,11},... | collective-permute-start | bytes 1572872 | tf_op jit(solution)/shard_map/ppermute | solution.py:775
  120.1 17.1 %collective-permute-start.8 = (bf16[384,768]{1,0:T(8,128)(2,1)S(1)}, bf16[384,768]{1,0:T(8,128)(2,1)S(1)}, u32[]{:S(2)}, u32[]{:S(2)}) collective-permute-start(bf16[384,768]{1,0:T(8,128)(2,1)S(1)} %copy-done.11), channel_id=1, source_target_pairs={{0,16},{8,24},{16,0},{24,8},{1,17},{9,25},{17,1},{25,9},{2,18},{10... | collective-permute-start | bytes 1769480 | tf_op jit(solution)/shard_map/ppermute | solution.py:628
  131.7 15.4 %collective-permute-start.4 = (bf16[1024,256]{1,0:T(8,128)(2,1)S(1)}, bf16[1024,256]{1,0:T(8,128)(2,1)}, u32[]{:S(2)}, u32[]{:S(2)}) collective-permute-start(bf16[1024,256]{1,0:T(8,128)(2,1)S(1)} %collective-permute-done.3), channel_id=1, source_target_pairs={{0,2},{2,4},{4,6},{1,3},{3,5},{5,7},{8,10},{10,12},{12,14},{9,11},... | collective-permute-start | bytes 1572872 | tf_op jit(solution)/shard_map/ppermute | solution.py:775
  137.2 17.5 %collective-permute-start.9 = (bf16[384,768]{1,0:T(8,128)(2,1)S(1)}, bf16[384,768]{1,0:T(8,128)(2,1)S(1)}, u32[]{:S(2)}, u32[]{:S(2)}) collective-permute-start(bf16[384,768]{1,0:T(8,128)(2,1)S(1)} %collective-permute-done.8.refs_2_), channel_id=1, source_target_pairs={{0,8},{8,0},{16,24},{24,16},{1,9},{9,1},{17,25},{25,17},{2,10},{10... | collective-permute-start | bytes 1769480 | tf_op jit(solution)/shard_map/ppermute | solution.py:628
  147.1 15.0 %collective-permute-start.5 = (bf16[1024,256]{1,0:T(8,128)(2,1)}, bf16[1024,256]{1,0:T(8,128)(2,1)}, u32[]{:S(2)}, u32[]{:S(2)}) collective-permute-start(bf16[1024,256]{1,0:T(8,128)(2,1)} %collective-permute-done.4), channel_id=1, source_target_pairs={{0,2},{2,4},{4,6},{1,3},{3,5},{5,7},{8,10},{10,12},{12,14},{9,11},... | collective-permute-start | bytes 1572872 | tf_op jit(solution)/shard_map/ppermute | solution.py:775
  153.3 26.0 %collective-permute-start.7 = (bf16[384,768]{1,0:T(8,128)(2,1)S(1)}, bf16[384,768]{1,0:T(8,128)(2,1)S(1)}, u32[]{:S(2)}, u32[]{:S(2)}) collective-permute-start(bf16[384,768]{1,0:T(8,128)(2,1)S(1)} %copy-done.11), channel_id=1, source_target_pairs={{0,8},{8,0},{16,24},{24,16},{1,9},{9,1},{17,25},{25,17},{2,10},{10... | collective-permute-start | bytes 1769480 | tf_op jit(solution)/shard_map/ppermute | solution.py:628
  154.7 107.0 %collective-permute-start.18 = (bf16[384,4480]{1,0:T(8,128)(2,1)}, bf16[384,4480]{1,0:T(8,128)(2,1)}, u32[]{:S(2)}, u32[]{:S(2)}) collective-permute-start(bf16[384,4480]{1,0:T(8,128)(2,1)} %refs_4_), channel_id=1, source_target_pairs={{0,16},{8,24},{16,0},{24,8},{1,17},{9,25},{17,1},{25,9},{2,18},{10... | collective-permute-start | bytes 10321928 | tf_op jit(solution)/shard_map/ppermute | solution.py:628
  156.3 149.2 %collective-permute-start.21 = (bf16[384,4480]{1,0:T(8,128)(2,1)}, bf16[384,4480]{1,0:T(8,128)(2,1)}, u32[]{:S(2)}, u32[]{:S(2)}) collective-permute-start(bf16[384,4480]{1,0:T(8,128)(2,1)} %refs_0_.5), channel_id=1, source_target_pairs={{0,16},{8,24},{16,0},{24,8},{1,17},{9,25},{17,1},{25,9},{2,18},{10... | collective-permute-start | bytes 10321928 | tf_op jit(solution)/shard_map/ppermute | solution.py:628
  163.2 142.2 %copy-start.70 = (bf16[1536]{0:T(1024)(128)(2,1)S(1)}, bf16[1536]{0:T(1024)(128)(2,1)}, u32[]{:S(2)}) copy-start(bf16[1536]{0:T(1024)(128)(2,1)} %param.20) | copy-start | bytes 9220
  176.1 86.2 %collective-permute-start.6 = (bf16[1024,768]{1,0:T(8,128)(2,1)S(1)}, bf16[1024,768]{1,0:T(8,128)(2,1)S(1)}, u32[]{:S(2)}, u32[]{:S(2)}) collective-permute-start(bf16[1024,768]{1,0:T(8,128)(2,1)S(1)} %get-tuple-element.56.own_ref.att_ref.right_ref), channel_id=1, source_target_pairs={{0,1},{1,0},{2,3},{3,2},{4,5},{5,4},{6,7},{7,6},{8,9},{9,8},{10,11... | collective-permute-start | bytes 4718600 | tf_op jit(solution)/shard_map/ppermute | solution.py:778
  178.8 47.3 %collective-permute-start.10 = (bf16[384,768]{1,0:T(8,128)(2,1)S(1)}, bf16[384,768]{1,0:T(8,128)(2,1)S(1)}, u32[]{:S(2)}, u32[]{:S(2)}) collective-permute-start(bf16[384,768]{1,0:T(8,128)(2,1)S(1)} %copy-done.11), channel_id=1, source_target_pairs={{0,1},{1,0},{2,3},{3,2},{4,5},{5,4},{6,7},{7,6},{8,9},{9,8},{10,11... | collective-permute-start | bytes 1769480 | tf_op jit(solution)/shard_map/ppermute | solution.py:737
  179.3 59.4 %collective-permute-start.11 = (bf16[384,768]{1,0:T(8,128)(2,1)S(1)}, bf16[384,768]{1,0:T(8,128)(2,1)S(1)}, u32[]{:S(2)}, u32[]{:S(2)}) collective-permute-start(bf16[384,768]{1,0:T(8,128)(2,1)S(1)} %collective-permute-done.7.refs_1_), channel_id=1, source_target_pairs={{0,1},{1,0},{2,3},{3,2},{4,5},{5,4},{6,7},{7,6},{8,9},{9,8},{10,11... | collective-permute-start | bytes 1769480 | tf_op jit(solution)/shard_map/ppermute | solution.py:737
  226.9 24.5 %collective-permute-start.12 = (bf16[384,768]{1,0:T(8,128)(2,1)S(1)}, bf16[384,768]{1,0:T(8,128)(2,1)S(1)}, u32[]{:S(2)}, u32[]{:S(2)}) collective-permute-start(bf16[384,768]{1,0:T(8,128)(2,1)S(1)} %collective-permute-done.8.refs_2_), channel_id=1, source_target_pairs={{0,1},{1,0},{2,3},{3,2},{4,5},{5,4},{6,7},{7,6},{8,9},{9,8},{10,11... | collective-permute-start | bytes 1769480 | tf_op jit(solution)/shard_map/ppermute | solution.py:737
  239.6 21.3 %collective-permute-start.13 = (bf16[384,768]{1,0:T(8,128)(2,1)S(1)}, bf16[384,768]{1,0:T(8,128)(2,1)S(1)}, u32[]{:S(2)}, u32[]{:S(2)}) collective-permute-start(bf16[384,768]{1,0:T(8,128)(2,1)S(1)} %collective-permute-done.9.refs_3_), channel_id=1, source_target_pairs={{0,1},{1,0},{2,3},{3,2},{4,5},{5,4},{6,7},{7,6},{8,9},{9,8},{10,11... | collective-permute-start | bytes 1769480 | tf_op jit(solution)/shard_map/ppermute | solution.py:737
  252.2 83.0 %collective-permute-start.14 = (bf16[384,4480]{1,0:T(8,128)(2,1)}, bf16[384,4480]{1,0:T(8,128)(2,1)}, u32[]{:S(2)}, u32[]{:S(2)}) collective-permute-start(bf16[384,4480]{1,0:T(8,128)(2,1)} %refs_0_.4), channel_id=1, source_target_pairs={{0,8},{8,0},{16,24},{24,16},{1,9},{9,1},{17,25},{25,17},{2,10},{10... | collective-permute-start | bytes 10321928 | tf_op jit(solution)/shard_map/ppermute | solution.py:628
  261.7 73.5 %collective-permute-start.17 = (bf16[384,4480]{1,0:T(8,128)(2,1)}, bf16[384,4480]{1,0:T(8,128)(2,1)}, u32[]{:S(2)}, u32[]{:S(2)}) collective-permute-start(bf16[384,4480]{1,0:T(8,128)(2,1)} %refs_4_), channel_id=1, source_target_pairs={{0,8},{8,0},{16,24},{24,16},{1,9},{9,1},{17,25},{25,17},{2,10},{10... | collective-permute-start | bytes 10321928 | tf_op jit(solution)/shard_map/ppermute | solution.py:628
  261.7 73.5 %collective-permute-start.19 = (bf16[384,4480]{1,0:T(8,128)(2,1)}, bf16[384,4480]{1,0:T(8,128)(2,1)}, u32[]{:S(2)}, u32[]{:S(2)}) collective-permute-start(bf16[384,4480]{1,0:T(8,128)(2,1)} %collective-permute-done.18.refs_6_), channel_id=1, source_target_pairs={{0,8},{8,0},{16,24},{24,16},{1,9},{9,1},{17,25},{25,17},{2,10},{10... | collective-permute-start | bytes 10321928 | tf_op jit(solution)/shard_map/ppermute | solution.py:628
  263.4 71.8 %collective-permute-start.20 = (bf16[384,4480]{1,0:T(8,128)(2,1)}, bf16[384,4480]{1,0:T(8,128)(2,1)}, u32[]{:S(2)}, u32[]{:S(2)}) collective-permute-start(bf16[384,4480]{1,0:T(8,128)(2,1)} %refs_0_.5), channel_id=1, source_target_pairs={{0,8},{8,0},{16,24},{24,16},{1,9},{9,1},{17,25},{25,17},{2,10},{10... | collective-permute-start | bytes 10321928 | tf_op jit(solution)/shard_map/ppermute | solution.py:628
  305.4 29.8 %collective-permute-start.22 = (bf16[384,4480]{1,0:T(8,128)(2,1)}, bf16[384,4480]{1,0:T(8,128)(2,1)}, u32[]{:S(2)}, u32[]{:S(2)}) collective-permute-start(bf16[384,4480]{1,0:T(8,128)(2,1)} %collective-permute-done.21.refs_10_.refs_2_), channel_id=1, source_target_pairs={{0,8},{8,0},{16,24},{24,16},{1,9},{9,1},{17,25},{25,17},{2,10},{10... | collective-permute-start | bytes 10321928 | tf_op jit(solution)/shard_map/ppermute | solution.py:628
  450.2 103.4 %collective-permute-start.44 = (bf16[768,4480]{1,0:T(8,128)(2,1)}, bf16[768,4480]{1,0:T(8,128)(2,1)}, u32[]{:S(2)}, u32[]{:S(2)}) collective-permute-start(bf16[768,4480]{1,0:T(8,128)(2,1)} %get-tuple-element.67), channel_id=1, source_target_pairs={{0,8},{8,0},{16,24},{24,16},{1,9},{9,1},{17,25},{25,17},{2,10},{10... | collective-permute-start | bytes 20643848 | tf_op jit(solution)/shard_map/ppermute | solution.py:628
  450.8 70.2 %collective-permute-start.24 = (bf16[1024,1536]{1,0:T(8,128)(2,1)S(1)}, bf16[1024,1536]{1,0:T(8,128)(2,1)}, u32[]{:S(2)}, u32[]{:S(2)}) collective-permute-start(bf16[1024,1536]{1,0:T(8,128)(2,1)S(1)} %copy-done.65), channel_id=1, source_target_pairs={{0,1},{1,0},{2,3},{3,2},{4,5},{5,4},{6,7},{7,6},{8,9},{9,8},{10,11... | collective-permute-start | bytes 9437192 | tf_op jit(solution)/shard_map/ppermute | solution.py:787
  471.5 87.1 %collective-permute-start.49 = (bf16[768,4480]{1,0:T(8,128)(2,1)}, bf16[768,4480]{1,0:T(8,128)(2,1)}, u32[]{:S(2)}, u32[]{:S(2)}) collective-permute-start(bf16[768,4480]{1,0:T(8,128)(2,1)} %get-tuple-element.71), channel_id=1, source_target_pairs={{0,8},{8,0},{16,24},{24,16},{1,9},{9,1},{17,25},{25,17},{2,10},{10... | collective-permute-start | bytes 20643848 | tf_op jit(solution)/shard_map/ppermute | solution.py:628
  490.7 89.5 %collective-permute-start.54 = (bf16[768,4480]{1,0:T(8,128)(2,1)}, bf16[768,4480]{1,0:T(8,128)(2,1)}, u32[]{:S(2)}, u32[]{:S(2)}) collective-permute-start(bf16[768,4480]{1,0:T(8,128)(2,1)} %get-tuple-element.74), channel_id=1, source_target_pairs={{0,8},{8,0},{16,24},{24,16},{1,9},{9,1},{17,25},{25,17},{2,10},{10... | collective-permute-start | bytes 20643848 | tf_op jit(solution)/shard_map/ppermute | solution.py:628
  552.3 26.3 %collective-permute-start.25 = (bf16[1024,256]{1,0:T(8,128)(2,1)S(1)}, bf16[1024,256]{1,0:T(8,128)(2,1)S(1)}, u32[]{:S(2)}, u32[]{:S(2)}) collective-permute-start(bf16[1024,256]{1,0:T(8,128)(2,1)S(1)} %slice.99), channel_id=1, source_target_pairs={{2,0},{4,2},{6,4},{3,1},{5,3},{7,5},{10,8},{12,10},{14,12},{11,9},... | collective-permute-start | bytes 1572872 | tf_op jit(solution)/shard_map/ppermute | solution.py:807
  557.0 77.5 %collective-permute-start.45 = (bf16[384,4480]{1,0:T(8,128)(2,1)S(1)}, bf16[384,4480]{1,0:T(8,128)(2,1)}, u32[]{:S(2)}, u32[]{:S(2)}) collective-permute-start(bf16[384,4480]{1,0:T(8,128)(2,1)S(1)} %slice_add_fusion.4), channel_id=1, source_target_pairs={{0,16},{8,24},{16,0},{24,8},{1,17},{9,25},{17,1},{25,9},{2,18},{10... | collective-permute-start | bytes 10321928 | tf_op jit(solution)/shard_map/ppermute | solution.py:628
  562.0 146.3 %collective-permute-start.50 = (bf16[384,4480]{1,0:T(8,128)(2,1)S(1)}, bf16[384,4480]{1,0:T(8,128)(2,1)}, u32[]{:S(2)}, u32[]{:S(2)}) collective-permute-start(bf16[384,4480]{1,0:T(8,128)(2,1)S(1)} %slice_add_fusion.2), channel_id=1, source_target_pairs={{0,16},{8,24},{16,0},{24,8},{1,17},{9,25},{17,1},{25,9},{2,18},{10... | collective-permute-start | bytes 10321928 | tf_op jit(solution)/shard_map/ppermute | solution.py:628
  578.7 14.8 %collective-permute-start.26 = (bf16[1024,256]{1,0:T(8,128)(2,1)S(1)}, bf16[1024,256]{1,0:T(8,128)(2,1)S(1)}, u32[]{:S(2)}, u32[]{:S(2)}) collective-permute-start(bf16[1024,256]{1,0:T(8,128)(2,1)S(1)} %slice_add_fusion.10), channel_id=1, source_target_pairs={{2,0},{4,2},{6,4},{3,1},{5,3},{7,5},{10,8},{12,10},{14,12},{11,9},... | collective-permute-start | bytes 1572872 | tf_op jit(solution)/shard_map/ppermute | solution.py:807
  584.0 196.1 %collective-permute-start.55 = (bf16[384,4480]{1,0:T(8,128)(2,1)S(1)}, bf16[384,4480]{1,0:T(8,128)(2,1)S(1)}, u32[]{:S(2)}, u32[]{:S(2)}) collective-permute-start(bf16[384,4480]{1,0:T(8,128)(2,1)S(1)} %slice_add_fusion), channel_id=1, source_target_pairs={{0,16},{8,24},{16,0},{24,8},{1,17},{9,25},{17,1},{25,9},{2,18},{10... | collective-permute-start | bytes 10321928 | tf_op jit(solution)/shard_map/ppermute | solution.py:628
  594.3 212.3 %collective-permute-start.27 = (bf16[1024,256]{1,0:T(8,128)(2,1)}, bf16[1024,256]{1,0:T(8,128)(2,1)}, u32[]{:S(2)}, u32[]{:S(2)}) collective-permute-start(bf16[1024,256]{1,0:T(8,128)(2,1)} %slice_add_fusion.11), channel_id=1, source_target_pairs={{2,0},{4,2},{6,4},{3,1},{5,3},{7,5},{10,8},{12,10},{14,12},{11,9},... | collective-permute-start | bytes 1572872 | tf_op jit(solution)/shard_map/ppermute | solution.py:807
  634.6 145.6 %slice-start.4 = ((s8[6881280]{0:T(1024)(128)(4,1)}), s8[4194304]{0:T(1024)(128)(4,1)S(1)}, s32[]{:S(2)}) async-start(s8[6881280]{0:T(1024)(128)(4,1)} %bitcast.32), calls=%async_computation.4 | async-start | bytes 8388608
  639.2 140.9 %slice-start.5 = ((s8[6881280]{0:T(1024)(128)(4,1)}), s8[2686976]{0:T(1024)(128)(4,1)S(1)}, s32[]{:S(2)}) async-start(s8[6881280]{0:T(1024)(128)(4,1)} %bitcast.32), calls=%async_computation.5 | async-start | bytes 5373952
  639.2 182.6 %collective-permute-start.46 = (bf16[384,4480]{1,0:T(8,128)(2,1)}, bf16[384,4480]{1,0:T(8,128)(2,1)}, u32[]{:S(2)}, u32[]{:S(2)}) collective-permute-start(bf16[384,4480]{1,0:T(8,128)(2,1)} %fusion.2), channel_id=1, source_target_pairs={{0,2},{6,4},{1,3},{7,5},{8,10},{14,12},{9,11},{15,13},{16,18},{22,... | collective-permute-start | bytes 10321928 | tf_op jit(solution)/shard_map/ppermute | solution.py:644
  714.3 120.8 %collective-permute-start.51 = (bf16[384,4480]{1,0:T(8,128)(2,1)}, bf16[384,4480]{1,0:T(8,128)(2,1)}, u32[]{:S(2)}, u32[]{:S(2)}) collective-permute-start(bf16[384,4480]{1,0:T(8,128)(2,1)} %fusion.1), channel_id=1, source_target_pairs={{0,2},{6,4},{1,3},{7,5},{8,10},{14,12},{9,11},{15,13},{16,18},{22,... | collective-permute-start | bytes 10321928 | tf_op jit(solution)/shard_map/ppermute | solution.py:644
  783.6 90.7 %collective-permute-start.56 = (bf16[384,4480]{1,0:T(8,128)(2,1)}, bf16[384,4480]{1,0:T(8,128)(2,1)}, u32[]{:S(2)}, u32[]{:S(2)}) collective-permute-start(bf16[384,4480]{1,0:T(8,128)(2,1)} %fusion), channel_id=1, source_target_pairs={{0,2},{6,4},{1,3},{7,5},{8,10},{14,12},{9,11},{15,13},{16,18},{22,... | collective-permute-start | bytes 10321928 | tf_op jit(solution)/shard_map/ppermute | solution.py:644
  806.6 22.3 %collective-permute-start.39 = (bf16[768,768]{1,0:T(8,128)(2,1)S(1)}, bf16[768,768]{1,0:T(8,128)(2,1)}, u32[]{:S(2)}, u32[]{:S(2)}) collective-permute-start(bf16[768,768]{1,0:T(8,128)(2,1)S(1)} %get-tuple-element.96), channel_id=1, source_target_pairs={{0,8},{8,0},{16,24},{24,16},{1,9},{9,1},{17,25},{25,17},{2,10},{10... | collective-permute-start | bytes 3538952 | tf_op jit(solution)/shard_map/ppermute | solution.py:628
  821.6 10.3 collective-permute-start.34
  821.8 70.7 %collective-permute-start.23 = (bf16[1024,1536]{1,0:T(8,128)(2,1)}, bf16[1024,1536]{1,0:T(8,128)(2,1)}, u32[]{:S(2)}, u32[]{:S(2)}) collective-permute-start(bf16[1024,1536]{1,0:T(8,128)(2,1)} %down_project.1), channel_id=1, source_target_pairs={{0,1},{1,0},{2,3},{3,2},{4,5},{5,4},{6,7},{7,6},{8,9},{9,8},{10,11... | collective-permute-start | bytes 9437192 | tf_op jit(solution)/shard_map/ppermute | solution.py:792
  828.9 225.8 %collective-permute-start.47 = (bf16[384,4480]{1,0:T(8,128)(2,1)}, bf16[384,4480]{1,0:T(8,128)(2,1)}, u32[]{:S(2)}, u32[]{:S(2)}) collective-permute-start(bf16[384,4480]{1,0:T(8,128)(2,1)} %add.309), channel_id=1, source_target_pairs={{2,4},{4,2},{3,5},{5,3},{10,12},{12,10},{11,13},{13,11},{18,20},{2... | collective-permute-start | bytes 10321928 | tf_op jit(solution)/shard_map/ppermute | solution.py:645
  832.0 1.6 collective-permute-start.29
  833.6 52.3 %collective-permute-start.35 = (bf16[384,1024]{1,0:T(8,128)(2,1)S(1)}, bf16[384,1024]{1,0:T(8,128)(2,1)S(1)}, u32[]{:S(2)}, u32[]{:S(2)}) collective-permute-start(bf16[384,1024]{1,0:T(8,128)(2,1)S(1)} %slice_add_fusion.6), channel_id=1, source_target_pairs={{0,16},{8,24},{16,0},{24,8},{1,17},{9,25},{17,1},{25,9},{2,18},{10... | collective-permute-start | bytes 2359304 | tf_op jit(solution)/shard_map/ppermute | solution.py:628
  835.1 18.9 %collective-permute-start.30 = (f32[5312]{0:T(1024)S(1)}, f32[5312]{0:T(1024)S(1)}, u32[]{:S(2)}, u32[]{:S(2)}) collective-permute-start(f32[5312]{0:T(1024)S(1)} %fusion.40), channel_id=1, source_target_pairs={{0,16},{8,24},{16,0},{24,8},{1,17},{9,25},{17,1},{25,9},{2,18},{10... | collective-permute-start | bytes 63752 | tf_op jit(solution)/shard_map/ppermute | solution.py:628
  854.0 216.8 %collective-permute-start.52 = (bf16[384,4480]{1,0:T(8,128)(2,1)S(1)}, bf16[384,4480]{1,0:T(8,128)(2,1)S(1)}, u32[]{:S(2)}, u32[]{:S(2)}) collective-permute-start(bf16[384,4480]{1,0:T(8,128)(2,1)S(1)} %add.314), channel_id=1, source_target_pairs={{2,4},{4,2},{3,5},{5,3},{10,12},{12,10},{11,13},{13,11},{18,20},{2... | collective-permute-start | bytes 10321928 | tf_op jit(solution)/shard_map/ppermute | solution.py:645
  874.3 8.0 collective-permute-start.31
  882.3 243.4 %collective-permute-start.57 = (bf16[384,4480]{1,0:T(8,128)(2,1)}, bf16[384,4480]{1,0:T(8,128)(2,1)}, u32[]{:S(2)}, u32[]{:S(2)}) collective-permute-start(bf16[384,4480]{1,0:T(8,128)(2,1)} %add.319), channel_id=1, source_target_pairs={{2,4},{4,2},{3,5},{5,3},{10,12},{12,10},{11,13},{13,11},{18,20},{2... | collective-permute-start | bytes 10321928 | tf_op jit(solution)/shard_map/ppermute | solution.py:645
  885.8 18.0 %collective-permute-start.40 = (bf16[384,768]{1,0:T(8,128)(2,1)S(1)}, bf16[384,768]{1,0:T(8,128)(2,1)S(1)}, u32[]{:S(2)}, u32[]{:S(2)}) collective-permute-start(bf16[384,768]{1,0:T(8,128)(2,1)S(1)} %slice_add_fusion.8), channel_id=1, source_target_pairs={{0,16},{8,24},{16,0},{24,8},{1,17},{9,25},{17,1},{25,9},{2,18},{10... | collective-permute-start | bytes 1769480 | tf_op jit(solution)/shard_map/ppermute | solution.py:628
  892.5 160.4 %collective-permute-start.32 = (f32[5312]{0:T(1024)S(1)}, f32[5312]{0:T(1024)S(1)}, u32[]{:S(2)}, u32[]{:S(2)}) collective-permute-start(f32[5312]{0:T(1024)S(1)} %add.292), channel_id=1, source_target_pairs={{0,4},{2,6},{4,0},{6,2},{1,5},{3,7},{5,1},{7,3},{8,12},{10,14},{12... | collective-permute-start | bytes 63752 | tf_op jit(solution)/shard_map/ppermute | solution.py:628
  903.9 164.2 %collective-permute-start.36 = (bf16[384,1024]{1,0:T(8,128)(2,1)S(1)}, bf16[384,1024]{1,0:T(8,128)(2,1)S(1)}, u32[]{:S(2)}, u32[]{:S(2)}) collective-permute-start(bf16[384,1024]{1,0:T(8,128)(2,1)S(1)} %fusion.3), channel_id=1, source_target_pairs={{0,2},{6,4},{1,3},{7,5},{8,10},{14,12},{9,11},{15,13},{16,18},{22,... | collective-permute-start | bytes 2359304 | tf_op jit(solution)/shard_map/ppermute | solution.py:644
  1052.9 13.7 %collective-permute-start.41 = (bf16[384,768]{1,0:T(8,128)(2,1)S(1)}, bf16[384,768]{1,0:T(8,128)(2,1)S(1)}, u32[]{:S(2)}, u32[]{:S(2)}) collective-permute-start(bf16[384,768]{1,0:T(8,128)(2,1)S(1)} %fusion.4), channel_id=1, source_target_pairs={{0,2},{6,4},{1,3},{7,5},{8,10},{14,12},{9,11},{15,13},{16,18},{22,... | collective-permute-start | bytes 1769480 | tf_op jit(solution)/shard_map/ppermute | solution.py:644
  1054.7 181.3 %collective-permute-start.28 = (bf16[1024,1536]{1,0:T(8,128)(2,1)}, bf16[1024,1536]{1,0:T(8,128)(2,1)}, u32[]{:S(2)}, u32[]{:S(2)}) collective-permute-start(bf16[1024,1536]{1,0:T(8,128)(2,1)} %get-tuple-element.83.own_ref), channel_id=1, source_target_pairs={{0,1},{1,0},{2,3},{3,2},{4,5},{5,4},{6,7},{7,6},{8,9},{9,8},{10,11... | collective-permute-start | bytes 9437192 | tf_op jit(solution)/shard_map/ppermute | solution.py:813
  1066.6 185.2 %collective-permute-start.48 = (bf16[384,4480]{1,0:T(8,128)(2,1)}, bf16[384,4480]{1,0:T(8,128)(2,1)}, u32[]{:S(2)}, u32[]{:S(2)}) collective-permute-start(bf16[384,4480]{1,0:T(8,128)(2,1)} %add.310), channel_id=1, source_target_pairs={{2,0},{4,6},{3,1},{5,7},{10,8},{12,14},{11,9},{13,15},{18,16},{20,... | collective-permute-start | bytes 10321928 | tf_op jit(solution)/shard_map/ppermute | solution.py:646
  1068.0 1.8 collective-permute-start.42
  1069.9 4.3 collective-permute-start.37
  1070.9 53.5 %collective-permute-start.33 = (f32[5312]{0:T(1024)S(1)}, f32[5312]{0:T(1024)S(1)}, u32[]{:S(2)}, u32[]{:S(2)}) collective-permute-start(f32[5312]{0:T(1024)S(1)} %add.293), channel_id=1, source_target_pairs={{0,1},{1,0},{2,3},{3,2},{4,5},{5,4},{6,7},{7,6},{8,9},{9,8},{10,11... | collective-permute-start | bytes 63752 | tf_op jit(solution)/shard_map/ppermute | solution.py:628
  1075.0 182.0 %collective-permute-start.53 = (bf16[384,4480]{1,0:T(8,128)(2,1)}, bf16[384,4480]{1,0:T(8,128)(2,1)}, u32[]{:S(2)}, u32[]{:S(2)}) collective-permute-start(bf16[384,4480]{1,0:T(8,128)(2,1)} %add.315), channel_id=1, source_target_pairs={{2,0},{4,6},{3,1},{5,7},{10,8},{12,14},{11,9},{13,15},{18,16},{20,... | collective-permute-start | bytes 10321928 | tf_op jit(solution)/shard_map/ppermute | solution.py:646
  1124.4 108.1 %collective-permute-start.43 = (bf16[384,768]{1,0:T(8,128)(2,1)}, bf16[384,768]{1,0:T(8,128)(2,1)}, u32[]{:S(2)}, u32[]{:S(2)}) collective-permute-start(bf16[384,768]{1,0:T(8,128)(2,1)} %add.305), channel_id=1, source_target_pairs={{2,0},{4,6},{3,1},{5,7},{10,8},{12,14},{11,9},{13,15},{18,16},{20,... | collective-permute-start | bytes 1769480 | tf_op jit(solution)/shard_map/ppermute | solution.py:646
  1125.7 123.6 %collective-permute-start.38 = (bf16[384,1024]{1,0:T(8,128)(2,1)}, bf16[384,1024]{1,0:T(8,128)(2,1)}, u32[]{:S(2)}, u32[]{:S(2)}) collective-permute-start(bf16[384,1024]{1,0:T(8,128)(2,1)} %add.299), channel_id=1, source_target_pairs={{2,0},{4,6},{3,1},{5,7},{10,8},{12,14},{11,9},{13,15},{18,16},{20,... | collective-permute-start | bytes 2359304 | tf_op jit(solution)/shard_map/ppermute | solution.py:646
  1135.9 100.1 %slice-start = ((s8[6291456]{0:T(1024)(128)(4,1)}), s8[4194304]{0:T(1024)(128)(4,1)S(1)}, s32[]{:S(2)}) async-start(s8[6291456]{0:T(1024)(128)(4,1)} %bitcast.26), calls=%async_computation | async-start | bytes 8388608
  1232.5 88.0 %collective-permute-start.58 = (bf16[384,4480]{1,0:T(8,128)(2,1)S(1)}, bf16[384,4480]{1,0:T(8,128)(2,1)S(1)}, u32[]{:S(2)}, u32[]{:S(2)}) collective-permute-start(bf16[384,4480]{1,0:T(8,128)(2,1)S(1)} %add.320), channel_id=1, source_target_pairs={{2,0},{4,6},{3,1},{5,7},{10,8},{12,14},{11,9},{13,15},{18,16},{20,... | collective-permute-start | bytes 10321928 | tf_op jit(solution)/shard_map/ppermute | solution.py:646
  (72 other events, 1535.3 us)

commit v2 on v1

--- a/solution.py
+++ b/solution.py
@@ -16,6 +16,8 @@
 SCALE = HEAD ** (-0.5)
 SCALE_2 = SCALE * math.log2(math.e)
 MIB = 1 << 20
+CUTS = 3
+LONG = pl.CostEstimate(flops=1_000_000_000_000, bytes_accessed=1_000_000, transcendentals=0)
 BF16 = jnp.bfloat16
 F32 = jnp.float32
 
@@ -104,9 +106,7 @@
             jax.ShapeDtypeStruct((group, rows), F32),
         ],
         compiler_params=pltpu.CompilerParams(vmem_limit_bytes=32 * MIB),
-        cost_estimate=pl.CostEstimate(
-            flops=18_000_000_000, bytes_accessed=8_000_000, transcendentals=0
-        ),
+        cost_estimate=LONG,
         name="attention_forward",
     )(*lists, queries, kv, reach_rows, hot)
 
@@ -201,18 +201,34 @@
             jax.ShapeDtypeStruct((slots, 2 * HEAD), BF16),
         ],
         compiler_params=pltpu.CompilerParams(vmem_limit_bytes=40 * MIB),
-        cost_estimate=pl.CostEstimate(
-            flops=32_000_000_000, bytes_accessed=12_000_000, transcendentals=0
-        ),
+        cost_estimate=LONG,
         name="attention_backward",
     )(*lists, queries, d_att, lse, delta, kv, reach_rows, hot, cosine, sine)
 
 
-def join(mine, pieces, joined, at_col=None):
-    depth, cols = pieces[0].shape
+def join(mine, depth, places, pieces, joined, at_col=None):
+    cols = pieces[0].shape[1]
     where = slice(None) if at_col is None else pl.ds(pl.multiple_of(at_col, HEAD), cols)
-    for j, piece in enumerate(pieces):
-        joined[pl.ds(pl.multiple_of((mine ^ j) * depth, 16), depth), where] = piece[...]
+    for (j, row), piece in zip(places, pieces):
+        at = pl.multiple_of((mine ^ j) * depth + row, 16)
+        joined[pl.ds(at, piece.shape[0]), where] = piece[...]
+
+
+class Rows:
+    def __init__(self, pieces, depth, tf=None):
+        self.depth = depth
+        self.places = [(j, row) for j, row, _ in pieces]
+        self.arrays = [array for _, _, array in pieces]
+        if tf is None:
+            self.specs = [once(array.shape) for array in self.arrays]
+        else:
+            self.specs = [pl.BlockSpec((array.shape[0], tf), col_block) for array in self.arrays]
+
+    def __len__(self):
+        return len(self.arrays)
+
+    def join(self, mine, refs, joined, at_col=None):
+        join(mine, self.depth, self.places, refs, joined, at_col)
 
 
 def whole_block(*_):
@@ -231,7 +247,7 @@
     return pl.BlockSpec(shape, whole_block, pipeline_mode=pl.Buffered(1))
 
 
-def call(kernel, grid, in_specs, out_specs, out_shape, scratch, vmem, flops, size, name):
+def call(kernel, grid, in_specs, out_specs, out_shape, scratch, vmem, name):
     return pl.pallas_call(
         kernel,
         grid_spec=pltpu.PrefetchScalarGridSpec(
@@ -243,7 +259,7 @@
         ),
         out_shape=out_shape,
         compiler_params=pltpu.CompilerParams(vmem_limit_bytes=vmem * MIB),
-        cost_estimate=pl.CostEstimate(flops=flops, bytes_accessed=size, transcendentals=0),
+        cost_estimate=LONG,
         name=name,
     )
 
@@ -252,28 +268,67 @@
     return jax.ShapeDtypeStruct(dims, dtype)
 
 
-def ffn_middle_kernel(parts, tail, place, h_ref, c_ref, *refs):
-    gates, ups, downs = refs[:parts], refs[parts : 2 * parts], refs[2 * parts : 3 * parts]
-    act_ref, dg_ref, du_ref, dh_ref, gate_s, up_s, down_s, sum_s = refs[3 * parts :]
-    step = pl.program_id(0)
-    join(place[0], gates, gate_s)
-    join(place[0], ups, up_s)
-    join(place[0], downs, down_s)
+def clear_tail(tail, *joined):
     if tail:
 
-        @pl.when(step == pl.num_programs(0) - 1)
+        @pl.when(pl.program_id(0) == pl.num_programs(0) - 1)
         def _():
-            for joined in (gate_s, up_s, down_s):
-                joined[:, tail:] = jnp.zeros_like(joined[:, tail:])
-
+            for one in joined:
+                one[:, tail:] = jnp.zeros_like(one[:, tail:])
+
+
+def gate_up_kernel(gates, ups, place, h_ref, *refs):
+    gate_refs, refs = refs[: len(gates)], refs[len(gates) :]
+    up_refs, refs = refs[: len(ups)], refs[len(ups) :]
+    act_ref, by_gate_ref, by_up_ref, gate_s, up_s = refs
+    gates.join(place[0], gate_refs, gate_s)
+    ups.join(place[0], up_refs, up_s)
     gate = dot_nn(h_ref[...], gate_s[...])
     up = dot_nn(h_ref[...], up_s[...])
-    d_act = dot_nn(c_ref[...], down_s[...])
     sig = jax.nn.sigmoid(gate)
     silu = gate * sig
     act_ref[...] = (silu * up).astype(BF16)
-    d_gate = (d_act * up * sig * (1.0 + gate * (1.0 - sig))).astype(BF16)
-    d_up = (d_act * silu).astype(BF16)
+    by_up_ref[...] = silu.astype(BF16)
+    by_gate_ref[...] = (up * sig * (1.0 + gate * (1.0 - sig))).astype(BF16)
+
+
+def gate_up(place, hidden, gates, ups, depth, tf):
+    rows, width = hidden.shape
+    units = gates[0][2].shape[1]
+    gates, ups = Rows(gates, depth, tf), Rows(ups, depth, tf)
+    return call(
+        functools.partial(gate_up_kernel, gates, ups),
+        pl.cdiv(units, tf),
+        [once((rows, width))] + gates.specs + ups.specs,
+        [pl.BlockSpec((rows, tf), col_block)] * 3,
+        [shape((rows, units), BF16)] * 3,
+        [pltpu.VMEM((width, tf), BF16)] * 2,
+        60,
+        "gate_up",
+    )(place, hidden, *gates.arrays, *ups.arrays)
+
+
+def gate_up_back_kernel(gates, ups, downs, tail, place, c_ref, by_gate_ref, by_up_ref, *refs):
+    gate_refs, refs = refs[: len(gates)], refs[len(gates) :]
+    up_refs, refs = refs[: len(ups)], refs[len(ups) :]
+    down_refs, refs = refs[: len(downs)], refs[len(downs) :]
+    dg_ref, du_ref, *dh_refs, gate_s, up_s, down_s, sum_s = refs
+    step = pl.program_id(0)
+    gates.join(place[0], gate_refs, gate_s)
+    ups.join(place[0], up_refs, up_s)
+    downs.join(place[0], down_refs, down_s)
+    clear_tail(tail, gate_s, up_s, down_s)
+    d_act = dot_nn(c_ref[...], down_s[...])
+    by_gate, by_up = by_gate_ref[...].astype(F32), by_up_ref[...].astype(F32)
+    if tail:
+        last = step == pl.num_programs(0) - 1
+        inside = lax.broadcasted_iota(jnp.int32, by_gate.shape, 1) < jnp.where(
+            last, tail, by_gate.shape[1]
+        )
+        by_gate = jnp.where(inside, by_gate, 0.0)
+        by_up = jnp.where(inside, by_up, 0.0)
+    d_gate = (d_act * by_gate).astype(BF16)
+    d_up = (d_act * by_up).astype(BF16)
     dg_ref[...] = d_gate
     du_ref[...] = d_up
 
@@ -285,25 +340,48 @@
 
     @pl.when(step == pl.num_programs(0) - 1)
     def _():
-        dh_ref[...] = sum_s[...].astype(BF16)
-
-
-def ffn_middle(place, hidden, cotangent, gates, ups, downs, tf):
-    rows, width = hidden.shape
-    depth, units = gates[0].shape
-    parts = len(gates)
+        cols = dh_refs[0].shape[1]
+        for k, dh_ref in enumerate(dh_refs):
+            dh_ref[...] = sum_s[:, k * cols : (k + 1) * cols].astype(BF16)
+
+
+def gate_up_back(place, cotangent, by_gate, by_up, gates, ups, downs, depth, tf):
+    rows, width = cotangent.shape
+    units = by_gate.shape[1]
+    gates, ups, downs = (Rows(p, depth, tf) for p in (gates, ups, downs))
     return call(
-        functools.partial(ffn_middle_kernel, parts, units % tf),
+        functools.partial(gate_up_back_kernel, gates, ups, downs, units % tf),
         pl.cdiv(units, tf),
-        [once((rows, width))] * 2 + [pl.BlockSpec((depth, tf), col_block)] * (3 * parts),
-        [pl.BlockSpec((rows, tf), col_block)] * 3 + [once((rows, width))],
-        [shape((rows, units), BF16)] * 3 + [shape((rows, width), BF16)],
+        [once((rows, width))]
+        + [pl.BlockSpec((rows, tf), col_block)] * 2
+        + gates.specs
+        + ups.specs
+        + downs.specs,
+        [pl.BlockSpec((rows, tf), col_block)] * 2 + [once((rows, width // CUTS))] * CUTS,
+        [shape((rows, units), BF16)] * 2 + [shape((rows, width // CUTS), BF16)] * CUTS,
         [pltpu.VMEM((width, tf), BF16)] * 3 + [pltpu.VMEM((rows, width), F32)],
         60,
-        10 * rows * width * units,
-        6 * width * units + 6 * rows * units,
-        "ffn_middle",
-    )(place, hidden, cotangent, *gates, *ups, *downs)
+        "gate_up_back",
+    )(place, cotangent, by_gate, by_up, *gates.arrays, *ups.arrays, *downs.arrays)
+
+
+def whole_grad_kernel(left_ref, right_ref, out_ref):
+    out_ref[...] = dot_nn(left_ref[...], right_ref[...]).astype(BF16)
+
+
+def whole_grad(left_t, right, tf):
+    width, rows = left_t.shape
+    units = right.shape[1]
+    return pl.pallas_call(
+        whole_grad_kernel,
+        grid=(pl.cdiv(units, tf),),
+        in_specs=[once((width, rows)), pl.BlockSpec((rows, tf), col_block)],
+        out_specs=pl.BlockSpec((width, tf), col_block),
+        out_shape=shape((width, units), BF16),
+        compiler_params=pltpu.CompilerParams(vmem_limit_bytes=48 * MIB),
+        cost_estimate=LONG,
+        name="whole_grad",
+    )(left_t, right)
 
 
 def weight_grad_kernel(depth, parts, place, left_ref, right_ref, keep_ref, send_ref):
@@ -325,16 +403,14 @@
         [shape((width // 2, units), BF16)] * 2,
         [],
         48,
-        2 * rows * width * units,
-        2 * width * units + 2 * rows * units,
         "weight_grad",
     )(place, left_t, right)
 
 
-def down_project_kernel(parts, place, act_ref, *refs):
-    downs, (out_ref, down_s, sum_s) = refs[:parts], refs[parts:]
+def down_project_kernel(downs, place, act_ref, *refs):
+    down_refs, (out_ref, down_s, sum_s) = refs[: len(downs)], refs[len(downs) :]
     step = pl.program_id(0)
-    join(place[0], downs, down_s)
+    downs.join(place[0], down_refs, down_s)
 
     @pl.when(step == 0)
     def _():
@@ -347,23 +423,19 @@
         out_ref[...] = sum_s[...].astype(BF16)
 
 
-def down_project(place, act, downs, tf):
+def down_project(place, act, downs, width, depth, tf):
     rows, units = act.shape
-    parts = len(downs)
-    depth = downs[0].shape[0]
-    width = depth * parts
+    downs = Rows(downs, depth, tf)
     return call(
-        functools.partial(down_project_kernel, parts),
+        functools.partial(down_project_kernel, downs),
         units // tf,
-        [pl.BlockSpec((rows, tf), col_block)] + [pl.BlockSpec((depth, tf), col_block)] * parts,
+        [pl.BlockSpec((rows, tf), col_block)] + downs.specs,
         once((rows, width)),
         shape((rows, width), BF16),
         [pltpu.VMEM((width, tf), BF16), pltpu.VMEM((rows, width), F32)],
         48,
-        2 * rows * width * units,
-        2 * width * units + 2 * rows * units,
         "down_project",
-    )(place, act, *downs)
+    )(place, act, *downs.arrays)
 
 
 def inverse_rms(values):
@@ -374,12 +446,12 @@
     return values * cosine + pltpu.roll(values, HEAD // 2, 1) * sine
 
 
-def mix_kernel(parts, group, place, x_ref, gain_ref, bias_ref, cos_ref, sin_ref, *refs):
-    pieces, (q_ref, kv_ref, ht_ref, weight_s) = refs[:parts], refs[parts:]
+def mix_kernel(weight, group, place, x_ref, gain_ref, bias_ref, cos_ref, sin_ref, *refs):
+    pieces, (q_ref, kv_ref, ht_ref, weight_s) = refs[: len(weight)], refs[len(weight) :]
 
     @pl.when(pl.program_id(0) == 0)
     def _():
-        join(place[0], pieces, weight_s)
+        weight.join(place[0], pieces, weight_s)
 
     x = x_ref[...].astype(F32)
     hidden = (x * inverse_rms(x) * gain_ref[...].astype(F32)).astype(BF16)
@@ -394,12 +466,12 @@
     kv_ref[:, HEAD:] = mixed[:, split + HEAD :].astype(BF16)
 
 
-def mix(place, tokens, gain, bias, cosine, sine, pieces, group, bq):
+def mix(place, tokens, gain, bias, cosine, sine, pieces, depth, group, bq):
     rows, width = tokens.shape
-    depth, cols = pieces[0].shape
-    parts = len(pieces)
+    cols = pieces[0][2].shape[1]
+    weight = Rows(pieces, depth)
     return call(
-        functools.partial(mix_kernel, parts, group),
+        functools.partial(mix_kernel, weight, group),
         rows // bq,
         [
             pl.BlockSpec((bq, width), row_block),
@@ -408,7 +480,7 @@
             pl.BlockSpec((bq, HEAD), row_block),
             pl.BlockSpec((bq, HEAD), row_block),
         ]
-        + [once((depth, cols))] * parts,
+        + weight.specs,
         [
             pl.BlockSpec((bq, group * HEAD), row_block),
             pl.BlockSpec((bq, 2 * HEAD), row_block),
@@ -421,23 +493,21 @@
         ],
         [pltpu.VMEM((width, cols), BF16)],
         32,
-        2 * rows * width * cols,
-        2 * width * cols + 10 * rows * width,
         "mix",
-    )(place, tokens, gain[None], bias[None], cosine, sine, *pieces)
-
-
-def branch_kernel(parts, place, x_ref, own_ref, other_ref, gain_ref, *refs):
-    own_w, other_w = refs[:parts], refs[parts : 2 * parts]
-    mid_ref, h_ref, ht_ref, weight_s, att_s = refs[2 * parts :]
+    )(place, tokens, gain[None], bias[None], cosine, sine, *weight.arrays)
+
+
+def branch_kernel(weight, parts, place, x_ref, own_ref, other_ref, gain_ref, *refs):
+    own_w, other_w = refs[: len(weight)], refs[len(weight) : len(weight) + parts]
+    mid_ref, h_ref, ht_ref, weight_s, att_s = refs[len(weight) + parts :]
     split = own_ref.shape[1]
     own_at = pl.multiple_of(place[1] * split, HEAD)
     other_at = pl.multiple_of((1 - place[1]) * split, HEAD)
 
     @pl.when(pl.program_id(0) == 0)
     def _():
-        join(place[0], own_w, weight_s, own_at)
-        join(place[0], other_w, weight_s, other_at)
+        weight.join(place[0], own_w, weight_s, own_at)
+        join(place[0], weight.depth, [(j, 0) for j in range(parts)], other_w, weight_s, other_at)
 
     att_s[:, pl.ds(own_at, split)] = own_ref[...]
     att_s[:, pl.ds(other_at, split)] = other_ref[...]
@@ -448,42 +518,48 @@
     ht_ref[...] = hidden.T
 
 
-def branch(place, tokens, own, other, gain, own_pieces, other_pieces, bq):
+def branch(place, tokens, own, other, gain, pieces, other_weight, depth, bq):
     rows, width = tokens.shape
-    depth, cols = own_pieces[0].shape
-    parts = len(own_pieces)
+    cols = own.shape[1]
+    parts = width // depth
+    weight = Rows(pieces, depth)
     wide = pl.BlockSpec((bq, width), row_block)
     narrow = pl.BlockSpec((bq, cols), row_block)
+    other_specs = [
+        pl.BlockSpec((depth, cols), lambda *_, j=j: (j, 0), pipeline_mode=pl.Buffered(1))
+        for j in range(parts)
+    ]
     return call(
-        functools.partial(branch_kernel, parts),
+        functools.partial(branch_kernel, weight, parts),
         rows // bq,
-        [wide, narrow, narrow, once((1, width))] + [once((depth, cols))] * (2 * parts),
+        [wide, narrow, narrow, once((1, width))] + weight.specs + other_specs,
         [wide, wide, pl.BlockSpec((width, bq), col_block)],
         [shape((rows, width), F32), shape((rows, width), BF16), shape((width, rows), BF16)],
         [pltpu.VMEM((width, 2 * cols), BF16), pltpu.VMEM((bq, 2 * cols), BF16)],
         40,
-        4 * rows * width * cols,
-        4 * width * cols + 14 * rows * width,
         "branch",
-    )(place, tokens, own, other, gain[None], *own_pieces, *other_pieces)
+    )(place, tokens, own, other, gain[None], *weight.arrays, *([other_weight] * parts))
 
 
 def middle_back_kernel(
-    parts, group, place, own_ref, other_ref, mid_ref, c_ref, gain_ref, att_ref, *refs
+    weight, group, place, mid_ref, c_ref, gain_ref, att_ref, *refs
 ):
-    pieces, (dm_ref, dbt_ref, da_ref, delta_ref, dgain_ref, weight_s) = refs[:parts], refs[parts:]
+    own_refs, other_refs, refs = refs[:CUTS], refs[CUTS : 2 * CUTS], refs[2 * CUTS :]
+    pieces, refs = refs[: len(weight)], refs[len(weight) :]
+    dm_ref, dbt_ref, da_ref, delta_ref, dgain_ref, weight_s = refs
 
     @pl.when(pl.program_id(0) == 0)
     def _():
-        join(place[0], pieces, weight_s)
+        weight.join(place[0], pieces, weight_s)
         dgain_ref[...] = jnp.zeros_like(dgain_ref)
 
     mid = mid_ref[...]
     inverse = inverse_rms(mid)
     normed = mid * inverse
-    own = own_ref[...].astype(F32)
+    own = jnp.concatenate([ref[...] for ref in own_refs], axis=1).astype(F32)
+    other = jnp.concatenate([ref[...] for ref in other_refs], axis=1).astype(F32)
     dgain_ref[...] += jnp.sum(own * normed, axis=0, keepdims=True)
-    scaled = (own + other_ref[...].astype(F32)) * gain_ref[...].astype(F32)
+    scaled = (own + other) * gain_ref[...].astype(F32)
     d_mid = c_ref[...].astype(F32) + inverse * (
         scaled - normed * jnp.mean(scaled * normed, axis=-1, keepdims=True)
     )
@@ -499,17 +575,19 @@
         )
 
 
-def middle_back(place, own, other, mid, cotangent, gain, attended, pieces, bq):
+def middle_back(place, own, other, mid, cotangent, gain, attended, pieces, depth, bq):
     rows, width = mid.shape
-    depth, cols = pieces[0].shape
-    parts = len(pieces)
+    cols = attended.shape[1]
+    weight = Rows(pieces, depth)
     group = cols // HEAD
     wide = pl.BlockSpec((bq, width), row_block)
     narrow = pl.BlockSpec((bq, cols), row_block)
     return call(
-        functools.partial(middle_back_kernel, parts, group),
+        functools.partial(middle_back_kernel, weight, group),
         rows // bq,
-        [wide, wide, wide, wide, once((1, width)), narrow] + [once((depth, cols))] * parts,
+        [wide, wide, once((1, width)), narrow]
+        + [pl.BlockSpec((bq, width // CUTS), row_block)] * (2 * CUTS)
+        + weight.specs,
         [
             wide,
             pl.BlockSpec((width, bq), col_block),
@@ -526,20 +604,19 @@
         ],
         [pltpu.VMEM((width, cols), BF16)],
         48,
-        2 * rows * width * cols,
-        2 * width * cols + 18 * rows * width,
         "middle_back",
-    )(place, own, other, mid, cotangent, gain[None], attended, *pieces)
+    )(place, mid, cotangent, gain[None], attended, *own, *other, *weight.arrays)
 
 
 def mix_back_kernel(
-    parts, group, place, dq_ref, dkv_ref, cos_ref, sin_ref, x_ref, *refs
+    weight, group, place, dq_ref, dkv_ref, cos_ref, sin_ref, x_ref, *refs
 ):
-    pieces, (dm_ref, dh_ref, dbias_ref, dgain_ref, weight_s) = refs[:parts], refs[parts:]
+    pieces, refs = refs[: len(weight)], refs[len(weight) :]
+    dm_ref, dbias_ref, dgain_ref, *dh_refs, weight_s = refs
 
     @pl.when(pl.program_id(0) == 0)
     def _():
-        join(place[0], pieces, weight_s)
+        weight.join(place[0], pieces, weight_s)
         dgain_ref[...] = jnp.zeros_like(dgain_ref)
         dbias_ref[...] = jnp.zeros_like(dbias_ref)
 
@@ -553,17 +630,19 @@
     d_hidden = dot_nt(d_mixed, weight_s[...])
     x = x_ref[...].astype(F32)
     dgain_ref[...] += jnp.sum(d_hidden * (x * inverse_rms(x)), axis=0, keepdims=True)
-    dh_ref[...] = d_hidden.astype(BF16)
-
-
-def mix_back(place, dq, dkv, cosine, sine, tokens, pieces, bq):
+    cols = dh_refs[0].shape[1]
+    for k, dh_ref in enumerate(dh_refs):
+        dh_ref[...] = d_hidden[:, k * cols : (k + 1) * cols].astype(BF16)
+
+
+def mix_back(place, dq, dkv, cosine, sine, tokens, pieces, depth, bq):
     rows, width = tokens.shape
-    depth, cols = pieces[0].shape
-    parts = len(pieces)
+    cols = pieces[0][2].shape[1]
+    weight = Rows(pieces, depth)
     group = dq.shape[1] // HEAD
     wide = pl.BlockSpec((bq, width), row_block)
     return call(
-        functools.partial(mix_back_kernel, parts, group),
+        functools.partial(mix_back_kernel, weight, group),
         rows // bq,
         [
             pl.BlockSpec((bq, group * HEAD), row_block),
@@ -572,32 +651,33 @@
             pl.BlockSpec((bq, HEAD), row_block),
             wide,
         ]
-        + [once((depth, cols))] * parts,
+        + weight.specs,
         [
             pl.BlockSpec((bq, cols), row_block),
-            wide,
             pl.BlockSpec((1, cols), whole_block),
             pl.BlockSpec((1, width), whole_block),
-        ],
+        ]
+        + [pl.BlockSpec((bq, width // CUTS), row_block)] * CUTS,
         [
             shape((rows, cols), BF16),
-            shape((rows, width), BF16),
             shape((1, cols), F32),
             shape((1, width), F32),
-        ],
+        ]
+        + [shape((rows, width // CUTS), BF16)] * CUTS,
         [pltpu.VMEM((width, cols), BF16)],
         32,
-        2 * rows * width * cols,
-        2 * width * cols + 8 * rows * width,
         "mix_back",
-    )(place, dq, dkv, cosine, sine, tokens, *pieces)
-
-
-def input_back_kernel(place, own_ref, other_ref, x_ref, gain_ref, dm_ref, out_ref):
+    )(place, dq, dkv, cosine, sine, tokens, *weight.arrays)
+
+
+def input_back_kernel(place, x_ref, gain_ref, dm_ref, *refs):
+    own_refs, other_refs, (out_ref,) = refs[:CUTS], refs[CUTS : 2 * CUTS], refs[2 * CUTS :]
+    own = jnp.concatenate([ref[...] for ref in own_refs], axis=1).astype(F32)
+    other = jnp.concatenate([ref[...] for ref in other_refs], axis=1).astype(F32)
     x = x_ref[...].astype(F32)
     inverse = inverse_rms(x)
     normed = x * inverse
-    scaled = (own_ref[...].astype(F32) + other_ref[...].astype(F32)) * gain_ref[...].astype(F32)
+    scaled = (own + other) * gain_ref[...].astype(F32)
     out_ref[...] = dm_ref[...] + inverse * (
         scaled - normed * jnp.mean(scaled * normed, axis=-1, keepdims=True)
     )
@@ -609,15 +689,13 @@
     return call(
         input_back_kernel,
         rows // bq,
-        [wide, wide, wide, once((1, width)), wide],
+        [wide, once((1, width)), wide] + [pl.BlockSpec((bq, width // CUTS), row_block)] * (2 * CUTS),
         wide,
         shape((rows, width), F32),
         [],
         32,
-        20 * rows * width,
-        14 * rows * width,
         "input_back",
-    )(place, own, other, tokens, gain[None], d_mid)
+    )(place, tokens, gain[None], d_mid, *own, *other)
 
 
 def after(values, *first):
@@ -628,46 +706,140 @@
     return lax.ppermute(value, axis, [(i, i ^ bit) for i in range(size)])
 
 
-def gather_pieces(own, size):
-    pieces = {0: own}
-    bit = size // 2
-    while bit:
-        pieces.update({j ^ bit: swap(p, "shard", size, bit) for j, p in pieces.items()})
-        bit //= 2
-    return [pieces[j] for j in range(size)]
-
-
-def sum_over_ctx(value, size):
-    if size != 4:
-        return lax.psum(value, "ctx").astype(F32)
-    place = lax.axis_index("ctx")
-    inner = value + lax.ppermute(value, "ctx", [(0, 1), (3, 2)])
-    total = inner + lax.ppermute(inner, "ctx", [(1, 2), (2, 1)])
-    outer = lax.ppermute(total, "ctx", [(1, 0), (2, 3)])
-    middle = (place == 1) | (place == 2)
-    return jnp.where(middle, total, outer).astype(F32)
-
-
-def reduce_rows(halves, shards, contexts):
-    keep, send = halves
-    held = [keep, swap(send, "shard", shards, 1)]
-    bit = 2
-    while bit < shards:
-        count = shards // bit
-        size = keep.shape[0] // (bit // 2) // count
-
-        def pick(odd):
-            return [
-                sum(part[at * size : (at + 1) * size] for part in held)
-                for at in range(odd, count, 2)
+class Pieces:
+    def __init__(self, own, size, slabs=1):
+        if size != 4 or own.shape[0] % (16 * slabs):
+            slabs = 1
+        self.size, self.own, self.slabs = size, own, slabs
+        self.depth = own.shape[0] // slabs
+        self.got = {}
+
+    def far(self, slab, *first):
+        if slab >= self.slabs:
+            return ()
+        own = after(self.own, first)
+        own = own[slab * self.depth : (slab + 1) * self.depth]
+        got, bit = {0: own}, self.size // 2
+        while bit > 1:
+            got.update({j ^ bit: swap(p, "shard", self.size, bit) for j, p in got.items()})
+            bit //= 2
+        self.got.update({(j, slab): p for j, p in got.items() if j})
+        return [p for j, p in got.items() if j]
+
+    def far_by_ctx(self, contexts, *first):
+        own = after(self.own, first)
+        rows = own.shape[0] // contexts
+        own = lax.dynamic_slice_in_dim(own, lax.axis_index("ctx") * rows, rows, 0)
+        got, bit = {0: own}, self.size // 2
+        while bit > 1:
+            got.update({j ^ bit: swap(p, "shard", self.size, bit) for j, p in got.items()})
+            bit //= 2
+        self.parts = {j: p for j, p in got.items() if j}
+        return list(self.parts.values())
+
+    def spread(self, *first):
+        js = list(self.parts)
+        parts = after(list(self.parts.values()), first)
+        for j, part in zip(js, parts):
+            self.got[j, 0] = lax.all_gather(part, "ctx", axis=0, tiled=True)
+        return [self.got[j, 0] for j in js]
+
+    def near_own(self, *first):
+        self.near = swap(after(self.own, first), "shard", self.size, 1)
+        return self.near
+
+    def near_rest(self, slab, *first):
+        if slab >= self.slabs:
+            return ()
+        far = [j for j in range(2, self.size, 2)]
+        held = after([self.got[j, slab] for j in far], first)
+        for j, piece in zip(far, held):
+            self.got[j ^ 1, slab] = swap(piece, "shard", self.size, 1)
+        return [self.got[j ^ 1, slab] for j in far]
+
+    def all(self):
+        found = [(0, 0, self.own), (1, 0, self.near)]
+        found += [(j, k * self.depth, p) for (j, k), p in sorted(self.got.items(), key=lambda i: i[0])]
+        return found
+
+
+class Reduction:
+    def __init__(self, halves, shards, contexts, slabs=1):
+        self.keep, self.send = halves
+        self.shards, self.chain = shards, contexts == 4
+        self.slabs = slabs if shards == 4 else 1
+        self.own, self.one, self.inner, self.two, self.total, self.three = ({} for _ in range(6))
+
+    def cores(self, *first):
+        self.got = swap(after(self.send, first), "shard", self.shards, 1)
+        return self.got
+
+    def chips(self, *first):
+        held = list(after((self.keep, self.got), first))
+        bit, count = 2, self.shards // 2
+        while bit < self.shards:
+            size = held[0].shape[0] // count // self.slabs
+
+            def pick(odd, slab):
+                blocks = [
+                    [part[(at * self.slabs + slab) * size :][:size] for part in held]
+                    for at in range(odd, count, 2)
+                ]
+                return blocks[0] if len(blocks) == 1 else [
+                    jnp.concatenate(same, axis=0) for same in zip(*blocks)
+                ]
+
+            self.away = [sum(pick(1, slab)) for slab in range(self.slabs)]
+            self.last = [swap(part, "shard", self.shards, bit) for part in self.away]
+            self.here = [pick(0, slab) for slab in range(self.slabs)]
+            held = self.here[0] + self.last
+            bit, count = 2 * bit, count // 2
+        return self.last
+
+    def arrived(self, slab, *first):
+        if slab >= self.slabs:
+            return ()
+        *here, last = after(self.here[slab] + [self.last[slab]], first)
+        self.own[slab] = sum(here) + last
+        return self.own[slab]
+
+    def inward(self, slab, *first):
+        if slab >= self.slabs:
+            return ()
+        own = after(self.own[slab], first)
+        if self.chain:
+            self.own[slab] = own
+            self.one[slab] = lax.ppermute(own, "ctx", [(0, 1), (3, 2)])
+        else:
+            self.one[slab] = self.total[slab] = lax.psum(own, "ctx")
+        return self.one[slab]
+
+    def middle(self, slab, *first):
+        if not self.chain or slab >= self.slabs:
+            return ()
+        own, one = after((self.own[slab], self.one[slab]), first)
+        self.inner[slab] = own + one
+        self.two[slab] = lax.ppermute(self.inner[slab], "ctx", [(1, 2), (2, 1)])
+        return self.two[slab]
+
+    def outward(self, slab, *first):
+        if not self.chain or slab >= self.slabs:
+            return ()
+        inner, two = after((self.inner[slab], self.two[slab]), first)
+        self.total[slab] = inner + two
+        self.three[slab] = lax.ppermute(self.total[slab], "ctx", [(1, 0), (2, 3)])
+        return self.three[slab]
+
+    def result(self):
+        totals = [self.total[slab] for slab in range(self.slabs)]
+        if self.chain:
+            place = lax.axis_index("ctx")
+            inside = (place == 1) | (place == 2)
+            totals = [
+                jnp.where(inside, total, self.three[slab]) for slab, total in enumerate(totals)
             ]
-
-        away, here = pick(1), pick(0)
-        away = away[0] if len(away) == 1 else jnp.concatenate(away, axis=0)
-        here = here[0] if len(here) == 1 else jnp.concatenate(here, axis=0)
-        held = [here, swap(away, "shard", shards, bit)]
-        bit *= 2
-    return sum_over_ctx(sum(held), contexts)
+        whole = totals[0] if len(totals) == 1 else jnp.concatenate(totals, axis=0)
+        return whole.astype(F32)
 
 
 def sum_of_all(value, sizes):
@@ -729,13 +901,6 @@
     place = jnp.stack([shard, half]).astype(jnp.int32)
     across = [(i, i ^ 1) for i in range(halves)]
 
-    qkv_pieces = gather_pieces(qkv_weight, shards)
-    out_pieces = gather_pieces(after(out_weight, qkv_pieces[-1]), shards)
-    gate_pieces = gather_pieces(after(gate_weight, qkv_pieces[-1]), shards)
-    up_pieces = gather_pieces(after(up_weight, out_pieces[-1]), shards)
-    down_pieces = gather_pieces(after(down_weight, gate_pieces[-1]), shards)
-    out_other = [lax.ppermute(piece, "tp", across) for piece in out_pieces]
-
     row_first = (ctx * rows).astype(jnp.int32)
     reach, offsets = tree_tables(segment[0], parent[0])
     seg_ids = jnp.arange(reach.shape[0], dtype=jnp.int32)
@@ -765,56 +930,128 @@
     cosine = jnp.cos(angles)
     sine = jnp.sin(angles) * jnp.where(lane < HEAD // 2, -1.0, 1.0)
 
+    depth = width // shards
+    qkv, out_w, gate, up, down = (
+        Pieces(qkv_weight, shards),
+        Pieces(out_weight, shards),
+        Pieces(gate_weight, shards, 3),
+        Pieces(up_weight, shards),
+        Pieces(down_weight, shards, 3),
+    )
+    qkv_far = qkv.far(0)
+    tables = (reach_rows, hot, lists_f, lists_b, cosine, sine, place)
+    tables, qkv_far, top_grad_t = after((tables, qkv_far, cotangent.T))
+    reach_rows, hot, lists_f, lists_b, cosine, sine, place = tables
+    out_far = out_w.far(0, qkv_far)
+    qkv_near = qkv.near_own(qkv_far), qkv.near_rest(0, qkv_far)
+    out_near = out_w.near_own(qkv_far)
+    place, qkv_near = after((place, qkv_near))
+    up_parts = up.far_by_ctx(contexts, qkv_near)
+
     queries, kv_own, hidden_one_t = mix(
-        place, tokens, gain_attn, qkv_bias, cosine, sine, qkv_pieces, group, bq
-    )
-    rightward = [(i, i + 1) for i in range(contexts - 1)]
-    leftward = [(i + 1, i) for i in range(contexts - 1)]
-    kv_blocks = [kv_own]
-    for _ in range(contexts - 1):
-        kv_blocks.append(lax.ppermute(kv_blocks[-1], "ctx", rightward))
-    kv_back = jnp.concatenate(kv_blocks, axis=0)
+        place, tokens, gain_attn, qkv_bias, cosine, sine, qkv.all(), depth, group, bq
+    )
+    kv_own, out_far, out_near = after((kv_own, out_far, out_near))
+    out_rest = out_w.near_rest(0, out_far)
+    out_joined = jnp.concatenate([p for _, _, p in out_w.all()], axis=0)
+    kv_own, out_joined = after((kv_own, out_joined))
+    out_other = lax.ppermute(out_joined, "tp", across)
+    kv_far = [
+        lax.ppermute(kv_own, "ctx", [(i, i + k) for i in range(contexts - k)])
+        for k in range(1, contexts)
+    ]
+    gate_far_0 = gate.far(0, kv_own)
+    kv_far, gate_far_0, up_parts = after((kv_far, gate_far_0, up_parts))
+    kv_back = jnp.concatenate([kv_own] + kv_far, axis=0)
+    up_spread = up.spread(up_parts)
+    gate_far_1 = gate.far(1, gate_far_0)
+    own_near = gate.near_own(kv_far), up.near_own(kv_far), down.near_own(kv_far)
     attended, lse, tops = attention_forward(lists_f, queries, kv_back, reach_rows, hot, bq, bk_f)
+    attended, gate_far_1, out_other, own_near = after((attended, gate_far_1, out_other, own_near))
+    gate_far_2 = gate.far(2, attended)
     attended_other = lax.ppermute(attended, "tp", across)
+    gate_near = gate.near_rest(0, attended), gate.near_rest(1, attended)
+    attended_other, gate_near, gate_far_2 = after((attended_other, gate_near, gate_far_2))
+    place = after(place, attended_other)
+    down_far_0 = down.far(0, attended_other)
+    gate_near_2 = gate.near_rest(2, attended_other)
     mid, hidden_two, hidden_two_t = branch(
-        place, tokens, attended, attended_other, gain_ffn, out_pieces, out_other, bq
-    )
-    top_grad_t = cotangent.T
-    act, d_gate, d_up, d_hidden_two = ffn_middle(
-        place, hidden_two, cotangent, gate_pieces, up_pieces, down_pieces, 512
-    )
-
-    d_hidden_two_other = lax.ppermute(d_hidden_two, "tp", across)
-    gate_halves = weight_grad(place, hidden_two_t, d_gate, shards, 512)
-    up_halves = weight_grad(place, after(hidden_two_t, gate_halves), d_up, shards, 512)
-    down_halves = weight_grad(place, after(top_grad_t, up_halves), act, shards, 512)
-    ffn_own = down_project(place, after(act, down_halves), down_pieces, 896)
+        place, tokens, attended, attended_other, gain_ffn, out_w.all(), out_other, depth, bq
+    )
+    mid, gate_near_2, up_spread = after((mid, gate_near_2, up_spread))
+    up_near = up.near_rest(0, up_spread)
+    place, up_near = after((place, up_near))
+    down_far_1 = down.far(1, up_near)
+    act, by_gate, by_up = gate_up(place, hidden_two, gate.all(), up.all(), depth, 512)
+    act, down_far_0, down_far_1 = after((act, down_far_0, down_far_1))
+    down_far_2 = down.far(2, act)
+    down_near = down.near_rest(0, act), down.near_rest(1, act)
+    down_part = whole_grad(top_grad_t, act, 512)
+    down_part, down_near, down_far_2 = after((down_part, down_near, down_far_2))
+    down_part = lax.psum_scatter(
+        down_part, ("shard", "ctx"), scatter_dimension=0, tiled=True
+    )
+    down_near_2 = down.near_rest(2, down_far_2)
+    place, down_near_2 = after((place, down_near_2))
+    d_gate, d_up, *d_hidden_two = gate_up_back(
+        place, cotangent, by_gate, by_up, gate.all(), up.all(), down.all(), depth, 512
+    )
+
+    d_gate, d_hidden_two = after((d_gate, d_hidden_two))
+    other = [lax.ppermute(d_hidden_two[0], "tp", across)]
+    gate_grad = Reduction(weight_grad(place, hidden_two_t, d_gate, shards, 512), shards, contexts, 2)
+    gate_grad.send, other[0] = after((gate_grad.send, other[0]))
+    place = after(place, gate_grad.send)
+    gate_cores = gate_grad.cores()
+    other.append(lax.ppermute(after(d_hidden_two[1], gate_grad.send), "tp", across))
+    up_grad = Reduction(weight_grad(place, hidden_two_t, d_up, shards, 512), shards, contexts, 2)
+    up_grad.send, gate_cores, other[1] = after((up_grad.send, gate_cores, other[1]))
+    gate_chips = gate_grad.chips(gate_cores)
+    gate_away, up_grad.send = after((gate_grad.away, up_grad.send))
+    up_cores = up_grad.cores(gate_away)
+    other.append(lax.ppermute(after(d_hidden_two[2], gate_away), "tp", across))
+    place = after(place, gate_away)
+    ffn_own = down_project(place, act, down.all(), width, depth, 896)
+    ffn_own, other[2], up_cores = after((ffn_own, other[2], up_cores))
     ffn_other = lax.ppermute(ffn_own, "tp", across)
-    output = (mid + (ffn_own.astype(F32) + ffn_other.astype(F32))).astype(BF16)
-    gate_total = reduce_rows(gate_halves, shards, contexts)
-    up_total = reduce_rows(up_halves, shards, contexts)
-    down_total = reduce_rows(down_halves, shards, contexts)
-
-    d_hidden_two_other = after(d_hidden_two_other, ffn_own)
+    up_chips = up_grad.chips(up_cores)
+
+    place = after(place, ffn_own, up_grad.away)
     d_mid, d_branch_t, d_att, delta, gain_two_part = middle_back(
-        place, d_hidden_two, d_hidden_two_other, mid, cotangent, gain_ffn, attended, out_pieces, bq
-    )
+        place, d_hidden_two, other, mid, cotangent, gain_ffn, attended, out_w.all(), depth, bq
+    )
+    place = after(place, d_mid)
+    out_grad = Reduction(weight_grad(place, d_branch_t, attended, shards, 768), shards, contexts)
+    out_grad.send, gate_grad.last[0], down_part = after(
+        (out_grad.send, gate_grad.last[0], down_part)
+    )
+    down_total = lax.all_gather(down_part, "ctx", axis=0, tiled=True)
+    out_cores = out_grad.cores()
+    gate_own_0 = gate_grad.arrived(0)
+    lists_b, gate_grad.own[0] = after((lists_b, gate_own_0), down_part)
+    gate_in_0 = gate_grad.inward(0)
     d_query, d_kv = attention_backward(
         lists_b, queries, d_att, lse, delta, kv_back, reach_rows, hot, cosine, sine, bq, bk_b
     )
-    d_kv_own = d_kv[(contexts - 1) * rows :]
-    for k in range(contexts - 2, -1, -1):
-        d_kv_own = d_kv[k * rows : (k + 1) * rows] + lax.ppermute(d_kv_own, "ctx", leftward)
-    out_halves = weight_grad(place, after(d_branch_t, d_kv), attended, shards, 768)
-    out_total = reduce_rows(out_halves, shards, contexts)
-    d_mixed, d_hidden_one, bias_part, gain_one_part = mix_back(
-        place, d_query, d_kv_own, cosine, sine, tokens, qkv_pieces, bq
-    )
-    d_hidden_one_other = lax.ppermute(d_hidden_one, "tp", across)
-    qkv_halves = weight_grad(place, hidden_one_t, d_mixed, shards, 512)
-    qkv_total = reduce_rows(qkv_halves, shards, contexts)
-    input_grad = input_back(place, d_hidden_one, d_hidden_one_other, tokens, gain_attn, d_mid, bq)
-
+    d_kv, gate_grad.last, gate_grad.one, out_grad.got, ffn_other = after(
+        (d_kv, gate_grad.last, gate_grad.one, out_grad.got, ffn_other)
+    )
+    d_kv_far = [
+        lax.ppermute(d_kv[k * rows : (k + 1) * rows], "ctx", [(i + k, i) for i in range(contexts - k)])
+        for k in range(1, contexts)
+    ]
+    gate_mid_0 = gate_grad.middle(0, d_kv)
+    gate_own_1 = gate_grad.arrived(1, d_kv)
+    gate_in_1 = gate_grad.inward(1)
+    out_chips = out_grad.chips(d_kv)
+    output = (after(mid, d_kv) + (ffn_own.astype(F32) + ffn_other.astype(F32))).astype(BF16)
+    d_kv_far, output, down_total = after(
+        (d_kv_far, output, down_total), out_grad.away, gate_grad.own, gate_grad.inner
+    )
+    d_kv_own = sum((p.astype(F32) for p in d_kv_far), d_kv[:rows].astype(F32)).astype(BF16)
+    d_mixed, bias_part, gain_one_part, *d_hidden_one = mix_back(
+        place, d_query, d_kv_own, cosine, sine, tokens, qkv.all(), depth, bq
+    )
     peak_own = jnp.max(tops, axis=1)
     device = shard * contexts + ctx
     spread = jnp.where(
@@ -827,7 +1064,67 @@
     vector = jnp.concatenate(
         [gain_one_part[0], gain_two_part[0], bias_both.reshape(-1), spread.reshape(-1)]
     )
-    vector = sum_of_all(vector, sizes)
+    d_mixed, vector, d_hidden_one = after((d_mixed, vector, d_hidden_one))
+    place = after(place, d_mixed)
+    back = [lax.ppermute(d_hidden_one[0], "tp", across)]
+    vector_got = swap(vector, "shard", shards, 1)
+    qkv_grad = Reduction(weight_grad(place, hidden_one_t, d_mixed, shards, 512), shards, contexts)
+
+    qkv_grad.send, vector_got, gate_grad.one, gate_grad.two, up_grad.last[0] = after(
+        (qkv_grad.send, vector_got, gate_grad.one, gate_grad.two, up_grad.last[0])
+    )
+    qkv_cores = qkv_grad.cores()
+    vector = vector + vector_got
+    up_grad.arrived(0)
+    up_grad.inward(0)
+    gate_grad.middle(1)
+    gate_grad.outward(0)
+    qkv_cores, vector, up_grad.last, out_grad.last = after(
+        (qkv_cores, vector, up_grad.last, out_grad.last),
+        up_grad.own, gate_grad.inner, gate_grad.total,
+    )
+    qkv_grad.got = qkv_cores
+    qkv_chips = qkv_grad.chips()
+    bit = 2
+    while bit < shards:
+        vector = vector + swap(vector, "shard", shards, bit)
+        bit *= 2
+    up_grad.arrived(1)
+    up_grad.inward(1)
+    out_grad.arrived(0)
+    out_grad.inward(0)
+    back.append(lax.ppermute(after(d_hidden_one[1], vector_got), "tp", across))
+    vector, back[0], up_grad.one, gate_grad.two = after(
+        (vector, back[0], up_grad.one, gate_grad.two), qkv_grad.away, up_grad.own, out_grad.own
+    )
+    up_grad.middle(0)
+    gate_grad.outward(1)
+    back.append(lax.ppermute(after(d_hidden_one[2], back[0]), "tp", across))
+    vector = sum_of_all(vector, {"ctx": contexts})
+    vector, qkv_grad.last, up_grad.one, up_grad.two, out_grad.one = after(
+        (vector, qkv_grad.last, up_grad.one, up_grad.two, out_grad.one),
+        up_grad.inner, gate_grad.total,
+    )
+    up_grad.middle(1)
+    up_grad.outward(0)
+    out_grad.middle(0)
+    qkv_grad.arrived(0)
+    qkv_grad.inward(0)
+    back = after(back, up_grad.inner, up_grad.total, out_grad.inner, qkv_grad.own)
+    vector_got = swap(vector, "tp", halves, 1)
+    input_grad = input_back(place, d_hidden_one, back, tokens, gain_attn, d_mid, bq)
+    input_grad, vector_got, qkv_grad.one, out_grad.two, up_grad.two = after(
+        (input_grad, vector_got, qkv_grad.one, out_grad.two, up_grad.two)
+    )
+    vector = vector + vector_got
+    up_grad.outward(1)
+    out_grad.outward(0)
+    qkv_grad.middle(0)
+    qkv_grad.outward(0)
+    down_total = down_total.astype(F32)
+    gate_total, up_total, out_total, qkv_total = (
+        one.result() for one in (gate_grad, up_grad, out_grad, qkv_grad)
+    )
     bias_at = 2 * width
     spread_at = bias_at + bias_both.size
     bias_grad = lax.dynamic_slice_in_dim(

time: 1340 us -> 973 us (0.73)
  waiting for transfers between devices: 769 us -> 418 us
  starting transfers between devices: 143 us -> 97.3 us
    ppermute x30 -> x38, waiting for transfers between devices: 458 us -> 125 us  [swap(): return lax.ppermute(value, axis, [(i, i ^ bit) for i in range(size)])]
    ppermute x27 -> x31, starting transfers between devices: 108 us -> 66.5 us  [the longest x6 25 us: inward(): self.one[slab] = lax.ppermute(own, 'ctx', [(0, 1), (3, 2)])]
    ppermute x27 -> x31, waiting for transfers between devices: 308 us -> 276 us  [the longest x6 93.5 us: outward(): self.three[slab] = lax.ppermute(self.total[slab], 'ctx', [(1, 0), (2, 3)])]
    pallas_call x7 -> x9, Pallas kernels: 162 us -> 192 us  [the longest x1 62.1 us: gate_up_back(): call(functools.partial(gate_up_back_kernel, gates, ups, downs, units % tf...]
    pallas_call x5 -> x4, Pallas kernels: 70.3 us -> 51.5 us  [weight_grad(): call(functools.partial(weight_grad_kernel, width // parts, parts), pl.cdi...]
    add x23 -> x22, other arithmetic: 64.5 us -> 50.5 us  [the longest x6 14.5 us: outward(): self.total[slab] = inner + two]
    unnamed x159 -> x145, local copies, waits for them, and re-layouts: 36.4 us -> 23.8 us
    ppermute x30 -> x38, starting transfers between devices: 32.3 us -> 26.7 us  [swap(): return lax.ppermute(value, axis, [(i, i ^ bit) for i in range(size)])]
  transfers between devices with their start and end apart: 59 -> 74, of which waited for: 26 -> 25; matrix products, arithmetic and copies ran while one was open for 8% -> 13% of each run, Pallas kernels for 11% -> 29%
where the time goes in v2:
time: 973 us; the launch traced here: 965 us
  waiting for transfers between devices  418 us (43%)
  Pallas kernels  275 us (28%)
  other arithmetic  116 us (12%)
  starting transfers between devices  97.3 us (10%)
  local copies, waits for them, and re-layouts  42.8 us (4%)
  between operations  15.1 us (2%)
    ppermute x38, waiting for transfers between devices, swap(): return lax.ppermute(value, axis, [(i, i ^ bit) for i in range(size)])  125 us
    ppermute x6, waiting for transfers between devices, outward(): self.three[slab] = lax.ppermute(self.total[slab], 'ctx', [(1, 0), (2, 3)])  93.5 us
    ppermute x6, waiting for transfers between devices, inward(): self.one[slab] = lax.ppermute(own, 'ctx', [(0, 1), (3, 2)])  86.2 us
    pallas_call x1, Pallas kernels, gate_up_back(): call(functools.partial(gate_up_back_kernel, gates, ups, downs, units % tf...  62.1 us
    pallas_call x4, Pallas kernels, weight_grad(): call(functools.partial(weight_grad_kernel, width // parts, parts), pl.cdi...  51.5 us
    pallas_call x1, Pallas kernels, gate_up(): call(functools.partial(gate_up_kernel, gates, ups), pl.cdiv(units, tf), [...  40.1 us
    ppermute x3, waiting for transfers between devices, layer(): lax.ppermute(d_kv[k * rows:(k + 1) * rows], 'ctx', [(i + k, i) for i in r...  38.7 us
    ppermute x1, waiting for transfers between devices, layer(): out_other = lax.ppermute(out_joined, 'tp', across)  27.8 us
  transfers between devices with their start and end apart: 74, of which 25 were waited for; matrix products, arithmetic and copies ran while one was open for 13% of the time, Pallas kernels for 29%

profile of v2, /device:TPU:0, one launch (start us, length us, event | category | flops | bytes accessed | tf_op | source)
XLA Modules:
  0.0 964.8 jit_solution(561035418726931367)
XLA Ops:
  7.2 3.0 collective-permute-start
  22.5 3.3 copy.37
  25.9 3.1 fusion
  32.0 15.4 %collective-permute-done.3.refs_2_.refs_8_ = bf16[384,768]{1,0:T(8,128)(2,1)} collective-permute-done((bf16[384,768]{1,0:T(8,128)(2,1)}, bf16[384,768]{1,0:T(8,128)(2,1)}, u32[]{:S(2)}, u32[]{:S(2)}) %collective-permute-start.3) | collective-permute-done | bytes 589856 | tf_op jit(solution)/shard_map/ppermute | solution.py:706
  51.3 8.7 mix.1
  60.1 4.9 pad_maximum_fusion
  69.4 4.2 collective-permute-start.6
  73.6 4.5 collective-permute-start.7
  81.3 31.2 %collective-permute-done.10 = bf16[96,4480]{1,0:T(8,128)(2,1)} collective-permute-done((bf16[96,4480]{1,0:T(8,128)(2,1)S(1)}, bf16[96,4480]{1,0:T(8,128)(2,1)}, u32[]{:S(2)}, u32[]{:S(2)}) %collective-permute-start.10) | collective-permute-done | bytes 860192 | tf_op jit(solution)/shard_map/ppermute | solution.py:706
  120.3 13.6 %attention_forward.1 = (bf16[1024,768]{1,0:T(8,128)(2,1)}, f32[6,1024]{1,0:T(8,128)S(1)}, f32[6,1024]{1,0:T(8,128)S(1)}) custom-call(s32[4]{0:T(128)S(1)} %get-tuple-element.224.count, s32[128]{0:T(128)S(1)} %reshape.674.chosen, s32[33]{0:T(128)S(1)} %pad_add_fusion.9.places, bf16[1024,768]{1,0:T(8,128)(2,1)S(1)} %copy-done.35, ...), custom_call_target="tpu_custom_call" | custom-call | flops 999999995904 | bytes 1000000 | tf_op jit(solution)/shard_map/attention_forward/pallas_call | solution.py:81
  133.9 5.8 collective-permute-done.11.refs_3_
  139.7 27.8 %collective-permute-done.12.refs_4_.refs_5_.refs_6_.refs_7_ = bf16[1536,768]{1,0:T(8,128)(2,1)} collective-permute-done((bf16[1536,768]{1,0:T(8,128)(2,1)}, bf16[1536,768]{1,0:T(8,128)(2,1)}, u32[]{:S(2)}, u32[]{:S(2)}) %collective-permute-start.12) | collective-permute-done | bytes 2359328 | tf_op jit(solution)/shard_map/ppermute | solution.py:958
  176.5 6.2 all-gather.3.cloned.1.call-done.refs_10_
  182.7 17.9 %collective-permute-done.19.refs_4_ = bf16[128,4480]{1,0:T(8,128)(2,1)} collective-permute-done((bf16[128,4480]{1,0:T(8,128)(2,1)}, bf16[128,4480]{1,0:T(8,128)(2,1)}, u32[]{:S(2)}, u32[]{:S(2)}) %collective-permute-start.19) | collective-permute-done | bytes 1146912 | tf_op jit(solution)/shard_map/ppermute | solution.py:706
  206.8 12.2 %branch.1 = (f32[1024,1536]{1,0:T(8,128)}, bf16[1024,1536]{1,0:T(8,128)(2,1)S(1)}, bf16[1536,1024]{1,0:T(8,128)(2,1)S(1)}) custom-call(s32[2]{0:T(128)S(1)} %copy-done.23, bf16[1024,1536]{1,0:T(8,128)(2,1)} %x_ref.7, bf16[1024,768]{1,0:T(8,128)(2,1)} %get-tuple-element.245.own_ref.att_ref.right_ref, bf16[1024,768]{1,0:T(8,128)(2,1)} %collective-permute-done.16.other_ref, ...), custom_call_target="tpu_custom_call" | custom-call | flops 999999995904 | bytes 1000000 | tf_op jit(solution)/shard_map/branch/pallas_call | solution.py:532
  222.3 40.1 %gate_up.1 = (bf16[1024,4480]{1,0:T(8,128)(2,1)}, bf16[1024,4480]{1,0:T(8,128)(2,1)}, bf16[1024,4480]{1,0:T(8,128)(2,1)}) custom-call(s32[2]{0:T(128)} %copy-done.22, bf16[1024,1536]{1,0:T(8,128)(2,1)} %copy-done.25, bf16[384,4480]{1,0:T(8,128)(2,1)} %refs_0_.9, bf16[384,4480]{1,0:T(8,128)(2,1)} %collective-permute-done.13.refs_1_, ...), custom_call_target="tpu_custom_call" | custom-call | flops 999999995904 | bytes 1000000 | tf_op jit(solution)/shard_map/gate_up/pallas_call | solution.py:299
  262.4 2.3 slice.147
  267.1 25.4 %collective-permute-done.24.refs_16_.refs_4_ = bf16[128,4480]{1,0:T(8,128)(2,1)} collective-permute-done((bf16[128,4480]{1,0:T(8,128)(2,1)}, bf16[128,4480]{1,0:T(8,128)(2,1)}, u32[]{:S(2)}, u32[]{:S(2)}) %collective-permute-start.24) | collective-permute-done | bytes 1146912 | tf_op jit(solution)/shard_map/ppermute | solution.py:706
  292.5 18.7 %whole_grad.1 = bf16[1536,4480]{1,0:T(8,128)(2,1)} custom-call(bf16[1536,1024]{1,0:T(8,128)(2,1)S(1)} %bitcast.26, bf16[1024,4480]{1,0:T(8,128)(2,1)} %get-tuple-element.257.act_ref.right_ref), custom_call_target="tpu_custom_call" | custom-call | flops 999999995904 | bytes 1000000 | tf_op jit(solution)/shard_map/whole_grad/pallas_call | solution.py:375
  311.5 62.1 %gate_up_back.1 = (bf16[1024,4480]{1,0:T(8,128)(2,1)}, bf16[1024,4480]{1,0:T(8,128)(2,1)}, bf16[1024,512]{1,0:T(8,128)(2,1)}, bf16[1024,512]{1,0:T(8,128)(2,1)}, bf16[1024,512]{1,0:T(8,128)(2,1)}) custom-call(s32[2]{0:T(128)} %copy-done.22, bf16[1024,1536]{1,0:T(8,128)(2,1)} %c_ref.3, bf16[1024,4480]{1,0:T(8,128)(2,1)} %get-tuple-element.261.by_gate_ref, ...), custom_call_target="tpu_custom_call" | custom-call | flops 999999995904 | bytes 1000000 | tf_op jit(solution)/shard_map/gate_up_back/pallas_call | solution.py:352
  375.1 19.1 %weight_grad.4 = (bf16[768,4480]{1,0:T(8,128)(2,1)}, bf16[768,4480]{1,0:T(8,128)(2,1)}) custom-call(s32[2]{0:T(128)S(1)} %copy-done.24, bf16[1536,1024]{1,0:T(8,128)(2,1)S(1)} %copy-done.27, bf16[1024,4480]{1,0:T(8,128)(2,1)} %get-tuple-element.269.right_ref), custom_call_target="tpu_custom_call" | custom-call | flops 999999995904 | bytes 1000000 | tf_op jit(solution)/shard_map/weight_grad/pallas_call | solution.py:398
  394.3 5.2 collective-permute-done.28.refs_3_
  401.0 19.2 %weight_grad.5 = (bf16[768,4480]{1,0:T(8,128)(2,1)}, bf16[768,4480]{1,0:T(8,128)(2,1)}) custom-call(s32[2]{0:T(128)S(1)} %copy-done.24, bf16[1536,1024]{1,0:T(8,128)(2,1)S(1)} %copy-done.27, bf16[1024,4480]{1,0:T(8,128)(2,1)} %get-tuple-element.277.right_ref), custom_call_target="tpu_custom_call" | custom-call | flops 999999995904 | bytes 1000000 | tf_op jit(solution)/shard_map/weight_grad/pallas_call | solution.py:398
  420.2 4.4 collective-permute-done.30.refs_4_
  424.6 9.2 slice_add_fusion.2
  437.4 23.7 %down_project.1 = bf16[1024,1536]{1,0:T(8,128)(2,1)} custom-call(s32[2]{0:T(128)S(1)} %copy-done.24, bf16[1024,4480]{1,0:T(8,128)(2,1)} %get-tuple-element.257.act_ref.right_ref, bf16[384,4480]{1,0:T(8,128)(2,1)} %refs_0_.10, bf16[384,4480]{1,0:T(8,128)(2,1)} %collective-permute-done.15.refs_13_.refs_1_, ...), custom_call_target="tpu_custom_call" | custom-call | flops 999999995904 | bytes 1000000 | tf_op jit(solution)/shard_map/down_project/pallas_call | solution.py:429
  463.3 9.1 fusion.34
  473.1 13.4 %middle_back.1 = (f32[1024,1536]{1,0:T(8,128)}, bf16[1536,1024]{1,0:T(8,128)(2,1)}, bf16[1024,768]{1,0:T(8,128)(2,1)}, f32[6,1024]{1,0:T(8,128)S(1)}, f32[1,1536]{1,0:T(1,128)S(1)}) custom-call(s32[2]{0:T(128)S(1)} %copy-done.24, f32[1024,1536]{1,0:T(8,128)} %get-tuple-element.320.mid_ref, bf16[1024,1536]{1,0:T(8,128)(2,1)} %c_ref.3, ...), custom_call_target="tpu_custom_call" | custom-call | flops 999999995904 | bytes 1000000 | tf_op jit(solution)/shard_map/middle_back/pallas_call | solution.py:585
  486.5 6.5 weight_grad.6
  493.7 4.1 add_add_fusion.3
  497.8 4.7 collective-permute-start.35
  504.1 17.9 %attention_backward.1 = (bf16[1024,768]{1,0:T(8,128)(2,1)S(1)}, bf16[4096,256]{1,0:T(8,128)(2,1)S(1)}) custom-call(s32[4]{0:T(128)S(1)} %get-tuple-element.310.count, s32[32]{0:T(128)S(1)} %reshape.675.chosen, s32[9]{0:T(128)S(1)} %pad_add_fusion.10.places, bf16[1024,768]{1,0:T(8,128)(2,1)S(1)} %copy-done.36, bf16[1024,768]{1,0:T(8,128)(2,1)S(1)} %copy-done.31, ...), custom_call_target="tpu_custom_call" | custom-call | flops 999999995904 | bytes 1000000 | tf_op jit(solution)/shard_map/attention_backward/pallas_call | solution.py:173
  523.5 8.4 collective-permute-done.37
  531.9 42.6 %collective-permute-done.35 = bf16[192,4480]{1,0:T(8,128)(2,1)} collective-permute-done((bf16[192,4480]{1,0:T(8,128)(2,1)}, bf16[192,4480]{1,0:T(8,128)(2,1)}, u32[]{:S(2)}, u32[]{:S(2)}) %collective-permute-start.35) | collective-permute-done | bytes 1720352 | tf_op jit(solution)/shard_map/ppermute | solution.py:812
  578.5 3.6 add_add_fusion.2
  583.0 5.8 add_convert_fusion
  588.7 3.6 add.316
  592.3 2.6 fusion.37
  597.0 38.7 %collective-permute-done.39 = bf16[1024,256]{1,0:T(8,128)(2,1)} collective-permute-done((bf16[1024,256]{1,0:T(8,128)(2,1)S(1)}, bf16[1024,256]{1,0:T(8,128)(2,1)}, u32[]{:S(2)}, u32[]{:S(2)}) %collective-permute-start.39) | collective-permute-done | bytes 524320 | tf_op jit(solution)/shard_map/ppermute | solution.py:1040
  635.7 2.5 collective-permute-start.42
  642.0 7.8 mix_back.1
  655.4 6.7 weight_grad.7
  662.1 7.0 collective-permute-done.42
  673.3 2.4 add.324
  676.6 6.0 collective-permute-start.50
  682.5 3.6 add.325
  688.1 3.2 collective-permute-start.51
  700.0 19.8 %collective-permute-done.49.refs_3_ = bf16[1024,512]{1,0:T(8,128)(2,1)S(1)} collective-permute-done((bf16[1024,512]{1,0:T(8,128)(2,1)S(1)}, bf16[1024,512]{1,0:T(8,128)(2,1)S(1)}, u32[]{:S(2)}, u32[]{:S(2)}) %collective-permute-start.49) | collective-permute-done | bytes 1048608 | tf_op jit(solution)/shard_map/ppermute | solution.py:1069
  720.3 36.0 %collective-permute-done.51 = bf16[192,4480]{1,0:T(8,128)(2,1)S(1)} collective-permute-done((bf16[192,4480]{1,0:T(8,128)(2,1)S(1)}, bf16[192,4480]{1,0:T(8,128)(2,1)S(1)}, u32[]{:S(2)}, u32[]{:S(2)}) %collective-permute-start.51) | collective-permute-done | bytes 1720352 | tf_op jit(solution)/shard_map/ppermute | solution.py:812
  760.1 4.1 collective-permute-start.55
  767.9 5.5 convert_element_type.93
  777.2 24.7 %collective-permute-done.56 = f32[5312]{0:T(1024)S(1)} collective-permute-done((f32[5312]{0:T(1024)S(1)}, f32[5312]{0:T(1024)S(1)}, u32[]{:S(2)}, u32[]{:S(2)}) %collective-permute-start.56) | collective-permute-done | bytes 21280 | tf_op jit(solution)/shard_map/ppermute | solution.py:706
  802.9 3.0 broadcast_select_fusion.3
  810.5 6.6 collective-permute-start.61
  819.7 3.6 add.337
  827.8 5.7 input_back.1
  837.5 13.3 %collective-permute-done.68 = bf16[192,4480]{1,0:T(8,128)(2,1)} collective-permute-done((bf16[192,4480]{1,0:T(8,128)(2,1)}, bf16[192,4480]{1,0:T(8,128)(2,1)}, u32[]{:S(2)}, u32[]{:S(2)}) %collective-permute-start.68) | collective-permute-done | bytes 1720352 | tf_op jit(solution)/shard_map/ppermute | solution.py:830
  852.5 3.3 maximum_convert_fusion
  855.8 2.4 add.346
  865.5 22.1 %collective-permute-done.69 = bf16[192,4480]{1,0:T(8,128)(2,1)S(1)} collective-permute-done((bf16[192,4480]{1,0:T(8,128)(2,1)S(1)}, bf16[192,4480]{1,0:T(8,128)(2,1)S(1)}, u32[]{:S(2)}, u32[]{:S(2)}) %collective-permute-start.69) | collective-permute-done | bytes 1720352 | tf_op jit(solution)/shard_map/ppermute | solution.py:830
  890.4 46.8 %collective-permute-done.66 = bf16[384,768]{1,0:T(8,128)(2,1)} collective-permute-done((bf16[384,768]{1,0:T(8,128)(2,1)}, bf16[384,768]{1,0:T(8,128)(2,1)}, u32[]{:S(2)}, u32[]{:S(2)}) %collective-permute-start.66) | collective-permute-done | bytes 589856 | tf_op jit(solution)/shard_map/ppermute | solution.py:830
  939.4 11.3 %collective-permute-done.65 = bf16[384,1024]{1,0:T(8,128)(2,1)} collective-permute-done((bf16[384,1024]{1,0:T(8,128)(2,1)}, bf16[384,1024]{1,0:T(8,128)(2,1)}, u32[]{:S(2)}, u32[]{:S(2)}) %collective-permute-start.65) | collective-permute-done | bytes 786464 | tf_op jit(solution)/shard_map/ppermute | solution.py:830
  950.7 2.4 select_convert_fusion
  954.7 3.3 maximum_convert_fusion.1
  (378 shorter events, 144.5 us)
Async XLA Ops:
  7.2 175.6 %all-gather.3.cloned.1.call-start = ((), (), s32[]{:S(2)}) async-start(), calls=%async_computation.1 | async-start | bytes 4300800 | tf_op jit(solution)/shard_map/all_gather | solution.py:744
  7.2 24.1 %collective-permute-start = (bf16[384,1024]{1,0:T(8,128)(2,1)}, bf16[384,1024]{1,0:T(8,128)(2,1)}, u32[]{:S(2)}, u32[]{:S(2)}) collective-permute-start(bf16[384,1024]{1,0:T(8,128)(2,1)} %refs_0_.11), channel_id=1, source_target_pairs={{0,16},{8,24},{16,0},{24,8},{1,17},{9,25},{17,1},{25,9},{2,18},{10... | collective-permute-start | bytes 2359304 | tf_op jit(solution)/shard_map/ppermute | solution.py:706
  31.3 16.1 %collective-permute-start.2 = (bf16[384,1024]{1,0:T(8,128)(2,1)}, bf16[384,1024]{1,0:T(8,128)(2,1)}, u32[]{:S(2)}, u32[]{:S(2)}) collective-permute-start(bf16[384,1024]{1,0:T(8,128)(2,1)} %collective-permute-done.refs_2_), channel_id=1, source_target_pairs={{0,8},{8,0},{16,24},{24,16},{1,9},{9,1},{17,25},{25,17},{2,10},{10... | collective-permute-start | bytes 2359304 | tf_op jit(solution)/shard_map/ppermute | solution.py:706
  31.9 28.2 %collective-permute-start.4 = (bf16[384,768]{1,0:T(8,128)(2,1)}, bf16[384,768]{1,0:T(8,128)(2,1)}, u32[]{:S(2)}, u32[]{:S(2)}) collective-permute-start(bf16[384,768]{1,0:T(8,128)(2,1)} %refs_6_.1), channel_id=1, source_target_pairs={{0,8},{8,0},{16,24},{24,16},{1,9},{9,1},{17,25},{25,17},{2,10},{10... | collective-permute-start | bytes 1769480 | tf_op jit(solution)/shard_map/ppermute | solution.py:706
  66.1 50.3 %collective-permute-start.9 = (bf16[128,4480]{1,0:T(8,128)(2,1)}, bf16[128,4480]{1,0:T(8,128)(2,1)}, u32[]{:S(2)}, u32[]{:S(2)}) collective-permute-start(bf16[128,4480]{1,0:T(8,128)(2,1)} %slice.142), channel_id=1, source_target_pairs={{0,16},{8,24},{16,0},{24,8},{1,17},{9,25},{17,1},{25,9},{2,18},{10... | collective-permute-start | bytes 3440648 | tf_op jit(solution)/shard_map/ppermute | solution.py:706
  67.6 44.9 %collective-permute-start.10 = (bf16[96,4480]{1,0:T(8,128)(2,1)S(1)}, bf16[96,4480]{1,0:T(8,128)(2,1)}, u32[]{:S(2)}, u32[]{:S(2)}) collective-permute-start(bf16[96,4480]{1,0:T(8,128)(2,1)S(1)} %constant_dynamic-slice_fusion.1), channel_id=1, source_target_pairs={{0,16},{8,24},{16,0},{24,8},{1,17},{9,25},{17,1},{25,9},{2,18},{10... | collective-permute-start | bytes 2580488 | tf_op jit(solution)/shard_map/ppermute | solution.py:706
  69.4 45.1 %collective-permute-start.6 = (bf16[1024,256]{1,0:T(8,128)(2,1)}, bf16[1024,256]{1,0:T(8,128)(2,1)}, u32[]{:S(2)}, u32[]{:S(2)}) collective-permute-start(bf16[1024,256]{1,0:T(8,128)(2,1)} %get-tuple-element.233), channel_id=1, source_target_pairs={{0,2},{2,4},{4,6},{1,3},{3,5},{5,7},{8,10},{10,12},{12,14},{9,11},... | collective-permute-start | bytes 1572872 | tf_op jit(solution)/shard_map/ppermute | solution.py:960
  73.6 42.7 %collective-permute-start.7 = (bf16[1024,256]{1,0:T(8,128)(2,1)}, bf16[1024,256]{1,0:T(8,128)(2,1)}, u32[]{:S(2)}, u32[]{:S(2)}) collective-permute-start(bf16[1024,256]{1,0:T(8,128)(2,1)} %get-tuple-element.233), channel_id=1, source_target_pairs={{0,4},{2,6},{1,5},{3,7},{8,12},{10,14},{9,13},{11,15},{16,20},{18,... | collective-permute-start | bytes 1572872 | tf_op jit(solution)/shard_map/ppermute | solution.py:960
  78.1 38.2 %collective-permute-start.8 = (bf16[1024,256]{1,0:T(8,128)(2,1)}, bf16[1024,256]{1,0:T(8,128)(2,1)}, u32[]{:S(2)}, u32[]{:S(2)}) collective-permute-start(bf16[1024,256]{1,0:T(8,128)(2,1)} %get-tuple-element.233), channel_id=1, source_target_pairs={{0,6},{1,7},{8,14},{9,15},{16,22},{17,23},{24,30},{25,31}} | collective-permute-start | bytes 1572872 | tf_op jit(solution)/shard_map/ppermute | solution.py:960
  112.5 27.2 %collective-permute-start.11 = (bf16[128,4480]{1,0:T(8,128)(2,1)}, bf16[128,4480]{1,0:T(8,128)(2,1)}, u32[]{:S(2)}, u32[]{:S(2)}) collective-permute-start(bf16[128,4480]{1,0:T(8,128)(2,1)} %slice.181), channel_id=1, source_target_pairs={{0,16},{8,24},{16,0},{24,8},{1,17},{9,25},{17,1},{25,9},{2,18},{10... | collective-permute-start | bytes 3440648 | tf_op jit(solution)/shard_map/ppermute | solution.py:706
  112.8 380.8 %reduce-scatter.2.cloned.1.call-start = ((), (), s32[]{:S(2)}) async-start(), calls=%async_computation.2 | async-start | bytes 14622720 | tf_op jit(solution)/shard_map/reduce_scatter | solution.py:991
  114.5 53.0 %collective-permute-start.12 = (bf16[1536,768]{1,0:T(8,128)(2,1)}, bf16[1536,768]{1,0:T(8,128)(2,1)}, u32[]{:S(2)}, u32[]{:S(2)}) collective-permute-start(bf16[1536,768]{1,0:T(8,128)(2,1)} %pad_maximum_fusion), channel_id=1, source_target_pairs={{0,1},{1,0},{2,3},{3,2},{4,5},{5,4},{6,7},{7,6},{8,9},{9,8},{10,11... | collective-permute-start | bytes 7077896 | tf_op jit(solution)/shard_map/ppermute | solution.py:958
  116.3 51.2 %collective-permute-start.15 = (bf16[384,4480]{1,0:T(8,128)(2,1)}, bf16[384,4480]{1,0:T(8,128)(2,1)}, u32[]{:S(2)}, u32[]{:S(2)}) collective-permute-start(bf16[384,4480]{1,0:T(8,128)(2,1)} %refs_0_.10), channel_id=1, source_target_pairs={{0,8},{8,0},{16,24},{24,16},{1,9},{9,1},{17,25},{25,17},{2,10},{10... | collective-permute-start | bytes 10321928 | tf_op jit(solution)/shard_map/ppermute | solution.py:706
  116.4 51.1 %collective-permute-start.14 = (bf16[384,4480]{1,0:T(8,128)(2,1)}, bf16[384,4480]{1,0:T(8,128)(2,1)}, u32[]{:S(2)}, u32[]{:S(2)}) collective-permute-start(bf16[384,4480]{1,0:T(8,128)(2,1)} %refs_8_.3), channel_id=1, source_target_pairs={{0,8},{8,0},{16,24},{24,16},{1,9},{9,1},{17,25},{25,17},{2,10},{10... | collective-permute-start | bytes 10321928 | tf_op jit(solution)/shard_map/ppermute | solution.py:706
  116.9 50.6 %collective-permute-start.13 = (bf16[384,4480]{1,0:T(8,128)(2,1)}, bf16[384,4480]{1,0:T(8,128)(2,1)}, u32[]{:S(2)}, u32[]{:S(2)}) collective-permute-start(bf16[384,4480]{1,0:T(8,128)(2,1)} %refs_0_.9), channel_id=1, source_target_pairs={{0,8},{8,0},{16,24},{24,16},{1,9},{9,1},{17,25},{25,17},{2,10},{10... | collective-permute-start | bytes 10321928 | tf_op jit(solution)/shard_map/ppermute | solution.py:706
  167.5 35.2 %collective-permute-start.16 = (bf16[1024,768]{1,0:T(8,128)(2,1)}, bf16[1024,768]{1,0:T(8,128)(2,1)}, u32[]{:S(2)}, u32[]{:S(2)}) collective-permute-start(bf16[1024,768]{1,0:T(8,128)(2,1)} %get-tuple-element.245.own_ref.att_ref.right_ref), channel_id=1, source_target_pairs={{0,1},{1,0},{2,3},{3,2},{4,5},{5,4},{6,7},{7,6},{8,9},{9,8},{10,11... | collective-permute-start | bytes 4718600 | tf_op jit(solution)/shard_map/ppermute | solution.py:972
  172.2 28.4 %collective-permute-start.19 = (bf16[128,4480]{1,0:T(8,128)(2,1)}, bf16[128,4480]{1,0:T(8,128)(2,1)}, u32[]{:S(2)}, u32[]{:S(2)}) collective-permute-start(bf16[128,4480]{1,0:T(8,128)(2,1)} %slice.144), channel_id=1, source_target_pairs={{0,16},{8,24},{16,0},{24,8},{1,17},{9,25},{17,1},{25,9},{2,18},{10... | collective-permute-start | bytes 3440648 | tf_op jit(solution)/shard_map/ppermute | solution.py:706
  176.0 86.4 %collective-permute-start.23 = (bf16[128,4480]{1,0:T(8,128)(2,1)}, bf16[128,4480]{1,0:T(8,128)(2,1)}, u32[]{:S(2)}, u32[]{:S(2)}) collective-permute-start(bf16[128,4480]{1,0:T(8,128)(2,1)} %slice.182), channel_id=1, source_target_pairs={{0,16},{8,24},{16,0},{24,8},{1,17},{9,25},{17,1},{25,9},{2,18},{10... | collective-permute-start | bytes 3440648 | tf_op jit(solution)/shard_map/ppermute | solution.py:706
  182.7 39.6 %collective-permute-start.20 = (bf16[384,4480]{1,0:T(8,128)(2,1)}, bf16[384,4480]{1,0:T(8,128)(2,1)}, u32[]{:S(2)}, u32[]{:S(2)}) collective-permute-start(bf16[384,4480]{1,0:T(8,128)(2,1)} %all-gather.3.cloned.1.call-done.refs_10_), channel_id=1, source_target_pairs={{0,8},{8,0},{16,24},{24,16},{1,9},{9,1},{17,25},{25,17},{2,10},{10... | collective-permute-start | bytes 10321928 | tf_op jit(solution)/shard_map/ppermute | solution.py:706
  202.7 19.6 %collective-permute-start.21 = (bf16[128,4480]{1,0:T(8,128)(2,1)}, bf16[128,4480]{1,0:T(8,128)(2,1)}, u32[]{:S(2)}, u32[]{:S(2)}) collective-permute-start(bf16[128,4480]{1,0:T(8,128)(2,1)} %collective-permute-done.19.refs_4_), channel_id=1, source_target_pairs={{0,8},{8,0},{16,24},{24,16},{1,9},{9,1},{17,25},{25,17},{2,10},{10... | collective-permute-start | bytes 3440648 | tf_op jit(solution)/shard_map/ppermute | solution.py:706
  205.1 57.4 %collective-permute-start.22 = (bf16[128,4480]{1,0:T(8,128)(2,1)}, bf16[128,4480]{1,0:T(8,128)(2,1)}, u32[]{:S(2)}, u32[]{:S(2)}) collective-permute-start(bf16[128,4480]{1,0:T(8,128)(2,1)} %slice.145), channel_id=1, source_target_pairs={{0,16},{8,24},{16,0},{24,8},{1,17},{9,25},{17,1},{25,9},{2,18},{10... | collective-permute-start | bytes 3440648 | tf_op jit(solution)/shard_map/ppermute | solution.py:706
  264.8 27.7 %collective-permute-start.24 = (bf16[128,4480]{1,0:T(8,128)(2,1)}, bf16[128,4480]{1,0:T(8,128)(2,1)}, u32[]{:S(2)}, u32[]{:S(2)}) collective-permute-start(bf16[128,4480]{1,0:T(8,128)(2,1)} %slice.147), channel_id=1, source_target_pairs={{0,16},{8,24},{16,0},{24,8},{1,17},{9,25},{17,1},{25,9},{2,18},{10... | collective-permute-start | bytes 3440648 | tf_op jit(solution)/shard_map/ppermute | solution.py:706
  266.6 44.6 %collective-permute-start.26 = (bf16[128,4480]{1,0:T(8,128)(2,1)}, bf16[128,4480]{1,0:T(8,128)(2,1)}, u32[]{:S(2)}, u32[]{:S(2)}) collective-permute-start(bf16[128,4480]{1,0:T(8,128)(2,1)} %collective-permute-done.22.refs_14_.refs_2_), channel_id=1, source_target_pairs={{0,8},{8,0},{16,24},{24,16},{1,9},{9,1},{17,25},{25,17},{2,10},{10... | collective-permute-start | bytes 3440648 | tf_op jit(solution)/shard_map/ppermute | solution.py:706
  266.6 44.6 %collective-permute-start.27 = (bf16[128,4480]{1,0:T(8,128)(2,1)}, bf16[128,4480]{1,0:T(8,128)(2,1)}, u32[]{:S(2)}, u32[]{:S(2)}) collective-permute-start(bf16[128,4480]{1,0:T(8,128)(2,1)} %collective-permute-done.23.refs_15_.refs_3_), channel_id=1, source_target_pairs={{0,8},{8,0},{16,24},{24,16},{1,9},{9,1},{17,25},{25,17},{2,10},{10... | collective-permute-start | bytes 3440648 | tf_op jit(solution)/shard_map/ppermute | solution.py:706
  292.5 18.9 %collective-permute-start.25 = (bf16[128,4480]{1,0:T(8,128)(2,1)}, bf16[128,4480]{1,0:T(8,128)(2,1)}, u32[]{:S(2)}, u32[]{:S(2)}) collective-permute-start(bf16[128,4480]{1,0:T(8,128)(2,1)} %collective-permute-done.24.refs_16_.refs_4_), channel_id=1, source_target_pairs={{0,8},{8,0},{16,24},{24,16},{1,9},{9,1},{17,25},{25,17},{2,10},{10... | collective-permute-start | bytes 3440648 | tf_op jit(solution)/shard_map/ppermute | solution.py:706
  311.2 327.0 %all-gather.5.cloned.1.call-start = ((), (), s32[]{:S(2)}) async-start(), calls=%async_computation.3 | async-start | bytes 4300800 | tf_op jit(solution)/shard_map/all_gather | solution.py:1028
  373.5 25.9 %collective-permute-start.28 = (bf16[1024,512]{1,0:T(8,128)(2,1)}, bf16[1024,512]{1,0:T(8,128)(2,1)}, u32[]{:S(2)}, u32[]{:S(2)}) collective-permute-start(bf16[1024,512]{1,0:T(8,128)(2,1)} %get-tuple-element.272.refs_0_), channel_id=1, source_target_pairs={{0,1},{1,0},{2,3},{3,2},{4,5},{5,4},{6,7},{7,6},{8,9},{9,8},{10,11... | collective-permute-start | bytes 3145736 | tf_op jit(solution)/shard_map/ppermute | solution.py:1001
  399.5 25.1 %collective-permute-start.30 = (bf16[1024,512]{1,0:T(8,128)(2,1)}, bf16[1024,512]{1,0:T(8,128)(2,1)}, u32[]{:S(2)}, u32[]{:S(2)}) collective-permute-start(bf16[1024,512]{1,0:T(8,128)(2,1)} %get-tuple-element.280.refs_1_), channel_id=1, source_target_pairs={{0,1},{1,0},{2,3},{3,2},{4,5},{5,4},{6,7},{7,6},{8,9},{9,8},{10,11... | collective-permute-start | bytes 3145736 | tf_op jit(solution)/shard_map/ppermute | solution.py:1006
  401.0 23.6 %collective-permute-start.29 = (bf16[768,4480]{1,0:T(8,128)(2,1)}, bf16[768,4480]{1,0:T(8,128)(2,1)}, u32[]{:S(2)}, u32[]{:S(2)}) collective-permute-start(bf16[768,4480]{1,0:T(8,128)(2,1)} %get-tuple-element.273), channel_id=1, source_target_pairs={{0,8},{8,0},{16,24},{24,16},{1,9},{9,1},{17,25},{25,17},{2,10},{10... | collective-permute-start | bytes 20643848 | tf_op jit(solution)/shard_map/ppermute | solution.py:706
  433.8 59.8 %collective-permute-start.33 = (bf16[192,4480]{1,0:T(8,128)(2,1)}, bf16[192,4480]{1,0:T(8,128)(2,1)}, u32[]{:S(2)}, u32[]{:S(2)}) collective-permute-start(bf16[192,4480]{1,0:T(8,128)(2,1)} %get-tuple-element.282), channel_id=1, source_target_pairs={{0,16},{8,24},{16,0},{24,8},{1,17},{9,25},{17,1},{25,9},{2,18},{10... | collective-permute-start | bytes 5160968 | tf_op jit(solution)/shard_map/ppermute | solution.py:706
  434.3 87.7 %collective-permute-start.34 = (bf16[192,4480]{1,0:T(8,128)(2,1)}, bf16[192,4480]{1,0:T(8,128)(2,1)}, u32[]{:S(2)}, u32[]{:S(2)}) collective-permute-start(bf16[192,4480]{1,0:T(8,128)(2,1)} %get-tuple-element.283), channel_id=1, source_target_pairs={{0,16},{8,24},{16,0},{24,8},{1,17},{9,25},{17,1},{25,9},{2,18},{10... | collective-permute-start | bytes 5160968 | tf_op jit(solution)/shard_map/ppermute | solution.py:706
  435.9 25.2 %collective-permute-start.32 = (bf16[768,4480]{1,0:T(8,128)(2,1)}, bf16[768,4480]{1,0:T(8,128)(2,1)}, u32[]{:S(2)}, u32[]{:S(2)}) collective-permute-start(bf16[768,4480]{1,0:T(8,128)(2,1)} %get-tuple-element.288), channel_id=1, source_target_pairs={{0,8},{8,0},{16,24},{24,16},{1,9},{9,1},{17,25},{25,17},{2,10},{10... | collective-permute-start | bytes 20643848 | tf_op jit(solution)/shard_map/ppermute | solution.py:706
  435.9 25.9 %collective-permute-start.31 = (bf16[1024,512]{1,0:T(8,128)(2,1)}, bf16[1024,512]{1,0:T(8,128)(2,1)}, u32[]{:S(2)}, u32[]{:S(2)}) collective-permute-start(bf16[1024,512]{1,0:T(8,128)(2,1)} %get-tuple-element.286.refs_2_), channel_id=1, source_target_pairs={{0,1},{1,0},{2,3},{3,2},{4,5},{5,4},{6,7},{7,6},{8,9},{9,8},{10,11... | collective-permute-start | bytes 3145736 | tf_op jit(solution)/shard_map/ppermute | solution.py:1012
  461.8 70.0 %collective-permute-start.37 = (bf16[1024,1536]{1,0:T(8,128)(2,1)}, bf16[1024,1536]{1,0:T(8,128)(2,1)}, u32[]{:S(2)}, u32[]{:S(2)}) collective-permute-start(bf16[1024,1536]{1,0:T(8,128)(2,1)} %down_project.1), channel_id=1, source_target_pairs={{0,1},{1,0},{2,3},{3,2},{4,5},{5,4},{6,7},{7,6},{8,9},{9,8},{10,11... | collective-permute-start | bytes 9437192 | tf_op jit(solution)/shard_map/ppermute | solution.py:1016
  472.4 189.6 %collective-permute-start.44 = (bf16[192,4480]{1,0:T(8,128)(2,1)}, bf16[192,4480]{1,0:T(8,128)(2,1)}, u32[]{:S(2)}, u32[]{:S(2)}) collective-permute-start(bf16[192,4480]{1,0:T(8,128)(2,1)} %get-tuple-element.441), channel_id=1, source_target_pairs={{0,16},{8,24},{16,0},{24,8},{1,17},{9,25},{17,1},{25,9},{2,18},{10... | collective-permute-start | bytes 5160968 | tf_op jit(solution)/shard_map/ppermute | solution.py:706
  497.8 76.7 %collective-permute-start.35 = (bf16[192,4480]{1,0:T(8,128)(2,1)}, bf16[192,4480]{1,0:T(8,128)(2,1)}, u32[]{:S(2)}, u32[]{:S(2)}) collective-permute-start(bf16[192,4480]{1,0:T(8,128)(2,1)} %add_add_fusion.3), channel_id=1, source_target_pairs={{0,2},{6,4},{1,3},{7,5},{8,10},{14,12},{9,11},{15,13},{16,18},{22,... | collective-permute-start | bytes 5160968 | tf_op jit(solution)/shard_map/ppermute | solution.py:812
  502.5 29.4 %collective-permute-start.36 = (bf16[768,768]{1,0:T(8,128)(2,1)}, bf16[768,768]{1,0:T(8,128)(2,1)}, u32[]{:S(2)}, u32[]{:S(2)}) collective-permute-start(bf16[768,768]{1,0:T(8,128)(2,1)} %get-tuple-element.318), channel_id=1, source_target_pairs={{0,8},{8,0},{16,24},{24,16},{1,9},{9,1},{17,25},{25,17},{2,10},{10... | collective-permute-start | bytes 3538952 | tf_op jit(solution)/shard_map/ppermute | solution.py:706
  522.0 164.1 %collective-permute-start.46 = (bf16[192,4480]{1,0:T(8,128)(2,1)}, bf16[192,4480]{1,0:T(8,128)(2,1)}, u32[]{:S(2)}, u32[]{:S(2)}) collective-permute-start(bf16[192,4480]{1,0:T(8,128)(2,1)} %get-tuple-element.442), channel_id=1, source_target_pairs={{0,16},{8,24},{16,0},{24,8},{1,17},{9,25},{17,1},{25,9},{2,18},{10... | collective-permute-start | bytes 5160968 | tf_op jit(solution)/shard_map/ppermute | solution.py:706
  574.6 20.4 %collective-permute-start.38 = (bf16[1024,256]{1,0:T(8,128)(2,1)S(1)}, bf16[1024,256]{1,0:T(8,128)(2,1)}, u32[]{:S(2)}, u32[]{:S(2)}) collective-permute-start(bf16[1024,256]{1,0:T(8,128)(2,1)S(1)} %get-tuple-element.451), channel_id=1, source_target_pairs={{2,0},{4,2},{6,4},{3,1},{5,3},{7,5},{10,8},{12,10},{14,12},{11,9},... | collective-permute-start | bytes 1572872 | tf_op jit(solution)/shard_map/ppermute | solution.py:1040
  575.9 59.8 %collective-permute-start.39 = (bf16[1024,256]{1,0:T(8,128)(2,1)S(1)}, bf16[1024,256]{1,0:T(8,128)(2,1)}, u32[]{:S(2)}, u32[]{:S(2)}) collective-permute-start(bf16[1024,256]{1,0:T(8,128)(2,1)S(1)} %get-tuple-element.450), channel_id=1, source_target_pairs={{4,0},{6,2},{5,1},{7,3},{12,8},{14,10},{13,9},{15,11},{20,16},{22,... | collective-permute-start | bytes 1572872 | tf_op jit(solution)/shard_map/ppermute | solution.py:1040
  577.2 61.0 %collective-permute-start.40 = (bf16[1024,256]{1,0:T(8,128)(2,1)S(1)}, bf16[1024,256]{1,0:T(8,128)(2,1)}, u32[]{:S(2)}, u32[]{:S(2)}) collective-permute-start(bf16[1024,256]{1,0:T(8,128)(2,1)S(1)} %get-tuple-element.449), channel_id=1, source_target_pairs={{6,0},{7,1},{14,8},{15,9},{22,16},{23,17},{30,24},{31,25}} | collective-permute-start | bytes 1572872 | tf_op jit(solution)/shard_map/ppermute | solution.py:1040
  595.0 67.1 %collective-permute-start.43 = (bf16[192,4480]{1,0:T(8,128)(2,1)}, bf16[192,4480]{1,0:T(8,128)(2,1)}, u32[]{:S(2)}, u32[]{:S(2)}) collective-permute-start(bf16[192,4480]{1,0:T(8,128)(2,1)} %add.316), channel_id=1, source_target_pairs={{2,4},{4,2},{3,5},{5,3},{10,12},{12,10},{11,13},{13,11},{18,20},{2... | collective-permute-start | bytes 5160968 | tf_op jit(solution)/shard_map/ppermute | solution.py:822
  635.7 33.4 %collective-permute-start.42 = (bf16[192,4480]{1,0:T(8,128)(2,1)}, bf16[192,4480]{1,0:T(8,128)(2,1)}, u32[]{:S(2)}, u32[]{:S(2)}) collective-permute-start(bf16[192,4480]{1,0:T(8,128)(2,1)} %add_add_fusion.2), channel_id=1, source_target_pairs={{0,2},{6,4},{1,3},{7,5},{8,10},{14,12},{9,11},{15,13},{16,18},{22,... | collective-permute-start | bytes 5160968 | tf_op jit(solution)/shard_map/ppermute | solution.py:812
  669.1 17.1 %collective-permute-start.45 = (bf16[768,1024]{1,0:T(8,128)(2,1)S(1)}, bf16[768,1024]{1,0:T(8,128)(2,1)S(1)}, u32[]{:S(2)}, u32[]{:S(2)}) collective-permute-start(bf16[768,1024]{1,0:T(8,128)(2,1)S(1)} %get-tuple-element.354), channel_id=1, source_target_pairs={{0,8},{8,0},{16,24},{24,16},{1,9},{9,1},{17,25},{25,17},{2,10},{10... | collective-permute-start | bytes 4718600 | tf_op jit(solution)/shard_map/ppermute | solution.py:706
  669.1 17.0 %collective-permute-start.47 = (bf16[384,768]{1,0:T(8,128)(2,1)S(1)}, bf16[384,768]{1,0:T(8,128)(2,1)S(1)}, u32[]{:S(2)}, u32[]{:S(2)}) collective-permute-start(bf16[384,768]{1,0:T(8,128)(2,1)S(1)} %copy-done.60), channel_id=1, source_target_pairs={{0,16},{8,24},{16,0},{24,8},{1,17},{9,25},{17,1},{25,9},{2,18},{10... | collective-permute-start | bytes 1769480 | tf_op jit(solution)/shard_map/ppermute | solution.py:706
  675.7 44.1 %collective-permute-start.52 = (bf16[192,4480]{1,0:T(8,128)(2,1)S(1)}, bf16[192,4480]{1,0:T(8,128)(2,1)S(1)}, u32[]{:S(2)}, u32[]{:S(2)}) collective-permute-start(bf16[192,4480]{1,0:T(8,128)(2,1)S(1)} %add.324), channel_id=1, source_target_pairs={{2,4},{4,2},{3,5},{5,3},{10,12},{12,10},{11,13},{13,11},{18,20},{2... | collective-permute-start | bytes 5160968 | tf_op jit(solution)/shard_map/ppermute | solution.py:822
  676.6 43.8 %collective-permute-start.50 = (bf16[192,4480]{1,0:T(8,128)(2,1)S(1)}, bf16[192,4480]{1,0:T(8,128)(2,1)S(1)}, u32[]{:S(2)}, u32[]{:S(2)}) collective-permute-start(bf16[192,4480]{1,0:T(8,128)(2,1)S(1)} %add_add_fusion.1), channel_id=1, source_target_pairs={{0,2},{6,4},{1,3},{7,5},{8,10},{14,12},{9,11},{15,13},{16,18},{22,... | collective-permute-start | bytes 5160968 | tf_op jit(solution)/shard_map/ppermute | solution.py:812
  688.1 68.3 %collective-permute-start.51 = (bf16[192,4480]{1,0:T(8,128)(2,1)S(1)}, bf16[192,4480]{1,0:T(8,128)(2,1)S(1)}, u32[]{:S(2)}, u32[]{:S(2)}) collective-permute-start(bf16[192,4480]{1,0:T(8,128)(2,1)S(1)} %add_add_fusion), channel_id=1, source_target_pairs={{0,2},{6,4},{1,3},{7,5},{8,10},{14,12},{9,11},{15,13},{16,18},{22,... | collective-permute-start | bytes 5160968 | tf_op jit(solution)/shard_map/ppermute | solution.py:812
  691.3 85.3 %collective-permute-start.67 = (bf16[192,4480]{1,0:T(8,128)(2,1)}, bf16[192,4480]{1,0:T(8,128)(2,1)}, u32[]{:S(2)}, u32[]{:S(2)}) collective-permute-start(bf16[192,4480]{1,0:T(8,128)(2,1)} %add.325), channel_id=1, source_target_pairs={{2,0},{4,6},{3,1},{5,7},{10,8},{12,14},{11,9},{13,15},{18,16},{20,... | collective-permute-start | bytes 5160968 | tf_op jit(solution)/shard_map/ppermute | solution.py:830
  696.5 23.3 %collective-permute-start.49 = (bf16[1024,512]{1,0:T(8,128)(2,1)S(1)}, bf16[1024,512]{1,0:T(8,128)(2,1)S(1)}, u32[]{:S(2)}, u32[]{:S(2)}) collective-permute-start(bf16[1024,512]{1,0:T(8,128)(2,1)S(1)} %get-tuple-element.348.refs_0_), channel_id=1, source_target_pairs={{0,1},{1,0},{2,3},{3,2},{4,5},{5,4},{6,7},{7,6},{8,9},{9,8},{10,11... | collective-permute-start | bytes 3145736 | tf_op jit(solution)/shard_map/ppermute | solution.py:1069
  758.1 51.3 %collective-permute-start.58 = (bf16[192,4480]{1,0:T(8,128)(2,1)}, bf16[192,4480]{1,0:T(8,128)(2,1)}, u32[]{:S(2)}, u32[]{:S(2)}) collective-permute-start(bf16[192,4480]{1,0:T(8,128)(2,1)} %add.332), channel_id=1, source_target_pairs={{2,4},{4,2},{3,5},{5,3},{10,12},{12,10},{11,13},{13,11},{18,20},{2... | collective-permute-start | bytes 5160968 | tf_op jit(solution)/shard_map/ppermute | solution.py:822
  766.0 35.9 %collective-permute-start.56 = (f32[5312]{0:T(1024)S(1)}, f32[5312]{0:T(1024)S(1)}, u32[]{:S(2)}, u32[]{:S(2)}) collective-permute-start(f32[5312]{0:T(1024)S(1)} %add.333), channel_id=1, source_target_pairs={{0,4},{2,6},{4,0},{6,2},{1,5},{3,7},{5,1},{7,3},{8,12},{10,14},{12... | collective-permute-start | bytes 63752 | tf_op jit(solution)/shard_map/ppermute | solution.py:706
  773.3 51.6 %collective-permute-start.53 = (bf16[1024,512]{1,0:T(8,128)(2,1)S(1)}, bf16[1024,512]{1,0:T(8,128)(2,1)S(1)}, u32[]{:S(2)}, u32[]{:S(2)}) collective-permute-start(bf16[1024,512]{1,0:T(8,128)(2,1)S(1)} %copy-done.18), channel_id=1, source_target_pairs={{0,1},{1,0},{2,3},{3,2},{4,5},{5,4},{6,7},{7,6},{8,9},{9,8},{10,11... | collective-permute-start | bytes 3145736 | tf_op jit(solution)/shard_map/ppermute | solution.py:1096
  774.5 33.7 %collective-permute-start.59 = (bf16[384,768]{1,0:T(8,128)(2,1)S(1)}, bf16[384,768]{1,0:T(8,128)(2,1)S(1)}, u32[]{:S(2)}, u32[]{:S(2)}) collective-permute-start(bf16[384,768]{1,0:T(8,128)(2,1)S(1)} %copy-done.52), channel_id=1, source_target_pairs={{0,2},{6,4},{1,3},{7,5},{8,10},{14,12},{9,11},{15,13},{16,18},{22,... | collective-permute-start | bytes 1769480 | tf_op jit(solution)/shard_map/ppermute | solution.py:812
  776.6 32.9 %collective-permute-start.57 = (bf16[384,1024]{1,0:T(8,128)(2,1)S(1)}, bf16[384,1024]{1,0:T(8,128)(2,1)S(1)}, u32[]{:S(2)}, u32[]{:S(2)}) collective-permute-start(bf16[384,1024]{1,0:T(8,128)(2,1)S(1)} %copy-done.59), channel_id=1, source_target_pairs={{0,16},{8,24},{16,0},{24,8},{1,17},{9,25},{17,1},{25,9},{2,18},{10... | collective-permute-start | bytes 2359304 | tf_op jit(solution)/shard_map/ppermute | solution.py:706
  801.9 24.9 %collective-permute-start.54 = (bf16[1024,512]{1,0:T(8,128)(2,1)S(1)}, bf16[1024,512]{1,0:T(8,128)(2,1)S(1)}, u32[]{:S(2)}, u32[]{:S(2)}) collective-permute-start(bf16[1024,512]{1,0:T(8,128)(2,1)S(1)} %copy-done.20), channel_id=1, source_target_pairs={{0,1},{1,0},{2,3},{3,2},{4,5},{5,4},{6,7},{7,6},{8,9},{9,8},{10,11... | collective-permute-start | bytes 3145736 | tf_op jit(solution)/shard_map/ppermute | solution.py:1102
  808.1 42.7 %collective-permute-start.68 = (bf16[192,4480]{1,0:T(8,128)(2,1)}, bf16[192,4480]{1,0:T(8,128)(2,1)}, u32[]{:S(2)}, u32[]{:S(2)}) collective-permute-start(bf16[192,4480]{1,0:T(8,128)(2,1)} %add.335), channel_id=1, source_target_pairs={{2,0},{4,6},{3,1},{5,7},{10,8},{12,14},{11,9},{13,15},{18,16},{20,... | collective-permute-start | bytes 5160968 | tf_op jit(solution)/shard_map/ppermute | solution.py:830
  810.5 24.3 %collective-permute-start.61 = (bf16[384,1024]{1,0:T(8,128)(2,1)}, bf16[384,1024]{1,0:T(8,128)(2,1)}, u32[]{:S(2)}, u32[]{:S(2)}) collective-permute-start(bf16[384,1024]{1,0:T(8,128)(2,1)} %add_add_fusion.4), channel_id=1, source_target_pairs={{0,2},{6,4},{1,3},{7,5},{8,10},{14,12},{9,11},{15,13},{16,18},{22,... | collective-permute-start | bytes 2359304 | tf_op jit(solution)/shard_map/ppermute | solution.py:812
  818.1 16.7 %collective-permute-start.62 = (bf16[384,768]{1,0:T(8,128)(2,1)}, bf16[384,768]{1,0:T(8,128)(2,1)}, u32[]{:S(2)}, u32[]{:S(2)}) collective-permute-start(bf16[384,768]{1,0:T(8,128)(2,1)} %add.338), channel_id=1, source_target_pairs={{2,4},{4,2},{3,5},{5,3},{10,12},{12,10},{11,13},{13,11},{18,20},{2... | collective-permute-start | bytes 1769480 | tf_op jit(solution)/shard_map/ppermute | solution.py:822
  833.5 54.1 %collective-permute-start.69 = (bf16[192,4480]{1,0:T(8,128)(2,1)S(1)}, bf16[192,4480]{1,0:T(8,128)(2,1)S(1)}, u32[]{:S(2)}, u32[]{:S(2)}) collective-permute-start(bf16[192,4480]{1,0:T(8,128)(2,1)S(1)} %copy-done.40), channel_id=1, source_target_pairs={{2,0},{4,6},{3,1},{5,7},{10,8},{12,14},{11,9},{13,15},{18,16},{20,... | collective-permute-start | bytes 5160968 | tf_op jit(solution)/shard_map/ppermute | solution.py:830
  836.5 26.5 %collective-permute-start.64 = (bf16[384,1024]{1,0:T(8,128)(2,1)S(1)}, bf16[384,1024]{1,0:T(8,128)(2,1)S(1)}, u32[]{:S(2)}, u32[]{:S(2)}) collective-permute-start(bf16[384,1024]{1,0:T(8,128)(2,1)S(1)} %add.342), channel_id=1, source_target_pairs={{2,4},{4,2},{3,5},{5,3},{10,12},{12,10},{11,13},{13,11},{18,20},{2... | collective-permute-start | bytes 2359304 | tf_op jit(solution)/shard_map/ppermute | solution.py:822
  858.2 94.9 %collective-permute-start.70 = (bf16[192,4480]{1,0:T(8,128)(2,1)S(1)}, bf16[192,4480]{1,0:T(8,128)(2,1)}, u32[]{:S(2)}, u32[]{:S(2)}) collective-permute-start(bf16[192,4480]{1,0:T(8,128)(2,1)S(1)} %add.346), channel_id=1, source_target_pairs={{2,0},{4,6},{3,1},{5,7},{10,8},{12,14},{11,9},{13,15},{18,16},{20,... | collective-permute-start | bytes 5160968 | tf_op jit(solution)/shard_map/ppermute | solution.py:830
  861.7 75.5 %collective-permute-start.66 = (bf16[384,768]{1,0:T(8,128)(2,1)}, bf16[384,768]{1,0:T(8,128)(2,1)}, u32[]{:S(2)}, u32[]{:S(2)}) collective-permute-start(bf16[384,768]{1,0:T(8,128)(2,1)} %add.345), channel_id=1, source_target_pairs={{2,0},{4,6},{3,1},{5,7},{10,8},{12,14},{11,9},{13,15},{18,16},{20,... | collective-permute-start | bytes 1769480 | tf_op jit(solution)/shard_map/ppermute | solution.py:830
  864.2 86.5 %collective-permute-start.65 = (bf16[384,1024]{1,0:T(8,128)(2,1)}, bf16[384,1024]{1,0:T(8,128)(2,1)}, u32[]{:S(2)}, u32[]{:S(2)}) collective-permute-start(bf16[384,1024]{1,0:T(8,128)(2,1)} %add.343), channel_id=1, source_target_pairs={{2,0},{4,6},{3,1},{5,7},{10,8},{12,14},{11,9},{13,15},{18,16},{20,... | collective-permute-start | bytes 2359304 | tf_op jit(solution)/shard_map/ppermute | solution.py:830
  (80 other events, 1181.4 us)
Sparse Core Ops, SparseCore 0:
  112.9 69.7 all-gather.2
  311.3 143.4 reduce-scatter.1
  493.8 99.1 all-gather.4

commit v3 on v2

--- a/solution.py
+++ b/solution.py
@@ -17,7 +17,19 @@
 SCALE_2 = SCALE * math.log2(math.e)
 MIB = 1 << 20
 CUTS = 3
-LONG = pl.CostEstimate(flops=1_000_000_000_000, bytes_accessed=1_000_000, transcendentals=0)
+
+
+def cuts(width):
+    return [width // 4, width // 4, width // 2]
+
+
+PACE = 175_000_000
+
+
+def cost(us):
+    return pl.CostEstimate(flops=int(us * PACE), bytes_accessed=1000, transcendentals=0)
+
+
 BF16 = jnp.bfloat16
 F32 = jnp.float32
 
@@ -38,10 +50,10 @@
 
 
 def attention_forward_kernel(
-    group, bq, bk, blocks, count, chosen, places, q_ref, kv_ref, reach_ref, hot_ref,
+    group, bq, bk, blocks, first, count, chosen, places, q_ref, kv_ref, reach_ref, hot_ref,
     out_ref, lse_ref, top_ref, max_s, sum_s, acc_s,
 ):
-    row_block = pl.program_id(0)
+    row_block = pl.program_id(0) + first
     max_s[...] = jnp.full_like(max_s, NEG_FILL)
     sum_s[...] = jnp.zeros_like(sum_s)
     acc_s[...] = jnp.zeros_like(acc_s)
@@ -71,22 +83,23 @@
         out_ref[:, h * HEAD : (h + 1) * HEAD] = (acc_s[h] / sum_s[h : h + 1, :]).T.astype(BF16)
 
 
-def attention_forward(lists, queries, kv, reach_rows, hot, bq, bk):
-    rows, width = queries.shape
+def attention_forward(lists, queries, kv, reach_rows, hot, bq, bk, first, rows):
+    width = queries.shape[1]
+    first //= bq
     slots = kv.shape[0]
     group = width // HEAD
     whole = lambda *_: (0, 0)
     row = lambda i, *_: (i, 0)
     col = lambda i, *_: (0, i)
     return pl.pallas_call(
-        functools.partial(attention_forward_kernel, group, bq, bk, slots // bk),
+        functools.partial(attention_forward_kernel, group, bq, bk, slots // bk, first),
         grid_spec=pltpu.PrefetchScalarGridSpec(
             num_scalar_prefetch=3,
             grid=(rows // bq,),
             in_specs=[
-                pl.BlockSpec((bq, width), row),
+                pl.BlockSpec((bq, width), lambda i, *_: (i + first, 0)),
                 pl.BlockSpec((slots, 2 * HEAD), whole),
-                pl.BlockSpec((bq, HEAD), row),
+                pl.BlockSpec((bq, HEAD), lambda i, *_: (i + first, 0)),
                 pl.BlockSpec((slots, HEAD), whole),
             ],
             out_specs=[
@@ -106,7 +119,7 @@
             jax.ShapeDtypeStruct((group, rows), F32),
         ],
         compiler_params=pltpu.CompilerParams(vmem_limit_bytes=32 * MIB),
-        cost_estimate=LONG,
+        cost_estimate=cost(15),
         name="attention_forward",
     )(*lists, queries, kv, reach_rows, hot)
 
@@ -201,7 +214,7 @@
             jax.ShapeDtypeStruct((slots, 2 * HEAD), BF16),
         ],
         compiler_params=pltpu.CompilerParams(vmem_limit_bytes=40 * MIB),
-        cost_estimate=LONG,
+        cost_estimate=cost(54),
         name="attention_backward",
     )(*lists, queries, d_att, lse, delta, kv, reach_rows, hot, cosine, sine)
 
@@ -247,7 +260,7 @@
     return pl.BlockSpec(shape, whole_block, pipeline_mode=pl.Buffered(1))
 
 
-def call(kernel, grid, in_specs, out_specs, out_shape, scratch, vmem, name):
+def call(kernel, grid, in_specs, out_specs, out_shape, scratch, vmem, us, name):
     return pl.pallas_call(
         kernel,
         grid_spec=pltpu.PrefetchScalarGridSpec(
@@ -259,7 +272,7 @@
         ),
         out_shape=out_shape,
         compiler_params=pltpu.CompilerParams(vmem_limit_bytes=vmem * MIB),
-        cost_estimate=LONG,
+        cost_estimate=cost(us),
         name=name,
     )
 
@@ -304,6 +317,7 @@
         [shape((rows, units), BF16)] * 3,
         [pltpu.VMEM((width, tf), BF16)] * 2,
         60,
+        40,
         "gate_up",
     )(place, hidden, *gates.arrays, *ups.arrays)
 
@@ -340,9 +354,11 @@
 
     @pl.when(step == pl.num_programs(0) - 1)
     def _():
-        cols = dh_refs[0].shape[1]
-        for k, dh_ref in enumerate(dh_refs):
-            dh_ref[...] = sum_s[:, k * cols : (k + 1) * cols].astype(BF16)
+        at = 0
+        for dh_ref in dh_refs:
+            cols = dh_ref.shape[1]
+            dh_ref[...] = sum_s[:, at : at + cols].astype(BF16)
+            at += cols
 
 
 def gate_up_back(place, cotangent, by_gate, by_up, gates, ups, downs, depth, tf):
@@ -357,10 +373,11 @@
         + gates.specs
         + ups.specs
         + downs.specs,
-        [pl.BlockSpec((rows, tf), col_block)] * 2 + [once((rows, width // CUTS))] * CUTS,
-        [shape((rows, units), BF16)] * 2 + [shape((rows, width // CUTS), BF16)] * CUTS,
+        [pl.BlockSpec((rows, tf), col_block)] * 2 + [once((rows, cut)) for cut in cuts(width)],
+        [shape((rows, units), BF16)] * 2 + [shape((rows, cut), BF16) for cut in cuts(width)],
         [pltpu.VMEM((width, tf), BF16)] * 3 + [pltpu.VMEM((rows, width), F32)],
         60,
+        62,
         "gate_up_back",
     )(place, cotangent, by_gate, by_up, *gates.arrays, *ups.arrays, *downs.arrays)
 
@@ -379,7 +396,7 @@
         out_specs=pl.BlockSpec((width, tf), col_block),
         out_shape=shape((width, units), BF16),
         compiler_params=pltpu.CompilerParams(vmem_limit_bytes=48 * MIB),
-        cost_estimate=LONG,
+        cost_estimate=cost(19 if units > 2048 else 6),
         name="whole_grad",
     )(left_t, right)
 
@@ -403,8 +420,55 @@
         [shape((width // 2, units), BF16)] * 2,
         [],
         48,
+        19 if units > 2048 else 7,
         "weight_grad",
     )(place, left_t, right)
+
+
+def add_kernel(counts, *refs):
+    out_ref, at, col = refs[-1], 0, 0
+    for count in counts:
+        parts = refs[at : at + count]
+        cols = parts[0].shape[1]
+        total = sum(ref[...].astype(F32) for ref in parts)
+        out_ref[:, col : col + cols] = total.astype(BF16)
+        at, col = at + count, col + cols
+
+
+def add_rows(rows, *groups):
+    parts = [part for group in groups for part in group]
+    cols = sum(group[0][0].shape[1] for group in groups)
+    step = math.gcd(rows, 64, *[row for _, row in parts])
+    return pl.pallas_call(
+        functools.partial(add_kernel, [len(group) for group in groups]),
+        grid=(rows // step,),
+        in_specs=[
+            pl.BlockSpec((step, array.shape[1]), lambda i, at=row // step: (at + i, 0))
+            for array, row in parts
+        ],
+        out_specs=pl.BlockSpec((step, cols), lambda i: (i, 0)),
+        out_shape=shape((rows, cols), BF16),
+        compiler_params=pltpu.CompilerParams(vmem_limit_bytes=32 * MIB),
+        cost_estimate=cost(4),
+        name="add_rows",
+    )(*[array for array, _ in parts])
+
+
+def mark_kernel(place_ref, out_ref):
+    for at in range(2):
+        out_ref[at] = place_ref[at]
+
+
+def mark(place):
+    place.v = pl.pallas_call(
+        mark_kernel,
+        in_specs=[pl.BlockSpec(memory_space=pltpu.SMEM)],
+        out_specs=pl.BlockSpec(memory_space=pltpu.SMEM),
+        out_shape=shape((2,), jnp.int32),
+        cost_estimate=cost(1),
+        name="mark",
+    )(place.v)
+    return place
 
 
 def down_project_kernel(downs, place, act_ref, *refs):
@@ -434,6 +498,7 @@
         shape((rows, width), BF16),
         [pltpu.VMEM((width, tf), BF16), pltpu.VMEM((rows, width), F32)],
         48,
+        24,
         "down_project",
     )(place, act, *downs.arrays)
 
@@ -493,11 +558,12 @@
         ],
         [pltpu.VMEM((width, cols), BF16)],
         32,
+        8,
         "mix",
     )(place, tokens, gain[None], bias[None], cosine, sine, *weight.arrays)
 
 
-def branch_kernel(weight, parts, place, x_ref, own_ref, other_ref, gain_ref, *refs):
+def branch_kernel(weight, parts, place, x_ref, own_ref, upper_ref, lower_ref, gain_ref, *refs):
     own_w, other_w = refs[: len(weight)], refs[len(weight) : len(weight) + parts]
     mid_ref, h_ref, ht_ref, weight_s, att_s = refs[len(weight) + parts :]
     split = own_ref.shape[1]
@@ -510,7 +576,16 @@
         join(place[0], weight.depth, [(j, 0) for j in range(parts)], other_w, weight_s, other_at)
 
     att_s[:, pl.ds(own_at, split)] = own_ref[...]
-    att_s[:, pl.ds(other_at, split)] = other_ref[...]
+    steps = pl.num_programs(0)
+
+    @pl.when(pl.program_id(0) < steps // 2)
+    def _():
+        att_s[:, pl.ds(other_at, split)] = upper_ref[...]
+
+    @pl.when(pl.program_id(0) >= steps // 2)
+    def _():
+        att_s[:, pl.ds(other_at, split)] = lower_ref[...]
+
     mid = x_ref[...].astype(F32) + dot_nt(att_s[...], weight_s[...])
     mid_ref[...] = mid
     hidden = (mid * inverse_rms(mid) * gain_ref[...].astype(F32)).astype(BF16)
@@ -518,27 +593,34 @@
     ht_ref[...] = hidden.T
 
 
-def branch(place, tokens, own, other, gain, pieces, other_weight, depth, bq):
+def branch(place, tokens, own, upper, lower, gain, pieces, other_pieces, depth, bq):
     rows, width = tokens.shape
     cols = own.shape[1]
     parts = width // depth
     weight = Rows(pieces, depth)
     wide = pl.BlockSpec((bq, width), row_block)
     narrow = pl.BlockSpec((bq, cols), row_block)
-    other_specs = [
-        pl.BlockSpec((depth, cols), lambda *_, j=j: (j, 0), pipeline_mode=pl.Buffered(1))
-        for j in range(parts)
-    ]
+    other_specs = [once((depth, cols))] * parts
+    half = rows // bq // 2
     return call(
         functools.partial(branch_kernel, weight, parts),
         rows // bq,
-        [wide, narrow, narrow, once((1, width))] + weight.specs + other_specs,
+        [
+            wide,
+            narrow,
+            pl.BlockSpec((bq, cols), lambda i, *_: (jnp.minimum(i, half - 1), 0)),
+            pl.BlockSpec((bq, cols), lambda i, *_: (jnp.maximum(i - half, 0), 0)),
+            once((1, width)),
+        ]
+        + weight.specs
+        + other_specs,
         [wide, wide, pl.BlockSpec((width, bq), col_block)],
         [shape((rows, width), F32), shape((rows, width), BF16), shape((width, rows), BF16)],
         [pltpu.VMEM((width, 2 * cols), BF16), pltpu.VMEM((bq, 2 * cols), BF16)],
         40,
+        12,
         "branch",
-    )(place, tokens, own, other, gain[None], *weight.arrays, *([other_weight] * parts))
+    )(place, tokens, own, upper, lower, gain[None], *weight.arrays, *other_pieces)
 
 
 def middle_back_kernel(
@@ -586,7 +668,7 @@
         functools.partial(middle_back_kernel, weight, group),
         rows // bq,
         [wide, wide, once((1, width)), narrow]
-        + [pl.BlockSpec((bq, width // CUTS), row_block)] * (2 * CUTS)
+        + [pl.BlockSpec((bq, cut), row_block) for cut in cuts(width)] * 2
         + weight.specs,
         [
             wide,
@@ -604,6 +686,7 @@
         ],
         [pltpu.VMEM((width, cols), BF16)],
         48,
+        13,
         "middle_back",
     )(place, mid, cotangent, gain[None], attended, *own, *other, *weight.arrays)
 
@@ -630,9 +713,11 @@
     d_hidden = dot_nt(d_mixed, weight_s[...])
     x = x_ref[...].astype(F32)
     dgain_ref[...] += jnp.sum(d_hidden * (x * inverse_rms(x)), axis=0, keepdims=True)
-    cols = dh_refs[0].shape[1]
-    for k, dh_ref in enumerate(dh_refs):
-        dh_ref[...] = d_hidden[:, k * cols : (k + 1) * cols].astype(BF16)
+    at = 0
+    for dh_ref in dh_refs:
+        cols = dh_ref.shape[1]
+        dh_ref[...] = d_hidden[:, at : at + cols].astype(BF16)
+        at += cols
 
 
 def mix_back(place, dq, dkv, cosine, sine, tokens, pieces, depth, bq):
@@ -657,15 +742,16 @@
             pl.BlockSpec((1, cols), whole_block),
             pl.BlockSpec((1, width), whole_block),
         ]
-        + [pl.BlockSpec((bq, width // CUTS), row_block)] * CUTS,
+        + [pl.BlockSpec((bq, cut), row_block) for cut in cuts(width)],
         [
             shape((rows, cols), BF16),
             shape((1, cols), F32),
             shape((1, width), F32),
         ]
-        + [shape((rows, width // CUTS), BF16)] * CUTS,
+        + [shape((rows, cut), BF16) for cut in cuts(width)],
         [pltpu.VMEM((width, cols), BF16)],
         32,
+        8,
         "mix_back",
     )(place, dq, dkv, cosine, sine, tokens, *weight.arrays)
 
@@ -689,17 +775,38 @@
     return call(
         input_back_kernel,
         rows // bq,
-        [wide, once((1, width)), wide] + [pl.BlockSpec((bq, width // CUTS), row_block)] * (2 * CUTS),
+        [wide, once((1, width)), wide]
+        + [pl.BlockSpec((bq, cut), row_block) for cut in cuts(width)] * 2,
         wide,
         shape((rows, width), F32),
         [],
         32,
+        8,
         "input_back",
     )(place, tokens, gain[None], d_mid, *own, *other)
 
 
-def after(values, *first):
-    return lax.optimization_barrier((values, first))[0]
+class Box:
+    def __init__(self, v):
+        self.v = v
+
+
+def boxes(values):
+    return [Box(v) for v in values]
+
+
+def fence(*items):
+    flat = []
+    for item in items:
+        flat += item if isinstance(item, (list, tuple)) else [item]
+    for item, v in zip(flat, lax.optimization_barrier([item.v for item in flat])):
+        item.v = v
+
+
+def held(value, *items):
+    one = Box(value)
+    fence(one, *items)
+    return one.v
 
 
 def swap(value, axis, size, bit):
@@ -714,141 +821,158 @@
         self.depth = own.shape[0] // slabs
         self.got = {}
 
-    def far(self, slab, *first):
-        if slab >= self.slabs:
-            return ()
-        own = after(self.own, first)
-        own = own[slab * self.depth : (slab + 1) * self.depth]
+    def away(self, own):
         got, bit = {0: own}, self.size // 2
         while bit > 1:
             got.update({j ^ bit: swap(p, "shard", self.size, bit) for j, p in got.items()})
             bit //= 2
-        self.got.update({(j, slab): p for j, p in got.items() if j})
-        return [p for j, p in got.items() if j]
+        return {j: Box(p) for j, p in got.items() if j}
+
+    def far(self, slab, *first):
+        if slab >= self.slabs:
+            return []
+        own = held(self.own, *first)[slab * self.depth : (slab + 1) * self.depth]
+        got = self.away(own)
+        self.got.update({(j, slab): p for j, p in got.items()})
+        return list(got.values())
 
     def far_by_ctx(self, contexts, *first):
-        own = after(self.own, first)
-        rows = own.shape[0] // contexts
-        own = lax.dynamic_slice_in_dim(own, lax.axis_index("ctx") * rows, rows, 0)
-        got, bit = {0: own}, self.size // 2
-        while bit > 1:
-            got.update({j ^ bit: swap(p, "shard", self.size, bit) for j, p in got.items()})
-            bit //= 2
-        self.parts = {j: p for j, p in got.items() if j}
+        rows = self.own.shape[0] // contexts
+        own = lax.dynamic_slice_in_dim(
+            held(self.own, *first), lax.axis_index("ctx") * rows, rows, 0
+        )
+        self.parts = self.away(own)
         return list(self.parts.values())
 
-    def spread(self, *first):
-        js = list(self.parts)
-        parts = after(list(self.parts.values()), first)
-        for j, part in zip(js, parts):
-            self.got[j, 0] = lax.all_gather(part, "ctx", axis=0, tiled=True)
-        return [self.got[j, 0] for j in js]
+    def spread(self):
+        for j, part in self.parts.items():
+            self.got[j, 0] = Box(lax.all_gather(part.v, "ctx", axis=0, tiled=True))
+        return [self.got[j, 0] for j in self.parts]
 
     def near_own(self, *first):
-        self.near = swap(after(self.own, first), "shard", self.size, 1)
-        return self.near
+        self.near = Box(swap(held(self.own, *first), "shard", self.size, 1))
+        return [self.near]
 
     def near_rest(self, slab, *first):
         if slab >= self.slabs:
-            return ()
+            return []
         far = [j for j in range(2, self.size, 2)]
-        held = after([self.got[j, slab] for j in far], first)
-        for j, piece in zip(far, held):
-            self.got[j ^ 1, slab] = swap(piece, "shard", self.size, 1)
+        if first:
+            fence(*[self.got[j, slab] for j in far], *first)
+        for j in far:
+            self.got[j ^ 1, slab] = Box(swap(self.got[j, slab].v, "shard", self.size, 1))
         return [self.got[j ^ 1, slab] for j in far]
 
     def all(self):
-        found = [(0, 0, self.own), (1, 0, self.near)]
-        found += [(j, k * self.depth, p) for (j, k), p in sorted(self.got.items(), key=lambda i: i[0])]
+        found = [(0, 0, self.own), (1, 0, self.near.v)]
+        found += [
+            (j, k * self.depth, p.v) for (j, k), p in sorted(self.got.items(), key=lambda i: i[0])
+        ]
         return found
 
 
 class Reduction:
-    def __init__(self, halves, shards, contexts, slabs=1):
-        self.keep, self.send = halves
+    def __init__(self, shards, contexts, slabs):
         self.shards, self.chain = shards, contexts == 4
         self.slabs = slabs if shards == 4 else 1
-        self.own, self.one, self.inner, self.two, self.total, self.three = ({} for _ in range(6))
-
-    def cores(self, *first):
-        self.got = swap(after(self.send, first), "shard", self.shards, 1)
-        return self.got
-
-    def chips(self, *first):
-        held = list(after((self.keep, self.got), first))
-        bit, count = 2, self.shards // 2
+        self.keep, self.send, self.got = [], [], []
+        self.own, self.one, self.two, self.three = {}, {}, {}, {}
+        self.by_sum = {}
+
+    def make(self, place, left_t, right, tf):
+        keep, send = boxes(weight_grad(place.v, left_t, right, self.shards, tf))
+        self.keep.append(keep)
+        self.send.append(send)
+        return send
+
+    def cores(self):
+        self.got.append(Box(swap(self.send[len(self.got)].v, "shard", self.shards, 1)))
+        return self.got[-1]
+
+    def pairs(self, row):
+        return [[(keep.v, row), (got.v, row)] for keep, got in zip(self.keep, self.got)]
+
+    def sum_away(self):
+        rows = self.keep[0].v.shape[0]
+        if self.shards == 4:
+            size = rows // 2 // self.slabs
+            self.away = [
+                Box(add_rows(size, *self.pairs(rows // 2 + slab * size)))
+                for slab in range(self.slabs)
+            ]
+        else:
+            self.away = [Box(add_rows(rows, *self.pairs(0)))]
+        return self.away
+
+    def chips(self):
+        if self.shards == 4:
+            self.last = [Box(swap(part.v, "shard", 4, 2)) for part in self.away]
+            return self.last
+        held, bit, count = self.away[0].v, 2, self.shards // 2
         while bit < self.shards:
-            size = held[0].shape[0] // count // self.slabs
-
-            def pick(odd, slab):
-                blocks = [
-                    [part[(at * self.slabs + slab) * size :][:size] for part in held]
-                    for at in range(odd, count, 2)
-                ]
-                return blocks[0] if len(blocks) == 1 else [
-                    jnp.concatenate(same, axis=0) for same in zip(*blocks)
-                ]
-
-            self.away = [sum(pick(1, slab)) for slab in range(self.slabs)]
-            self.last = [swap(part, "shard", self.shards, bit) for part in self.away]
-            self.here = [pick(0, slab) for slab in range(self.slabs)]
-            held = self.here[0] + self.last
+            size = held.shape[0] // count
+            blocks = [held[at * size : (at + 1) * size] for at in range(count)]
+            away = swap(jnp.concatenate(blocks[1::2], axis=0), "shard", self.shards, bit)
+            here = jnp.concatenate(blocks[::2], axis=0)
+            held = here if 2 * bit >= self.shards else here + away
             bit, count = 2 * bit, count // 2
+        self.here, self.last = held, boxes([away])
         return self.last
 
-    def arrived(self, slab, *first):
+    def arrived(self, slab):
         if slab >= self.slabs:
-            return ()
-        *here, last = after(self.here[slab] + [self.last[slab]], first)
-        self.own[slab] = sum(here) + last
-        return self.own[slab]
-
-    def inward(self, slab, *first):
+            return []
+        last = self.last[slab].v
+        if self.shards != 4:
+            self.own[slab] = Box(self.here + last)
+        elif len(self.keep) == 1:
+            size = last.shape[0]
+            self.own[slab] = Box(add_rows(size, self.pairs(slab * size)[0] + [(last, 0)]))
+        else:
+            size = last.shape[0]
+            here = add_rows(size, *self.pairs(slab * size))
+            self.own[slab] = Box(add_rows(size, [(here, 0), (last, 0)]))
+        return [self.own[slab]]
+
+    def whole_sum(self, slab):
         if slab >= self.slabs:
-            return ()
-        own = after(self.own[slab], first)
-        if self.chain:
-            self.own[slab] = own
-            self.one[slab] = lax.ppermute(own, "ctx", [(0, 1), (3, 2)])
-        else:
-            self.one[slab] = self.total[slab] = lax.psum(own, "ctx")
-        return self.one[slab]
-
-    def middle(self, slab, *first):
+            return []
+        self.by_sum[slab] = Box(lax.psum(self.own[slab].v, "ctx"))
+        return [self.by_sum[slab]]
+
+    def inward(self, slab):
+        if slab >= self.slabs:
+            return []
+        if not self.chain:
+            return self.whole_sum(slab)
+        self.one[slab] = Box(lax.ppermute(self.own[slab].v, "ctx", [(0, 1), (3, 2)]))
+        return [self.one[slab]]
+
+    def middle(self, slab):
         if not self.chain or slab >= self.slabs:
-            return ()
-        own, one = after((self.own[slab], self.one[slab]), first)
-        self.inner[slab] = own + one
-        self.two[slab] = lax.ppermute(self.inner[slab], "ctx", [(1, 2), (2, 1)])
-        return self.two[slab]
-
-    def outward(self, slab, *first):
+            return []
+        self.own[slab] = Box(self.own[slab].v + self.one[slab].v)
+        self.two[slab] = Box(lax.ppermute(self.own[slab].v, "ctx", [(1, 2), (2, 1)]))
+        return [self.two[slab]]
+
+    def outward(self, slab):
         if not self.chain or slab >= self.slabs:
-            return ()
-        inner, two = after((self.inner[slab], self.two[slab]), first)
-        self.total[slab] = inner + two
-        self.three[slab] = lax.ppermute(self.total[slab], "ctx", [(1, 0), (2, 3)])
-        return self.three[slab]
+            return []
+        self.own[slab] = Box(self.own[slab].v + self.two[slab].v)
+        self.three[slab] = Box(lax.ppermute(self.own[slab].v, "ctx", [(1, 0), (2, 3)]))
+        return [self.three[slab]]
 
     def result(self):
-        totals = [self.total[slab] for slab in range(self.slabs)]
-        if self.chain:
-            place = lax.axis_index("ctx")
-            inside = (place == 1) | (place == 2)
-            totals = [
-                jnp.where(inside, total, self.three[slab]) for slab, total in enumerate(totals)
-            ]
+        place = lax.axis_index("ctx")
+        inside = (place == 1) | (place == 2)
+        totals = [
+            self.by_sum[slab].v
+            if slab in self.by_sum
+            else jnp.where(inside, self.own[slab].v, self.three[slab].v)
+            for slab in range(self.slabs)
+        ]
         whole = totals[0] if len(totals) == 1 else jnp.concatenate(totals, axis=0)
         return whole.astype(F32)
-
-
-def sum_of_all(value, sizes):
-    for axis, size in sizes.items():
-        bit = 1
-        while bit < size:
-            value = value + swap(value, axis, size, bit)
-            bit *= 2
-    return value
 
 
 def tree_tables(seg_row, parent_row):
@@ -936,121 +1060,158 @@
         Pieces(out_weight, shards),
         Pieces(gate_weight, shards, 3),
         Pieces(up_weight, shards),
-        Pieces(down_weight, shards, 3),
-    )
+        Pieces(down_weight, shards, 4),
+    )
+
+    def over_tp(box):
+        return Box(lax.ppermute(box.v, "tp", across))
+
     qkv_far = qkv.far(0)
-    tables = (reach_rows, hot, lists_f, lists_b, cosine, sine, place)
-    tables, qkv_far, top_grad_t = after((tables, qkv_far, cotangent.T))
-    reach_rows, hot, lists_f, lists_b, cosine, sine, place = tables
+    leaves, tree = jax.tree.flatten((reach_rows, hot, lists_f, lists_b, cosine, sine))
+    leaves, place = boxes(leaves), Box(place)
+    fence(leaves, place, qkv_far)
+    reach_rows, hot, lists_f, lists_b, cosine, sine = tree.unflatten([leaf.v for leaf in leaves])
+    qkv_near = qkv.near_own(qkv_far) + qkv.near_rest(0)
     out_far = out_w.far(0, qkv_far)
-    qkv_near = qkv.near_own(qkv_far), qkv.near_rest(0, qkv_far)
     out_near = out_w.near_own(qkv_far)
-    place, qkv_near = after((place, qkv_near))
+    out_other = {0: Box(lax.ppermute(held(out_weight, qkv_far), "tp", across))}
+    fence(mark(place), qkv_near)
     up_parts = up.far_by_ctx(contexts, qkv_near)
 
     queries, kv_own, hidden_one_t = mix(
-        place, tokens, gain_attn, qkv_bias, cosine, sine, qkv.all(), depth, group, bq
-    )
-    kv_own, out_far, out_near = after((kv_own, out_far, out_near))
-    out_rest = out_w.near_rest(0, out_far)
-    out_joined = jnp.concatenate([p for _, _, p in out_w.all()], axis=0)
-    kv_own, out_joined = after((kv_own, out_joined))
-    out_other = lax.ppermute(out_joined, "tp", across)
-    kv_far = [
-        lax.ppermute(kv_own, "ctx", [(i, i + k) for i in range(contexts - k)])
-        for k in range(1, contexts)
-    ]
-    gate_far_0 = gate.far(0, kv_own)
-    kv_far, gate_far_0, up_parts = after((kv_far, gate_far_0, up_parts))
-    kv_back = jnp.concatenate([kv_own] + kv_far, axis=0)
-    up_spread = up.spread(up_parts)
-    gate_far_1 = gate.far(1, gate_far_0)
-    own_near = gate.near_own(kv_far), up.near_own(kv_far), down.near_own(kv_far)
-    attended, lse, tops = attention_forward(lists_f, queries, kv_back, reach_rows, hot, bq, bk_f)
-    attended, gate_far_1, out_other, own_near = after((attended, gate_far_1, out_other, own_near))
-    gate_far_2 = gate.far(2, attended)
-    attended_other = lax.ppermute(attended, "tp", across)
-    gate_near = gate.near_rest(0, attended), gate.near_rest(1, attended)
-    attended_other, gate_near, gate_far_2 = after((attended_other, gate_near, gate_far_2))
-    place = after(place, attended_other)
-    down_far_0 = down.far(0, attended_other)
-    gate_near_2 = gate.near_rest(2, attended_other)
+        place.v, tokens, gain_attn, qkv_bias, cosine, sine, qkv.all(), depth, group, bq
+    )
+    kv_own = Box(kv_own)
+    fence(kv_own, out_near, place)
+    kv = [kv_own]
+    rightward = [(i, i + 1) for i in range(contexts - 1)]
+    for k in range(1, contexts):
+        kv.append(Box(lax.ppermute(kv[-1].v, "ctx", rightward)))
+        if k == 1:
+            out_other[1] = over_tp(out_w.near)
+            out_rest = out_w.near_rest(0, kv_own)
+            fence(mark(place), kv, out_rest, out_far, out_other[0])
+        elif k == 2:
+            gate_far = gate.far(0, kv[1])
+            out_other.update({j: over_tp(piece) for (j, _), piece in out_w.got.items()})
+            top_grad_t = Box(held(cotangent, *kv).T)
+            fence(mark(place), kv, out_other[1], up_parts)
+        elif k == contexts - 1:
+            fence(mark(place), kv, gate_far, top_grad_t)
+            fence(kv, up_parts)
+        else:
+            fence(mark(place), kv)
+    kv_back = jnp.concatenate([p.v for p in kv], axis=0)
+    up_spread = up.spread()
+    gate_far = gate.far(1, kv)
+    out_other = [out_other[j] for j in range(shards)]
+    upper_rows = rows // 2
+    upper, *upper_sums = attention_forward(
+        lists_f, queries, kv_back, reach_rows, hot, bq, bk_f, 0, upper_rows
+    )
+    upper, leaves = Box(upper), boxes(lists_f)
+    fence(upper, leaves, out_other)
+    upper_other = over_tp(upper)
+    gate_far_2 = gate.far(2, upper)
+    lower, *lower_sums = attention_forward(
+        [leaf.v for leaf in leaves], queries, kv_back, reach_rows, hot, bq, bk_f, upper_rows,
+        upper_rows,
+    )
+    lower = Box(lower)
+    fence(lower, gate_far, place, upper_other)
+    lower_other = over_tp(lower)
+    gate_rest = gate.near_rest(0) + gate.near_rest(1, lower)
+    attended = Box(jnp.concatenate([upper.v, lower.v], axis=0))
+    lse, tops = (jnp.concatenate(both, axis=1) for both in zip(upper_sums, lower_sums))
+    attended_other = lower_other
+    fence(mark(place), lower_other, gate_far_2, gate_rest, up_spread, attended)
+    down_far = down.far(0, attended_other)
+    gate_rest = gate.near_rest(2) + up.near_rest(0)
+    own_near = gate.near_own(attended_other) + up.near_own(attended_other)
     mid, hidden_two, hidden_two_t = branch(
-        place, tokens, attended, attended_other, gain_ffn, out_w.all(), out_other, depth, bq
-    )
-    mid, gate_near_2, up_spread = after((mid, gate_near_2, up_spread))
-    up_near = up.near_rest(0, up_spread)
-    place, up_near = after((place, up_near))
-    down_far_1 = down.far(1, up_near)
-    act, by_gate, by_up = gate_up(place, hidden_two, gate.all(), up.all(), depth, 512)
-    act, down_far_0, down_far_1 = after((act, down_far_0, down_far_1))
-    down_far_2 = down.far(2, act)
-    down_near = down.near_rest(0, act), down.near_rest(1, act)
-    down_part = whole_grad(top_grad_t, act, 512)
-    down_part, down_near, down_far_2 = after((down_part, down_near, down_far_2))
-    down_part = lax.psum_scatter(
-        down_part, ("shard", "ctx"), scatter_dimension=0, tiled=True
-    )
-    down_near_2 = down.near_rest(2, down_far_2)
-    place, down_near_2 = after((place, down_near_2))
+        place.v, tokens, attended.v, upper_other.v, lower_other.v, gain_ffn, out_w.all(),
+        [p.v for p in out_other], depth, bq,
+    )
+    mid = Box(mid)
+    fence(mid, gate_rest, own_near, place, down_far)
+    down_far = down.far(1, mid) + down.far(2, mid)
+    down_near = down.near_own(mid)
+    act, by_gate, by_up = gate_up(place.v, hidden_two, gate.all(), up.all(), depth, 512)
+    act = Box(act)
+    fence(act, down_far, down_near, top_grad_t, place)
+    down_far = down.far(3, act)
+    down_rest = down.near_rest(0, act) + down.near_rest(1) + down.near_rest(2)
+    down_part = Box(whole_grad(top_grad_t.v, act.v, 512))
+    fence(down_part, down_rest, down_far, place)
+    down_part = Box(lax.psum_scatter(down_part.v, ("shard", "ctx"), scatter_dimension=0, tiled=True))
+    down_rest = down.near_rest(3)
+    fence(mark(place), down_rest)
     d_gate, d_up, *d_hidden_two = gate_up_back(
-        place, cotangent, by_gate, by_up, gate.all(), up.all(), down.all(), depth, 512
-    )
-
-    d_gate, d_hidden_two = after((d_gate, d_hidden_two))
-    other = [lax.ppermute(d_hidden_two[0], "tp", across)]
-    gate_grad = Reduction(weight_grad(place, hidden_two_t, d_gate, shards, 512), shards, contexts, 2)
-    gate_grad.send, other[0] = after((gate_grad.send, other[0]))
-    place = after(place, gate_grad.send)
-    gate_cores = gate_grad.cores()
-    other.append(lax.ppermute(after(d_hidden_two[1], gate_grad.send), "tp", across))
-    up_grad = Reduction(weight_grad(place, hidden_two_t, d_up, shards, 512), shards, contexts, 2)
-    up_grad.send, gate_cores, other[1] = after((up_grad.send, gate_cores, other[1]))
-    gate_chips = gate_grad.chips(gate_cores)
-    gate_away, up_grad.send = after((gate_grad.away, up_grad.send))
-    up_cores = up_grad.cores(gate_away)
-    other.append(lax.ppermute(after(d_hidden_two[2], gate_away), "tp", across))
-    place = after(place, gate_away)
-    ffn_own = down_project(place, act, down.all(), width, depth, 896)
-    ffn_own, other[2], up_cores = after((ffn_own, other[2], up_cores))
-    ffn_other = lax.ppermute(ffn_own, "tp", across)
-    up_chips = up_grad.chips(up_cores)
-
-    place = after(place, ffn_own, up_grad.away)
+        place.v, cotangent, by_gate, by_up, gate.all(), up.all(), down.all(), depth, 512
+    )
+
+    d_hidden_two = boxes(d_hidden_two)
+    gate_grad = Reduction(shards, contexts, 2)
+    up_grad = Reduction(shards, contexts, 2)
+    last_grad = Reduction(shards, contexts, 1)
+    fence(place, d_hidden_two)
+    other = [over_tp(d_hidden_two[0])]
+    fence(place, gate_grad.make(place, hidden_two_t, d_gate, 512), other[0], d_hidden_two[1])
+    gate_got = gate_grad.cores()
+    other.append(over_tp(d_hidden_two[1]))
+    fence(
+        place, up_grad.make(place, hidden_two_t, d_up, 512), gate_got, other[1], d_hidden_two[2], act
+    )
+    up_got = up_grad.cores()
+    other.append(over_tp(d_hidden_two[2]))
+    fence(place, gate_grad.sum_away())
+    gate_last = gate_grad.chips()
+    ffn_own = Box(down_project(place.v, act.v, down.all(), width, depth, 896))
+    fence(place, ffn_own, up_got, other[2], down_part)
+    down_total = Box(lax.all_gather(down_part.v, "ctx", axis=0, tiled=True))
+    ffn_other = over_tp(ffn_own)
+    fence(place, up_grad.sum_away())
+    up_last = up_grad.chips()
+
     d_mid, d_branch_t, d_att, delta, gain_two_part = middle_back(
-        place, d_hidden_two, other, mid, cotangent, gain_ffn, attended, out_w.all(), depth, bq
-    )
-    place = after(place, d_mid)
-    out_grad = Reduction(weight_grad(place, d_branch_t, attended, shards, 768), shards, contexts)
-    out_grad.send, gate_grad.last[0], down_part = after(
-        (out_grad.send, gate_grad.last[0], down_part)
-    )
-    down_total = lax.all_gather(down_part, "ctx", axis=0, tiled=True)
-    out_cores = out_grad.cores()
-    gate_own_0 = gate_grad.arrived(0)
-    lists_b, gate_grad.own[0] = after((lists_b, gate_own_0), down_part)
-    gate_in_0 = gate_grad.inward(0)
+        place.v, [p.v for p in d_hidden_two], [p.v for p in other], mid.v, cotangent, gain_ffn,
+        attended.v, out_w.all(), depth, bq,
+    )
+    d_mid = Box(d_mid)
+    fence(place, d_mid)
+    out_sent = last_grad.make(place, d_branch_t, attended.v, 768)
+    leaves = boxes(lists_b)
+    fence(place, out_sent, gate_last[:1])
+    out_got = last_grad.cores()
+    fence(leaves, gate_grad.arrived(0))
+    gate_one = gate_grad.inward(0)
     d_query, d_kv = attention_backward(
-        lists_b, queries, d_att, lse, delta, kv_back, reach_rows, hot, cosine, sine, bq, bk_b
-    )
-    d_kv, gate_grad.last, gate_grad.one, out_grad.got, ffn_other = after(
-        (d_kv, gate_grad.last, gate_grad.one, out_grad.got, ffn_other)
-    )
-    d_kv_far = [
-        lax.ppermute(d_kv[k * rows : (k + 1) * rows], "ctx", [(i + k, i) for i in range(contexts - k)])
-        for k in range(1, contexts)
-    ]
-    gate_mid_0 = gate_grad.middle(0, d_kv)
-    gate_own_1 = gate_grad.arrived(1, d_kv)
-    gate_in_1 = gate_grad.inward(1)
-    out_chips = out_grad.chips(d_kv)
-    output = (after(mid, d_kv) + (ffn_own.astype(F32) + ffn_other.astype(F32))).astype(BF16)
-    d_kv_far, output, down_total = after(
-        (d_kv_far, output, down_total), out_grad.away, gate_grad.own, gate_grad.inner
-    )
-    d_kv_own = sum((p.astype(F32) for p in d_kv_far), d_kv[:rows].astype(F32)).astype(BF16)
+        [leaf.v for leaf in leaves], queries, d_att, lse, delta, kv_back, reach_rows, hot,
+        cosine, sine, bq, bk_b,
+    )
+    d_kv = Box(d_kv)
+    fence(d_kv, gate_one, gate_last[1:], out_got, ffn_other, mid, place)
+    output = (mid.v + (ffn_own.v.astype(F32) + ffn_other.v.astype(F32))).astype(BF16)
+    output = Box(output)
+    leftward = [(i + 1, i) for i in range(contexts - 1)]
+    d_kv_own = Box(d_kv.v[(contexts - 1) * rows :])
+    for k in range(contexts - 2, -1, -1):
+        got = Box(lax.ppermute(d_kv_own.v, "ctx", leftward))
+        if k == contexts - 2:
+            fence(got, output, gate_grad.arrived(1), gate_grad.own[0])
+            gate_two = gate_grad.middle(0)
+            gate_one = gate_grad.inward(1)
+        elif k == 0:
+            fence(mark(place), got, down_total, up_grad.arrived(0), gate_one, gate_two, up_last[1:])
+        else:
+            fence(mark(place), got, up_last[:1])
+        d_kv_own = Box(d_kv.v[k * rows : (k + 1) * rows] + got.v)
+    gate_three = gate_grad.outward(0)
+    gate_two = gate_grad.middle(1)
+    up_one = up_grad.inward(0)
+    fence(place, d_kv_own, list(gate_grad.own.values()))
     d_mixed, bias_part, gain_one_part, *d_hidden_one = mix_back(
-        place, d_query, d_kv_own, cosine, sine, tokens, qkv.all(), depth, bq
+        place.v, d_query, d_kv_own.v, cosine, sine, tokens, qkv.all(), depth, bq
     )
     peak_own = jnp.max(tops, axis=1)
     device = shard * contexts + ctx
@@ -1061,69 +1222,59 @@
         0.0,
     )
     bias_both = jnp.where(jnp.arange(halves)[:, None] == half, bias_part, 0.0)
-    vector = jnp.concatenate(
-        [gain_one_part[0], gain_two_part[0], bias_both.reshape(-1), spread.reshape(-1)]
-    )
-    d_mixed, vector, d_hidden_one = after((d_mixed, vector, d_hidden_one))
-    place = after(place, d_mixed)
-    back = [lax.ppermute(d_hidden_one[0], "tp", across)]
-    vector_got = swap(vector, "shard", shards, 1)
-    qkv_grad = Reduction(weight_grad(place, hidden_one_t, d_mixed, shards, 512), shards, contexts)
-
-    qkv_grad.send, vector_got, gate_grad.one, gate_grad.two, up_grad.last[0] = after(
-        (qkv_grad.send, vector_got, gate_grad.one, gate_grad.two, up_grad.last[0])
-    )
-    qkv_cores = qkv_grad.cores()
-    vector = vector + vector_got
-    up_grad.arrived(0)
-    up_grad.inward(0)
-    gate_grad.middle(1)
-    gate_grad.outward(0)
-    qkv_cores, vector, up_grad.last, out_grad.last = after(
-        (qkv_cores, vector, up_grad.last, out_grad.last),
-        up_grad.own, gate_grad.inner, gate_grad.total,
-    )
-    qkv_grad.got = qkv_cores
-    qkv_chips = qkv_grad.chips()
+    vector = Box(
+        jnp.concatenate(
+            [gain_one_part[0], gain_two_part[0], bias_both.reshape(-1), spread.reshape(-1)]
+        )
+    )
+    d_hidden_one = boxes(d_hidden_one)
+    fence(place, vector, d_hidden_one)
+
+    def hop(axis, bit):
+        vector.v = vector.v + swap(vector.v, axis, sizes[axis], bit)
+        return vector
+
+    back = [over_tp(d_hidden_one[0])]
+    q_sent = last_grad.make(place, hidden_one_t, d_mixed, 512)
+    fence(place, q_sent, back[0], d_hidden_one[1], up_grad.arrived(1))
+    qkv_got = last_grad.cores()
+    back.append(over_tp(d_hidden_one[1]))
+    hop("shard", 1)
+    fence(mark(place), qkv_got, gate_two, up_one, vector)
+    up_two = up_grad.middle(0)
+    up_one = up_grad.inward(1)
+    gate_three += gate_grad.outward(1)
     bit = 2
     while bit < shards:
-        vector = vector + swap(vector, "shard", shards, bit)
+        hop("shard", bit)
         bit *= 2
-    up_grad.arrived(1)
-    up_grad.inward(1)
-    out_grad.arrived(0)
-    out_grad.inward(0)
-    back.append(lax.ppermute(after(d_hidden_one[1], vector_got), "tp", across))
-    vector, back[0], up_grad.one, gate_grad.two = after(
-        (vector, back[0], up_grad.one, gate_grad.two), qkv_grad.away, up_grad.own, out_grad.own
-    )
-    up_grad.middle(0)
-    gate_grad.outward(1)
-    back.append(lax.ppermute(after(d_hidden_one[2], back[0]), "tp", across))
-    vector = sum_of_all(vector, {"ctx": contexts})
-    vector, qkv_grad.last, up_grad.one, up_grad.two, out_grad.one = after(
-        (vector, qkv_grad.last, up_grad.one, up_grad.two, out_grad.one),
-        up_grad.inner, gate_grad.total,
-    )
-    up_grad.middle(1)
-    up_grad.outward(0)
-    out_grad.middle(0)
-    qkv_grad.arrived(0)
-    qkv_grad.inward(0)
-    back = after(back, up_grad.inner, up_grad.total, out_grad.inner, qkv_grad.own)
-    vector_got = swap(vector, "tp", halves, 1)
-    input_grad = input_back(place, d_hidden_one, back, tokens, gain_attn, d_mid, bq)
-    input_grad, vector_got, qkv_grad.one, out_grad.two, up_grad.two = after(
-        (input_grad, vector_got, qkv_grad.one, out_grad.two, up_grad.two)
-    )
-    vector = vector + vector_got
-    up_grad.outward(1)
-    out_grad.outward(0)
-    qkv_grad.middle(0)
-    qkv_grad.outward(0)
-    down_total = down_total.astype(F32)
-    gate_total, up_total, out_total, qkv_total = (
-        one.result() for one in (gate_grad, up_grad, out_grad, qkv_grad)
+    fence(place, last_grad.sum_away(), vector)
+    last_last = last_grad.chips()
+    hop("tp", 1)
+    fence(mark(place), up_two, up_one, vector, last_last, back[1], d_hidden_one[2])
+    back.append(over_tp(d_hidden_one[2]))
+    vectors = Reduction(shards, contexts, 1)
+    vectors.own[0] = vector
+    up_three = up_grad.outward(0)
+    up_two = up_grad.middle(1)
+    last_grad.arrived(0)
+    last_one = last_grad.inward(0) + vectors.inward(0)
+    fence(mark(place), up_two, last_one, back[2], d_mid)
+    up_three += up_grad.outward(1)
+    last_two = last_grad.middle(0) + vectors.middle(0)
+    input_grad = Box(
+        input_back(
+            place.v, [p.v for p in d_hidden_one], [p.v for p in back], tokens, gain_attn, d_mid.v, bq
+        )
+    )
+    fence(input_grad, last_two, place)
+    last_three = last_grad.outward(0) + vectors.outward(0)
+    vector = Box(vectors.result())
+    gate_total, up_total, last_total = (one.result() for one in (gate_grad, up_grad, last_grad))
+    out_total = last_total[:, : out_weight.shape[1]]
+    qkv_total = last_total[:, out_weight.shape[1] :]
+    down_total, input_grad, output, vector = (
+        down_total.v.astype(F32), input_grad.v, output.v, vector.v
     )
     bias_at = 2 * width
     spread_at = bias_at + bias_both.size

time: 973 us -> 890 us (0.915)
  waiting for transfers between devices: 418 us -> 261 us
  local copies, waits for them, and re-layouts: 42.8 us -> 95.9 us
  Pallas kernels: 275 us -> 322 us
  other arithmetic: 116 us -> 80.4 us
    ppermute x38 -> x37, waiting for transfers between devices: 125 us -> 26.4 us  [swap(): return lax.ppermute(value, axis, [(i, i ^ bit) for i in range(size)])]
    ppermute x33 -> x37, waiting for transfers between devices: 287 us -> 235 us  [the longest x6 70.1 us: outward(): lax.ppermute(self.own[slab].v, 'ctx', [(1, 0), (2, 3)])]
    pallas_call x0 -> x22, Pallas kernels: none -> 43.9 us  [the longest x11 30.9 us: add_rows(): pl.pallas_call(functools.partial(add_kernel, [len(group) for group in gro...]
    unnamed x145 -> x220, local copies, waits for them, and re-layouts: 23.8 us -> 65.6 us
    add x24 -> x18, other arithmetic: 51.1 us -> 35.2 us  [the longest x6 15.4 us: middle(): self.own[slab] = Box(self.own[slab].v + self.one[slab].v)]
    slice x3 -> x0, other arithmetic: 13.1 us -> none  [pick(): part[(at * self.slabs + slab) * size:][:size]]
    ppermute x33 -> x37, starting transfers between devices: 69.8 us -> 82.4 us  [the longest x6 34.5 us: inward(): lax.ppermute(self.own[slab].v, 'ctx', [(0, 1), (3, 2)])]
    ppermute x38 -> x37, starting transfers between devices: 26.7 us -> 22.1 us  [swap(): return lax.ppermute(value, axis, [(i, i ^ bit) for i in range(size)])]
  transfers between devices with their start and end apart: 74 -> 77, of which waited for: 25 -> 27; matrix products, arithmetic and copies ran while one was open for 13% -> 11% of each run, Pallas kernels for 29% -> 36%
where the time goes in v3:
time: 890 us; the launch traced here: 880 us
  Pallas kernels  322 us (36%)
  waiting for transfers between devices  261 us (29%)
  starting transfers between devices  105 us (12%)
  local copies, waits for them, and re-layouts  95.9 us (11%)
  other arithmetic  80.4 us (9%)
  between operations  15.4 us (2%)
    ppermute x6, waiting for transfers between devices, outward(): lax.ppermute(self.own[slab].v, 'ctx', [(1, 0), (2, 3)])  70.1 us
    unnamed x220, local copies, waits for them, and re-layouts  65.6 us
    ppermute x6, waiting for transfers between devices, inward(): lax.ppermute(self.own[slab].v, 'ctx', [(0, 1), (3, 2)])  64.2 us
    pallas_call x1, Pallas kernels, gate_up_back(): call(functools.partial(gate_up_back_kernel, gates, ups, downs, units % tf...  62.3 us
    pallas_call x4, Pallas kernels, weight_grad(): call(functools.partial(weight_grad_kernel, width // parts, parts), pl.cdi...  50.5 us
    ppermute x3, waiting for transfers between devices, layer(): got = Box(lax.ppermute(d_kv_own.v, 'ctx', leftward))  42.4 us
    pallas_call x1, Pallas kernels, gate_up(): call(functools.partial(gate_up_kernel, gates, ups), pl.cdiv(units, tf), [...  40.3 us
    ppermute x12, waiting for transfers between devices, over_tp(): return Box(lax.ppermute(box.v, 'tp', across))  39.7 us
  transfers between devices with their start and end apart: 77, of which 27 were waited for; matrix products, arithmetic and copies ran while one was open for 11% of the time, Pallas kernels for 36%

profile of v3, /device:TPU:0, one launch (start us, length us, event | category | flops | bytes accessed | tf_op | source)
XLA Modules:
  0.0 880.1 jit_solution(10768151525936746340)
XLA Ops:
  7.2 3.0 collective-permute-start
  23.1 3.0 fusion
  37.1 8.4 mix.1
  48.3 3.5 collective-permute-start.5
  55.9 7.5 collective-permute-done.5
  67.3 5.1 collective-permute-start.8
  73.5 8.2 collective-permute-done.8
  81.7 5.3 collective-permute-start.11
  87.0 4.7 copy.37
  95.8 4.7 collective-permute-done.12.refs_2_
  108.8 4.5 attention_forward.2
  113.3 4.3 collective-permute-done.13.refs_6_
  118.3 10.5 %collective-permute-done.14.refs_7_ = bf16[384,768]{1,0:T(8,128)(2,1)S(1)} collective-permute-done((bf16[384,768]{1,0:T(8,128)(2,1)S(1)}, bf16[384,768]{1,0:T(8,128)(2,1)S(1)}, u32[]{:S(2)}, u32[]{:S(2)}) %collective-permute-start.14) | collective-permute-done | bytes 589856 | tf_op jit(solution)/shard_map/ppermute | solution.py:1067
  133.9 9.8 %attention_forward.3 = (bf16[512,768]{1,0:T(8,128)(2,1)}, f32[6,512]{1,0:T(8,128)S(1)}, f32[6,512]{1,0:T(8,128)S(1)}) custom-call(s32[4]{0:T(128)S(1)} %get-tuple-element.327.count, s32[128]{0:T(128)S(1)} %reshape.678.chosen, s32[33]{0:T(128)S(1)} %pad_add_fusion.9.places, bf16[1024,768]{1,0:T(8,128)(2,1)S(1)} %copy-done.86, ...), custom_call_target="tpu_custom_call" | custom-call | flops 2624999936 | bytes 1000 | tf_op jit(solution)/shard_map/attention_forward/pallas_call | solution.py:94
  143.7 4.4 collective-permute-done.16.upper_ref
  152.3 8.3 collective-permute-done.18.refs_4_
  160.6 8.5 collective-permute-done.17.lower_ref
  178.4 11.1 %branch.1 = (f32[1024,1536]{1,0:T(8,128)}, bf16[1024,1536]{1,0:T(8,128)(2,1)S(1)}, bf16[1536,1024]{1,0:T(8,128)(2,1)S(1)}) custom-call(s32[2]{0:T(128)S(1)} %copy-done.81, bf16[1024,1536]{1,0:T(8,128)(2,1)} %x_ref.7, bf16[1024,768]{1,0:T(8,128)(2,1)S(1)} %pad_maximum_fusion.own_ref.att_ref.right_ref, bf16[512,768]{1,0:T(8,128)(2,1)S(1)} %copy-done.64, ...), custom_call_target="tpu_custom_call" | custom-call | flops 2100000000 | bytes 1000 | tf_op jit(solution)/shard_map/branch/pallas_call | solution.py:605
  193.5 3.4 slice.68
  201.2 40.3 %gate_up.1 = (bf16[1024,4480]{1,0:T(8,128)(2,1)}, bf16[1024,4480]{1,0:T(8,128)(2,1)}, bf16[1024,4480]{1,0:T(8,128)(2,1)}) custom-call(s32[2]{0:T(128)} %mark.15.place.place_ref, bf16[1024,1536]{1,0:T(8,128)(2,1)} %copy-done.37, bf16[384,4480]{1,0:T(8,128)(2,1)} %refs_0_.9, bf16[384,4480]{1,0:T(8,128)(2,1)} %copy-done.92, ...), custom_call_target="tpu_custom_call" | custom-call | flops 7000000000 | bytes 1000 | tf_op jit(solution)/shard_map/gate_up/pallas_call | solution.py:312
  244.8 18.7 %whole_grad.1 = bf16[1536,4480]{1,0:T(8,128)(2,1)} custom-call(bf16[1536,1024]{1,0:T(8,128)(2,1)S(1)} %bitcast.28, bf16[1024,4480]{1,0:T(8,128)(2,1)} %get-tuple-element.415.right_ref.act_ref), custom_call_target="tpu_custom_call" | custom-call | flops 3324999936 | bytes 1000 | tf_op jit(solution)/shard_map/whole_grad/pallas_call | solution.py:392
  268.1 62.3 %gate_up_back.1 = (bf16[1024,4480]{1,0:T(8,128)(2,1)}, bf16[1024,4480]{1,0:T(8,128)(2,1)}, bf16[1024,384]{1,0:T(8,128)(2,1)}, bf16[1024,384]{1,0:T(8,128)(2,1)}, bf16[1024,768]{1,0:T(8,128)(2,1)}) custom-call(s32[2]{0:T(128)} %mark.16.place.place_ref, bf16[1024,1536]{1,0:T(8,128)(2,1)} %c_ref.3, bf16[1024,4480]{1,0:T(8,128)(2,1)} %get-tuple-element.389.by_gate_ref, ...), custom_call_target="tpu_custom_call" | custom-call | flops 10849999872 | bytes 1000 | tf_op jit(solution)/shard_map/gate_up_back/pallas_call | solution.py:368
  331.2 19.1 %weight_grad.4 = (bf16[768,4480]{1,0:T(8,128)(2,1)}, bf16[768,4480]{1,0:T(8,128)(2,1)}) custom-call(s32[2]{0:T(128)S(1)} %copy-done.80, bf16[1536,1024]{1,0:T(8,128)(2,1)S(1)} %copy-done.18, bf16[1024,4480]{1,0:T(8,128)(2,1)} %get-tuple-element.401.right_ref), custom_call_target="tpu_custom_call" | custom-call | flops 3324999936 | bytes 1000 | tf_op jit(solution)/shard_map/weight_grad/pallas_call | solution.py:415
  351.8 19.2 %weight_grad.5 = (bf16[768,4480]{1,0:T(8,128)(2,1)}, bf16[768,4480]{1,0:T(8,128)(2,1)}) custom-call(s32[2]{0:T(128)S(1)} %copy-done.80, bf16[1536,1024]{1,0:T(8,128)(2,1)S(1)} %copy-done.18, bf16[1024,4480]{1,0:T(8,128)(2,1)} %get-tuple-element.407.right_ref), custom_call_target="tpu_custom_call" | custom-call | flops 3324999936 | bytes 1000 | tf_op jit(solution)/shard_map/weight_grad/pallas_call | solution.py:415
  375.7 3.1 copy-done.7
  386.8 23.7 %down_project.1 = bf16[1024,1536]{1,0:T(8,128)(2,1)} custom-call(s32[2]{0:T(128)S(1)} %copy-done.80, bf16[1024,4480]{1,0:T(8,128)(2,1)} %get-tuple-element.415.right_ref.act_ref, bf16[384,4480]{1,0:T(8,128)(2,1)} %refs_0_.10, bf16[384,4480]{1,0:T(8,128)(2,1)} %collective-permute-done.28.refs_13_.refs_1_, bf16[96,4480]{1,0:T(8,128)(2,1)S(1)} %copy-done.36, ...), custom_call_target="tpu_custom_call" | custom-call | flops 4200000000 | bytes 1000 | tf_op jit(solution)/shard_map/down_project/pallas_call | solution.py:493
  427.3 13.8 %middle_back.1 = (f32[1024,1536]{1,0:T(8,128)}, bf16[1536,1024]{1,0:T(8,128)(2,1)}, bf16[1024,768]{1,0:T(8,128)(2,1)}, f32[6,1024]{1,0:T(8,128)S(1)}, f32[1,1536]{1,0:T(1,128)S(1)}) custom-call(s32[2]{0:T(128)S(1)} %copy-done.80, f32[1024,1536]{1,0:T(8,128)} %get-tuple-element.447.mid_ref, bf16[1024,1536]{1,0:T(8,128)(2,1)} %c_ref.3, ...), custom_call_target="tpu_custom_call" | custom-call | flops 2275000064 | bytes 1000 | tf_op jit(solution)/shard_map/middle_back/pallas_call | solution.py:667
  441.1 5.0 weight_grad.6
  448.2 3.0 copy-done.10
  451.2 3.5 add_rows.15
  454.7 6.0 collective-permute-start.40
  461.9 19.3 %attention_backward.1 = (bf16[1024,768]{1,0:T(8,128)(2,1)S(1)}, bf16[4096,256]{1,0:T(8,128)(2,1)}) custom-call(s32[4]{0:T(128)S(1)} %get-tuple-element.433.count, s32[32]{0:T(128)S(1)} %reshape.679.chosen, s32[9]{0:T(128)S(1)} %pad_add_fusion.10.places, bf16[1024,768]{1,0:T(8,128)(2,1)S(1)} %copy-done.87, bf16[1024,768]{1,0:T(8,128)(2,1)S(1)} %copy-done.88, ...), custom_call_target="tpu_custom_call" | custom-call | flops 9450000384 | bytes 1000 | tf_op jit(solution)/shard_map/attention_backward/pallas_call | solution.py:186
  482.1 43.9 %collective-permute-done.40 = bf16[192,4480]{1,0:T(8,128)(2,1)} collective-permute-done((bf16[192,4480]{1,0:T(8,128)(2,1)S(1)}, bf16[192,4480]{1,0:T(8,128)(2,1)}, u32[]{:S(2)}, u32[]{:S(2)}) %collective-permute-start.40) | collective-permute-done | bytes 1720352 | tf_op jit(solution)/shard_map/ppermute | solution.py:948
  534.0 7.6 add_convert_fusion
  543.2 3.2 add.249
  548.2 7.7 collective-permute-start.48
  560.4 12.3 %collective-permute-done.45 = bf16[1024,256]{1,0:T(8,128)(2,1)} collective-permute-done((bf16[1024,256]{1,0:T(8,128)(2,1)}, bf16[1024,256]{1,0:T(8,128)(2,1)}, u32[]{:S(2)}, u32[]{:S(2)}) %collective-permute-start.45) | collective-permute-done | bytes 524320 | tf_op jit(solution)/shard_map/ppermute | solution.py:1199
  587.5 28.5 %collective-permute-done.47 = bf16[1024,256]{1,0:T(8,128)(2,1)} collective-permute-done((bf16[1024,256]{1,0:T(8,128)(2,1)}, bf16[1024,256]{1,0:T(8,128)(2,1)}, u32[]{:S(2)}, u32[]{:S(2)}) %collective-permute-start.47) | collective-permute-done | bytes 524320 | tf_op jit(solution)/shard_map/ppermute | solution.py:1199
  616.1 3.0 add.252
  619.1 3.8 add.251
  624.5 7.9 mix_back.1
  638.1 8.0 collective-permute-start.54
  652.0 3.9 add_rows.18
  655.9 7.1 weight_grad.7
  671.9 11.3 %collective-permute-done.54 = bf16[192,4480]{1,0:T(8,128)(2,1)} collective-permute-done((bf16[192,4480]{1,0:T(8,128)(2,1)}, bf16[192,4480]{1,0:T(8,128)(2,1)}, u32[]{:S(2)}, u32[]{:S(2)}) %collective-permute-start.54) | collective-permute-done | bytes 1720352 | tf_op jit(solution)/shard_map/ppermute | solution.py:948
  683.2 3.6 add.256
  690.1 4.4 add_rows.19
  697.1 3.6 collective-permute-done.59
  702.5 10.5 %collective-permute-done.61.refs_4_ = bf16[1024,384]{1,0:T(8,128)(2,1)} collective-permute-done((bf16[1024,384]{1,0:T(8,128)(2,1)}, bf16[1024,384]{1,0:T(8,128)(2,1)}, u32[]{:S(2)}, u32[]{:S(2)}) %collective-permute-start.61) | collective-permute-done | bytes 786464 | tf_op jit(solution)/shard_map/ppermute | solution.py:1067
  718.9 3.6 add.258
  724.4 3.1 add.264
  729.4 3.0 add_rows.20.refs_0_
  732.5 4.6 add_rows.21
  737.1 9.0 %collective-permute-start.63 = (bf16[384,1792]{1,0:T(8,128)(2,1)}, bf16[384,1792]{1,0:T(8,128)(2,1)}, u32[]{:S(2)}, u32[]{:S(2)}) collective-permute-start(bf16[384,1792]{1,0:T(8,128)(2,1)} %add_rows.21), channel_id=1, source_target_pairs={{0,2},{6,4},{1,3},{7,5},{8,10},{14,12},{9,11},{15,13},{16,18},{22,... | collective-permute-start | bytes 4128776 | tf_op jit(solution)/shard_map/ppermute | solution.py:948
  746.0 5.3 convert_element_type.69
  755.5 3.6 add.265
  760.3 6.0 collective-permute-done.64
  772.4 3.3 maximum_convert_fusion
  775.8 3.7 add.266
  781.6 7.7 input_back.1
  790.6 18.2 %collective-permute-done.72 = bf16[192,4480]{1,0:T(8,128)(2,1)S(1)} collective-permute-done((bf16[192,4480]{1,0:T(8,128)(2,1)}, bf16[192,4480]{1,0:T(8,128)(2,1)S(1)}, u32[]{:S(2)}, u32[]{:S(2)}) %collective-permute-start.72) | collective-permute-done | bytes 1720352 | tf_op jit(solution)/shard_map/ppermute | solution.py:962
  810.7 35.6 %collective-permute-done.68 = f32[5312]{0:T(1024)S(1)} collective-permute-done((f32[5312]{0:T(1024)S(1)}, f32[5312]{0:T(1024)S(1)}, u32[]{:S(2)}, u32[]{:S(2)}) %collective-permute-start.68) | collective-permute-done | bytes 21280 | tf_op jit(solution)/shard_map/ppermute | solution.py:962
  849.8 3.3 maximum_convert_fusion.1
  853.1 16.2 %collective-permute-done.69 = bf16[384,1792]{1,0:T(8,128)(2,1)} collective-permute-done((bf16[384,1792]{1,0:T(8,128)(2,1)S(1)}, bf16[384,1792]{1,0:T(8,128)(2,1)}, u32[]{:S(2)}, u32[]{:S(2)}) %collective-permute-start.69) | collective-permute-done | bytes 1376288 | tf_op jit(solution)/shard_map/ppermute | solution.py:962
  (478 shorter events, 213.0 us)
Async XLA Ops:
  7.2 162.8 %all-gather.3.cloned.1.call-start = ((), (), s32[]{:S(2)}) async-start(), calls=%async_computation.1 | async-start | bytes 4300800 | tf_op jit(solution)/shard_map/all_gather | solution.py:849
  7.2 21.3 %collective-permute-start = (bf16[384,1024]{1,0:T(8,128)(2,1)}, bf16[384,1024]{1,0:T(8,128)(2,1)}, u32[]{:S(2)}, u32[]{:S(2)}) collective-permute-start(bf16[384,1024]{1,0:T(8,128)(2,1)} %refs_0_.11), channel_id=1, source_target_pairs={{0,16},{8,24},{16,0},{24,8},{1,17},{9,25},{17,1},{25,9},{2,18},{10... | collective-permute-start | bytes 2359304 | tf_op jit(solution)/shard_map/ppermute | solution.py:813
  29.0 19.3 %collective-permute-start.3 = (bf16[384,768]{1,0:T(8,128)(2,1)}, bf16[384,768]{1,0:T(8,128)(2,1)}, u32[]{:S(2)}, u32[]{:S(2)}) collective-permute-start(bf16[384,768]{1,0:T(8,128)(2,1)} %refs_6_.1), channel_id=1, source_target_pairs={{0,8},{8,0},{16,24},{24,16},{1,9},{9,1},{17,25},{25,17},{2,10},{10... | collective-permute-start | bytes 1769480 | tf_op jit(solution)/shard_map/ppermute | solution.py:813
  29.0 22.8 %collective-permute-start.4 = (bf16[384,768]{1,0:T(8,128)(2,1)}, bf16[384,768]{1,0:T(8,128)(2,1)}, u32[]{:S(2)}, u32[]{:S(2)}) collective-permute-start(bf16[384,768]{1,0:T(8,128)(2,1)} %refs_6_.1), channel_id=1, source_target_pairs={{0,16},{8,24},{16,0},{24,8},{1,17},{9,25},{17,1},{25,9},{2,18},{10... | collective-permute-start | bytes 1769480 | tf_op jit(solution)/shard_map/ppermute | solution.py:813
  30.4 25.5 %collective-permute-start.7 = (bf16[384,768]{1,0:T(8,128)(2,1)}, bf16[384,768]{1,0:T(8,128)(2,1)}, u32[]{:S(2)}, u32[]{:S(2)}) collective-permute-start(bf16[384,768]{1,0:T(8,128)(2,1)} %refs_6_.1), channel_id=1, source_target_pairs={{0,1},{1,0},{2,3},{3,2},{4,5},{5,4},{6,7},{7,6},{8,9},{9,8},{10,11... | collective-permute-start | bytes 1769480 | tf_op jit(solution)/shard_map/ppermute | solution.py:1077
  48.3 15.1 %collective-permute-start.5 = (bf16[1024,256]{1,0:T(8,128)(2,1)}, bf16[1024,256]{1,0:T(8,128)(2,1)S(1)}, u32[]{:S(2)}, u32[]{:S(2)}) collective-permute-start(bf16[1024,256]{1,0:T(8,128)(2,1)} %get-tuple-element.316), channel_id=1, source_target_pairs={{0,2},{2,4},{4,6},{1,3},{3,5},{5,7},{8,10},{10,12},{12,14},{9,11},... | collective-permute-start | bytes 1572872 | tf_op jit(solution)/shard_map/ppermute | solution.py:1089
  54.0 27.7 %collective-permute-start.10 = (bf16[96,4480]{1,0:T(8,128)(2,1)}, bf16[96,4480]{1,0:T(8,128)(2,1)}, u32[]{:S(2)}, u32[]{:S(2)}) collective-permute-start(bf16[96,4480]{1,0:T(8,128)(2,1)} %constant_dynamic-slice_fusion.1), channel_id=1, source_target_pairs={{0,16},{8,24},{16,0},{24,8},{1,17},{9,25},{17,1},{25,9},{2,18},{10... | collective-permute-start | bytes 2580488 | tf_op jit(solution)/shard_map/ppermute | solution.py:813
  65.1 35.3 %collective-permute-start.12 = (bf16[128,4480]{1,0:T(8,128)(2,1)S(1)}, bf16[128,4480]{1,0:T(8,128)(2,1)}, u32[]{:S(2)}, u32[]{:S(2)}) collective-permute-start(bf16[128,4480]{1,0:T(8,128)(2,1)S(1)} %slice.63), channel_id=1, source_target_pairs={{0,16},{8,24},{16,0},{24,8},{1,17},{9,25},{17,1},{25,9},{2,18},{10... | collective-permute-start | bytes 3440648 | tf_op jit(solution)/shard_map/ppermute | solution.py:813
  65.9 15.8 %collective-permute-start.9 = (bf16[384,768]{1,0:T(8,128)(2,1)}, bf16[384,768]{1,0:T(8,128)(2,1)S(1)}, u32[]{:S(2)}, u32[]{:S(2)}) collective-permute-start(bf16[384,768]{1,0:T(8,128)(2,1)} %collective-permute-done.3.refs_1_.refs_7_), channel_id=1, source_target_pairs={{0,1},{1,0},{2,3},{3,2},{4,5},{5,4},{6,7},{7,6},{8,9},{9,8},{10,11... | collective-permute-start | bytes 1769480 | tf_op jit(solution)/shard_map/ppermute | solution.py:1067
  100.5 314.3 %reduce-scatter.2.cloned.1.call-start = ((), (), s32[]{:S(2)}) async-start(), calls=%async_computation.2 | async-start | bytes 14622720 | tf_op jit(solution)/shard_map/reduce_scatter | solution.py:1146
  101.0 16.5 %collective-permute-start.13 = (bf16[384,768]{1,0:T(8,128)(2,1)}, bf16[384,768]{1,0:T(8,128)(2,1)S(1)}, u32[]{:S(2)}, u32[]{:S(2)}) collective-permute-start(bf16[384,768]{1,0:T(8,128)(2,1)} %collective-permute-done.4.refs_2_.refs_8_), channel_id=1, source_target_pairs={{0,1},{1,0},{2,3},{3,2},{4,5},{5,4},{6,7},{7,6},{8,9},{9,8},{10,11... | collective-permute-start | bytes 1769480 | tf_op jit(solution)/shard_map/ppermute | solution.py:1067
  101.6 27.2 %collective-permute-start.14 = (bf16[384,768]{1,0:T(8,128)(2,1)S(1)}, bf16[384,768]{1,0:T(8,128)(2,1)S(1)}, u32[]{:S(2)}, u32[]{:S(2)}) collective-permute-start(bf16[384,768]{1,0:T(8,128)(2,1)S(1)} %collective-permute-done.6.refs_3_.refs_9_), channel_id=1, source_target_pairs={{0,1},{1,0},{2,3},{3,2},{4,5},{5,4},{6,7},{7,6},{8,9},{9,8},{10,11... | collective-permute-start | bytes 1769480 | tf_op jit(solution)/shard_map/ppermute | solution.py:1067
  104.4 44.5 %collective-permute-start.15 = (bf16[128,4480]{1,0:T(8,128)(2,1)S(1)}, bf16[128,4480]{1,0:T(8,128)(2,1)}, u32[]{:S(2)}, u32[]{:S(2)}) collective-permute-start(bf16[128,4480]{1,0:T(8,128)(2,1)S(1)} %slice.64), channel_id=1, source_target_pairs={{0,16},{8,24},{16,0},{24,8},{1,17},{9,25},{17,1},{25,9},{2,18},{10... | collective-permute-start | bytes 3440648 | tf_op jit(solution)/shard_map/ppermute | solution.py:813
  129.7 18.4 %collective-permute-start.16 = (bf16[512,768]{1,0:T(8,128)(2,1)S(1)}, bf16[512,768]{1,0:T(8,128)(2,1)S(1)}, u32[]{:S(2)}, u32[]{:S(2)}) collective-permute-start(bf16[512,768]{1,0:T(8,128)(2,1)S(1)} %get-tuple-element.341), channel_id=1, source_target_pairs={{0,1},{1,0},{2,3},{3,2},{4,5},{5,4},{6,7},{7,6},{8,9},{9,8},{10,11... | collective-permute-start | bytes 2359304 | tf_op jit(solution)/shard_map/ppermute | solution.py:1067
  130.3 22.0 %collective-permute-start.19 = (bf16[128,4480]{1,0:T(8,128)(2,1)}, bf16[128,4480]{1,0:T(8,128)(2,1)}, u32[]{:S(2)}, u32[]{:S(2)}) collective-permute-start(bf16[128,4480]{1,0:T(8,128)(2,1)} %collective-permute-done.12.refs_2_), channel_id=1, source_target_pairs={{0,8},{8,0},{16,24},{24,16},{1,9},{9,1},{17,25},{25,17},{2,10},{10... | collective-permute-start | bytes 3440648 | tf_op jit(solution)/shard_map/ppermute | solution.py:813
  132.6 28.0 %collective-permute-start.18 = (bf16[128,4480]{1,0:T(8,128)(2,1)}, bf16[128,4480]{1,0:T(8,128)(2,1)}, u32[]{:S(2)}, u32[]{:S(2)}) collective-permute-start(bf16[128,4480]{1,0:T(8,128)(2,1)} %slice.65), channel_id=1, source_target_pairs={{0,16},{8,24},{16,0},{24,8},{1,17},{9,25},{17,1},{25,9},{2,18},{10... | collective-permute-start | bytes 3440648 | tf_op jit(solution)/shard_map/ppermute | solution.py:813
  148.9 21.1 %collective-permute-start.20 = (bf16[128,4480]{1,0:T(8,128)(2,1)}, bf16[128,4480]{1,0:T(8,128)(2,1)}, u32[]{:S(2)}, u32[]{:S(2)}) collective-permute-start(bf16[128,4480]{1,0:T(8,128)(2,1)} %collective-permute-done.15.refs_3_), channel_id=1, source_target_pairs={{0,8},{8,0},{16,24},{24,16},{1,9},{9,1},{17,25},{25,17},{2,10},{10... | collective-permute-start | bytes 3440648 | tf_op jit(solution)/shard_map/ppermute | solution.py:813
  148.9 20.2 %collective-permute-start.17 = (bf16[512,768]{1,0:T(8,128)(2,1)}, bf16[512,768]{1,0:T(8,128)(2,1)S(1)}, u32[]{:S(2)}, u32[]{:S(2)}) collective-permute-start(bf16[512,768]{1,0:T(8,128)(2,1)} %get-tuple-element.342), channel_id=1, source_target_pairs={{0,1},{1,0},{2,3},{3,2},{4,5},{5,4},{6,7},{7,6},{8,9},{9,8},{10,11... | collective-permute-start | bytes 2359304 | tf_op jit(solution)/shard_map/ppermute | solution.py:1067
  170.0 23.4 %collective-permute-start.24 = (bf16[384,4480]{1,0:T(8,128)(2,1)}, bf16[384,4480]{1,0:T(8,128)(2,1)S(1)}, u32[]{:S(2)}, u32[]{:S(2)}) collective-permute-start(bf16[384,4480]{1,0:T(8,128)(2,1)} %refs_8_.3), channel_id=1, source_target_pairs={{0,8},{8,0},{16,24},{24,16},{1,9},{9,1},{17,25},{25,17},{2,10},{10... | collective-permute-start | bytes 10321928 | tf_op jit(solution)/shard_map/ppermute | solution.py:813
  170.0 23.4 %collective-permute-start.23 = (bf16[384,4480]{1,0:T(8,128)(2,1)}, bf16[384,4480]{1,0:T(8,128)(2,1)S(1)}, u32[]{:S(2)}, u32[]{:S(2)}) collective-permute-start(bf16[384,4480]{1,0:T(8,128)(2,1)} %refs_0_.9), channel_id=1, source_target_pairs={{0,8},{8,0},{16,24},{24,16},{1,9},{9,1},{17,25},{25,17},{2,10},{10... | collective-permute-start | bytes 10321928 | tf_op jit(solution)/shard_map/ppermute | solution.py:813
  170.5 23.0 %collective-permute-start.22 = (bf16[384,4480]{1,0:T(8,128)(2,1)}, bf16[384,4480]{1,0:T(8,128)(2,1)}, u32[]{:S(2)}, u32[]{:S(2)}) collective-permute-start(bf16[384,4480]{1,0:T(8,128)(2,1)} %all-gather.3.cloned.1.call-done.refs_10_), channel_id=1, source_target_pairs={{0,8},{8,0},{16,24},{24,16},{1,9},{9,1},{17,25},{25,17},{2,10},{10... | collective-permute-start | bytes 10321928 | tf_op jit(solution)/shard_map/ppermute | solution.py:813
  170.6 22.8 %collective-permute-start.21 = (bf16[128,4480]{1,0:T(8,128)(2,1)}, bf16[128,4480]{1,0:T(8,128)(2,1)S(1)}, u32[]{:S(2)}, u32[]{:S(2)}) collective-permute-start(bf16[128,4480]{1,0:T(8,128)(2,1)} %collective-permute-done.18.refs_4_), channel_id=1, source_target_pairs={{0,8},{8,0},{16,24},{24,16},{1,9},{9,1},{17,25},{25,17},{2,10},{10... | collective-permute-start | bytes 3440648 | tf_op jit(solution)/shard_map/ppermute | solution.py:813
  172.2 21.2 %collective-permute-start.25 = (bf16[96,4480]{1,0:T(8,128)(2,1)S(1)}, bf16[96,4480]{1,0:T(8,128)(2,1)S(1)}, u32[]{:S(2)}, u32[]{:S(2)}) collective-permute-start(bf16[96,4480]{1,0:T(8,128)(2,1)S(1)} %slice.66), channel_id=1, source_target_pairs={{0,16},{8,24},{16,0},{24,8},{1,17},{9,25},{17,1},{25,9},{2,18},{10... | collective-permute-start | bytes 2580488 | tf_op jit(solution)/shard_map/ppermute | solution.py:813
  193.5 48.1 %collective-permute-start.28 = (bf16[384,4480]{1,0:T(8,128)(2,1)}, bf16[384,4480]{1,0:T(8,128)(2,1)}, u32[]{:S(2)}, u32[]{:S(2)}) collective-permute-start(bf16[384,4480]{1,0:T(8,128)(2,1)} %refs_0_.10), channel_id=1, source_target_pairs={{0,8},{8,0},{16,24},{24,16},{1,9},{9,1},{17,25},{25,17},{2,10},{10... | collective-permute-start | bytes 10321928 | tf_op jit(solution)/shard_map/ppermute | solution.py:813
  199.2 42.4 %collective-permute-start.26 = (bf16[96,4480]{1,0:T(8,128)(2,1)}, bf16[96,4480]{1,0:T(8,128)(2,1)}, u32[]{:S(2)}, u32[]{:S(2)}) collective-permute-start(bf16[96,4480]{1,0:T(8,128)(2,1)} %slice.67), channel_id=1, source_target_pairs={{0,16},{8,24},{16,0},{24,8},{1,17},{9,25},{17,1},{25,9},{2,18},{10... | collective-permute-start | bytes 2580488 | tf_op jit(solution)/shard_map/ppermute | solution.py:813
  199.8 41.7 %collective-permute-start.27 = (bf16[96,4480]{1,0:T(8,128)(2,1)}, bf16[96,4480]{1,0:T(8,128)(2,1)}, u32[]{:S(2)}, u32[]{:S(2)}) collective-permute-start(bf16[96,4480]{1,0:T(8,128)(2,1)} %slice.68), channel_id=1, source_target_pairs={{0,16},{8,24},{16,0},{24,8},{1,17},{9,25},{17,1},{25,9},{2,18},{10... | collective-permute-start | bytes 2580488 | tf_op jit(solution)/shard_map/ppermute | solution.py:813
  243.7 20.6 %collective-permute-start.32 = (bf16[96,4480]{1,0:T(8,128)(2,1)}, bf16[96,4480]{1,0:T(8,128)(2,1)}, u32[]{:S(2)}, u32[]{:S(2)}) collective-permute-start(bf16[96,4480]{1,0:T(8,128)(2,1)} %slice.69), channel_id=1, source_target_pairs={{0,16},{8,24},{16,0},{24,8},{1,17},{9,25},{17,1},{25,9},{2,18},{10... | collective-permute-start | bytes 2580488 | tf_op jit(solution)/shard_map/ppermute | solution.py:813
  244.3 20.0 %collective-permute-start.29 = (bf16[96,4480]{1,0:T(8,128)(2,1)S(1)}, bf16[96,4480]{1,0:T(8,128)(2,1)}, u32[]{:S(2)}, u32[]{:S(2)}) collective-permute-start(bf16[96,4480]{1,0:T(8,128)(2,1)S(1)} %collective-permute-done.25.refs_14_.refs_2_), channel_id=1, source_target_pairs={{0,8},{8,0},{16,24},{24,16},{1,9},{9,1},{17,25},{25,17},{2,10},{10... | collective-permute-start | bytes 2580488 | tf_op jit(solution)/shard_map/ppermute | solution.py:813
  244.3 20.0 %collective-permute-start.30 = (bf16[96,4480]{1,0:T(8,128)(2,1)}, bf16[96,4480]{1,0:T(8,128)(2,1)}, u32[]{:S(2)}, u32[]{:S(2)}) collective-permute-start(bf16[96,4480]{1,0:T(8,128)(2,1)} %collective-permute-done.26.refs_15_.refs_3_), channel_id=1, source_target_pairs={{0,8},{8,0},{16,24},{24,16},{1,9},{9,1},{17,25},{25,17},{2,10},{10... | collective-permute-start | bytes 2580488 | tf_op jit(solution)/shard_map/ppermute | solution.py:813
  244.8 19.5 %collective-permute-start.31 = (bf16[96,4480]{1,0:T(8,128)(2,1)}, bf16[96,4480]{1,0:T(8,128)(2,1)}, u32[]{:S(2)}, u32[]{:S(2)}) collective-permute-start(bf16[96,4480]{1,0:T(8,128)(2,1)} %collective-permute-done.27.refs_16_.refs_4_), channel_id=1, source_target_pairs={{0,8},{8,0},{16,24},{24,16},{1,9},{9,1},{17,25},{25,17},{2,10},{10... | collective-permute-start | bytes 2580488 | tf_op jit(solution)/shard_map/ppermute | solution.py:813
  264.3 351.8 %all-gather.5.cloned.1.call-start = ((), (), s32[]{:S(2)}) async-start(), calls=%async_computation.3 | async-start | bytes 4300800 | tf_op jit(solution)/shard_map/all_gather | solution.py:1171
  330.4 19.9 %collective-permute-start.34 = (bf16[1024,384]{1,0:T(8,128)(2,1)}, bf16[1024,384]{1,0:T(8,128)(2,1)S(1)}, u32[]{:S(2)}, u32[]{:S(2)}) collective-permute-start(bf16[1024,384]{1,0:T(8,128)(2,1)} %get-tuple-element.404.refs_0_), channel_id=1, source_target_pairs={{0,1},{1,0},{2,3},{3,2},{4,5},{5,4},{6,7},{7,6},{8,9},{9,8},{10,11... | collective-permute-start | bytes 2359304 | tf_op jit(solution)/shard_map/ppermute | solution.py:1067
  350.3 21.6 %collective-permute-start.35 = (bf16[768,4480]{1,0:T(8,128)(2,1)}, bf16[768,4480]{1,0:T(8,128)(2,1)S(1)}, u32[]{:S(2)}, u32[]{:S(2)}) collective-permute-start(bf16[768,4480]{1,0:T(8,128)(2,1)} %get-tuple-element.409), channel_id=1, source_target_pairs={{0,8},{8,0},{16,24},{24,16},{1,9},{9,1},{17,25},{25,17},{2,10},{10... | collective-permute-start | bytes 20643848 | tf_op jit(solution)/shard_map/ppermute | solution.py:813
  350.5 20.6 %collective-permute-start.36 = (bf16[1024,384]{1,0:T(8,128)(2,1)S(1)}, bf16[1024,384]{1,0:T(8,128)(2,1)S(1)}, u32[]{:S(2)}, u32[]{:S(2)}) collective-permute-start(bf16[1024,384]{1,0:T(8,128)(2,1)S(1)} %copy-done.57), channel_id=1, source_target_pairs={{0,1},{1,0},{2,3},{3,2},{4,5},{5,4},{6,7},{7,6},{8,9},{9,8},{10,11... | collective-permute-start | bytes 2359304 | tf_op jit(solution)/shard_map/ppermute | solution.py:1067
  374.8 37.1 %collective-permute-start.37 = (bf16[768,4480]{1,0:T(8,128)(2,1)}, bf16[768,4480]{1,0:T(8,128)(2,1)S(1)}, u32[]{:S(2)}, u32[]{:S(2)}) collective-permute-start(bf16[768,4480]{1,0:T(8,128)(2,1)} %get-tuple-element.416), channel_id=1, source_target_pairs={{0,8},{8,0},{16,24},{24,16},{1,9},{9,1},{17,25},{25,17},{2,10},{10... | collective-permute-start | bytes 20643848 | tf_op jit(solution)/shard_map/ppermute | solution.py:813
  375.0 36.9 %collective-permute-start.38 = (bf16[1024,768]{1,0:T(8,128)(2,1)}, bf16[1024,768]{1,0:T(8,128)(2,1)}, u32[]{:S(2)}, u32[]{:S(2)}) collective-permute-start(bf16[1024,768]{1,0:T(8,128)(2,1)} %get-tuple-element.417.refs_2_), channel_id=1, source_target_pairs={{0,1},{1,0},{2,3},{3,2},{4,5},{5,4},{6,7},{7,6},{8,9},{9,8},{10,11... | collective-permute-start | bytes 4718600 | tf_op jit(solution)/shard_map/ppermute | solution.py:1067
  385.6 62.5 %collective-permute-start.39 = (bf16[192,4480]{1,0:T(8,128)(2,1)}, bf16[192,4480]{1,0:T(8,128)(2,1)}, u32[]{:S(2)}, u32[]{:S(2)}) collective-permute-start(bf16[192,4480]{1,0:T(8,128)(2,1)} %add_rows.11), channel_id=1, source_target_pairs={{0,16},{8,24},{16,0},{24,8},{1,17},{9,25},{17,1},{25,9},{2,18},{10... | collective-permute-start | bytes 5160968 | tf_op jit(solution)/shard_map/ppermute | solution.py:813
  414.8 111.2 %collective-permute-start.43 = (bf16[1024,1536]{1,0:T(8,128)(2,1)}, bf16[1024,1536]{1,0:T(8,128)(2,1)}, u32[]{:S(2)}, u32[]{:S(2)}) collective-permute-start(bf16[1024,1536]{1,0:T(8,128)(2,1)} %down_project.1), channel_id=1, source_target_pairs={{0,1},{1,0},{2,3},{3,2},{4,5},{5,4},{6,7},{7,6},{8,9},{9,8},{10,11... | collective-permute-start | bytes 9437192 | tf_op jit(solution)/shard_map/ppermute | solution.py:1067
  416.2 65.0 %collective-permute-start.41 = (bf16[192,4480]{1,0:T(8,128)(2,1)}, bf16[192,4480]{1,0:T(8,128)(2,1)}, u32[]{:S(2)}, u32[]{:S(2)}) collective-permute-start(bf16[192,4480]{1,0:T(8,128)(2,1)} %add_rows.12), channel_id=1, source_target_pairs={{0,16},{8,24},{16,0},{24,8},{1,17},{9,25},{17,1},{25,9},{2,18},{10... | collective-permute-start | bytes 5160968 | tf_op jit(solution)/shard_map/ppermute | solution.py:813
  454.7 71.4 %collective-permute-start.40 = (bf16[192,4480]{1,0:T(8,128)(2,1)S(1)}, bf16[192,4480]{1,0:T(8,128)(2,1)}, u32[]{:S(2)}, u32[]{:S(2)}) collective-permute-start(bf16[192,4480]{1,0:T(8,128)(2,1)S(1)} %add_rows.15), channel_id=1, source_target_pairs={{0,2},{6,4},{1,3},{7,5},{8,10},{14,12},{9,11},{15,13},{16,18},{22,... | collective-permute-start | bytes 5160968 | tf_op jit(solution)/shard_map/ppermute | solution.py:948
  460.7 21.4 %collective-permute-start.42 = (bf16[768,768]{1,0:T(8,128)(2,1)S(1)}, bf16[768,768]{1,0:T(8,128)(2,1)S(1)}, u32[]{:S(2)}, u32[]{:S(2)}) collective-permute-start(bf16[768,768]{1,0:T(8,128)(2,1)S(1)} %copy-done.90), channel_id=1, source_target_pairs={{0,8},{8,0},{16,24},{24,16},{1,9},{9,1},{17,25},{25,17},{2,10},{10... | collective-permute-start | bytes 3538952 | tf_op jit(solution)/shard_map/ppermute | solution.py:813
  460.7 99.6 %collective-permute-start.46 = (bf16[192,4480]{1,0:T(8,128)(2,1)}, bf16[192,4480]{1,0:T(8,128)(2,1)}, u32[]{:S(2)}, u32[]{:S(2)}) collective-permute-start(bf16[192,4480]{1,0:T(8,128)(2,1)} %add_rows.13), channel_id=1, source_target_pairs={{0,16},{8,24},{16,0},{24,8},{1,17},{9,25},{17,1},{25,9},{2,18},{10... | collective-permute-start | bytes 5160968 | tf_op jit(solution)/shard_map/ppermute | solution.py:813
  481.2 106.4 %collective-permute-start.50 = (bf16[192,4480]{1,0:T(8,128)(2,1)S(1)}, bf16[192,4480]{1,0:T(8,128)(2,1)}, u32[]{:S(2)}, u32[]{:S(2)}) collective-permute-start(bf16[192,4480]{1,0:T(8,128)(2,1)S(1)} %add_rows.14), channel_id=1, source_target_pairs={{0,16},{8,24},{16,0},{24,8},{1,17},{9,25},{17,1},{25,9},{2,18},{10... | collective-permute-start | bytes 5160968 | tf_op jit(solution)/shard_map/ppermute | solution.py:813
  527.1 16.0 %collective-permute-start.44 = (bf16[1024,256]{1,0:T(8,128)(2,1)S(1)}, bf16[1024,256]{1,0:T(8,128)(2,1)S(1)}, u32[]{:S(2)}, u32[]{:S(2)}) collective-permute-start(bf16[1024,256]{1,0:T(8,128)(2,1)S(1)} %slice.70), channel_id=1, source_target_pairs={{2,0},{4,2},{6,4},{3,1},{5,3},{7,5},{10,8},{12,10},{14,12},{11,9},... | collective-permute-start | bytes 1572872 | tf_op jit(solution)/shard_map/ppermute | solution.py:1199
  546.3 69.8 %collective-permute-start.49 = (bf16[192,4480]{1,0:T(8,128)(2,1)}, bf16[192,4480]{1,0:T(8,128)(2,1)}, u32[]{:S(2)}, u32[]{:S(2)}) collective-permute-start(bf16[192,4480]{1,0:T(8,128)(2,1)} %add.249), channel_id=1, source_target_pairs={{2,4},{4,2},{3,5},{5,3},{10,12},{12,10},{11,13},{13,11},{18,20},{2... | collective-permute-start | bytes 5160968 | tf_op jit(solution)/shard_map/ppermute | solution.py:955
  548.2 67.9 %collective-permute-start.48 = (bf16[192,4480]{1,0:T(8,128)(2,1)S(1)}, bf16[192,4480]{1,0:T(8,128)(2,1)}, u32[]{:S(2)}, u32[]{:S(2)}) collective-permute-start(bf16[192,4480]{1,0:T(8,128)(2,1)S(1)} %add_rows.16), channel_id=1, source_target_pairs={{0,2},{6,4},{1,3},{7,5},{8,10},{14,12},{9,11},{15,13},{16,18},{22,... | collective-permute-start | bytes 5160968 | tf_op jit(solution)/shard_map/ppermute | solution.py:948
  574.7 41.4 %collective-permute-start.47 = (bf16[1024,256]{1,0:T(8,128)(2,1)}, bf16[1024,256]{1,0:T(8,128)(2,1)}, u32[]{:S(2)}, u32[]{:S(2)}) collective-permute-start(bf16[1024,256]{1,0:T(8,128)(2,1)} %slice_add_fusion.1), channel_id=1, source_target_pairs={{2,0},{4,2},{6,4},{3,1},{5,3},{7,5},{10,8},{12,10},{14,12},{11,9},... | collective-permute-start | bytes 1572872 | tf_op jit(solution)/shard_map/ppermute | solution.py:1199
  634.7 29.5 %collective-permute-start.51 = (bf16[1024,384]{1,0:T(8,128)(2,1)}, bf16[1024,384]{1,0:T(8,128)(2,1)S(1)}, u32[]{:S(2)}, u32[]{:S(2)}) collective-permute-start(bf16[1024,384]{1,0:T(8,128)(2,1)} %copy-done.52), channel_id=1, source_target_pairs={{0,1},{1,0},{2,3},{3,2},{4,5},{5,4},{6,7},{7,6},{8,9},{9,8},{10,11... | collective-permute-start | bytes 2359304 | tf_op jit(solution)/shard_map/ppermute | solution.py:1067
  636.2 35.7 %collective-permute-start.53 = (bf16[192,4480]{1,0:T(8,128)(2,1)}, bf16[192,4480]{1,0:T(8,128)(2,1)}, u32[]{:S(2)}, u32[]{:S(2)}) collective-permute-start(bf16[192,4480]{1,0:T(8,128)(2,1)} %add.252), channel_id=1, source_target_pairs={{2,4},{4,2},{3,5},{5,3},{10,12},{12,10},{11,13},{13,11},{18,20},{2... | collective-permute-start | bytes 5160968 | tf_op jit(solution)/shard_map/ppermute | solution.py:955
  638.1 45.1 %collective-permute-start.54 = (bf16[192,4480]{1,0:T(8,128)(2,1)}, bf16[192,4480]{1,0:T(8,128)(2,1)}, u32[]{:S(2)}, u32[]{:S(2)}) collective-permute-start(bf16[192,4480]{1,0:T(8,128)(2,1)} %copy-done.19), channel_id=1, source_target_pairs={{0,2},{6,4},{1,3},{7,5},{8,10},{14,12},{9,11},{15,13},{16,18},{22,... | collective-permute-start | bytes 5160968 | tf_op jit(solution)/shard_map/ppermute | solution.py:948
  665.1 18.1 %collective-permute-start.52 = (bf16[768,1024]{1,0:T(8,128)(2,1)}, bf16[768,1024]{1,0:T(8,128)(2,1)}, u32[]{:S(2)}, u32[]{:S(2)}) collective-permute-start(bf16[768,1024]{1,0:T(8,128)(2,1)} %get-tuple-element.485), channel_id=1, source_target_pairs={{0,8},{8,0},{16,24},{24,16},{1,9},{9,1},{17,25},{25,17},{2,10},{10... | collective-permute-start | bytes 4718600 | tf_op jit(solution)/shard_map/ppermute | solution.py:813
  668.2 47.8 %collective-permute-start.58 = (bf16[192,4480]{1,0:T(8,128)(2,1)}, bf16[192,4480]{1,0:T(8,128)(2,1)}, u32[]{:S(2)}, u32[]{:S(2)}) collective-permute-start(bf16[192,4480]{1,0:T(8,128)(2,1)} %add_rows.18), channel_id=1, source_target_pairs={{0,2},{6,4},{1,3},{7,5},{8,10},{14,12},{9,11},{15,13},{16,18},{22,... | collective-permute-start | bytes 5160968 | tf_op jit(solution)/shard_map/ppermute | solution.py:948
  686.8 32.1 %collective-permute-start.57 = (bf16[192,4480]{1,0:T(8,128)(2,1)}, bf16[192,4480]{1,0:T(8,128)(2,1)}, u32[]{:S(2)}, u32[]{:S(2)}) collective-permute-start(bf16[192,4480]{1,0:T(8,128)(2,1)} %add.256), channel_id=1, source_target_pairs={{2,4},{4,2},{3,5},{5,3},{10,12},{12,10},{11,13},{13,11},{18,20},{2... | collective-permute-start | bytes 5160968 | tf_op jit(solution)/shard_map/ppermute | solution.py:955
  694.5 24.3 %collective-permute-start.60 = (bf16[384,1792]{1,0:T(8,128)(2,1)}, bf16[384,1792]{1,0:T(8,128)(2,1)}, u32[]{:S(2)}, u32[]{:S(2)}) collective-permute-start(bf16[384,1792]{1,0:T(8,128)(2,1)} %add_rows.19), channel_id=1, source_target_pairs={{0,16},{8,24},{16,0},{24,8},{1,17},{9,25},{17,1},{25,9},{2,18},{10... | collective-permute-start | bytes 4128776 | tf_op jit(solution)/shard_map/ppermute | solution.py:813
  695.2 56.1 %collective-permute-start.70 = (bf16[192,4480]{1,0:T(8,128)(2,1)}, bf16[192,4480]{1,0:T(8,128)(2,1)}, u32[]{:S(2)}, u32[]{:S(2)}) collective-permute-start(bf16[192,4480]{1,0:T(8,128)(2,1)} %add.251), channel_id=1, source_target_pairs={{2,0},{4,6},{3,1},{5,7},{10,8},{12,14},{11,9},{13,15},{18,16},{20,... | collective-permute-start | bytes 5160968 | tf_op jit(solution)/shard_map/ppermute | solution.py:962
  722.4 45.1 %collective-permute-start.62 = (bf16[192,4480]{1,0:T(8,128)(2,1)}, bf16[192,4480]{1,0:T(8,128)(2,1)}, u32[]{:S(2)}, u32[]{:S(2)}) collective-permute-start(bf16[192,4480]{1,0:T(8,128)(2,1)} %add.258), channel_id=1, source_target_pairs={{2,4},{4,2},{3,5},{5,3},{10,12},{12,10},{11,13},{13,11},{18,20},{2... | collective-permute-start | bytes 5160968 | tf_op jit(solution)/shard_map/ppermute | solution.py:955
  727.5 43.0 %collective-permute-start.71 = (bf16[192,4480]{1,0:T(8,128)(2,1)}, bf16[192,4480]{1,0:T(8,128)(2,1)}, u32[]{:S(2)}, u32[]{:S(2)}) collective-permute-start(bf16[192,4480]{1,0:T(8,128)(2,1)} %add.264), channel_id=1, source_target_pairs={{2,0},{4,6},{3,1},{5,7},{10,8},{12,14},{11,9},{13,15},{18,16},{20,... | collective-permute-start | bytes 5160968 | tf_op jit(solution)/shard_map/ppermute | solution.py:962
  728.8 38.7 %collective-permute-start.65 = (bf16[1024,768]{1,0:T(8,128)(2,1)}, bf16[1024,768]{1,0:T(8,128)(2,1)}, u32[]{:S(2)}, u32[]{:S(2)}) collective-permute-start(bf16[1024,768]{1,0:T(8,128)(2,1)} %get-tuple-element.505.refs_2_), channel_id=1, source_target_pairs={{0,1},{1,0},{2,3},{3,2},{4,5},{5,4},{6,7},{7,6},{8,9},{9,8},{10,11... | collective-permute-start | bytes 4718600 | tf_op jit(solution)/shard_map/ppermute | solution.py:1067
  737.1 30.5 %collective-permute-start.63 = (bf16[384,1792]{1,0:T(8,128)(2,1)}, bf16[384,1792]{1,0:T(8,128)(2,1)}, u32[]{:S(2)}, u32[]{:S(2)}) collective-permute-start(bf16[384,1792]{1,0:T(8,128)(2,1)} %add_rows.21), channel_id=1, source_target_pairs={{0,2},{6,4},{1,3},{7,5},{8,10},{14,12},{9,11},{15,13},{16,18},{22,... | collective-permute-start | bytes 4128776 | tf_op jit(solution)/shard_map/ppermute | solution.py:948
  766.3 42.6 %collective-permute-start.72 = (bf16[192,4480]{1,0:T(8,128)(2,1)}, bf16[192,4480]{1,0:T(8,128)(2,1)S(1)}, u32[]{:S(2)}, u32[]{:S(2)}) collective-permute-start(bf16[192,4480]{1,0:T(8,128)(2,1)} %add.265), channel_id=1, source_target_pairs={{2,0},{4,6},{3,1},{5,7},{10,8},{12,14},{11,9},{13,15},{18,16},{20,... | collective-permute-start | bytes 5160968 | tf_op jit(solution)/shard_map/ppermute | solution.py:962
  769.7 19.6 %collective-permute-start.66 = (bf16[384,1792]{1,0:T(8,128)(2,1)S(1)}, bf16[384,1792]{1,0:T(8,128)(2,1)S(1)}, u32[]{:S(2)}, u32[]{:S(2)}) collective-permute-start(bf16[384,1792]{1,0:T(8,128)(2,1)S(1)} %add.259), channel_id=1, source_target_pairs={{2,4},{4,2},{3,5},{5,3},{10,12},{12,10},{11,13},{13,11},{18,20},{2... | collective-permute-start | bytes 4128776 | tf_op jit(solution)/shard_map/ppermute | solution.py:955
  780.3 67.9 %collective-permute-start.73 = (bf16[192,4480]{1,0:T(8,128)(2,1)}, bf16[192,4480]{1,0:T(8,128)(2,1)}, u32[]{:S(2)}, u32[]{:S(2)}) collective-permute-start(bf16[192,4480]{1,0:T(8,128)(2,1)} %add.266), channel_id=1, source_target_pairs={{2,0},{4,6},{3,1},{5,7},{10,8},{12,14},{11,9},{13,15},{18,16},{20,... | collective-permute-start | bytes 5160968 | tf_op jit(solution)/shard_map/ppermute | solution.py:962
  789.3 56.9 %collective-permute-start.68 = (f32[5312]{0:T(1024)S(1)}, f32[5312]{0:T(1024)S(1)}, u32[]{:S(2)}, u32[]{:S(2)}) collective-permute-start(f32[5312]{0:T(1024)S(1)} %add.261), channel_id=1, source_target_pairs={{2,0},{4,6},{3,1},{5,7},{10,8},{12,14},{11,9},{13,15},{18,16},{20,... | collective-permute-start | bytes 63752 | tf_op jit(solution)/shard_map/ppermute | solution.py:962
  809.4 60.0 %collective-permute-start.69 = (bf16[384,1792]{1,0:T(8,128)(2,1)S(1)}, bf16[384,1792]{1,0:T(8,128)(2,1)}, u32[]{:S(2)}, u32[]{:S(2)}) collective-permute-start(bf16[384,1792]{1,0:T(8,128)(2,1)S(1)} %add.262), channel_id=1, source_target_pairs={{2,0},{4,6},{3,1},{5,7},{10,8},{12,14},{11,9},{13,15},{18,16},{20,... | collective-permute-start | bytes 4128776 | tf_op jit(solution)/shard_map/ppermute | solution.py:962
  (121 other events, 1347.0 us)
Sparse Core Ops, SparseCore 0:
  100.6 67.4 all-gather.2
  264.4 150.2 reduce-scatter.1
  416.4 102.9 all-gather.4

commit v4 on v3

--- a/solution.py
+++ b/solution.py
@@ -1198,18 +1198,19 @@
     for k in range(contexts - 2, -1, -1):
         got = Box(lax.ppermute(d_kv_own.v, "ctx", leftward))
         if k == contexts - 2:
-            fence(got, output, gate_grad.arrived(1), gate_grad.own[0])
             gate_two = gate_grad.middle(0)
+            gate_own = gate_grad.arrived(1)
             gate_one = gate_grad.inward(1)
+            fence(mark(place), got, output, gate_two, gate_one)
         elif k == 0:
-            fence(mark(place), got, down_total, up_grad.arrived(0), gate_one, gate_two, up_last[1:])
+            fence(mark(place), got, down_total, up_grad.arrived(0), up_last[1:])
         else:
             fence(mark(place), got, up_last[:1])
         d_kv_own = Box(d_kv.v[k * rows : (k + 1) * rows] + got.v)
+    fence(place, d_kv_own, list(gate_grad.own.values()), gate_one, gate_two, list(up_grad.own.values()))
     gate_three = gate_grad.outward(0)
     gate_two = gate_grad.middle(1)
     up_one = up_grad.inward(0)
-    fence(place, d_kv_own, list(gate_grad.own.values()))
     d_mixed, bias_part, gain_one_part, *d_hidden_one = mix_back(
         place.v, d_query, d_kv_own.v, cosine, sine, tokens, qkv.all(), depth, bq
     )
@@ -1240,10 +1241,10 @@
     qkv_got = last_grad.cores()
     back.append(over_tp(d_hidden_one[1]))
     hop("shard", 1)
-    fence(mark(place), qkv_got, gate_two, up_one, vector)
+    fence(mark(place), qkv_got, gate_two, up_one, vector, gate_three)
     up_two = up_grad.middle(0)
     up_one = up_grad.inward(1)
-    gate_three += gate_grad.outward(1)
+    gate_three = gate_grad.outward(1)
     bit = 2
     while bit < shards:
         hop("shard", bit)
@@ -1251,7 +1252,7 @@
     fence(place, last_grad.sum_away(), vector)
     last_last = last_grad.chips()
     hop("tp", 1)
-    fence(mark(place), up_two, up_one, vector, last_last, back[1], d_hidden_one[2])
+    fence(mark(place), up_two, up_one, vector, last_last, back[1], d_hidden_one[2], gate_three)
     back.append(over_tp(d_hidden_one[2]))
     vectors = Reduction(shards, contexts, 1)
     vectors.own[0] = vector
@@ -1259,15 +1260,15 @@
     up_two = up_grad.middle(1)
     last_grad.arrived(0)
     last_one = last_grad.inward(0) + vectors.inward(0)
-    fence(mark(place), up_two, last_one, back[2], d_mid)
-    up_three += up_grad.outward(1)
+    fence(mark(place), up_two, last_one, back[2], d_mid, up_three)
+    up_three = up_grad.outward(1)
     last_two = last_grad.middle(0) + vectors.middle(0)
     input_grad = Box(
         input_back(
             place.v, [p.v for p in d_hidden_one], [p.v for p in back], tokens, gain_attn, d_mid.v, bq
         )
     )
-    fence(input_grad, last_two, place)
+    fence(input_grad, last_two, place, up_three)
     last_three = last_grad.outward(0) + vectors.outward(0)
     vector = Box(vectors.result())
     gate_total, up_total, last_total = (one.result() for one in (gate_grad, up_grad, last_grad))

time: 890 us -> 879 us (0.988)
  waiting for transfers between devices: 261 us -> 242 us
    ppermute x6, waiting for transfers between devices: 70.1 us -> 49.9 us  [outward(): lax.ppermute(self.own[slab].v, 'ctx', [(1, 0), (2, 3)])]
    ppermute x3, waiting for transfers between devices: 42.4 us -> 24.4 us  [layer(): got = Box(lax.ppermute(d_kv_own.v, 'ctx', leftward))]
    ppermute x6, waiting for transfers between devices: 64.2 us -> 75.8 us  [inward(): lax.ppermute(self.own[slab].v, 'ctx', [(0, 1), (3, 2)])]
    unnamed x220 -> x224, local copies, waits for them, and re-layouts: 65.6 us -> 72.1 us
  transfers between devices with their start and end apart: 77 -> 77, of which waited for: 27 -> 31; matrix products, arithmetic and copies ran while one was open for 11% -> 11% of each run, Pallas kernels for 36% -> 36%
where the time goes in v4:
time: 879 us; the launch traced here: 869 us
  Pallas kernels  323 us (37%)
  waiting for transfers between devices  242 us (28%)
  starting transfers between devices  108 us (12%)
  local copies, waits for them, and re-layouts  104 us (12%)
  other arithmetic  76.2 us (9%)
  between operations  15.4 us (2%)
    ppermute x6, waiting for transfers between devices, inward(): lax.ppermute(self.own[slab].v, 'ctx', [(0, 1), (3, 2)])  75.8 us
    unnamed x224, local copies, waits for them, and re-layouts  72.1 us
    pallas_call x1, Pallas kernels, gate_up_back(): call(functools.partial(gate_up_back_kernel, gates, ups, downs, units % tf...  62.3 us
    pallas_call x4, Pallas kernels, weight_grad(): call(functools.partial(weight_grad_kernel, width // parts, parts), pl.cdi...  51.7 us
    ppermute x6, waiting for transfers between devices, outward(): lax.ppermute(self.own[slab].v, 'ctx', [(1, 0), (2, 3)])  49.9 us
    pallas_call x1, Pallas kernels, gate_up(): call(functools.partial(gate_up_kernel, gates, ups), pl.cdiv(units, tf), [...  40.4 us
    ppermute x6, starting transfers between devices, inward(): lax.ppermute(self.own[slab].v, 'ctx', [(0, 1), (3, 2)])  39.3 us
    ppermute x12, waiting for transfers between devices, over_tp(): return Box(lax.ppermute(box.v, 'tp', across))  38.9 us
  transfers between devices with their start and end apart: 77, of which 31 were waited for; matrix products, arithmetic and copies ran while one was open for 11% of the time, Pallas kernels for 36%

profile of v4, /device:TPU:0, one launch (start us, length us, event | category | flops | bytes accessed | tf_op | source)
XLA Modules:
  0.0 869.1 jit_solution(977340968451159723)
XLA Ops:
  23.1 3.1 fusion
  37.1 8.5 mix.1
  48.3 3.5 collective-permute-start.5
  55.9 7.5 collective-permute-done.5
  67.3 5.1 collective-permute-start.8
  73.6 8.2 collective-permute-done.8
  81.8 5.3 collective-permute-start.11
  87.1 4.6 copy.37
  95.9 4.6 collective-permute-done.12.refs_2_
  108.9 4.4 attention_forward.2
  113.3 4.2 collective-permute-done.13.refs_6_
  118.4 10.5 %collective-permute-done.14.refs_7_ = bf16[384,768]{1,0:T(8,128)(2,1)S(1)} collective-permute-done((bf16[384,768]{1,0:T(8,128)(2,1)S(1)}, bf16[384,768]{1,0:T(8,128)(2,1)S(1)}, u32[]{:S(2)}, u32[]{:S(2)}) %collective-permute-start.14) | collective-permute-done | bytes 589856 | tf_op jit(solution)/shard_map/ppermute | solution.py:1067
  134.0 9.7 %attention_forward.3 = (bf16[512,768]{1,0:T(8,128)(2,1)}, f32[6,512]{1,0:T(8,128)S(1)}, f32[6,512]{1,0:T(8,128)S(1)}) custom-call(s32[4]{0:T(128)S(1)} %get-tuple-element.333.count, s32[128]{0:T(128)S(1)} %reshape.678.chosen, s32[33]{0:T(128)S(1)} %pad_add_fusion.9.places, bf16[1024,768]{1,0:T(8,128)(2,1)S(1)} %copy-done.88, ...), custom_call_target="tpu_custom_call" | custom-call | flops 2624999936 | bytes 1000 | tf_op jit(solution)/shard_map/attention_forward/pallas_call | solution.py:94
  143.7 4.4 collective-permute-done.16.upper_ref
  152.4 8.3 collective-permute-done.18.refs_4_
  160.7 8.5 collective-permute-done.17.lower_ref
  179.3 11.1 %branch.1 = (f32[1024,1536]{1,0:T(8,128)}, bf16[1024,1536]{1,0:T(8,128)(2,1)S(1)}, bf16[1536,1024]{1,0:T(8,128)(2,1)S(1)}) custom-call(s32[2]{0:T(128)S(1)} %copy-done.83, bf16[1024,1536]{1,0:T(8,128)(2,1)} %x_ref.7, bf16[1024,768]{1,0:T(8,128)(2,1)S(1)} %pad_maximum_fusion.own_ref.att_ref.right_ref, bf16[512,768]{1,0:T(8,128)(2,1)S(1)} %copy-done.66, ...), custom_call_target="tpu_custom_call" | custom-call | flops 2100000000 | bytes 1000 | tf_op jit(solution)/shard_map/branch/pallas_call | solution.py:605
  194.6 3.4 slice.68
  202.3 40.4 %gate_up.1 = (bf16[1024,4480]{1,0:T(8,128)(2,1)}, bf16[1024,4480]{1,0:T(8,128)(2,1)}, bf16[1024,4480]{1,0:T(8,128)(2,1)}) custom-call(s32[2]{0:T(128)} %mark.16.place.place_ref, bf16[1024,1536]{1,0:T(8,128)(2,1)} %copy-done.38, bf16[384,4480]{1,0:T(8,128)(2,1)} %refs_0_.9, bf16[384,4480]{1,0:T(8,128)(2,1)} %copy-done.92, ...), custom_call_target="tpu_custom_call" | custom-call | flops 7000000000 | bytes 1000 | tf_op jit(solution)/shard_map/gate_up/pallas_call | solution.py:312
  246.0 18.7 %whole_grad.1 = bf16[1536,4480]{1,0:T(8,128)(2,1)} custom-call(bf16[1536,1024]{1,0:T(8,128)(2,1)S(1)} %bitcast.30, bf16[1024,4480]{1,0:T(8,128)(2,1)} %get-tuple-element.421.right_ref.act_ref), custom_call_target="tpu_custom_call" | custom-call | flops 3324999936 | bytes 1000 | tf_op jit(solution)/shard_map/whole_grad/pallas_call | solution.py:392
  269.2 62.3 %gate_up_back.1 = (bf16[1024,4480]{1,0:T(8,128)(2,1)}, bf16[1024,4480]{1,0:T(8,128)(2,1)}, bf16[1024,384]{1,0:T(8,128)(2,1)}, bf16[1024,384]{1,0:T(8,128)(2,1)}, bf16[1024,768]{1,0:T(8,128)(2,1)}) custom-call(s32[2]{0:T(128)} %mark.17.place.place_ref, bf16[1024,1536]{1,0:T(8,128)(2,1)} %c_ref.3, bf16[1024,4480]{1,0:T(8,128)(2,1)} %get-tuple-element.395.by_gate_ref, ...), custom_call_target="tpu_custom_call" | custom-call | flops 10849999872 | bytes 1000 | tf_op jit(solution)/shard_map/gate_up_back/pallas_call | solution.py:368
  332.3 19.1 %weight_grad.4 = (bf16[768,4480]{1,0:T(8,128)(2,1)}, bf16[768,4480]{1,0:T(8,128)(2,1)}) custom-call(s32[2]{0:T(128)S(1)} %copy-done.82, bf16[1536,1024]{1,0:T(8,128)(2,1)S(1)} %copy-done.18, bf16[1024,4480]{1,0:T(8,128)(2,1)} %get-tuple-element.407.right_ref), custom_call_target="tpu_custom_call" | custom-call | flops 3324999936 | bytes 1000 | tf_op jit(solution)/shard_map/weight_grad/pallas_call | solution.py:415
  353.0 19.4 %weight_grad.5 = (bf16[768,4480]{1,0:T(8,128)(2,1)}, bf16[768,4480]{1,0:T(8,128)(2,1)}) custom-call(s32[2]{0:T(128)S(1)} %copy-done.82, bf16[1536,1024]{1,0:T(8,128)(2,1)S(1)} %copy-done.18, bf16[1024,4480]{1,0:T(8,128)(2,1)} %get-tuple-element.413.right_ref), custom_call_target="tpu_custom_call" | custom-call | flops 3324999936 | bytes 1000 | tf_op jit(solution)/shard_map/weight_grad/pallas_call | solution.py:415
  386.4 23.7 %down_project.1 = bf16[1024,1536]{1,0:T(8,128)(2,1)} custom-call(s32[2]{0:T(128)S(1)} %copy-done.82, bf16[1024,4480]{1,0:T(8,128)(2,1)} %get-tuple-element.421.right_ref.act_ref, bf16[384,4480]{1,0:T(8,128)(2,1)} %refs_0_.10, bf16[384,4480]{1,0:T(8,128)(2,1)} %collective-permute-done.28.refs_13_.refs_1_, bf16[96,4480]{1,0:T(8,128)(2,1)S(1)} %copy-done.37, ...), custom_call_target="tpu_custom_call" | custom-call | flops 4200000000 | bytes 1000 | tf_op jit(solution)/shard_map/down_project/pallas_call | solution.py:493
  410.1 3.1 collective-permute-done.38.refs_5_
  428.4 13.7 %middle_back.1 = (f32[1024,1536]{1,0:T(8,128)}, bf16[1536,1024]{1,0:T(8,128)(2,1)}, bf16[1024,768]{1,0:T(8,128)(2,1)}, f32[6,1024]{1,0:T(8,128)S(1)}, f32[1,1536]{1,0:T(1,128)S(1)}) custom-call(s32[2]{0:T(128)S(1)} %copy-done.82, f32[1024,1536]{1,0:T(8,128)} %get-tuple-element.454.mid_ref, bf16[1024,1536]{1,0:T(8,128)(2,1)} %c_ref.3, ...), custom_call_target="tpu_custom_call" | custom-call | flops 2275000064 | bytes 1000 | tf_op jit(solution)/shard_map/middle_back/pallas_call | solution.py:667
  442.1 6.1 weight_grad.6
  448.2 3.4 copy-done.9
  451.6 3.4 add_rows.15
  455.1 7.5 collective-permute-start.40
  464.1 19.2 %attention_backward.1 = (bf16[1024,768]{1,0:T(8,128)(2,1)S(1)}, bf16[4096,256]{1,0:T(8,128)(2,1)}) custom-call(s32[4]{0:T(128)S(1)} %get-tuple-element.439.count, s32[32]{0:T(128)S(1)} %reshape.679.chosen, s32[9]{0:T(128)S(1)} %pad_add_fusion.10.places, bf16[1024,768]{1,0:T(8,128)(2,1)S(1)} %copy-done.89, bf16[1024,768]{1,0:T(8,128)(2,1)S(1)} %copy-done.90, ...), custom_call_target="tpu_custom_call" | custom-call | flops 9450000384 | bytes 1000 | tf_op jit(solution)/shard_map/attention_backward/pallas_call | solution.py:186
  485.5 41.5 %collective-permute-done.40 = bf16[192,4480]{1,0:T(8,128)(2,1)} collective-permute-done((bf16[192,4480]{1,0:T(8,128)(2,1)S(1)}, bf16[192,4480]{1,0:T(8,128)(2,1)}, u32[]{:S(2)}, u32[]{:S(2)}) %collective-permute-start.40) | collective-permute-done | bytes 1720352 | tf_op jit(solution)/shard_map/ppermute | solution.py:948
  527.0 3.2 add.247
  537.7 8.5 collective-permute-start.46
  551.4 6.7 add_convert_fusion
  559.3 5.1 collective-permute-done.44
  564.5 16.8 %collective-permute-done.46 = bf16[192,4480]{1,0:T(8,128)(2,1)} collective-permute-done((bf16[192,4480]{1,0:T(8,128)(2,1)S(1)}, bf16[192,4480]{1,0:T(8,128)(2,1)}, u32[]{:S(2)}, u32[]{:S(2)}) %collective-permute-start.46) | collective-permute-done | bytes 1720352 | tf_op jit(solution)/shard_map/ppermute | solution.py:948
  587.1 18.8 %collective-permute-done.47 = bf16[1024,256]{1,0:T(8,128)(2,1)S(1)} collective-permute-done((bf16[1024,256]{1,0:T(8,128)(2,1)S(1)}, bf16[1024,256]{1,0:T(8,128)(2,1)S(1)}, u32[]{:S(2)}, u32[]{:S(2)}) %collective-permute-start.47) | collective-permute-done | bytes 524320 | tf_op jit(solution)/shard_map/ppermute | solution.py:1199
  616.0 4.1 add_rows.17
  628.9 7.8 mix_back.1
  641.6 3.9 add.254
  646.8 3.1 add.252
  651.7 10.5 %collective-permute-start.54 = (bf16[192,4480]{1,0:T(8,128)(2,1)}, bf16[192,4480]{1,0:T(8,128)(2,1)}, u32[]{:S(2)}, u32[]{:S(2)}) collective-permute-start(bf16[192,4480]{1,0:T(8,128)(2,1)} %add_rows.17), channel_id=1, source_target_pairs={{0,2},{6,4},{1,3},{7,5},{8,10},{14,12},{9,11},{15,13},{16,18},{22,... | collective-permute-start | bytes 5160968 | tf_op jit(solution)/shard_map/ppermute | solution.py:948
  670.5 7.1 weight_grad.7
  685.3 14.0 %collective-permute-done.54 = bf16[192,4480]{1,0:T(8,128)(2,1)} collective-permute-done((bf16[192,4480]{1,0:T(8,128)(2,1)}, bf16[192,4480]{1,0:T(8,128)(2,1)}, u32[]{:S(2)}, u32[]{:S(2)}) %collective-permute-start.54) | collective-permute-done | bytes 1720352 | tf_op jit(solution)/shard_map/ppermute | solution.py:948
  699.3 3.6 add.258
  702.8 3.7 add.256
  711.3 4.4 add_rows.19
  716.8 3.7 collective-permute-done.60
  721.0 5.5 convert_element_type.69
  732.8 7.0 collective-permute-done.61.refs_1_
  742.2 3.6 add.260
  745.8 3.1 add.259
  749.0 3.3 add_rows.21
  752.3 4.5 collective-permute-start.65
  763.3 5.7 collective-permute-start.66
  773.1 3.6 collective-permute-done.66
  776.6 7.1 collective-permute-done.67.refs_5_
  783.8 10.6 %collective-permute-done.68 = bf16[192,4480]{1,0:T(8,128)(2,1)} collective-permute-done((bf16[192,4480]{1,0:T(8,128)(2,1)}, bf16[192,4480]{1,0:T(8,128)(2,1)}, u32[]{:S(2)}, u32[]{:S(2)}) %collective-permute-start.68) | collective-permute-done | bytes 1720352 | tf_op jit(solution)/shard_map/ppermute | solution.py:962
  798.4 3.3 maximum_convert_fusion
  806.9 7.7 input_back.1
  814.5 19.9 %collective-permute-done.71 = bf16[192,4480]{1,0:T(8,128)(2,1)S(1)} collective-permute-done((bf16[192,4480]{1,0:T(8,128)(2,1)S(1)}, bf16[192,4480]{1,0:T(8,128)(2,1)S(1)}, u32[]{:S(2)}, u32[]{:S(2)}) %collective-permute-start.71) | collective-permute-done | bytes 1720352 | tf_op jit(solution)/shard_map/ppermute | solution.py:962
  837.6 3.3 maximum_convert_fusion.1
  840.9 16.9 %collective-permute-done.72 = f32[5312]{0:T(1024)S(1)} collective-permute-done((f32[5312]{0:T(1024)S(1)}, f32[5312]{0:T(1024)S(1)}, u32[]{:S(2)}, u32[]{:S(2)}) %collective-permute-start.72) | collective-permute-done | bytes 21280 | tf_op jit(solution)/shard_map/ppermute | solution.py:962
  (484 shorter events, 227.1 us)
Async XLA Ops:
  7.2 162.8 %all-gather.3.cloned.1.call-start = ((), (), s32[]{:S(2)}) async-start(), calls=%async_computation.1 | async-start | bytes 4300800 | tf_op jit(solution)/shard_map/all_gather | solution.py:849
  7.2 21.3 %collective-permute-start = (bf16[384,1024]{1,0:T(8,128)(2,1)}, bf16[384,1024]{1,0:T(8,128)(2,1)}, u32[]{:S(2)}, u32[]{:S(2)}) collective-permute-start(bf16[384,1024]{1,0:T(8,128)(2,1)} %refs_0_.11), channel_id=1, source_target_pairs={{0,16},{8,24},{16,0},{24,8},{1,17},{9,25},{17,1},{25,9},{2,18},{10... | collective-permute-start | bytes 2359304 | tf_op jit(solution)/shard_map/ppermute | solution.py:813
  29.0 19.3 %collective-permute-start.3 = (bf16[384,768]{1,0:T(8,128)(2,1)}, bf16[384,768]{1,0:T(8,128)(2,1)}, u32[]{:S(2)}, u32[]{:S(2)}) collective-permute-start(bf16[384,768]{1,0:T(8,128)(2,1)} %refs_6_.1), channel_id=1, source_target_pairs={{0,8},{8,0},{16,24},{24,16},{1,9},{9,1},{17,25},{25,17},{2,10},{10... | collective-permute-start | bytes 1769480 | tf_op jit(solution)/shard_map/ppermute | solution.py:813
  29.1 22.8 %collective-permute-start.4 = (bf16[384,768]{1,0:T(8,128)(2,1)}, bf16[384,768]{1,0:T(8,128)(2,1)}, u32[]{:S(2)}, u32[]{:S(2)}) collective-permute-start(bf16[384,768]{1,0:T(8,128)(2,1)} %refs_6_.1), channel_id=1, source_target_pairs={{0,16},{8,24},{16,0},{24,8},{1,17},{9,25},{17,1},{25,9},{2,18},{10... | collective-permute-start | bytes 1769480 | tf_op jit(solution)/shard_map/ppermute | solution.py:813
  30.4 25.5 %collective-permute-start.7 = (bf16[384,768]{1,0:T(8,128)(2,1)}, bf16[384,768]{1,0:T(8,128)(2,1)}, u32[]{:S(2)}, u32[]{:S(2)}) collective-permute-start(bf16[384,768]{1,0:T(8,128)(2,1)} %refs_6_.1), channel_id=1, source_target_pairs={{0,1},{1,0},{2,3},{3,2},{4,5},{5,4},{6,7},{7,6},{8,9},{9,8},{10,11... | collective-permute-start | bytes 1769480 | tf_op jit(solution)/shard_map/ppermute | solution.py:1077
  48.3 15.1 %collective-permute-start.5 = (bf16[1024,256]{1,0:T(8,128)(2,1)}, bf16[1024,256]{1,0:T(8,128)(2,1)S(1)}, u32[]{:S(2)}, u32[]{:S(2)}) collective-permute-start(bf16[1024,256]{1,0:T(8,128)(2,1)} %get-tuple-element.322), channel_id=1, source_target_pairs={{0,2},{2,4},{4,6},{1,3},{3,5},{5,7},{8,10},{10,12},{12,14},{9,11},... | collective-permute-start | bytes 1572872 | tf_op jit(solution)/shard_map/ppermute | solution.py:1089
  54.0 27.8 %collective-permute-start.10 = (bf16[96,4480]{1,0:T(8,128)(2,1)}, bf16[96,4480]{1,0:T(8,128)(2,1)}, u32[]{:S(2)}, u32[]{:S(2)}) collective-permute-start(bf16[96,4480]{1,0:T(8,128)(2,1)} %constant_dynamic-slice_fusion.1), channel_id=1, source_target_pairs={{0,16},{8,24},{16,0},{24,8},{1,17},{9,25},{17,1},{25,9},{2,18},{10... | collective-permute-start | bytes 2580488 | tf_op jit(solution)/shard_map/ppermute | solution.py:813
  65.1 35.3 %collective-permute-start.12 = (bf16[128,4480]{1,0:T(8,128)(2,1)S(1)}, bf16[128,4480]{1,0:T(8,128)(2,1)}, u32[]{:S(2)}, u32[]{:S(2)}) collective-permute-start(bf16[128,4480]{1,0:T(8,128)(2,1)S(1)} %slice.63), channel_id=1, source_target_pairs={{0,16},{8,24},{16,0},{24,8},{1,17},{9,25},{17,1},{25,9},{2,18},{10... | collective-permute-start | bytes 3440648 | tf_op jit(solution)/shard_map/ppermute | solution.py:813
  65.9 15.9 %collective-permute-start.9 = (bf16[384,768]{1,0:T(8,128)(2,1)}, bf16[384,768]{1,0:T(8,128)(2,1)S(1)}, u32[]{:S(2)}, u32[]{:S(2)}) collective-permute-start(bf16[384,768]{1,0:T(8,128)(2,1)} %collective-permute-done.3.refs_1_.refs_7_), channel_id=1, source_target_pairs={{0,1},{1,0},{2,3},{3,2},{4,5},{5,4},{6,7},{7,6},{8,9},{9,8},{10,11... | collective-permute-start | bytes 1769480 | tf_op jit(solution)/shard_map/ppermute | solution.py:1067
  67.3 14.5 %collective-permute-start.8 = (bf16[1024,256]{1,0:T(8,128)(2,1)S(1)}, bf16[1024,256]{1,0:T(8,128)(2,1)}, u32[]{:S(2)}, u32[]{:S(2)}) collective-permute-start(bf16[1024,256]{1,0:T(8,128)(2,1)S(1)} %collective-permute-done.5), channel_id=1, source_target_pairs={{0,2},{2,4},{4,6},{1,3},{3,5},{5,7},{8,10},{10,12},{12,14},{9,11},... | collective-permute-start | bytes 1572872 | tf_op jit(solution)/shard_map/ppermute | solution.py:1089
  100.5 315.6 %reduce-scatter.2.cloned.1.call-start = ((), (), s32[]{:S(2)}) async-start(), calls=%async_computation.2 | async-start | bytes 14622720 | tf_op jit(solution)/shard_map/reduce_scatter | solution.py:1146
  101.0 16.5 %collective-permute-start.13 = (bf16[384,768]{1,0:T(8,128)(2,1)}, bf16[384,768]{1,0:T(8,128)(2,1)S(1)}, u32[]{:S(2)}, u32[]{:S(2)}) collective-permute-start(bf16[384,768]{1,0:T(8,128)(2,1)} %collective-permute-done.4.refs_2_.refs_8_), channel_id=1, source_target_pairs={{0,1},{1,0},{2,3},{3,2},{4,5},{5,4},{6,7},{7,6},{8,9},{9,8},{10,11... | collective-permute-start | bytes 1769480 | tf_op jit(solution)/shard_map/ppermute | solution.py:1067
  101.7 27.2 %collective-permute-start.14 = (bf16[384,768]{1,0:T(8,128)(2,1)S(1)}, bf16[384,768]{1,0:T(8,128)(2,1)S(1)}, u32[]{:S(2)}, u32[]{:S(2)}) collective-permute-start(bf16[384,768]{1,0:T(8,128)(2,1)S(1)} %collective-permute-done.6.refs_3_.refs_9_), channel_id=1, source_target_pairs={{0,1},{1,0},{2,3},{3,2},{4,5},{5,4},{6,7},{7,6},{8,9},{9,8},{10,11... | collective-permute-start | bytes 1769480 | tf_op jit(solution)/shard_map/ppermute | solution.py:1067
  104.5 44.5 %collective-permute-start.15 = (bf16[128,4480]{1,0:T(8,128)(2,1)S(1)}, bf16[128,4480]{1,0:T(8,128)(2,1)}, u32[]{:S(2)}, u32[]{:S(2)}) collective-permute-start(bf16[128,4480]{1,0:T(8,128)(2,1)S(1)} %slice.64), channel_id=1, source_target_pairs={{0,16},{8,24},{16,0},{24,8},{1,17},{9,25},{17,1},{25,9},{2,18},{10... | collective-permute-start | bytes 3440648 | tf_op jit(solution)/shard_map/ppermute | solution.py:813
  129.7 18.4 %collective-permute-start.16 = (bf16[512,768]{1,0:T(8,128)(2,1)S(1)}, bf16[512,768]{1,0:T(8,128)(2,1)S(1)}, u32[]{:S(2)}, u32[]{:S(2)}) collective-permute-start(bf16[512,768]{1,0:T(8,128)(2,1)S(1)} %get-tuple-element.347), channel_id=1, source_target_pairs={{0,1},{1,0},{2,3},{3,2},{4,5},{5,4},{6,7},{7,6},{8,9},{9,8},{10,11... | collective-permute-start | bytes 2359304 | tf_op jit(solution)/shard_map/ppermute | solution.py:1067
  130.3 22.0 %collective-permute-start.19 = (bf16[128,4480]{1,0:T(8,128)(2,1)}, bf16[128,4480]{1,0:T(8,128)(2,1)}, u32[]{:S(2)}, u32[]{:S(2)}) collective-permute-start(bf16[128,4480]{1,0:T(8,128)(2,1)} %collective-permute-done.12.refs_2_), channel_id=1, source_target_pairs={{0,8},{8,0},{16,24},{24,16},{1,9},{9,1},{17,25},{25,17},{2,10},{10... | collective-permute-start | bytes 3440648 | tf_op jit(solution)/shard_map/ppermute | solution.py:813
  132.7 28.0 %collective-permute-start.18 = (bf16[128,4480]{1,0:T(8,128)(2,1)}, bf16[128,4480]{1,0:T(8,128)(2,1)}, u32[]{:S(2)}, u32[]{:S(2)}) collective-permute-start(bf16[128,4480]{1,0:T(8,128)(2,1)} %slice.65), channel_id=1, source_target_pairs={{0,16},{8,24},{16,0},{24,8},{1,17},{9,25},{17,1},{25,9},{2,18},{10... | collective-permute-start | bytes 3440648 | tf_op jit(solution)/shard_map/ppermute | solution.py:813
  149.0 21.1 %collective-permute-start.20 = (bf16[128,4480]{1,0:T(8,128)(2,1)}, bf16[128,4480]{1,0:T(8,128)(2,1)}, u32[]{:S(2)}, u32[]{:S(2)}) collective-permute-start(bf16[128,4480]{1,0:T(8,128)(2,1)} %collective-permute-done.15.refs_3_), channel_id=1, source_target_pairs={{0,8},{8,0},{16,24},{24,16},{1,9},{9,1},{17,25},{25,17},{2,10},{10... | collective-permute-start | bytes 3440648 | tf_op jit(solution)/shard_map/ppermute | solution.py:813
  149.0 20.2 %collective-permute-start.17 = (bf16[512,768]{1,0:T(8,128)(2,1)}, bf16[512,768]{1,0:T(8,128)(2,1)S(1)}, u32[]{:S(2)}, u32[]{:S(2)}) collective-permute-start(bf16[512,768]{1,0:T(8,128)(2,1)} %get-tuple-element.348), channel_id=1, source_target_pairs={{0,1},{1,0},{2,3},{3,2},{4,5},{5,4},{6,7},{7,6},{8,9},{9,8},{10,11... | collective-permute-start | bytes 2359304 | tf_op jit(solution)/shard_map/ppermute | solution.py:1067
  170.0 24.5 %collective-permute-start.24 = (bf16[384,4480]{1,0:T(8,128)(2,1)}, bf16[384,4480]{1,0:T(8,128)(2,1)S(1)}, u32[]{:S(2)}, u32[]{:S(2)}) collective-permute-start(bf16[384,4480]{1,0:T(8,128)(2,1)} %refs_8_.3), channel_id=1, source_target_pairs={{0,8},{8,0},{16,24},{24,16},{1,9},{9,1},{17,25},{25,17},{2,10},{10... | collective-permute-start | bytes 10321928 | tf_op jit(solution)/shard_map/ppermute | solution.py:813
  170.0 24.5 %collective-permute-start.23 = (bf16[384,4480]{1,0:T(8,128)(2,1)}, bf16[384,4480]{1,0:T(8,128)(2,1)S(1)}, u32[]{:S(2)}, u32[]{:S(2)}) collective-permute-start(bf16[384,4480]{1,0:T(8,128)(2,1)} %refs_0_.9), channel_id=1, source_target_pairs={{0,8},{8,0},{16,24},{24,16},{1,9},{9,1},{17,25},{25,17},{2,10},{10... | collective-permute-start | bytes 10321928 | tf_op jit(solution)/shard_map/ppermute | solution.py:813
  170.5 24.0 %collective-permute-start.22 = (bf16[384,4480]{1,0:T(8,128)(2,1)}, bf16[384,4480]{1,0:T(8,128)(2,1)}, u32[]{:S(2)}, u32[]{:S(2)}) collective-permute-start(bf16[384,4480]{1,0:T(8,128)(2,1)} %all-gather.3.cloned.1.call-done.refs_10_), channel_id=1, source_target_pairs={{0,8},{8,0},{16,24},{24,16},{1,9},{9,1},{17,25},{25,17},{2,10},{10... | collective-permute-start | bytes 10321928 | tf_op jit(solution)/shard_map/ppermute | solution.py:813
  170.6 23.9 %collective-permute-start.21 = (bf16[128,4480]{1,0:T(8,128)(2,1)}, bf16[128,4480]{1,0:T(8,128)(2,1)S(1)}, u32[]{:S(2)}, u32[]{:S(2)}) collective-permute-start(bf16[128,4480]{1,0:T(8,128)(2,1)} %collective-permute-done.18.refs_4_), channel_id=1, source_target_pairs={{0,8},{8,0},{16,24},{24,16},{1,9},{9,1},{17,25},{25,17},{2,10},{10... | collective-permute-start | bytes 3440648 | tf_op jit(solution)/shard_map/ppermute | solution.py:813
  173.2 21.3 %collective-permute-start.25 = (bf16[96,4480]{1,0:T(8,128)(2,1)}, bf16[96,4480]{1,0:T(8,128)(2,1)S(1)}, u32[]{:S(2)}, u32[]{:S(2)}) collective-permute-start(bf16[96,4480]{1,0:T(8,128)(2,1)} %slice.66), channel_id=1, source_target_pairs={{0,16},{8,24},{16,0},{24,8},{1,17},{9,25},{17,1},{25,9},{2,18},{10... | collective-permute-start | bytes 2580488 | tf_op jit(solution)/shard_map/ppermute | solution.py:813
  194.5 48.1 %collective-permute-start.28 = (bf16[384,4480]{1,0:T(8,128)(2,1)}, bf16[384,4480]{1,0:T(8,128)(2,1)}, u32[]{:S(2)}, u32[]{:S(2)}) collective-permute-start(bf16[384,4480]{1,0:T(8,128)(2,1)} %refs_0_.10), channel_id=1, source_target_pairs={{0,8},{8,0},{16,24},{24,16},{1,9},{9,1},{17,25},{25,17},{2,10},{10... | collective-permute-start | bytes 10321928 | tf_op jit(solution)/shard_map/ppermute | solution.py:813
  200.2 42.4 %collective-permute-start.26 = (bf16[96,4480]{1,0:T(8,128)(2,1)}, bf16[96,4480]{1,0:T(8,128)(2,1)}, u32[]{:S(2)}, u32[]{:S(2)}) collective-permute-start(bf16[96,4480]{1,0:T(8,128)(2,1)} %slice.67), channel_id=1, source_target_pairs={{0,16},{8,24},{16,0},{24,8},{1,17},{9,25},{17,1},{25,9},{2,18},{10... | collective-permute-start | bytes 2580488 | tf_op jit(solution)/shard_map/ppermute | solution.py:813
  200.9 41.7 %collective-permute-start.27 = (bf16[96,4480]{1,0:T(8,128)(2,1)}, bf16[96,4480]{1,0:T(8,128)(2,1)}, u32[]{:S(2)}, u32[]{:S(2)}) collective-permute-start(bf16[96,4480]{1,0:T(8,128)(2,1)} %slice.68), channel_id=1, source_target_pairs={{0,16},{8,24},{16,0},{24,8},{1,17},{9,25},{17,1},{25,9},{2,18},{10... | collective-permute-start | bytes 2580488 | tf_op jit(solution)/shard_map/ppermute | solution.py:813
  244.8 20.6 %collective-permute-start.32 = (bf16[96,4480]{1,0:T(8,128)(2,1)}, bf16[96,4480]{1,0:T(8,128)(2,1)}, u32[]{:S(2)}, u32[]{:S(2)}) collective-permute-start(bf16[96,4480]{1,0:T(8,128)(2,1)} %slice.69), channel_id=1, source_target_pairs={{0,16},{8,24},{16,0},{24,8},{1,17},{9,25},{17,1},{25,9},{2,18},{10... | collective-permute-start | bytes 2580488 | tf_op jit(solution)/shard_map/ppermute | solution.py:813
  245.5 19.9 %collective-permute-start.29 = (bf16[96,4480]{1,0:T(8,128)(2,1)S(1)}, bf16[96,4480]{1,0:T(8,128)(2,1)}, u32[]{:S(2)}, u32[]{:S(2)}) collective-permute-start(bf16[96,4480]{1,0:T(8,128)(2,1)S(1)} %collective-permute-done.25.refs_14_.refs_2_), channel_id=1, source_target_pairs={{0,8},{8,0},{16,24},{24,16},{1,9},{9,1},{17,25},{25,17},{2,10},{10... | collective-permute-start | bytes 2580488 | tf_op jit(solution)/shard_map/ppermute | solution.py:813
  245.5 19.9 %collective-permute-start.30 = (bf16[96,4480]{1,0:T(8,128)(2,1)}, bf16[96,4480]{1,0:T(8,128)(2,1)}, u32[]{:S(2)}, u32[]{:S(2)}) collective-permute-start(bf16[96,4480]{1,0:T(8,128)(2,1)} %collective-permute-done.26.refs_15_.refs_3_), channel_id=1, source_target_pairs={{0,8},{8,0},{16,24},{24,16},{1,9},{9,1},{17,25},{25,17},{2,10},{10... | collective-permute-start | bytes 2580488 | tf_op jit(solution)/shard_map/ppermute | solution.py:813
  246.0 19.4 %collective-permute-start.31 = (bf16[96,4480]{1,0:T(8,128)(2,1)}, bf16[96,4480]{1,0:T(8,128)(2,1)}, u32[]{:S(2)}, u32[]{:S(2)}) collective-permute-start(bf16[96,4480]{1,0:T(8,128)(2,1)} %collective-permute-done.27.refs_16_.refs_4_), channel_id=1, source_target_pairs={{0,8},{8,0},{16,24},{24,16},{1,9},{9,1},{17,25},{25,17},{2,10},{10... | collective-permute-start | bytes 2580488 | tf_op jit(solution)/shard_map/ppermute | solution.py:813
  265.4 356.4 %all-gather.5.cloned.1.call-start = ((), (), s32[]{:S(2)}) async-start(), calls=%async_computation.3 | async-start | bytes 4300800 | tf_op jit(solution)/shard_map/all_gather | solution.py:1171
  331.6 19.9 %collective-permute-start.34 = (bf16[1024,384]{1,0:T(8,128)(2,1)}, bf16[1024,384]{1,0:T(8,128)(2,1)S(1)}, u32[]{:S(2)}, u32[]{:S(2)}) collective-permute-start(bf16[1024,384]{1,0:T(8,128)(2,1)} %get-tuple-element.410.refs_0_), channel_id=1, source_target_pairs={{0,1},{1,0},{2,3},{3,2},{4,5},{5,4},{6,7},{7,6},{8,9},{9,8},{10,11... | collective-permute-start | bytes 2359304 | tf_op jit(solution)/shard_map/ppermute | solution.py:1067
  351.5 21.7 %collective-permute-start.35 = (bf16[768,4480]{1,0:T(8,128)(2,1)}, bf16[768,4480]{1,0:T(8,128)(2,1)S(1)}, u32[]{:S(2)}, u32[]{:S(2)}) collective-permute-start(bf16[768,4480]{1,0:T(8,128)(2,1)} %get-tuple-element.415), channel_id=1, source_target_pairs={{0,8},{8,0},{16,24},{24,16},{1,9},{9,1},{17,25},{25,17},{2,10},{10... | collective-permute-start | bytes 20643848 | tf_op jit(solution)/shard_map/ppermute | solution.py:813
  351.6 20.7 %collective-permute-start.36 = (bf16[1024,384]{1,0:T(8,128)(2,1)S(1)}, bf16[1024,384]{1,0:T(8,128)(2,1)S(1)}, u32[]{:S(2)}, u32[]{:S(2)}) collective-permute-start(bf16[1024,384]{1,0:T(8,128)(2,1)S(1)} %copy-done.60), channel_id=1, source_target_pairs={{0,1},{1,0},{2,3},{3,2},{4,5},{5,4},{6,7},{7,6},{8,9},{9,8},{10,11... | collective-permute-start | bytes 2359304 | tf_op jit(solution)/shard_map/ppermute | solution.py:1067
  376.1 37.1 %collective-permute-start.37 = (bf16[768,4480]{1,0:T(8,128)(2,1)}, bf16[768,4480]{1,0:T(8,128)(2,1)S(1)}, u32[]{:S(2)}, u32[]{:S(2)}) collective-permute-start(bf16[768,4480]{1,0:T(8,128)(2,1)} %get-tuple-element.422), channel_id=1, source_target_pairs={{0,8},{8,0},{16,24},{24,16},{1,9},{9,1},{17,25},{25,17},{2,10},{10... | collective-permute-start | bytes 20643848 | tf_op jit(solution)/shard_map/ppermute | solution.py:813
  376.2 37.1 %collective-permute-start.38 = (bf16[1024,768]{1,0:T(8,128)(2,1)}, bf16[1024,768]{1,0:T(8,128)(2,1)}, u32[]{:S(2)}, u32[]{:S(2)}) collective-permute-start(bf16[1024,768]{1,0:T(8,128)(2,1)} %get-tuple-element.423.refs_2_), channel_id=1, source_target_pairs={{0,1},{1,0},{2,3},{3,2},{4,5},{5,4},{6,7},{7,6},{8,9},{9,8},{10,11... | collective-permute-start | bytes 4718600 | tf_op jit(solution)/shard_map/ppermute | solution.py:1067
  385.2 62.9 %collective-permute-start.39 = (bf16[192,4480]{1,0:T(8,128)(2,1)}, bf16[192,4480]{1,0:T(8,128)(2,1)}, u32[]{:S(2)}, u32[]{:S(2)}) collective-permute-start(bf16[192,4480]{1,0:T(8,128)(2,1)} %add_rows.11), channel_id=1, source_target_pairs={{0,16},{8,24},{16,0},{24,8},{1,17},{9,25},{17,1},{25,9},{2,18},{10... | collective-permute-start | bytes 5160968 | tf_op jit(solution)/shard_map/ppermute | solution.py:813
  416.1 110.9 %collective-permute-start.43 = (bf16[1024,1536]{1,0:T(8,128)(2,1)}, bf16[1024,1536]{1,0:T(8,128)(2,1)}, u32[]{:S(2)}, u32[]{:S(2)}) collective-permute-start(bf16[1024,1536]{1,0:T(8,128)(2,1)} %down_project.1), channel_id=1, source_target_pairs={{0,1},{1,0},{2,3},{3,2},{4,5},{5,4},{6,7},{7,6},{8,9},{9,8},{10,11... | collective-permute-start | bytes 9437192 | tf_op jit(solution)/shard_map/ppermute | solution.py:1067
  416.7 67.8 %collective-permute-start.41 = (bf16[192,4480]{1,0:T(8,128)(2,1)S(1)}, bf16[192,4480]{1,0:T(8,128)(2,1)}, u32[]{:S(2)}, u32[]{:S(2)}) collective-permute-start(bf16[192,4480]{1,0:T(8,128)(2,1)S(1)} %add_rows.12), channel_id=1, source_target_pairs={{0,16},{8,24},{16,0},{24,8},{1,17},{9,25},{17,1},{25,9},{2,18},{10... | collective-permute-start | bytes 5160968 | tf_op jit(solution)/shard_map/ppermute | solution.py:813
  455.1 71.9 %collective-permute-start.40 = (bf16[192,4480]{1,0:T(8,128)(2,1)S(1)}, bf16[192,4480]{1,0:T(8,128)(2,1)}, u32[]{:S(2)}, u32[]{:S(2)}) collective-permute-start(bf16[192,4480]{1,0:T(8,128)(2,1)S(1)} %add_rows.15), channel_id=1, source_target_pairs={{0,2},{6,4},{1,3},{7,5},{8,10},{14,12},{9,11},{15,13},{16,18},{22,... | collective-permute-start | bytes 5160968 | tf_op jit(solution)/shard_map/ppermute | solution.py:948
  462.6 21.9 %collective-permute-start.42 = (bf16[768,768]{1,0:T(8,128)(2,1)}, bf16[768,768]{1,0:T(8,128)(2,1)S(1)}, u32[]{:S(2)}, u32[]{:S(2)}) collective-permute-start(bf16[768,768]{1,0:T(8,128)(2,1)} %get-tuple-element.449), channel_id=1, source_target_pairs={{0,8},{8,0},{16,24},{24,16},{1,9},{9,1},{17,25},{25,17},{2,10},{10... | collective-permute-start | bytes 3538952 | tf_op jit(solution)/shard_map/ppermute | solution.py:813
  535.9 28.6 %collective-permute-start.45 = (bf16[192,4480]{1,0:T(8,128)(2,1)}, bf16[192,4480]{1,0:T(8,128)(2,1)}, u32[]{:S(2)}, u32[]{:S(2)}) collective-permute-start(bf16[192,4480]{1,0:T(8,128)(2,1)} %add.247), channel_id=1, source_target_pairs={{2,4},{4,2},{3,5},{5,3},{10,12},{12,10},{11,13},{13,11},{18,20},{2... | collective-permute-start | bytes 5160968 | tf_op jit(solution)/shard_map/ppermute | solution.py:955
  537.7 43.5 %collective-permute-start.46 = (bf16[192,4480]{1,0:T(8,128)(2,1)S(1)}, bf16[192,4480]{1,0:T(8,128)(2,1)}, u32[]{:S(2)}, u32[]{:S(2)}) collective-permute-start(bf16[192,4480]{1,0:T(8,128)(2,1)S(1)} %add_rows.16), channel_id=1, source_target_pairs={{0,2},{6,4},{1,3},{7,5},{8,10},{14,12},{9,11},{15,13},{16,18},{22,... | collective-permute-start | bytes 5160968 | tf_op jit(solution)/shard_map/ppermute | solution.py:948
  546.3 40.8 %collective-permute-start.48 = (bf16[192,4480]{1,0:T(8,128)(2,1)}, bf16[192,4480]{1,0:T(8,128)(2,1)}, u32[]{:S(2)}, u32[]{:S(2)}) collective-permute-start(bf16[192,4480]{1,0:T(8,128)(2,1)} %add_rows.13), channel_id=1, source_target_pairs={{0,16},{8,24},{16,0},{24,8},{1,17},{9,25},{17,1},{25,9},{2,18},{10... | collective-permute-start | bytes 5160968 | tf_op jit(solution)/shard_map/ppermute | solution.py:813
  547.7 74.1 %collective-permute-start.50 = (bf16[192,4480]{1,0:T(8,128)(2,1)}, bf16[192,4480]{1,0:T(8,128)(2,1)}, u32[]{:S(2)}, u32[]{:S(2)}) collective-permute-start(bf16[192,4480]{1,0:T(8,128)(2,1)} %add_rows.14), channel_id=1, source_target_pairs={{0,16},{8,24},{16,0},{24,8},{1,17},{9,25},{17,1},{25,9},{2,18},{10... | collective-permute-start | bytes 5160968 | tf_op jit(solution)/shard_map/ppermute | solution.py:813
  582.3 23.6 %collective-permute-start.47 = (bf16[1024,256]{1,0:T(8,128)(2,1)S(1)}, bf16[1024,256]{1,0:T(8,128)(2,1)S(1)}, u32[]{:S(2)}, u32[]{:S(2)}) collective-permute-start(bf16[1024,256]{1,0:T(8,128)(2,1)S(1)} %slice_add_fusion.2), channel_id=1, source_target_pairs={{2,0},{4,2},{6,4},{3,1},{5,3},{7,5},{10,8},{12,10},{14,12},{11,9},... | collective-permute-start | bytes 1572872 | tf_op jit(solution)/shard_map/ppermute | solution.py:1199
  607.0 15.3 %collective-permute-start.49 = (bf16[1024,256]{1,0:T(8,128)(2,1)S(1)}, bf16[1024,256]{1,0:T(8,128)(2,1)S(1)}, u32[]{:S(2)}, u32[]{:S(2)}) collective-permute-start(bf16[1024,256]{1,0:T(8,128)(2,1)S(1)} %slice_add_fusion.1), channel_id=1, source_target_pairs={{2,0},{4,2},{6,4},{3,1},{5,3},{7,5},{10,8},{12,10},{14,12},{11,9},... | collective-permute-start | bytes 1572872 | tf_op jit(solution)/shard_map/ppermute | solution.py:1199
  640.1 37.5 %collective-permute-start.51 = (bf16[1024,384]{1,0:T(8,128)(2,1)}, bf16[1024,384]{1,0:T(8,128)(2,1)S(1)}, u32[]{:S(2)}, u32[]{:S(2)}) collective-permute-start(bf16[1024,384]{1,0:T(8,128)(2,1)} %copy-done.55), channel_id=1, source_target_pairs={{0,1},{1,0},{2,3},{3,2},{4,5},{5,4},{6,7},{7,6},{8,9},{9,8},{10,11... | collective-permute-start | bytes 2359304 | tf_op jit(solution)/shard_map/ppermute | solution.py:1067
  645.5 39.8 %collective-permute-start.56 = (bf16[192,4480]{1,0:T(8,128)(2,1)}, bf16[192,4480]{1,0:T(8,128)(2,1)}, u32[]{:S(2)}, u32[]{:S(2)}) collective-permute-start(bf16[192,4480]{1,0:T(8,128)(2,1)} %add.254), channel_id=1, source_target_pairs={{2,0},{4,6},{3,1},{5,7},{10,8},{12,14},{11,9},{13,15},{18,16},{20,... | collective-permute-start | bytes 5160968 | tf_op jit(solution)/shard_map/ppermute | solution.py:962
  649.9 35.4 %collective-permute-start.53 = (bf16[192,4480]{1,0:T(8,128)(2,1)}, bf16[192,4480]{1,0:T(8,128)(2,1)}, u32[]{:S(2)}, u32[]{:S(2)}) collective-permute-start(bf16[192,4480]{1,0:T(8,128)(2,1)} %add.252), channel_id=1, source_target_pairs={{2,4},{4,2},{3,5},{5,3},{10,12},{12,10},{11,13},{13,11},{18,20},{2... | collective-permute-start | bytes 5160968 | tf_op jit(solution)/shard_map/ppermute | solution.py:955
  651.7 47.5 %collective-permute-start.54 = (bf16[192,4480]{1,0:T(8,128)(2,1)}, bf16[192,4480]{1,0:T(8,128)(2,1)}, u32[]{:S(2)}, u32[]{:S(2)}) collective-permute-start(bf16[192,4480]{1,0:T(8,128)(2,1)} %add_rows.17), channel_id=1, source_target_pairs={{0,2},{6,4},{1,3},{7,5},{8,10},{14,12},{9,11},{15,13},{16,18},{22,... | collective-permute-start | bytes 5160968 | tf_op jit(solution)/shard_map/ppermute | solution.py:948
  678.5 20.8 %collective-permute-start.52 = (bf16[768,1024]{1,0:T(8,128)(2,1)}, bf16[768,1024]{1,0:T(8,128)(2,1)}, u32[]{:S(2)}, u32[]{:S(2)}) collective-permute-start(bf16[768,1024]{1,0:T(8,128)(2,1)} %get-tuple-element.491), channel_id=1, source_target_pairs={{0,8},{8,0},{16,24},{24,16},{1,9},{9,1},{17,25},{25,17},{2,10},{10... | collective-permute-start | bytes 4718600 | tf_op jit(solution)/shard_map/ppermute | solution.py:813
  681.6 51.2 %collective-permute-start.59 = (bf16[192,4480]{1,0:T(8,128)(2,1)S(1)}, bf16[192,4480]{1,0:T(8,128)(2,1)}, u32[]{:S(2)}, u32[]{:S(2)}) collective-permute-start(bf16[192,4480]{1,0:T(8,128)(2,1)S(1)} %copy-done.22), channel_id=1, source_target_pairs={{0,2},{6,4},{1,3},{7,5},{8,10},{14,12},{9,11},{15,13},{16,18},{22,... | collective-permute-start | bytes 5160968 | tf_op jit(solution)/shard_map/ppermute | solution.py:948
  706.6 33.2 %collective-permute-start.58 = (bf16[192,4480]{1,0:T(8,128)(2,1)}, bf16[192,4480]{1,0:T(8,128)(2,1)}, u32[]{:S(2)}, u32[]{:S(2)}) collective-permute-start(bf16[192,4480]{1,0:T(8,128)(2,1)} %add.256), channel_id=1, source_target_pairs={{2,4},{4,2},{3,5},{5,3},{10,12},{12,10},{11,13},{13,11},{18,20},{2... | collective-permute-start | bytes 5160968 | tf_op jit(solution)/shard_map/ppermute | solution.py:955
  708.4 33.8 %collective-permute-start.63 = (bf16[192,4480]{1,0:T(8,128)(2,1)}, bf16[192,4480]{1,0:T(8,128)(2,1)}, u32[]{:S(2)}, u32[]{:S(2)}) collective-permute-start(bf16[192,4480]{1,0:T(8,128)(2,1)} %add.258), channel_id=1, source_target_pairs={{2,0},{4,6},{3,1},{5,7},{10,8},{12,14},{11,9},{13,15},{18,16},{20,... | collective-permute-start | bytes 5160968 | tf_op jit(solution)/shard_map/ppermute | solution.py:962
  715.7 24.0 %collective-permute-start.61 = (bf16[384,1792]{1,0:T(8,128)(2,1)}, bf16[384,1792]{1,0:T(8,128)(2,1)}, u32[]{:S(2)}, u32[]{:S(2)}) collective-permute-start(bf16[384,1792]{1,0:T(8,128)(2,1)} %add_rows.19), channel_id=1, source_target_pairs={{0,16},{8,24},{16,0},{24,8},{1,17},{9,25},{17,1},{25,9},{2,18},{10... | collective-permute-start | bytes 4128776 | tf_op jit(solution)/shard_map/ppermute | solution.py:813
  752.3 24.4 %collective-permute-start.65 = (bf16[384,1792]{1,0:T(8,128)(2,1)S(1)}, bf16[384,1792]{1,0:T(8,128)(2,1)}, u32[]{:S(2)}, u32[]{:S(2)}) collective-permute-start(bf16[384,1792]{1,0:T(8,128)(2,1)S(1)} %add_rows.21), channel_id=1, source_target_pairs={{0,2},{6,4},{1,3},{7,5},{8,10},{14,12},{9,11},{15,13},{16,18},{22,... | collective-permute-start | bytes 4128776 | tf_op jit(solution)/shard_map/ppermute | solution.py:948
  756.8 26.9 %collective-permute-start.67 = (bf16[1024,768]{1,0:T(8,128)(2,1)S(1)}, bf16[1024,768]{1,0:T(8,128)(2,1)}, u32[]{:S(2)}, u32[]{:S(2)}) collective-permute-start(bf16[1024,768]{1,0:T(8,128)(2,1)S(1)} %copy-done.52), channel_id=1, source_target_pairs={{0,1},{1,0},{2,3},{3,2},{4,5},{5,4},{6,7},{7,6},{8,9},{9,8},{10,11... | collective-permute-start | bytes 4718600 | tf_op jit(solution)/shard_map/ppermute | solution.py:1067
  757.3 26.5 %collective-permute-start.64 = (bf16[192,4480]{1,0:T(8,128)(2,1)}, bf16[192,4480]{1,0:T(8,128)(2,1)}, u32[]{:S(2)}, u32[]{:S(2)}) collective-permute-start(bf16[192,4480]{1,0:T(8,128)(2,1)} %add.259), channel_id=1, source_target_pairs={{2,4},{4,2},{3,5},{5,3},{10,12},{12,10},{11,13},{13,11},{18,20},{2... | collective-permute-start | bytes 5160968 | tf_op jit(solution)/shard_map/ppermute | solution.py:955
  759.1 35.2 %collective-permute-start.68 = (bf16[192,4480]{1,0:T(8,128)(2,1)}, bf16[192,4480]{1,0:T(8,128)(2,1)}, u32[]{:S(2)}, u32[]{:S(2)}) collective-permute-start(bf16[192,4480]{1,0:T(8,128)(2,1)} %add.260), channel_id=1, source_target_pairs={{2,0},{4,6},{3,1},{5,7},{10,8},{12,14},{11,9},{13,15},{18,16},{20,... | collective-permute-start | bytes 5160968 | tf_op jit(solution)/shard_map/ppermute | solution.py:962
  796.9 37.5 %collective-permute-start.71 = (bf16[192,4480]{1,0:T(8,128)(2,1)S(1)}, bf16[192,4480]{1,0:T(8,128)(2,1)S(1)}, u32[]{:S(2)}, u32[]{:S(2)}) collective-permute-start(bf16[192,4480]{1,0:T(8,128)(2,1)S(1)} %add.263), channel_id=1, source_target_pairs={{2,0},{4,6},{3,1},{5,7},{10,8},{12,14},{11,9},{13,15},{18,16},{20,... | collective-permute-start | bytes 5160968 | tf_op jit(solution)/shard_map/ppermute | solution.py:962
  834.8 25.0 %collective-permute-start.73 = (bf16[384,1792]{1,0:T(8,128)(2,1)S(1)}, bf16[384,1792]{1,0:T(8,128)(2,1)S(1)}, u32[]{:S(2)}, u32[]{:S(2)}) collective-permute-start(bf16[384,1792]{1,0:T(8,128)(2,1)S(1)} %add.265), channel_id=1, source_target_pairs={{2,0},{4,6},{3,1},{5,7},{10,8},{12,14},{11,9},{13,15},{18,16},{20,... | collective-permute-start | bytes 4128776 | tf_op jit(solution)/shard_map/ppermute | solution.py:962
  836.3 21.6 %collective-permute-start.72 = (f32[5312]{0:T(1024)S(1)}, f32[5312]{0:T(1024)S(1)}, u32[]{:S(2)}, u32[]{:S(2)}) collective-permute-start(f32[5312]{0:T(1024)S(1)} %add.264), channel_id=1, source_target_pairs={{2,0},{4,6},{3,1},{5,7},{10,8},{12,14},{11,9},{13,15},{18,16},{20,... | collective-permute-start | bytes 63752 | tf_op jit(solution)/shard_map/ppermute | solution.py:962
  (123 other events, 1282.6 us)
Sparse Core Ops, SparseCore 0:
  100.6 67.4 all-gather.2
  265.5 149.0 reduce-scatter.1
  418.1 101.2 all-gather.4

commit v5 on v4

--- a/solution.py
+++ b/solution.py
@@ -819,7 +819,7 @@
             slabs = 1
         self.size, self.own, self.slabs = size, own, slabs
         self.depth = own.shape[0] // slabs
-        self.got = {}
+        self.got, self.cuts = {}, []
 
     def away(self, own):
         got, bit = {0: own}, self.size // 2
@@ -831,10 +831,21 @@
     def far(self, slab, *first):
         if slab >= self.slabs:
             return []
-        own = held(self.own, *first)[slab * self.depth : (slab + 1) * self.depth]
+        if self.cuts:
+            own = held(self.cuts[slab].v, *first)
+        else:
+            own = held(self.own, *first)[slab * self.depth : (slab + 1) * self.depth]
         got = self.away(own)
         self.got.update({(j, slab): p for j, p in got.items()})
         return list(got.values())
+
+    def cut(self, *first):
+        own = held(self.own, *first)
+        if self.slabs > 1:
+            self.cuts = boxes(
+                [own[k * self.depth : (k + 1) * self.depth] for k in range(self.slabs)]
+            )
+        return self.cuts
 
     def far_by_ctx(self, contexts, *first):
         rows = self.own.shape[0] // contexts
@@ -1090,7 +1101,7 @@
         if k == 1:
             out_other[1] = over_tp(out_w.near)
             out_rest = out_w.near_rest(0, kv_own)
-            fence(mark(place), kv, out_rest, out_far, out_other[0])
+            fence(mark(place), kv, out_rest, out_far, out_other[0], gate.cut(kv_own))
         elif k == 2:
             gate_far = gate.far(0, kv[1])
             out_other.update({j: over_tp(piece) for (j, _), piece in out_w.got.items()})
@@ -1118,13 +1129,16 @@
         upper_rows,
     )
     lower = Box(lower)
-    fence(lower, gate_far, place, upper_other)
+    fence(lower, place)
     lower_other = over_tp(lower)
-    gate_rest = gate.near_rest(0) + gate.near_rest(1, lower)
+    gate_rest = gate.near_rest(0) + gate.near_rest(1)
     attended = Box(jnp.concatenate([upper.v, lower.v], axis=0))
     lse, tops = (jnp.concatenate(both, axis=1) for both in zip(upper_sums, lower_sums))
     attended_other = lower_other
-    fence(mark(place), lower_other, gate_far_2, gate_rest, up_spread, attended)
+    cuts = down.cut(lower)
+    fence(
+        mark(place), lower_other, upper_other, gate_far_2, gate_rest, up_spread, attended, cuts
+    )
     down_far = down.far(0, attended_other)
     gate_rest = gate.near_rest(2) + up.near_rest(0)
     own_near = gate.near_own(attended_other) + up.near_own(attended_other)

time: 879 us -> 864 us (0.983)
  local copies, waits for them, and re-layouts: 104 us -> 93.4 us
    ppermute x37, waiting for transfers between devices: 34.6 us -> 20.7 us  [swap(): return lax.ppermute(value, axis, [(i, i ^ bit) for i in range(size)])]
    all_gather x1, waiting for transfers between devices: 0.01 us -> 10.1 us  [spread(): self.got[j, 0] = Box(lax.all_gather(part.v, 'ctx', axis=0, tiled=True))]
    slice x7 -> x2, local copies, waits for them, and re-layouts: 15.2 us -> 6.03 us  [cut(): own[k * self.depth:(k + 1) * self.depth]]
    unnamed x224 -> x216, local copies, waits for them, and re-layouts: 72.1 us -> 70.6 us
  transfers between devices with their start and end apart: 77 -> 77, of which waited for: 31 -> 31; matrix products, arithmetic and copies ran while one was open for 11% -> 10% of each run, Pallas kernels for 36% -> 37%
where the time goes in v5:
time: 864 us; the launch traced here: 854 us
  Pallas kernels  324 us (38%)
  waiting for transfers between devices  238 us (28%)
  starting transfers between devices  107 us (12%)
  local copies, waits for them, and re-layouts  93.4 us (11%)
  other arithmetic  76.4 us (9%)
  between operations  15.4 us (2%)
    ppermute x6, waiting for transfers between devices, inward(): lax.ppermute(self.own[slab].v, 'ctx', [(0, 1), (3, 2)])  77.6 us
    unnamed x216, local copies, waits for them, and re-layouts  70.6 us
    pallas_call x1, Pallas kernels, gate_up_back(): call(functools.partial(gate_up_back_kernel, gates, ups, downs, units % tf...  62.3 us
    pallas_call x4, Pallas kernels, weight_grad(): call(functools.partial(weight_grad_kernel, width // parts, parts), pl.cdi...  51.5 us
    ppermute x6, waiting for transfers between devices, outward(): lax.ppermute(self.own[slab].v, 'ctx', [(1, 0), (2, 3)])  49.5 us
    pallas_call x1, Pallas kernels, gate_up(): call(functools.partial(gate_up_kernel, gates, ups), pl.cdiv(units, tf), [...  40.2 us
    ppermute x12, waiting for transfers between devices, over_tp(): return Box(lax.ppermute(box.v, 'tp', across))  36.4 us
    ppermute x6, starting transfers between devices, inward(): lax.ppermute(self.own[slab].v, 'ctx', [(0, 1), (3, 2)])  34.4 us
  transfers between devices with their start and end apart: 77, of which 31 were waited for; matrix products, arithmetic and copies ran while one was open for 10% of the time, Pallas kernels for 37%

profile of v5, /device:TPU:0, one launch (start us, length us, event | category | flops | bytes accessed | tf_op | source)
XLA Modules:
  0.0 854.0 jit_solution(12308971873531005895)
XLA Ops:
  7.2 3.0 collective-permute-start
  23.1 3.1 fusion
  38.4 8.8 %mix.1 = (bf16[1024,768]{1,0:T(8,128)(2,1)S(1)}, bf16[1024,256]{1,0:T(8,128)(2,1)}, bf16[1536,1024]{1,0:T(8,128)(2,1)S(1)}) custom-call(s32[2]{0:T(128)S(1)} %copy-done.83, bf16[1024,1536]{1,0:T(8,128)(2,1)S(1)} %copy-done.11, bf16[1,1536]{1,0:T(2,128)(2,1)S(1)} %broadcast_in_dim.114.gain_ref, bf16[1,1024]{1,0:T(2,128)(2,1)S(1)} %broadcast_in_dim.115.bias_ref, ...), custom_call_target="tpu_custom_call" | custom-call | flops 1400000000 | bytes 1000 | tf_op jit(solution)/shard_map/mix/pallas_call | solution.py:538
  50.0 3.4 collective-permute-start.5
  56.3 8.6 %collective-permute-done.5 = bf16[1024,256]{1,0:T(8,128)(2,1)S(1)} collective-permute-done((bf16[1024,256]{1,0:T(8,128)(2,1)}, bf16[1024,256]{1,0:T(8,128)(2,1)S(1)}, u32[]{:S(2)}, u32[]{:S(2)}) %collective-permute-start.5) | collective-permute-done | bytes 524320 | tf_op jit(solution)/shard_map/ppermute | solution.py:1100
  66.8 5.1 collective-permute-start.8
  73.0 7.9 collective-permute-done.8
  81.0 5.3 collective-permute-start.11
  86.3 4.6 copy.37
  102.0 5.2 attention_forward.2
  107.2 4.7 collective-permute-done.13.refs_6_
  111.9 9.5 %collective-permute-done.14.refs_7_ = bf16[384,768]{1,0:T(8,128)(2,1)S(1)} collective-permute-done((bf16[384,768]{1,0:T(8,128)(2,1)S(1)}, bf16[384,768]{1,0:T(8,128)(2,1)S(1)}, u32[]{:S(2)}, u32[]{:S(2)}) %collective-permute-start.14) | collective-permute-done | bytes 589856 | tf_op jit(solution)/shard_map/ppermute | solution.py:1078
  123.0 9.7 %attention_forward.3 = (bf16[512,768]{1,0:T(8,128)(2,1)}, f32[6,512]{1,0:T(8,128)S(1)}, f32[6,512]{1,0:T(8,128)S(1)}) custom-call(s32[4]{0:T(128)S(1)} %get-tuple-element.343.count, s32[128]{0:T(128)S(1)} %reshape.678.chosen, s32[33]{0:T(128)S(1)} %pad_add_fusion.9.places, bf16[1024,768]{1,0:T(8,128)(2,1)S(1)} %copy-done.85, ...), custom_call_target="tpu_custom_call" | custom-call | flops 2624999936 | bytes 1000 | tf_op jit(solution)/shard_map/attention_forward/pallas_call | solution.py:94
  137.0 4.4 fusion.34
  143.0 11.0 %collective-permute-done.15.lower_ref = bf16[512,768]{1,0:T(8,128)(2,1)} collective-permute-done((bf16[512,768]{1,0:T(8,128)(2,1)}, bf16[512,768]{1,0:T(8,128)(2,1)}, u32[]{:S(2)}, u32[]{:S(2)}) %collective-permute-start.15) | collective-permute-done | bytes 786464 | tf_op jit(solution)/shard_map/ppermute | solution.py:1078
  154.8 10.1 %all-gather.3.cloned.1.call-done.refs_10_ = bf16[384,4480]{1,0:T(8,128)(2,1)} async-done(((bf16[96,4480]{1,0:T(8,128)(2,1)}), bf16[384,4480]{1,0:T(8,128)(2,1)}) %all-gather.3.cloned.1.call-update) | async-done | bytes 3440656 | tf_op jit(solution)/shard_map/all_gather | solution.py:860
  172.8 11.3 %branch.1 = (f32[1024,1536]{1,0:T(8,128)}, bf16[1024,1536]{1,0:T(8,128)(2,1)S(1)}, bf16[1536,1024]{1,0:T(8,128)(2,1)S(1)}) custom-call(s32[2]{0:T(128)S(1)} %copy-done.80, bf16[1024,1536]{1,0:T(8,128)(2,1)} %x_ref.7, bf16[1024,768]{1,0:T(8,128)(2,1)S(1)} %pad_maximum_fusion.own_ref.att_ref.right_ref, bf16[512,768]{1,0:T(8,128)(2,1)S(1)} %copy-done.66, ...), custom_call_target="tpu_custom_call" | custom-call | flops 2100000000 | bytes 1000 | tf_op jit(solution)/shard_map/branch/pallas_call | solution.py:605
  190.6 40.2 %gate_up.1 = (bf16[1024,4480]{1,0:T(8,128)(2,1)}, bf16[1024,4480]{1,0:T(8,128)(2,1)}, bf16[1024,4480]{1,0:T(8,128)(2,1)}) custom-call(s32[2]{0:T(128)} %mark.16.place.place_ref, bf16[1024,1536]{1,0:T(8,128)(2,1)} %copy-done.38, bf16[384,4480]{1,0:T(8,128)(2,1)} %refs_0_.9, bf16[384,4480]{1,0:T(8,128)(2,1)} %copy-done.90, ...), custom_call_target="tpu_custom_call" | custom-call | flops 7000000000 | bytes 1000 | tf_op jit(solution)/shard_map/gate_up/pallas_call | solution.py:312
  232.8 18.7 %whole_grad.1 = bf16[1536,4480]{1,0:T(8,128)(2,1)} custom-call(bf16[1536,1024]{1,0:T(8,128)(2,1)S(1)} %bitcast.30, bf16[1024,4480]{1,0:T(8,128)(2,1)} %get-tuple-element.435.right_ref.act_ref), custom_call_target="tpu_custom_call" | custom-call | flops 3324999936 | bytes 1000 | tf_op jit(solution)/shard_map/whole_grad/pallas_call | solution.py:392
  256.7 62.3 %gate_up_back.1 = (bf16[1024,4480]{1,0:T(8,128)(2,1)}, bf16[1024,4480]{1,0:T(8,128)(2,1)}, bf16[1024,384]{1,0:T(8,128)(2,1)}, bf16[1024,384]{1,0:T(8,128)(2,1)}, bf16[1024,768]{1,0:T(8,128)(2,1)}) custom-call(s32[2]{0:T(128)} %mark.17.place.place_ref, bf16[1024,1536]{1,0:T(8,128)(2,1)} %c_ref.3, bf16[1024,4480]{1,0:T(8,128)(2,1)} %get-tuple-element.409.by_gate_ref, ...), custom_call_target="tpu_custom_call" | custom-call | flops 10849999872 | bytes 1000 | tf_op jit(solution)/shard_map/gate_up_back/pallas_call | solution.py:368
  320.6 19.1 %weight_grad.4 = (bf16[768,4480]{1,0:T(8,128)(2,1)}, bf16[768,4480]{1,0:T(8,128)(2,1)}) custom-call(s32[2]{0:T(128)S(1)} %copy-done.79, bf16[1536,1024]{1,0:T(8,128)(2,1)S(1)} %copy-done.18, bf16[1024,4480]{1,0:T(8,128)(2,1)} %get-tuple-element.421.right_ref), custom_call_target="tpu_custom_call" | custom-call | flops 3324999936 | bytes 1000 | tf_op jit(solution)/shard_map/weight_grad/pallas_call | solution.py:415
  340.4 19.2 %weight_grad.5 = (bf16[768,4480]{1,0:T(8,128)(2,1)}, bf16[768,4480]{1,0:T(8,128)(2,1)}) custom-call(s32[2]{0:T(128)S(1)} %copy-done.79, bf16[1536,1024]{1,0:T(8,128)(2,1)S(1)} %copy-done.18, bf16[1024,4480]{1,0:T(8,128)(2,1)} %get-tuple-element.427.right_ref), custom_call_target="tpu_custom_call" | custom-call | flops 3324999936 | bytes 1000 | tf_op jit(solution)/shard_map/weight_grad/pallas_call | solution.py:415
  365.1 3.1 copy-done.6
  368.2 3.0 copy-done.8
  374.8 23.7 %down_project.1 = bf16[1024,1536]{1,0:T(8,128)(2,1)} custom-call(s32[2]{0:T(128)S(1)} %copy-done.79, bf16[1024,4480]{1,0:T(8,128)(2,1)} %get-tuple-element.435.right_ref.act_ref, bf16[384,4480]{1,0:T(8,128)(2,1)} %refs_0_.10, bf16[384,4480]{1,0:T(8,128)(2,1)} %collective-permute-done.28.refs_13_.refs_1_, bf16[96,4480]{1,0:T(8,128)(2,1)S(1)} %copy-done.37, ...), custom_call_target="tpu_custom_call" | custom-call | flops 4200000000 | bytes 1000 | tf_op jit(solution)/shard_map/down_project/pallas_call | solution.py:493
  416.5 13.5 %middle_back.1 = (f32[1024,1536]{1,0:T(8,128)}, bf16[1536,1024]{1,0:T(8,128)(2,1)}, bf16[1024,768]{1,0:T(8,128)(2,1)}, f32[6,1024]{1,0:T(8,128)S(1)}, f32[1,1536]{1,0:T(1,128)S(1)}) custom-call(s32[2]{0:T(128)S(1)} %copy-done.79, f32[1024,1536]{1,0:T(8,128)} %get-tuple-element.468.mid_ref, bf16[1024,1536]{1,0:T(8,128)(2,1)} %c_ref.3, ...), custom_call_target="tpu_custom_call" | custom-call | flops 2275000064 | bytes 1000 | tf_op jit(solution)/shard_map/middle_back/pallas_call | solution.py:667
  430.1 6.1 weight_grad.6
  436.2 3.4 copy-done.9
  439.6 3.4 add_rows.15
  447.0 19.2 %attention_backward.1 = (bf16[1024,768]{1,0:T(8,128)(2,1)S(1)}, bf16[4096,256]{1,0:T(8,128)(2,1)}) custom-call(s32[4]{0:T(128)S(1)} %get-tuple-element.453.count, s32[32]{0:T(128)S(1)} %reshape.679.chosen, s32[9]{0:T(128)S(1)} %pad_add_fusion.10.places, bf16[1024,768]{1,0:T(8,128)(2,1)S(1)} %copy-done.86, bf16[1024,768]{1,0:T(8,128)(2,1)S(1)} %copy-done.87, ...), custom_call_target="tpu_custom_call" | custom-call | flops 9450000384 | bytes 1000 | tf_op jit(solution)/shard_map/attention_backward/pallas_call | solution.py:186
  468.4 43.0 %collective-permute-done.40 = bf16[192,4480]{1,0:T(8,128)(2,1)} collective-permute-done((bf16[192,4480]{1,0:T(8,128)(2,1)S(1)}, bf16[192,4480]{1,0:T(8,128)(2,1)}, u32[]{:S(2)}, u32[]{:S(2)}) %collective-permute-start.40) | collective-permute-done | bytes 1720352 | tf_op jit(solution)/shard_map/ppermute | solution.py:959
  511.4 3.2 add.247
  522.1 8.5 collective-permute-start.46
  535.8 6.7 add_convert_fusion
  543.7 5.3 collective-permute-done.44
  548.9 16.8 %collective-permute-done.46 = bf16[192,4480]{1,0:T(8,128)(2,1)} collective-permute-done((bf16[192,4480]{1,0:T(8,128)(2,1)S(1)}, bf16[192,4480]{1,0:T(8,128)(2,1)}, u32[]{:S(2)}, u32[]{:S(2)}) %collective-permute-start.46) | collective-permute-done | bytes 1720352 | tf_op jit(solution)/shard_map/ppermute | solution.py:959
  571.4 19.1 %collective-permute-done.47 = bf16[1024,256]{1,0:T(8,128)(2,1)S(1)} collective-permute-done((bf16[1024,256]{1,0:T(8,128)(2,1)S(1)}, bf16[1024,256]{1,0:T(8,128)(2,1)S(1)}, u32[]{:S(2)}, u32[]{:S(2)}) %collective-permute-start.47) | collective-permute-done | bytes 524320 | tf_op jit(solution)/shard_map/ppermute | solution.py:1213
  600.5 4.2 add_rows.17
  613.6 7.8 mix_back.1
  626.2 4.0 add.254
  631.5 3.1 add.252
  636.4 10.4 %collective-permute-start.54 = (bf16[192,4480]{1,0:T(8,128)(2,1)}, bf16[192,4480]{1,0:T(8,128)(2,1)}, u32[]{:S(2)}, u32[]{:S(2)}) collective-permute-start(bf16[192,4480]{1,0:T(8,128)(2,1)} %add_rows.17), channel_id=1, source_target_pairs={{0,2},{6,4},{1,3},{7,5},{8,10},{14,12},{9,11},{15,13},{16,18},{22,... | collective-permute-start | bytes 5160968 | tf_op jit(solution)/shard_map/ppermute | solution.py:959
  655.1 7.1 weight_grad.7
  669.9 14.0 %collective-permute-done.54 = bf16[192,4480]{1,0:T(8,128)(2,1)} collective-permute-done((bf16[192,4480]{1,0:T(8,128)(2,1)}, bf16[192,4480]{1,0:T(8,128)(2,1)}, u32[]{:S(2)}, u32[]{:S(2)}) %collective-permute-start.54) | collective-permute-done | bytes 1720352 | tf_op jit(solution)/shard_map/ppermute | solution.py:959
  683.9 3.6 add.258
  687.4 3.7 add.256
  695.8 4.4 add_rows.19
  701.4 3.7 collective-permute-done.60
  705.5 5.5 convert_element_type.69
  711.0 3.0 add_rows.20.refs_0_
  717.4 7.2 collective-permute-done.61.refs_1_
  726.7 3.6 add.260
  730.3 3.1 add.259
  733.4 3.3 add_rows.21
  736.7 4.9 collective-permute-start.65
  748.0 5.7 collective-permute-start.66
  757.8 3.9 collective-permute-done.66
  761.7 7.1 collective-permute-done.67.refs_5_
  768.8 10.4 %collective-permute-done.68 = bf16[192,4480]{1,0:T(8,128)(2,1)} collective-permute-done((bf16[192,4480]{1,0:T(8,128)(2,1)}, bf16[192,4480]{1,0:T(8,128)(2,1)}, u32[]{:S(2)}, u32[]{:S(2)}) %collective-permute-start.68) | collective-permute-done | bytes 1720352 | tf_op jit(solution)/shard_map/ppermute | solution.py:973
  783.1 3.3 maximum_convert_fusion
  791.6 7.7 input_back.1
  799.3 19.9 %collective-permute-done.71 = bf16[192,4480]{1,0:T(8,128)(2,1)S(1)} collective-permute-done((bf16[192,4480]{1,0:T(8,128)(2,1)S(1)}, bf16[192,4480]{1,0:T(8,128)(2,1)S(1)}, u32[]{:S(2)}, u32[]{:S(2)}) %collective-permute-start.71) | collective-permute-done | bytes 1720352 | tf_op jit(solution)/shard_map/ppermute | solution.py:973
  822.3 3.3 maximum_convert_fusion.1
  825.7 17.1 %collective-permute-done.72 = f32[5312]{0:T(1024)S(1)} collective-permute-done((f32[5312]{0:T(1024)S(1)}, f32[5312]{0:T(1024)S(1)}, u32[]{:S(2)}, u32[]{:S(2)}) %collective-permute-start.72) | collective-permute-done | bytes 21280 | tf_op jit(solution)/shard_map/ppermute | solution.py:973
  (471 shorter events, 210.7 us)
Async XLA Ops:
  7.2 157.7 %all-gather.3.cloned.1.call-start = ((), (), s32[]{:S(2)}) async-start(), calls=%async_computation.1 | async-start | bytes 4300800 | tf_op jit(solution)/shard_map/all_gather | solution.py:860
  7.2 21.5 %collective-permute-start = (bf16[384,1024]{1,0:T(8,128)(2,1)}, bf16[384,1024]{1,0:T(8,128)(2,1)}, u32[]{:S(2)}, u32[]{:S(2)}) collective-permute-start(bf16[384,1024]{1,0:T(8,128)(2,1)} %refs_0_.11), channel_id=1, source_target_pairs={{0,16},{8,24},{16,0},{24,8},{1,17},{9,25},{17,1},{25,9},{2,18},{10... | collective-permute-start | bytes 2359304 | tf_op jit(solution)/shard_map/ppermute | solution.py:813
  29.2 27.1 %collective-permute-start.7 = (bf16[384,768]{1,0:T(8,128)(2,1)}, bf16[384,768]{1,0:T(8,128)(2,1)}, u32[]{:S(2)}, u32[]{:S(2)}) collective-permute-start(bf16[384,768]{1,0:T(8,128)(2,1)} %refs_6_.1), channel_id=1, source_target_pairs={{0,1},{1,0},{2,3},{3,2},{4,5},{5,4},{6,7},{7,6},{8,9},{9,8},{10,11... | collective-permute-start | bytes 1769480 | tf_op jit(solution)/shard_map/ppermute | solution.py:1088
  30.8 19.2 %collective-permute-start.3 = (bf16[384,768]{1,0:T(8,128)(2,1)}, bf16[384,768]{1,0:T(8,128)(2,1)}, u32[]{:S(2)}, u32[]{:S(2)}) collective-permute-start(bf16[384,768]{1,0:T(8,128)(2,1)} %refs_6_.1), channel_id=1, source_target_pairs={{0,8},{8,0},{16,24},{24,16},{1,9},{9,1},{17,25},{25,17},{2,10},{10... | collective-permute-start | bytes 1769480 | tf_op jit(solution)/shard_map/ppermute | solution.py:813
  30.8 22.6 %collective-permute-start.4 = (bf16[384,768]{1,0:T(8,128)(2,1)}, bf16[384,768]{1,0:T(8,128)(2,1)}, u32[]{:S(2)}, u32[]{:S(2)}) collective-permute-start(bf16[384,768]{1,0:T(8,128)(2,1)} %refs_6_.1), channel_id=1, source_target_pairs={{0,16},{8,24},{16,0},{24,8},{1,17},{9,25},{17,1},{25,9},{2,18},{10... | collective-permute-start | bytes 1769480 | tf_op jit(solution)/shard_map/ppermute | solution.py:813
  35.4 45.6 %collective-permute-start.10 = (bf16[96,4480]{1,0:T(8,128)(2,1)}, bf16[96,4480]{1,0:T(8,128)(2,1)}, u32[]{:S(2)}, u32[]{:S(2)}) collective-permute-start(bf16[96,4480]{1,0:T(8,128)(2,1)} %constant_dynamic-slice_fusion.1), channel_id=1, source_target_pairs={{0,16},{8,24},{16,0},{24,8},{1,17},{9,25},{17,1},{25,9},{2,18},{10... | collective-permute-start | bytes 2580488 | tf_op jit(solution)/shard_map/ppermute | solution.py:813
  50.0 15.0 %collective-permute-start.5 = (bf16[1024,256]{1,0:T(8,128)(2,1)}, bf16[1024,256]{1,0:T(8,128)(2,1)S(1)}, u32[]{:S(2)}, u32[]{:S(2)}) collective-permute-start(bf16[1024,256]{1,0:T(8,128)(2,1)} %get-tuple-element.332), channel_id=1, source_target_pairs={{0,2},{2,4},{4,6},{1,3},{3,5},{5,7},{8,10},{10,12},{12,14},{9,11},... | collective-permute-start | bytes 1572872 | tf_op jit(solution)/shard_map/ppermute | solution.py:1100
  65.0 29.7 %collective-permute-start.12 = (bf16[128,4480]{1,0:T(8,128)(2,1)S(1)}, bf16[128,4480]{1,0:T(8,128)(2,1)}, u32[]{:S(2)}, u32[]{:S(2)}) collective-permute-start(bf16[128,4480]{1,0:T(8,128)(2,1)S(1)} %get-tuple-element.325), channel_id=1, source_target_pairs={{0,16},{8,24},{16,0},{24,8},{1,17},{9,25},{17,1},{25,9},{2,18},{10... | collective-permute-start | bytes 3440648 | tf_op jit(solution)/shard_map/ppermute | solution.py:813
  66.2 14.8 %collective-permute-start.9 = (bf16[384,768]{1,0:T(8,128)(2,1)}, bf16[384,768]{1,0:T(8,128)(2,1)S(1)}, u32[]{:S(2)}, u32[]{:S(2)}) collective-permute-start(bf16[384,768]{1,0:T(8,128)(2,1)} %collective-permute-done.3.refs_1_.refs_7_), channel_id=1, source_target_pairs={{0,1},{1,0},{2,3},{3,2},{4,5},{5,4},{6,7},{7,6},{8,9},{9,8},{10,11... | collective-permute-start | bytes 1769480 | tf_op jit(solution)/shard_map/ppermute | solution.py:1078
  94.8 308.7 %reduce-scatter.2.cloned.1.call-start = ((), (), s32[]{:S(2)}) async-start(), calls=%async_computation.2 | async-start | bytes 14622720 | tf_op jit(solution)/shard_map/reduce_scatter | solution.py:1160
  95.3 16.5 %collective-permute-start.13 = (bf16[384,768]{1,0:T(8,128)(2,1)}, bf16[384,768]{1,0:T(8,128)(2,1)S(1)}, u32[]{:S(2)}, u32[]{:S(2)}) collective-permute-start(bf16[384,768]{1,0:T(8,128)(2,1)} %collective-permute-done.4.refs_2_.refs_8_), channel_id=1, source_target_pairs={{0,1},{1,0},{2,3},{3,2},{4,5},{5,4},{6,7},{7,6},{8,9},{9,8},{10,11... | collective-permute-start | bytes 1769480 | tf_op jit(solution)/shard_map/ppermute | solution.py:1078
  97.0 24.5 %collective-permute-start.14 = (bf16[384,768]{1,0:T(8,128)(2,1)S(1)}, bf16[384,768]{1,0:T(8,128)(2,1)S(1)}, u32[]{:S(2)}, u32[]{:S(2)}) collective-permute-start(bf16[384,768]{1,0:T(8,128)(2,1)S(1)} %collective-permute-done.6.refs_3_.refs_9_), channel_id=1, source_target_pairs={{0,1},{1,0},{2,3},{3,2},{4,5},{5,4},{6,7},{7,6},{8,9},{9,8},{10,11... | collective-permute-start | bytes 1769480 | tf_op jit(solution)/shard_map/ppermute | solution.py:1078
  97.4 39.5 %collective-permute-start.19 = (bf16[128,4480]{1,0:T(8,128)(2,1)}, bf16[128,4480]{1,0:T(8,128)(2,1)}, u32[]{:S(2)}, u32[]{:S(2)}) collective-permute-start(bf16[128,4480]{1,0:T(8,128)(2,1)} %get-tuple-element.355), channel_id=1, source_target_pairs={{0,16},{8,24},{16,0},{24,8},{1,17},{9,25},{17,1},{25,9},{2,18},{10... | collective-permute-start | bytes 3440648 | tf_op jit(solution)/shard_map/ppermute | solution.py:813
  98.5 55.5 %collective-permute-start.18 = (bf16[128,4480]{1,0:T(8,128)(2,1)}, bf16[128,4480]{1,0:T(8,128)(2,1)}, u32[]{:S(2)}, u32[]{:S(2)}) collective-permute-start(bf16[128,4480]{1,0:T(8,128)(2,1)} %collective-permute-done.12.refs_2_), channel_id=1, source_target_pairs={{0,8},{8,0},{16,24},{24,16},{1,9},{9,1},{17,25},{25,17},{2,10},{10... | collective-permute-start | bytes 3440648 | tf_op jit(solution)/shard_map/ppermute | solution.py:813
  121.4 20.7 %collective-permute-start.16 = (bf16[512,768]{1,0:T(8,128)(2,1)}, bf16[512,768]{1,0:T(8,128)(2,1)S(1)}, u32[]{:S(2)}, u32[]{:S(2)}) collective-permute-start(bf16[512,768]{1,0:T(8,128)(2,1)} %get-tuple-element.357), channel_id=1, source_target_pairs={{0,1},{1,0},{2,3},{3,2},{4,5},{5,4},{6,7},{7,6},{8,9},{9,8},{10,11... | collective-permute-start | bytes 2359304 | tf_op jit(solution)/shard_map/ppermute | solution.py:1078
  132.7 21.3 %collective-permute-start.15 = (bf16[512,768]{1,0:T(8,128)(2,1)}, bf16[512,768]{1,0:T(8,128)(2,1)}, u32[]{:S(2)}, u32[]{:S(2)}) collective-permute-start(bf16[512,768]{1,0:T(8,128)(2,1)} %get-tuple-element.349), channel_id=1, source_target_pairs={{0,1},{1,0},{2,3},{3,2},{4,5},{5,4},{6,7},{7,6},{8,9},{9,8},{10,11... | collective-permute-start | bytes 2359304 | tf_op jit(solution)/shard_map/ppermute | solution.py:1078
  133.2 21.6 %collective-permute-start.17 = (bf16[128,4480]{1,0:T(8,128)(2,1)}, bf16[128,4480]{1,0:T(8,128)(2,1)}, u32[]{:S(2)}, u32[]{:S(2)}) collective-permute-start(bf16[128,4480]{1,0:T(8,128)(2,1)} %get-tuple-element.352), channel_id=1, source_target_pairs={{0,16},{8,24},{16,0},{24,8},{1,17},{9,25},{17,1},{25,9},{2,18},{10... | collective-permute-start | bytes 3440648 | tf_op jit(solution)/shard_map/ppermute | solution.py:813
  136.9 17.8 %collective-permute-start.20 = (bf16[128,4480]{1,0:T(8,128)(2,1)}, bf16[128,4480]{1,0:T(8,128)(2,1)}, u32[]{:S(2)}, u32[]{:S(2)}) collective-permute-start(bf16[128,4480]{1,0:T(8,128)(2,1)} %collective-permute-done.19.refs_3_), channel_id=1, source_target_pairs={{0,8},{8,0},{16,24},{24,16},{1,9},{9,1},{17,25},{25,17},{2,10},{10... | collective-permute-start | bytes 3440648 | tf_op jit(solution)/shard_map/ppermute | solution.py:813
  164.8 22.5 %collective-permute-start.24 = (bf16[384,4480]{1,0:T(8,128)(2,1)}, bf16[384,4480]{1,0:T(8,128)(2,1)S(1)}, u32[]{:S(2)}, u32[]{:S(2)}) collective-permute-start(bf16[384,4480]{1,0:T(8,128)(2,1)} %refs_8_.3), channel_id=1, source_target_pairs={{0,8},{8,0},{16,24},{24,16},{1,9},{9,1},{17,25},{25,17},{2,10},{10... | collective-permute-start | bytes 10321928 | tf_op jit(solution)/shard_map/ppermute | solution.py:813
  164.8 22.6 %collective-permute-start.23 = (bf16[384,4480]{1,0:T(8,128)(2,1)}, bf16[384,4480]{1,0:T(8,128)(2,1)S(1)}, u32[]{:S(2)}, u32[]{:S(2)}) collective-permute-start(bf16[384,4480]{1,0:T(8,128)(2,1)} %refs_0_.9), channel_id=1, source_target_pairs={{0,8},{8,0},{16,24},{24,16},{1,9},{9,1},{17,25},{25,17},{2,10},{10... | collective-permute-start | bytes 10321928 | tf_op jit(solution)/shard_map/ppermute | solution.py:813
  165.3 22.1 %collective-permute-start.22 = (bf16[384,4480]{1,0:T(8,128)(2,1)}, bf16[384,4480]{1,0:T(8,128)(2,1)}, u32[]{:S(2)}, u32[]{:S(2)}) collective-permute-start(bf16[384,4480]{1,0:T(8,128)(2,1)} %all-gather.3.cloned.1.call-done.refs_10_), channel_id=1, source_target_pairs={{0,8},{8,0},{16,24},{24,16},{1,9},{9,1},{17,25},{25,17},{2,10},{10... | collective-permute-start | bytes 10321928 | tf_op jit(solution)/shard_map/ppermute | solution.py:813
  165.3 22.0 %collective-permute-start.21 = (bf16[128,4480]{1,0:T(8,128)(2,1)}, bf16[128,4480]{1,0:T(8,128)(2,1)S(1)}, u32[]{:S(2)}, u32[]{:S(2)}) collective-permute-start(bf16[128,4480]{1,0:T(8,128)(2,1)} %collective-permute-done.17.refs_4_), channel_id=1, source_target_pairs={{0,8},{8,0},{16,24},{24,16},{1,9},{9,1},{17,25},{25,17},{2,10},{10... | collective-permute-start | bytes 3440648 | tf_op jit(solution)/shard_map/ppermute | solution.py:813
  165.9 21.5 %collective-permute-start.25 = (bf16[96,4480]{1,0:T(8,128)(2,1)}, bf16[96,4480]{1,0:T(8,128)(2,1)S(1)}, u32[]{:S(2)}, u32[]{:S(2)}) collective-permute-start(bf16[96,4480]{1,0:T(8,128)(2,1)} %get-tuple-element.376), channel_id=1, source_target_pairs={{0,16},{8,24},{16,0},{24,8},{1,17},{9,25},{17,1},{25,9},{2,18},{10... | collective-permute-start | bytes 2580488 | tf_op jit(solution)/shard_map/ppermute | solution.py:813
  187.4 43.5 %collective-permute-start.28 = (bf16[384,4480]{1,0:T(8,128)(2,1)}, bf16[384,4480]{1,0:T(8,128)(2,1)}, u32[]{:S(2)}, u32[]{:S(2)}) collective-permute-start(bf16[384,4480]{1,0:T(8,128)(2,1)} %refs_0_.10), channel_id=1, source_target_pairs={{0,8},{8,0},{16,24},{24,16},{1,9},{9,1},{17,25},{25,17},{2,10},{10... | collective-permute-start | bytes 10321928 | tf_op jit(solution)/shard_map/ppermute | solution.py:813
  187.5 43.4 %collective-permute-start.27 = (bf16[96,4480]{1,0:T(8,128)(2,1)}, bf16[96,4480]{1,0:T(8,128)(2,1)}, u32[]{:S(2)}, u32[]{:S(2)}) collective-permute-start(bf16[96,4480]{1,0:T(8,128)(2,1)} %get-tuple-element.391), channel_id=1, source_target_pairs={{0,16},{8,24},{16,0},{24,8},{1,17},{9,25},{17,1},{25,9},{2,18},{10... | collective-permute-start | bytes 2580488 | tf_op jit(solution)/shard_map/ppermute | solution.py:813
  188.8 42.1 %collective-permute-start.26 = (bf16[96,4480]{1,0:T(8,128)(2,1)}, bf16[96,4480]{1,0:T(8,128)(2,1)}, u32[]{:S(2)}, u32[]{:S(2)}) collective-permute-start(bf16[96,4480]{1,0:T(8,128)(2,1)} %get-tuple-element.388), channel_id=1, source_target_pairs={{0,16},{8,24},{16,0},{24,8},{1,17},{9,25},{17,1},{25,9},{2,18},{10... | collective-permute-start | bytes 2580488 | tf_op jit(solution)/shard_map/ppermute | solution.py:813
  230.9 20.5 %collective-permute-start.29 = (bf16[96,4480]{1,0:T(8,128)(2,1)S(1)}, bf16[96,4480]{1,0:T(8,128)(2,1)}, u32[]{:S(2)}, u32[]{:S(2)}) collective-permute-start(bf16[96,4480]{1,0:T(8,128)(2,1)S(1)} %collective-permute-done.25.refs_14_.refs_2_), channel_id=1, source_target_pairs={{0,8},{8,0},{16,24},{24,16},{1,9},{9,1},{17,25},{25,17},{2,10},{10... | collective-permute-start | bytes 2580488 | tf_op jit(solution)/shard_map/ppermute | solution.py:813
  231.0 21.9 %collective-permute-start.32 = (bf16[96,4480]{1,0:T(8,128)(2,1)}, bf16[96,4480]{1,0:T(8,128)(2,1)}, u32[]{:S(2)}, u32[]{:S(2)}) collective-permute-start(bf16[96,4480]{1,0:T(8,128)(2,1)} %get-tuple-element.404), channel_id=1, source_target_pairs={{0,16},{8,24},{16,0},{24,8},{1,17},{9,25},{17,1},{25,9},{2,18},{10... | collective-permute-start | bytes 2580488 | tf_op jit(solution)/shard_map/ppermute | solution.py:813
  232.3 20.6 %collective-permute-start.30 = (bf16[96,4480]{1,0:T(8,128)(2,1)}, bf16[96,4480]{1,0:T(8,128)(2,1)}, u32[]{:S(2)}, u32[]{:S(2)}) collective-permute-start(bf16[96,4480]{1,0:T(8,128)(2,1)} %collective-permute-done.26.refs_15_.refs_3_), channel_id=1, source_target_pairs={{0,8},{8,0},{16,24},{24,16},{1,9},{9,1},{17,25},{25,17},{2,10},{10... | collective-permute-start | bytes 2580488 | tf_op jit(solution)/shard_map/ppermute | solution.py:813
  232.4 20.4 %collective-permute-start.31 = (bf16[96,4480]{1,0:T(8,128)(2,1)}, bf16[96,4480]{1,0:T(8,128)(2,1)}, u32[]{:S(2)}, u32[]{:S(2)}) collective-permute-start(bf16[96,4480]{1,0:T(8,128)(2,1)} %collective-permute-done.27.refs_16_.refs_4_), channel_id=1, source_target_pairs={{0,8},{8,0},{16,24},{24,16},{1,9},{9,1},{17,25},{25,17},{2,10},{10... | collective-permute-start | bytes 2580488 | tf_op jit(solution)/shard_map/ppermute | solution.py:813
  252.9 353.4 %all-gather.5.cloned.1.call-start = ((), (), s32[]{:S(2)}) async-start(), calls=%async_computation.3 | async-start | bytes 4300800 | tf_op jit(solution)/shard_map/all_gather | solution.py:1185
  319.0 20.7 %collective-permute-start.34 = (bf16[1024,384]{1,0:T(8,128)(2,1)}, bf16[1024,384]{1,0:T(8,128)(2,1)S(1)}, u32[]{:S(2)}, u32[]{:S(2)}) collective-permute-start(bf16[1024,384]{1,0:T(8,128)(2,1)} %get-tuple-element.424.refs_0_), channel_id=1, source_target_pairs={{0,1},{1,0},{2,3},{3,2},{4,5},{5,4},{6,7},{7,6},{8,9},{9,8},{10,11... | collective-permute-start | bytes 2359304 | tf_op jit(solution)/shard_map/ppermute | solution.py:1078
  339.7 20.9 %collective-permute-start.35 = (bf16[768,4480]{1,0:T(8,128)(2,1)}, bf16[768,4480]{1,0:T(8,128)(2,1)S(1)}, u32[]{:S(2)}, u32[]{:S(2)}) collective-permute-start(bf16[768,4480]{1,0:T(8,128)(2,1)} %get-tuple-element.429), channel_id=1, source_target_pairs={{0,8},{8,0},{16,24},{24,16},{1,9},{9,1},{17,25},{25,17},{2,10},{10... | collective-permute-start | bytes 20643848 | tf_op jit(solution)/shard_map/ppermute | solution.py:813
  339.8 20.0 %collective-permute-start.36 = (bf16[1024,384]{1,0:T(8,128)(2,1)S(1)}, bf16[1024,384]{1,0:T(8,128)(2,1)S(1)}, u32[]{:S(2)}, u32[]{:S(2)}) collective-permute-start(bf16[1024,384]{1,0:T(8,128)(2,1)S(1)} %copy-done.60), channel_id=1, source_target_pairs={{0,1},{1,0},{2,3},{3,2},{4,5},{5,4},{6,7},{7,6},{8,9},{9,8},{10,11... | collective-permute-start | bytes 2359304 | tf_op jit(solution)/shard_map/ppermute | solution.py:1078
  363.5 37.1 %collective-permute-start.37 = (bf16[768,4480]{1,0:T(8,128)(2,1)}, bf16[768,4480]{1,0:T(8,128)(2,1)S(1)}, u32[]{:S(2)}, u32[]{:S(2)}) collective-permute-start(bf16[768,4480]{1,0:T(8,128)(2,1)} %get-tuple-element.436), channel_id=1, source_target_pairs={{0,8},{8,0},{16,24},{24,16},{1,9},{9,1},{17,25},{25,17},{2,10},{10... | collective-permute-start | bytes 20643848 | tf_op jit(solution)/shard_map/ppermute | solution.py:813
  363.6 37.1 %collective-permute-start.38 = (bf16[1024,768]{1,0:T(8,128)(2,1)}, bf16[1024,768]{1,0:T(8,128)(2,1)}, u32[]{:S(2)}, u32[]{:S(2)}) collective-permute-start(bf16[1024,768]{1,0:T(8,128)(2,1)} %get-tuple-element.437.refs_2_), channel_id=1, source_target_pairs={{0,1},{1,0},{2,3},{3,2},{4,5},{5,4},{6,7},{7,6},{8,9},{9,8},{10,11... | collective-permute-start | bytes 4718600 | tf_op jit(solution)/shard_map/ppermute | solution.py:1078
  373.5 62.6 %collective-permute-start.39 = (bf16[192,4480]{1,0:T(8,128)(2,1)}, bf16[192,4480]{1,0:T(8,128)(2,1)}, u32[]{:S(2)}, u32[]{:S(2)}) collective-permute-start(bf16[192,4480]{1,0:T(8,128)(2,1)} %add_rows.11), channel_id=1, source_target_pairs={{0,16},{8,24},{16,0},{24,8},{1,17},{9,25},{17,1},{25,9},{2,18},{10... | collective-permute-start | bytes 5160968 | tf_op jit(solution)/shard_map/ppermute | solution.py:813
  403.5 107.9 %collective-permute-start.43 = (bf16[1024,1536]{1,0:T(8,128)(2,1)}, bf16[1024,1536]{1,0:T(8,128)(2,1)}, u32[]{:S(2)}, u32[]{:S(2)}) collective-permute-start(bf16[1024,1536]{1,0:T(8,128)(2,1)} %down_project.1), channel_id=1, source_target_pairs={{0,1},{1,0},{2,3},{3,2},{4,5},{5,4},{6,7},{7,6},{8,9},{9,8},{10,11... | collective-permute-start | bytes 9437192 | tf_op jit(solution)/shard_map/ppermute | solution.py:1078
  404.8 62.6 %collective-permute-start.41 = (bf16[192,4480]{1,0:T(8,128)(2,1)S(1)}, bf16[192,4480]{1,0:T(8,128)(2,1)}, u32[]{:S(2)}, u32[]{:S(2)}) collective-permute-start(bf16[192,4480]{1,0:T(8,128)(2,1)S(1)} %add_rows.12), channel_id=1, source_target_pairs={{0,16},{8,24},{16,0},{24,8},{1,17},{9,25},{17,1},{25,9},{2,18},{10... | collective-permute-start | bytes 5160968 | tf_op jit(solution)/shard_map/ppermute | solution.py:813
  443.0 68.4 %collective-permute-start.40 = (bf16[192,4480]{1,0:T(8,128)(2,1)S(1)}, bf16[192,4480]{1,0:T(8,128)(2,1)}, u32[]{:S(2)}, u32[]{:S(2)}) collective-permute-start(bf16[192,4480]{1,0:T(8,128)(2,1)S(1)} %add_rows.15), channel_id=1, source_target_pairs={{0,2},{6,4},{1,3},{7,5},{8,10},{14,12},{9,11},{15,13},{16,18},{22,... | collective-permute-start | bytes 5160968 | tf_op jit(solution)/shard_map/ppermute | solution.py:959
  445.5 21.9 %collective-permute-start.42 = (bf16[768,768]{1,0:T(8,128)(2,1)}, bf16[768,768]{1,0:T(8,128)(2,1)S(1)}, u32[]{:S(2)}, u32[]{:S(2)}) collective-permute-start(bf16[768,768]{1,0:T(8,128)(2,1)} %get-tuple-element.463), channel_id=1, source_target_pairs={{0,8},{8,0},{16,24},{24,16},{1,9},{9,1},{17,25},{25,17},{2,10},{10... | collective-permute-start | bytes 3538952 | tf_op jit(solution)/shard_map/ppermute | solution.py:813
  520.2 28.7 %collective-permute-start.45 = (bf16[192,4480]{1,0:T(8,128)(2,1)}, bf16[192,4480]{1,0:T(8,128)(2,1)}, u32[]{:S(2)}, u32[]{:S(2)}) collective-permute-start(bf16[192,4480]{1,0:T(8,128)(2,1)} %add.247), channel_id=1, source_target_pairs={{2,4},{4,2},{3,5},{5,3},{10,12},{12,10},{11,13},{13,11},{18,20},{2... | collective-permute-start | bytes 5160968 | tf_op jit(solution)/shard_map/ppermute | solution.py:966
  522.1 43.6 %collective-permute-start.46 = (bf16[192,4480]{1,0:T(8,128)(2,1)S(1)}, bf16[192,4480]{1,0:T(8,128)(2,1)}, u32[]{:S(2)}, u32[]{:S(2)}) collective-permute-start(bf16[192,4480]{1,0:T(8,128)(2,1)S(1)} %add_rows.16), channel_id=1, source_target_pairs={{0,2},{6,4},{1,3},{7,5},{8,10},{14,12},{9,11},{15,13},{16,18},{22,... | collective-permute-start | bytes 5160968 | tf_op jit(solution)/shard_map/ppermute | solution.py:959
  530.6 40.8 %collective-permute-start.48 = (bf16[192,4480]{1,0:T(8,128)(2,1)}, bf16[192,4480]{1,0:T(8,128)(2,1)}, u32[]{:S(2)}, u32[]{:S(2)}) collective-permute-start(bf16[192,4480]{1,0:T(8,128)(2,1)} %add_rows.13), channel_id=1, source_target_pairs={{0,16},{8,24},{16,0},{24,8},{1,17},{9,25},{17,1},{25,9},{2,18},{10... | collective-permute-start | bytes 5160968 | tf_op jit(solution)/shard_map/ppermute | solution.py:813
  532.1 74.2 %collective-permute-start.50 = (bf16[192,4480]{1,0:T(8,128)(2,1)}, bf16[192,4480]{1,0:T(8,128)(2,1)}, u32[]{:S(2)}, u32[]{:S(2)}) collective-permute-start(bf16[192,4480]{1,0:T(8,128)(2,1)} %add_rows.14), channel_id=1, source_target_pairs={{0,16},{8,24},{16,0},{24,8},{1,17},{9,25},{17,1},{25,9},{2,18},{10... | collective-permute-start | bytes 5160968 | tf_op jit(solution)/shard_map/ppermute | solution.py:813
  534.5 14.4 %collective-permute-start.44 = (bf16[1024,256]{1,0:T(8,128)(2,1)}, bf16[1024,256]{1,0:T(8,128)(2,1)S(1)}, u32[]{:S(2)}, u32[]{:S(2)}) collective-permute-start(bf16[1024,256]{1,0:T(8,128)(2,1)} %slice.70), channel_id=1, source_target_pairs={{2,0},{4,2},{6,4},{3,1},{5,3},{7,5},{10,8},{12,10},{14,12},{11,9},... | collective-permute-start | bytes 1572872 | tf_op jit(solution)/shard_map/ppermute | solution.py:1213
  566.8 23.7 %collective-permute-start.47 = (bf16[1024,256]{1,0:T(8,128)(2,1)S(1)}, bf16[1024,256]{1,0:T(8,128)(2,1)S(1)}, u32[]{:S(2)}, u32[]{:S(2)}) collective-permute-start(bf16[1024,256]{1,0:T(8,128)(2,1)S(1)} %slice_add_fusion.2), channel_id=1, source_target_pairs={{2,0},{4,2},{6,4},{3,1},{5,3},{7,5},{10,8},{12,10},{14,12},{11,9},... | collective-permute-start | bytes 1572872 | tf_op jit(solution)/shard_map/ppermute | solution.py:1213
  591.6 15.4 %collective-permute-start.49 = (bf16[1024,256]{1,0:T(8,128)(2,1)S(1)}, bf16[1024,256]{1,0:T(8,128)(2,1)S(1)}, u32[]{:S(2)}, u32[]{:S(2)}) collective-permute-start(bf16[1024,256]{1,0:T(8,128)(2,1)S(1)} %slice_add_fusion.1), channel_id=1, source_target_pairs={{2,0},{4,2},{6,4},{3,1},{5,3},{7,5},{10,8},{12,10},{14,12},{11,9},... | collective-permute-start | bytes 1572872 | tf_op jit(solution)/shard_map/ppermute | solution.py:1213
  624.9 37.4 %collective-permute-start.51 = (bf16[1024,384]{1,0:T(8,128)(2,1)}, bf16[1024,384]{1,0:T(8,128)(2,1)S(1)}, u32[]{:S(2)}, u32[]{:S(2)}) collective-permute-start(bf16[1024,384]{1,0:T(8,128)(2,1)} %copy-done.55), channel_id=1, source_target_pairs={{0,1},{1,0},{2,3},{3,2},{4,5},{5,4},{6,7},{7,6},{8,9},{9,8},{10,11... | collective-permute-start | bytes 2359304 | tf_op jit(solution)/shard_map/ppermute | solution.py:1078
  630.2 39.7 %collective-permute-start.56 = (bf16[192,4480]{1,0:T(8,128)(2,1)}, bf16[192,4480]{1,0:T(8,128)(2,1)}, u32[]{:S(2)}, u32[]{:S(2)}) collective-permute-start(bf16[192,4480]{1,0:T(8,128)(2,1)} %add.254), channel_id=1, source_target_pairs={{2,0},{4,6},{3,1},{5,7},{10,8},{12,14},{11,9},{13,15},{18,16},{20,... | collective-permute-start | bytes 5160968 | tf_op jit(solution)/shard_map/ppermute | solution.py:973
  634.6 35.3 %collective-permute-start.53 = (bf16[192,4480]{1,0:T(8,128)(2,1)}, bf16[192,4480]{1,0:T(8,128)(2,1)}, u32[]{:S(2)}, u32[]{:S(2)}) collective-permute-start(bf16[192,4480]{1,0:T(8,128)(2,1)} %add.252), channel_id=1, source_target_pairs={{2,4},{4,2},{3,5},{5,3},{10,12},{12,10},{11,13},{13,11},{18,20},{2... | collective-permute-start | bytes 5160968 | tf_op jit(solution)/shard_map/ppermute | solution.py:966
  636.4 47.4 %collective-permute-start.54 = (bf16[192,4480]{1,0:T(8,128)(2,1)}, bf16[192,4480]{1,0:T(8,128)(2,1)}, u32[]{:S(2)}, u32[]{:S(2)}) collective-permute-start(bf16[192,4480]{1,0:T(8,128)(2,1)} %add_rows.17), channel_id=1, source_target_pairs={{0,2},{6,4},{1,3},{7,5},{8,10},{14,12},{9,11},{15,13},{16,18},{22,... | collective-permute-start | bytes 5160968 | tf_op jit(solution)/shard_map/ppermute | solution.py:959
  663.1 20.7 %collective-permute-start.52 = (bf16[768,1024]{1,0:T(8,128)(2,1)}, bf16[768,1024]{1,0:T(8,128)(2,1)}, u32[]{:S(2)}, u32[]{:S(2)}) collective-permute-start(bf16[768,1024]{1,0:T(8,128)(2,1)} %get-tuple-element.505), channel_id=1, source_target_pairs={{0,8},{8,0},{16,24},{24,16},{1,9},{9,1},{17,25},{25,17},{2,10},{10... | collective-permute-start | bytes 4718600 | tf_op jit(solution)/shard_map/ppermute | solution.py:813
  666.2 51.2 %collective-permute-start.59 = (bf16[192,4480]{1,0:T(8,128)(2,1)S(1)}, bf16[192,4480]{1,0:T(8,128)(2,1)}, u32[]{:S(2)}, u32[]{:S(2)}) collective-permute-start(bf16[192,4480]{1,0:T(8,128)(2,1)S(1)} %copy-done.22), channel_id=1, source_target_pairs={{0,2},{6,4},{1,3},{7,5},{8,10},{14,12},{9,11},{15,13},{16,18},{22,... | collective-permute-start | bytes 5160968 | tf_op jit(solution)/shard_map/ppermute | solution.py:959
  691.1 33.4 %collective-permute-start.58 = (bf16[192,4480]{1,0:T(8,128)(2,1)}, bf16[192,4480]{1,0:T(8,128)(2,1)}, u32[]{:S(2)}, u32[]{:S(2)}) collective-permute-start(bf16[192,4480]{1,0:T(8,128)(2,1)} %add.256), channel_id=1, source_target_pairs={{2,4},{4,2},{3,5},{5,3},{10,12},{12,10},{11,13},{13,11},{18,20},{2... | collective-permute-start | bytes 5160968 | tf_op jit(solution)/shard_map/ppermute | solution.py:966
  693.0 33.6 %collective-permute-start.63 = (bf16[192,4480]{1,0:T(8,128)(2,1)}, bf16[192,4480]{1,0:T(8,128)(2,1)}, u32[]{:S(2)}, u32[]{:S(2)}) collective-permute-start(bf16[192,4480]{1,0:T(8,128)(2,1)} %add.258), channel_id=1, source_target_pairs={{2,0},{4,6},{3,1},{5,7},{10,8},{12,14},{11,9},{13,15},{18,16},{20,... | collective-permute-start | bytes 5160968 | tf_op jit(solution)/shard_map/ppermute | solution.py:973
  700.3 24.3 %collective-permute-start.61 = (bf16[384,1792]{1,0:T(8,128)(2,1)}, bf16[384,1792]{1,0:T(8,128)(2,1)}, u32[]{:S(2)}, u32[]{:S(2)}) collective-permute-start(bf16[384,1792]{1,0:T(8,128)(2,1)} %add_rows.19), channel_id=1, source_target_pairs={{0,16},{8,24},{16,0},{24,8},{1,17},{9,25},{17,1},{25,9},{2,18},{10... | collective-permute-start | bytes 4128776 | tf_op jit(solution)/shard_map/ppermute | solution.py:813
  736.7 24.9 %collective-permute-start.65 = (bf16[384,1792]{1,0:T(8,128)(2,1)S(1)}, bf16[384,1792]{1,0:T(8,128)(2,1)}, u32[]{:S(2)}, u32[]{:S(2)}) collective-permute-start(bf16[384,1792]{1,0:T(8,128)(2,1)S(1)} %add_rows.21), channel_id=1, source_target_pairs={{0,2},{6,4},{1,3},{7,5},{8,10},{14,12},{9,11},{15,13},{16,18},{22,... | collective-permute-start | bytes 4128776 | tf_op jit(solution)/shard_map/ppermute | solution.py:959
  741.6 27.2 %collective-permute-start.67 = (bf16[1024,768]{1,0:T(8,128)(2,1)S(1)}, bf16[1024,768]{1,0:T(8,128)(2,1)}, u32[]{:S(2)}, u32[]{:S(2)}) collective-permute-start(bf16[1024,768]{1,0:T(8,128)(2,1)S(1)} %copy-done.52), channel_id=1, source_target_pairs={{0,1},{1,0},{2,3},{3,2},{4,5},{5,4},{6,7},{7,6},{8,9},{9,8},{10,11... | collective-permute-start | bytes 4718600 | tf_op jit(solution)/shard_map/ppermute | solution.py:1078
  742.0 26.7 %collective-permute-start.64 = (bf16[192,4480]{1,0:T(8,128)(2,1)}, bf16[192,4480]{1,0:T(8,128)(2,1)}, u32[]{:S(2)}, u32[]{:S(2)}) collective-permute-start(bf16[192,4480]{1,0:T(8,128)(2,1)} %add.259), channel_id=1, source_target_pairs={{2,4},{4,2},{3,5},{5,3},{10,12},{12,10},{11,13},{13,11},{18,20},{2... | collective-permute-start | bytes 5160968 | tf_op jit(solution)/shard_map/ppermute | solution.py:966
  743.9 35.2 %collective-permute-start.68 = (bf16[192,4480]{1,0:T(8,128)(2,1)}, bf16[192,4480]{1,0:T(8,128)(2,1)}, u32[]{:S(2)}, u32[]{:S(2)}) collective-permute-start(bf16[192,4480]{1,0:T(8,128)(2,1)} %add.260), channel_id=1, source_target_pairs={{2,0},{4,6},{3,1},{5,7},{10,8},{12,14},{11,9},{13,15},{18,16},{20,... | collective-permute-start | bytes 5160968 | tf_op jit(solution)/shard_map/ppermute | solution.py:973
  781.7 37.5 %collective-permute-start.71 = (bf16[192,4480]{1,0:T(8,128)(2,1)S(1)}, bf16[192,4480]{1,0:T(8,128)(2,1)S(1)}, u32[]{:S(2)}, u32[]{:S(2)}) collective-permute-start(bf16[192,4480]{1,0:T(8,128)(2,1)S(1)} %add.263), channel_id=1, source_target_pairs={{2,0},{4,6},{3,1},{5,7},{10,8},{12,14},{11,9},{13,15},{18,16},{20,... | collective-permute-start | bytes 5160968 | tf_op jit(solution)/shard_map/ppermute | solution.py:973
  819.5 25.2 %collective-permute-start.73 = (bf16[384,1792]{1,0:T(8,128)(2,1)S(1)}, bf16[384,1792]{1,0:T(8,128)(2,1)S(1)}, u32[]{:S(2)}, u32[]{:S(2)}) collective-permute-start(bf16[384,1792]{1,0:T(8,128)(2,1)S(1)} %add.265), channel_id=1, source_target_pairs={{2,0},{4,6},{3,1},{5,7},{10,8},{12,14},{11,9},{13,15},{18,16},{20,... | collective-permute-start | bytes 4128776 | tf_op jit(solution)/shard_map/ppermute | solution.py:973
  821.0 21.8 %collective-permute-start.72 = (f32[5312]{0:T(1024)S(1)}, f32[5312]{0:T(1024)S(1)}, u32[]{:S(2)}, u32[]{:S(2)}) collective-permute-start(f32[5312]{0:T(1024)S(1)} %add.264), channel_id=1, source_target_pairs={{2,0},{4,6},{3,1},{5,7},{10,8},{12,14},{11,9},{13,15},{18,16},{20,... | collective-permute-start | bytes 63752 | tf_op jit(solution)/shard_map/ppermute | solution.py:973
  (119 other events, 1195.6 us)
Sparse Core Ops, SparseCore 0:
  94.9 69.9 all-gather.2
  253.0 146.7 reduce-scatter.1
  406.2 98.8 all-gather.4

commit v6 on v5

--- a/solution.py
+++ b/solution.py
@@ -1078,10 +1078,11 @@
         return Box(lax.ppermute(box.v, "tp", across))
 
     qkv_far = qkv.far(0)
-    leaves, tree = jax.tree.flatten((reach_rows, hot, lists_f, lists_b, cosine, sine))
-    leaves, place = boxes(leaves), Box(place)
-    fence(leaves, place, qkv_far)
-    reach_rows, hot, lists_f, lists_b, cosine, sine = tree.unflatten([leaf.v for leaf in leaves])
+    turns, place = boxes((cosine, sine)), Box(place)
+    fence(turns, place, qkv_far)
+    cosine, sine = (turn.v for turn in turns)
+    leaves, tree = jax.tree.flatten((reach_rows, hot, lists_f, lists_b))
+    leaves = boxes(leaves)
     qkv_near = qkv.near_own(qkv_far) + qkv.near_rest(0)
     out_far = out_w.far(0, qkv_far)
     out_near = out_w.near_own(qkv_far)
@@ -1106,12 +1107,13 @@
             gate_far = gate.far(0, kv[1])
             out_other.update({j: over_tp(piece) for (j, _), piece in out_w.got.items()})
             top_grad_t = Box(held(cotangent, *kv).T)
-            fence(mark(place), kv, out_other[1], up_parts)
+            fence(mark(place), kv, out_other[1], up_parts, leaves)
         elif k == contexts - 1:
             fence(mark(place), kv, gate_far, top_grad_t)
             fence(kv, up_parts)
         else:
             fence(mark(place), kv)
+    reach_rows, hot, lists_f, lists_b = tree.unflatten([leaf.v for leaf in leaves])
     kv_back = jnp.concatenate([p.v for p in kv], axis=0)
     up_spread = up.spread()
     gate_far = gate.far(1, kv)

time: 864 us -> 868 us (level)
    unnamed x216 -> x214, local copies, waits for them, and re-layouts: 70.6 us -> 71.5 us
  transfers between devices with their start and end apart: 77 -> 77, of which waited for: 31 -> 32; matrix products, arithmetic and copies ran while one was open for 10% -> 10% of each run, Pallas kernels for 37% -> 36%
where the time goes in v6:
time: 868 us; the launch traced here: 859 us
  Pallas kernels  324 us (37%)
  waiting for transfers between devices  243 us (28%)
  starting transfers between devices  107 us (12%)
  local copies, waits for them, and re-layouts  95.5 us (11%)
  other arithmetic  74.9 us (9%)
  between operations  15.3 us (2%)
    ppermute x6, waiting for transfers between devices, inward(): lax.ppermute(self.own[slab].v, 'ctx', [(0, 1), (3, 2)])  80.1 us
    unnamed x214, local copies, waits for them, and re-layouts  71.5 us
    pallas_call x1, Pallas kernels, gate_up_back(): call(functools.partial(gate_up_back_kernel, gates, ups, downs, units % tf...  62.3 us
    pallas_call x4, Pallas kernels, weight_grad(): call(functools.partial(weight_grad_kernel, width // parts, parts), pl.cdi...  51.6 us
    ppermute x6, waiting for transfers between devices, outward(): lax.ppermute(self.own[slab].v, 'ctx', [(1, 0), (2, 3)])  49.8 us
    pallas_call x1, Pallas kernels, gate_up(): call(functools.partial(gate_up_kernel, gates, ups), pl.cdiv(units, tf), [...  40.3 us
    ppermute x12, waiting for transfers between devices, over_tp(): return Box(lax.ppermute(box.v, 'tp', across))  37.3 us
    ppermute x6, starting transfers between devices, inward(): lax.ppermute(self.own[slab].v, 'ctx', [(0, 1), (3, 2)])  35.2 us
  transfers between devices with their start and end apart: 77, of which 32 were waited for; matrix products, arithmetic and copies ran while one was open for 10% of the time, Pallas kernels for 36%

profile of v6, /device:TPU:0, one launch (start us, length us, event | category | flops | bytes accessed | tf_op | source)
XLA Modules:
  0.0 859.5 jit_solution(2397789339568849875)
XLA Ops:
  7.2 3.0 collective-permute-start
  24.1 3.1 fusion
  39.6 8.8 %mix.1 = (bf16[1024,768]{1,0:T(8,128)(2,1)S(1)}, bf16[1024,256]{1,0:T(8,128)(2,1)}, bf16[1536,1024]{1,0:T(8,128)(2,1)S(1)}) custom-call(s32[2]{0:T(128)S(1)} %copy-done.83, bf16[1024,1536]{1,0:T(8,128)(2,1)S(1)} %copy-done.11, bf16[1,1536]{1,0:T(2,128)(2,1)S(1)} %broadcast_in_dim.109.gain_ref, bf16[1,1024]{1,0:T(2,128)(2,1)S(1)} %broadcast_in_dim.110.bias_ref, ...), custom_call_target="tpu_custom_call" | custom-call | flops 1400000000 | bytes 1000 | tf_op jit(solution)/shard_map/mix/pallas_call | solution.py:538
  51.2 4.4 collective-permute-start.5
  58.6 7.7 collective-permute-done.5
  68.4 5.2 collective-permute-start.8
  75.3 7.6 collective-permute-done.8
  82.9 4.4 collective-permute-start.11
  87.4 4.7 copy.37
  93.2 3.3 collective-permute-done.11
  103.3 5.2 attention_forward.2
  108.5 5.2 collective-permute-done.13.refs_6_
  113.7 9.5 %collective-permute-done.14.refs_7_ = bf16[384,768]{1,0:T(8,128)(2,1)S(1)} collective-permute-done((bf16[384,768]{1,0:T(8,128)(2,1)S(1)}, bf16[384,768]{1,0:T(8,128)(2,1)S(1)}, u32[]{:S(2)}, u32[]{:S(2)}) %collective-permute-start.14) | collective-permute-done | bytes 589856 | tf_op jit(solution)/shard_map/ppermute | solution.py:1078
  125.0 9.8 %attention_forward.3 = (bf16[512,768]{1,0:T(8,128)(2,1)}, f32[6,512]{1,0:T(8,128)S(1)}, f32[6,512]{1,0:T(8,128)S(1)}) custom-call(s32[4]{0:T(128)S(1)} %get-tuple-element.343.count, s32[128]{0:T(128)S(1)} %reshape.678.chosen, s32[33]{0:T(128)S(1)} %pad_add_fusion.10.places, bf16[1024,768]{1,0:T(8,128)(2,1)S(1)} %copy-done.85, ...), custom_call_target="tpu_custom_call" | custom-call | flops 2624999936 | bytes 1000 | tf_op jit(solution)/shard_map/attention_forward/pallas_call | solution.py:94
  138.4 4.4 fusion.34
  144.8 11.0 %collective-permute-done.15.lower_ref = bf16[512,768]{1,0:T(8,128)(2,1)} collective-permute-done((bf16[512,768]{1,0:T(8,128)(2,1)}, bf16[512,768]{1,0:T(8,128)(2,1)}, u32[]{:S(2)}, u32[]{:S(2)}) %collective-permute-start.15) | collective-permute-done | bytes 786464 | tf_op jit(solution)/shard_map/ppermute | solution.py:1078
  156.7 9.6 %all-gather.3.cloned.1.call-done.refs_10_ = bf16[384,4480]{1,0:T(8,128)(2,1)} async-done(((bf16[96,4480]{1,0:T(8,128)(2,1)}), bf16[384,4480]{1,0:T(8,128)(2,1)}) %all-gather.3.cloned.1.call-update) | async-done | bytes 3440656 | tf_op jit(solution)/shard_map/all_gather | solution.py:860
  174.2 11.3 %branch.1 = (f32[1024,1536]{1,0:T(8,128)}, bf16[1024,1536]{1,0:T(8,128)(2,1)S(1)}, bf16[1536,1024]{1,0:T(8,128)(2,1)S(1)}) custom-call(s32[2]{0:T(128)S(1)} %copy-done.80, bf16[1024,1536]{1,0:T(8,128)(2,1)} %x_ref.7, bf16[1024,768]{1,0:T(8,128)(2,1)S(1)} %pad_maximum_fusion.own_ref.att_ref.right_ref, bf16[512,768]{1,0:T(8,128)(2,1)S(1)} %copy-done.66, ...), custom_call_target="tpu_custom_call" | custom-call | flops 2100000000 | bytes 1000 | tf_op jit(solution)/shard_map/branch/pallas_call | solution.py:605
  192.1 40.3 %gate_up.1 = (bf16[1024,4480]{1,0:T(8,128)(2,1)}, bf16[1024,4480]{1,0:T(8,128)(2,1)}, bf16[1024,4480]{1,0:T(8,128)(2,1)}) custom-call(s32[2]{0:T(128)} %mark.16.place.place_ref, bf16[1024,1536]{1,0:T(8,128)(2,1)} %copy-done.38, bf16[384,4480]{1,0:T(8,128)(2,1)} %refs_0_.9, bf16[384,4480]{1,0:T(8,128)(2,1)} %copy-done.90, ...), custom_call_target="tpu_custom_call" | custom-call | flops 7000000000 | bytes 1000 | tf_op jit(solution)/shard_map/gate_up/pallas_call | solution.py:312
  234.3 18.7 %whole_grad.1 = bf16[1536,4480]{1,0:T(8,128)(2,1)} custom-call(bf16[1536,1024]{1,0:T(8,128)(2,1)S(1)} %bitcast.30, bf16[1024,4480]{1,0:T(8,128)(2,1)} %get-tuple-element.435.right_ref.act_ref), custom_call_target="tpu_custom_call" | custom-call | flops 3324999936 | bytes 1000 | tf_op jit(solution)/shard_map/whole_grad/pallas_call | solution.py:392
  258.2 62.3 %gate_up_back.1 = (bf16[1024,4480]{1,0:T(8,128)(2,1)}, bf16[1024,4480]{1,0:T(8,128)(2,1)}, bf16[1024,384]{1,0:T(8,128)(2,1)}, bf16[1024,384]{1,0:T(8,128)(2,1)}, bf16[1024,768]{1,0:T(8,128)(2,1)}) custom-call(s32[2]{0:T(128)} %mark.17.place.place_ref, bf16[1024,1536]{1,0:T(8,128)(2,1)} %c_ref.3, bf16[1024,4480]{1,0:T(8,128)(2,1)} %get-tuple-element.409.by_gate_ref, ...), custom_call_target="tpu_custom_call" | custom-call | flops 10849999872 | bytes 1000 | tf_op jit(solution)/shard_map/gate_up_back/pallas_call | solution.py:368
  322.1 19.1 %weight_grad.4 = (bf16[768,4480]{1,0:T(8,128)(2,1)}, bf16[768,4480]{1,0:T(8,128)(2,1)}) custom-call(s32[2]{0:T(128)S(1)} %copy-done.79, bf16[1536,1024]{1,0:T(8,128)(2,1)S(1)} %copy-done.18, bf16[1024,4480]{1,0:T(8,128)(2,1)} %get-tuple-element.421.right_ref), custom_call_target="tpu_custom_call" | custom-call | flops 3324999936 | bytes 1000 | tf_op jit(solution)/shard_map/weight_grad/pallas_call | solution.py:415
  342.0 19.3 %weight_grad.5 = (bf16[768,4480]{1,0:T(8,128)(2,1)}, bf16[768,4480]{1,0:T(8,128)(2,1)}) custom-call(s32[2]{0:T(128)S(1)} %copy-done.79, bf16[1536,1024]{1,0:T(8,128)(2,1)S(1)} %copy-done.18, bf16[1024,4480]{1,0:T(8,128)(2,1)} %get-tuple-element.427.right_ref), custom_call_target="tpu_custom_call" | custom-call | flops 3324999936 | bytes 1000 | tf_op jit(solution)/shard_map/weight_grad/pallas_call | solution.py:415
  376.2 23.7 %down_project.1 = bf16[1024,1536]{1,0:T(8,128)(2,1)} custom-call(s32[2]{0:T(128)S(1)} %copy-done.79, bf16[1024,4480]{1,0:T(8,128)(2,1)} %get-tuple-element.435.right_ref.act_ref, bf16[384,4480]{1,0:T(8,128)(2,1)} %refs_0_.10, bf16[384,4480]{1,0:T(8,128)(2,1)} %collective-permute-done.28.refs_13_.refs_1_, bf16[96,4480]{1,0:T(8,128)(2,1)S(1)} %copy-done.37, ...), custom_call_target="tpu_custom_call" | custom-call | flops 4200000000 | bytes 1000 | tf_op jit(solution)/shard_map/down_project/pallas_call | solution.py:493
  418.9 13.5 %middle_back.1 = (f32[1024,1536]{1,0:T(8,128)}, bf16[1536,1024]{1,0:T(8,128)(2,1)}, bf16[1024,768]{1,0:T(8,128)(2,1)}, f32[6,1024]{1,0:T(8,128)S(1)}, f32[1,1536]{1,0:T(1,128)S(1)}) custom-call(s32[2]{0:T(128)S(1)} %copy-done.79, f32[1024,1536]{1,0:T(8,128)} %get-tuple-element.468.mid_ref, bf16[1024,1536]{1,0:T(8,128)(2,1)} %c_ref.3, ...), custom_call_target="tpu_custom_call" | custom-call | flops 2275000064 | bytes 1000 | tf_op jit(solution)/shard_map/middle_back/pallas_call | solution.py:667
  432.4 6.1 weight_grad.6
  438.5 3.4 copy-done.9
  442.0 3.4 add_rows.15
  445.4 3.5 collective-permute-start.40
  450.5 19.2 %attention_backward.1 = (bf16[1024,768]{1,0:T(8,128)(2,1)S(1)}, bf16[4096,256]{1,0:T(8,128)(2,1)}) custom-call(s32[4]{0:T(128)S(1)} %get-tuple-element.453.count, s32[32]{0:T(128)S(1)} %reshape.679.chosen, s32[9]{0:T(128)S(1)} %pad_add_fusion.11.places, bf16[1024,768]{1,0:T(8,128)(2,1)S(1)} %copy-done.86, bf16[1024,768]{1,0:T(8,128)(2,1)S(1)} %copy-done.87, ...), custom_call_target="tpu_custom_call" | custom-call | flops 9450000384 | bytes 1000 | tf_op jit(solution)/shard_map/attention_backward/pallas_call | solution.py:186
  471.9 44.9 %collective-permute-done.40 = bf16[192,4480]{1,0:T(8,128)(2,1)} collective-permute-done((bf16[192,4480]{1,0:T(8,128)(2,1)S(1)}, bf16[192,4480]{1,0:T(8,128)(2,1)}, u32[]{:S(2)}, u32[]{:S(2)}) %collective-permute-start.40) | collective-permute-done | bytes 1720352 | tf_op jit(solution)/shard_map/ppermute | solution.py:959
  516.8 3.2 add.247
  527.5 8.6 collective-permute-start.46
  541.3 6.7 add_convert_fusion
  549.2 5.1 collective-permute-done.44
  554.3 16.8 %collective-permute-done.46 = bf16[192,4480]{1,0:T(8,128)(2,1)} collective-permute-done((bf16[192,4480]{1,0:T(8,128)(2,1)S(1)}, bf16[192,4480]{1,0:T(8,128)(2,1)}, u32[]{:S(2)}, u32[]{:S(2)}) %collective-permute-start.46) | collective-permute-done | bytes 1720352 | tf_op jit(solution)/shard_map/ppermute | solution.py:959
  576.9 18.9 %collective-permute-done.47 = bf16[1024,256]{1,0:T(8,128)(2,1)S(1)} collective-permute-done((bf16[1024,256]{1,0:T(8,128)(2,1)S(1)}, bf16[1024,256]{1,0:T(8,128)(2,1)S(1)}, u32[]{:S(2)}, u32[]{:S(2)}) %collective-permute-start.47) | collective-permute-done | bytes 524320 | tf_op jit(solution)/shard_map/ppermute | solution.py:1215
  605.8 4.2 add_rows.17
  618.8 7.8 mix_back.1
  631.6 3.8 add.254
  636.7 3.1 add.252
  641.6 10.5 %collective-permute-start.54 = (bf16[192,4480]{1,0:T(8,128)(2,1)}, bf16[192,4480]{1,0:T(8,128)(2,1)}, u32[]{:S(2)}, u32[]{:S(2)}) collective-permute-start(bf16[192,4480]{1,0:T(8,128)(2,1)} %add_rows.17), channel_id=1, source_target_pairs={{0,2},{6,4},{1,3},{7,5},{8,10},{14,12},{9,11},{15,13},{16,18},{22,... | collective-permute-start | bytes 5160968 | tf_op jit(solution)/shard_map/ppermute | solution.py:959
  660.4 7.1 weight_grad.7
  675.2 13.9 %collective-permute-done.54 = bf16[192,4480]{1,0:T(8,128)(2,1)} collective-permute-done((bf16[192,4480]{1,0:T(8,128)(2,1)}, bf16[192,4480]{1,0:T(8,128)(2,1)}, u32[]{:S(2)}, u32[]{:S(2)}) %collective-permute-start.54) | collective-permute-done | bytes 1720352 | tf_op jit(solution)/shard_map/ppermute | solution.py:959
  689.2 3.6 add.258
  692.7 3.7 add.256
  701.1 4.4 add_rows.19
  706.7 3.7 collective-permute-done.60
  710.8 5.5 convert_element_type.69
  716.3 3.0 add_rows.20.refs_0_
  722.7 7.3 collective-permute-done.61.refs_1_
  732.5 3.6 add.260
  736.1 3.1 add.259
  739.3 3.3 add_rows.21
  742.6 4.4 collective-permute-start.65
  753.0 5.7 collective-permute-start.66
  762.8 4.4 collective-permute-done.66
  767.2 7.1 collective-permute-done.67.refs_5_
  774.3 9.8 %collective-permute-done.68 = bf16[192,4480]{1,0:T(8,128)(2,1)} collective-permute-done((bf16[192,4480]{1,0:T(8,128)(2,1)}, bf16[192,4480]{1,0:T(8,128)(2,1)}, u32[]{:S(2)}, u32[]{:S(2)}) %collective-permute-start.68) | collective-permute-done | bytes 1720352 | tf_op jit(solution)/shard_map/ppermute | solution.py:973
  788.1 3.3 maximum_convert_fusion
  796.6 7.7 input_back.1
  804.3 19.9 %collective-permute-done.71 = bf16[192,4480]{1,0:T(8,128)(2,1)S(1)} collective-permute-done((bf16[192,4480]{1,0:T(8,128)(2,1)S(1)}, bf16[192,4480]{1,0:T(8,128)(2,1)S(1)}, u32[]{:S(2)}, u32[]{:S(2)}) %collective-permute-start.71) | collective-permute-done | bytes 1720352 | tf_op jit(solution)/shard_map/ppermute | solution.py:973
  827.3 3.3 maximum_convert_fusion.1
  830.7 17.6 %collective-permute-done.72 = f32[5312]{0:T(1024)S(1)} collective-permute-done((f32[5312]{0:T(1024)S(1)}, f32[5312]{0:T(1024)S(1)}, u32[]{:S(2)}, u32[]{:S(2)}) %collective-permute-start.72) | collective-permute-done | bytes 21280 | tf_op jit(solution)/shard_map/ppermute | solution.py:973
  (471 shorter events, 214.3 us)
Async XLA Ops:
  7.2 159.1 %all-gather.3.cloned.1.call-start = ((), (), s32[]{:S(2)}) async-start(), calls=%async_computation.1 | async-start | bytes 4300800 | tf_op jit(solution)/shard_map/all_gather | solution.py:860
  7.2 20.9 %collective-permute-start = (bf16[384,1024]{1,0:T(8,128)(2,1)}, bf16[384,1024]{1,0:T(8,128)(2,1)}, u32[]{:S(2)}, u32[]{:S(2)}) collective-permute-start(bf16[384,1024]{1,0:T(8,128)(2,1)} %refs_0_.11), channel_id=1, source_target_pairs={{0,16},{8,24},{16,0},{24,8},{1,17},{9,25},{17,1},{25,9},{2,18},{10... | collective-permute-start | bytes 2359304 | tf_op jit(solution)/shard_map/ppermute | solution.py:813
  30.1 28.4 %collective-permute-start.7 = (bf16[384,768]{1,0:T(8,128)(2,1)}, bf16[384,768]{1,0:T(8,128)(2,1)}, u32[]{:S(2)}, u32[]{:S(2)}) collective-permute-start(bf16[384,768]{1,0:T(8,128)(2,1)} %refs_6_.1), channel_id=1, source_target_pairs={{0,1},{1,0},{2,3},{3,2},{4,5},{5,4},{6,7},{7,6},{8,9},{9,8},{10,11... | collective-permute-start | bytes 1769480 | tf_op jit(solution)/shard_map/ppermute | solution.py:1089
  32.0 19.2 %collective-permute-start.3 = (bf16[384,768]{1,0:T(8,128)(2,1)}, bf16[384,768]{1,0:T(8,128)(2,1)}, u32[]{:S(2)}, u32[]{:S(2)}) collective-permute-start(bf16[384,768]{1,0:T(8,128)(2,1)} %refs_6_.1), channel_id=1, source_target_pairs={{0,8},{8,0},{16,24},{24,16},{1,9},{9,1},{17,25},{25,17},{2,10},{10... | collective-permute-start | bytes 1769480 | tf_op jit(solution)/shard_map/ppermute | solution.py:813
  32.0 23.6 %collective-permute-start.4 = (bf16[384,768]{1,0:T(8,128)(2,1)}, bf16[384,768]{1,0:T(8,128)(2,1)}, u32[]{:S(2)}, u32[]{:S(2)}) collective-permute-start(bf16[384,768]{1,0:T(8,128)(2,1)} %refs_6_.1), channel_id=1, source_target_pairs={{0,16},{8,24},{16,0},{24,8},{1,17},{9,25},{17,1},{25,9},{2,18},{10... | collective-permute-start | bytes 1769480 | tf_op jit(solution)/shard_map/ppermute | solution.py:813
  36.9 46.1 %collective-permute-start.10 = (bf16[96,4480]{1,0:T(8,128)(2,1)}, bf16[96,4480]{1,0:T(8,128)(2,1)}, u32[]{:S(2)}, u32[]{:S(2)}) collective-permute-start(bf16[96,4480]{1,0:T(8,128)(2,1)} %constant_dynamic-slice_fusion.1), channel_id=1, source_target_pairs={{0,16},{8,24},{16,0},{24,8},{1,17},{9,25},{17,1},{25,9},{2,18},{10... | collective-permute-start | bytes 2580488 | tf_op jit(solution)/shard_map/ppermute | solution.py:813
  51.2 15.2 %collective-permute-start.5 = (bf16[1024,256]{1,0:T(8,128)(2,1)}, bf16[1024,256]{1,0:T(8,128)(2,1)}, u32[]{:S(2)}, u32[]{:S(2)}) collective-permute-start(bf16[1024,256]{1,0:T(8,128)(2,1)} %get-tuple-element.332), channel_id=1, source_target_pairs={{0,2},{2,4},{4,6},{1,3},{3,5},{5,7},{8,10},{10,12},{12,14},{9,11},... | collective-permute-start | bytes 1572872 | tf_op jit(solution)/shard_map/ppermute | solution.py:1101
  66.3 30.2 %collective-permute-start.12 = (bf16[128,4480]{1,0:T(8,128)(2,1)}, bf16[128,4480]{1,0:T(8,128)(2,1)}, u32[]{:S(2)}, u32[]{:S(2)}) collective-permute-start(bf16[128,4480]{1,0:T(8,128)(2,1)} %get-tuple-element.325), channel_id=1, source_target_pairs={{0,16},{8,24},{16,0},{24,8},{1,17},{9,25},{17,1},{25,9},{2,18},{10... | collective-permute-start | bytes 3440648 | tf_op jit(solution)/shard_map/ppermute | solution.py:813
  67.9 15.0 %collective-permute-start.9 = (bf16[384,768]{1,0:T(8,128)(2,1)}, bf16[384,768]{1,0:T(8,128)(2,1)S(1)}, u32[]{:S(2)}, u32[]{:S(2)}) collective-permute-start(bf16[384,768]{1,0:T(8,128)(2,1)} %collective-permute-done.3.refs_1_.refs_7_), channel_id=1, source_target_pairs={{0,1},{1,0},{2,3},{3,2},{4,5},{5,4},{6,7},{7,6},{8,9},{9,8},{10,11... | collective-permute-start | bytes 1769480 | tf_op jit(solution)/shard_map/ppermute | solution.py:1078
  68.4 14.5 %collective-permute-start.8 = (bf16[1024,256]{1,0:T(8,128)(2,1)}, bf16[1024,256]{1,0:T(8,128)(2,1)}, u32[]{:S(2)}, u32[]{:S(2)}) collective-permute-start(bf16[1024,256]{1,0:T(8,128)(2,1)} %collective-permute-done.5), channel_id=1, source_target_pairs={{0,2},{2,4},{4,6},{1,3},{3,5},{5,7},{8,10},{10,12},{12,14},{9,11},... | collective-permute-start | bytes 1572872 | tf_op jit(solution)/shard_map/ppermute | solution.py:1101
  96.6 309.6 %reduce-scatter.2.cloned.1.call-start = ((), (), s32[]{:S(2)}) async-start(), calls=%async_computation.2 | async-start | bytes 14622720 | tf_op jit(solution)/shard_map/reduce_scatter | solution.py:1162
  97.2 16.5 %collective-permute-start.13 = (bf16[384,768]{1,0:T(8,128)(2,1)}, bf16[384,768]{1,0:T(8,128)(2,1)S(1)}, u32[]{:S(2)}, u32[]{:S(2)}) collective-permute-start(bf16[384,768]{1,0:T(8,128)(2,1)} %collective-permute-done.4.refs_2_.refs_8_), channel_id=1, source_target_pairs={{0,1},{1,0},{2,3},{3,2},{4,5},{5,4},{6,7},{7,6},{8,9},{9,8},{10,11... | collective-permute-start | bytes 1769480 | tf_op jit(solution)/shard_map/ppermute | solution.py:1078
  98.9 24.3 %collective-permute-start.14 = (bf16[384,768]{1,0:T(8,128)(2,1)S(1)}, bf16[384,768]{1,0:T(8,128)(2,1)S(1)}, u32[]{:S(2)}, u32[]{:S(2)}) collective-permute-start(bf16[384,768]{1,0:T(8,128)(2,1)S(1)} %collective-permute-done.6.refs_3_.refs_9_), channel_id=1, source_target_pairs={{0,1},{1,0},{2,3},{3,2},{4,5},{5,4},{6,7},{7,6},{8,9},{9,8},{10,11... | collective-permute-start | bytes 1769480 | tf_op jit(solution)/shard_map/ppermute | solution.py:1078
  99.3 39.1 %collective-permute-start.19 = (bf16[128,4480]{1,0:T(8,128)(2,1)}, bf16[128,4480]{1,0:T(8,128)(2,1)}, u32[]{:S(2)}, u32[]{:S(2)}) collective-permute-start(bf16[128,4480]{1,0:T(8,128)(2,1)} %get-tuple-element.355), channel_id=1, source_target_pairs={{0,16},{8,24},{16,0},{24,8},{1,17},{9,25},{17,1},{25,9},{2,18},{10... | collective-permute-start | bytes 3440648 | tf_op jit(solution)/shard_map/ppermute | solution.py:813
  99.8 56.0 %collective-permute-start.18 = (bf16[128,4480]{1,0:T(8,128)(2,1)}, bf16[128,4480]{1,0:T(8,128)(2,1)}, u32[]{:S(2)}, u32[]{:S(2)}) collective-permute-start(bf16[128,4480]{1,0:T(8,128)(2,1)} %collective-permute-done.12.refs_2_), channel_id=1, source_target_pairs={{0,8},{8,0},{16,24},{24,16},{1,9},{9,1},{17,25},{25,17},{2,10},{10... | collective-permute-start | bytes 3440648 | tf_op jit(solution)/shard_map/ppermute | solution.py:813
  123.2 20.7 %collective-permute-start.16 = (bf16[512,768]{1,0:T(8,128)(2,1)}, bf16[512,768]{1,0:T(8,128)(2,1)S(1)}, u32[]{:S(2)}, u32[]{:S(2)}) collective-permute-start(bf16[512,768]{1,0:T(8,128)(2,1)} %get-tuple-element.357), channel_id=1, source_target_pairs={{0,1},{1,0},{2,3},{3,2},{4,5},{5,4},{6,7},{7,6},{8,9},{9,8},{10,11... | collective-permute-start | bytes 2359304 | tf_op jit(solution)/shard_map/ppermute | solution.py:1078
  134.7 21.1 %collective-permute-start.15 = (bf16[512,768]{1,0:T(8,128)(2,1)}, bf16[512,768]{1,0:T(8,128)(2,1)}, u32[]{:S(2)}, u32[]{:S(2)}) collective-permute-start(bf16[512,768]{1,0:T(8,128)(2,1)} %get-tuple-element.349), channel_id=1, source_target_pairs={{0,1},{1,0},{2,3},{3,2},{4,5},{5,4},{6,7},{7,6},{8,9},{9,8},{10,11... | collective-permute-start | bytes 2359304 | tf_op jit(solution)/shard_map/ppermute | solution.py:1078
  135.0 21.7 %collective-permute-start.17 = (bf16[128,4480]{1,0:T(8,128)(2,1)}, bf16[128,4480]{1,0:T(8,128)(2,1)}, u32[]{:S(2)}, u32[]{:S(2)}) collective-permute-start(bf16[128,4480]{1,0:T(8,128)(2,1)} %get-tuple-element.352), channel_id=1, source_target_pairs={{0,16},{8,24},{16,0},{24,8},{1,17},{9,25},{17,1},{25,9},{2,18},{10... | collective-permute-start | bytes 3440648 | tf_op jit(solution)/shard_map/ppermute | solution.py:813
  138.3 18.4 %collective-permute-start.20 = (bf16[128,4480]{1,0:T(8,128)(2,1)}, bf16[128,4480]{1,0:T(8,128)(2,1)}, u32[]{:S(2)}, u32[]{:S(2)}) collective-permute-start(bf16[128,4480]{1,0:T(8,128)(2,1)} %collective-permute-done.19.refs_3_), channel_id=1, source_target_pairs={{0,8},{8,0},{16,24},{24,16},{1,9},{9,1},{17,25},{25,17},{2,10},{10... | collective-permute-start | bytes 3440648 | tf_op jit(solution)/shard_map/ppermute | solution.py:813
  166.3 22.6 %collective-permute-start.24 = (bf16[384,4480]{1,0:T(8,128)(2,1)}, bf16[384,4480]{1,0:T(8,128)(2,1)S(1)}, u32[]{:S(2)}, u32[]{:S(2)}) collective-permute-start(bf16[384,4480]{1,0:T(8,128)(2,1)} %refs_8_.3), channel_id=1, source_target_pairs={{0,8},{8,0},{16,24},{24,16},{1,9},{9,1},{17,25},{25,17},{2,10},{10... | collective-permute-start | bytes 10321928 | tf_op jit(solution)/shard_map/ppermute | solution.py:813
  166.3 22.6 %collective-permute-start.23 = (bf16[384,4480]{1,0:T(8,128)(2,1)}, bf16[384,4480]{1,0:T(8,128)(2,1)S(1)}, u32[]{:S(2)}, u32[]{:S(2)}) collective-permute-start(bf16[384,4480]{1,0:T(8,128)(2,1)} %refs_0_.9), channel_id=1, source_target_pairs={{0,8},{8,0},{16,24},{24,16},{1,9},{9,1},{17,25},{25,17},{2,10},{10... | collective-permute-start | bytes 10321928 | tf_op jit(solution)/shard_map/ppermute | solution.py:813
  166.8 22.1 %collective-permute-start.22 = (bf16[384,4480]{1,0:T(8,128)(2,1)}, bf16[384,4480]{1,0:T(8,128)(2,1)}, u32[]{:S(2)}, u32[]{:S(2)}) collective-permute-start(bf16[384,4480]{1,0:T(8,128)(2,1)} %all-gather.3.cloned.1.call-done.refs_10_), channel_id=1, source_target_pairs={{0,8},{8,0},{16,24},{24,16},{1,9},{9,1},{17,25},{25,17},{2,10},{10... | collective-permute-start | bytes 10321928 | tf_op jit(solution)/shard_map/ppermute | solution.py:813
  166.8 22.0 %collective-permute-start.21 = (bf16[128,4480]{1,0:T(8,128)(2,1)}, bf16[128,4480]{1,0:T(8,128)(2,1)S(1)}, u32[]{:S(2)}, u32[]{:S(2)}) collective-permute-start(bf16[128,4480]{1,0:T(8,128)(2,1)} %collective-permute-done.17.refs_4_), channel_id=1, source_target_pairs={{0,8},{8,0},{16,24},{24,16},{1,9},{9,1},{17,25},{25,17},{2,10},{10... | collective-permute-start | bytes 3440648 | tf_op jit(solution)/shard_map/ppermute | solution.py:813
  167.3 21.5 %collective-permute-start.25 = (bf16[96,4480]{1,0:T(8,128)(2,1)}, bf16[96,4480]{1,0:T(8,128)(2,1)S(1)}, u32[]{:S(2)}, u32[]{:S(2)}) collective-permute-start(bf16[96,4480]{1,0:T(8,128)(2,1)} %get-tuple-element.376), channel_id=1, source_target_pairs={{0,16},{8,24},{16,0},{24,8},{1,17},{9,25},{17,1},{25,9},{2,18},{10... | collective-permute-start | bytes 2580488 | tf_op jit(solution)/shard_map/ppermute | solution.py:813
  188.9 43.5 %collective-permute-start.28 = (bf16[384,4480]{1,0:T(8,128)(2,1)}, bf16[384,4480]{1,0:T(8,128)(2,1)}, u32[]{:S(2)}, u32[]{:S(2)}) collective-permute-start(bf16[384,4480]{1,0:T(8,128)(2,1)} %refs_0_.10), channel_id=1, source_target_pairs={{0,8},{8,0},{16,24},{24,16},{1,9},{9,1},{17,25},{25,17},{2,10},{10... | collective-permute-start | bytes 10321928 | tf_op jit(solution)/shard_map/ppermute | solution.py:813
  189.0 43.4 %collective-permute-start.27 = (bf16[96,4480]{1,0:T(8,128)(2,1)}, bf16[96,4480]{1,0:T(8,128)(2,1)}, u32[]{:S(2)}, u32[]{:S(2)}) collective-permute-start(bf16[96,4480]{1,0:T(8,128)(2,1)} %get-tuple-element.391), channel_id=1, source_target_pairs={{0,16},{8,24},{16,0},{24,8},{1,17},{9,25},{17,1},{25,9},{2,18},{10... | collective-permute-start | bytes 2580488 | tf_op jit(solution)/shard_map/ppermute | solution.py:813
  190.2 42.2 %collective-permute-start.26 = (bf16[96,4480]{1,0:T(8,128)(2,1)}, bf16[96,4480]{1,0:T(8,128)(2,1)}, u32[]{:S(2)}, u32[]{:S(2)}) collective-permute-start(bf16[96,4480]{1,0:T(8,128)(2,1)} %get-tuple-element.388), channel_id=1, source_target_pairs={{0,16},{8,24},{16,0},{24,8},{1,17},{9,25},{17,1},{25,9},{2,18},{10... | collective-permute-start | bytes 2580488 | tf_op jit(solution)/shard_map/ppermute | solution.py:813
  232.5 20.6 %collective-permute-start.29 = (bf16[96,4480]{1,0:T(8,128)(2,1)S(1)}, bf16[96,4480]{1,0:T(8,128)(2,1)}, u32[]{:S(2)}, u32[]{:S(2)}) collective-permute-start(bf16[96,4480]{1,0:T(8,128)(2,1)S(1)} %collective-permute-done.25.refs_14_.refs_2_), channel_id=1, source_target_pairs={{0,8},{8,0},{16,24},{24,16},{1,9},{9,1},{17,25},{25,17},{2,10},{10... | collective-permute-start | bytes 2580488 | tf_op jit(solution)/shard_map/ppermute | solution.py:813
  232.6 21.9 %collective-permute-start.32 = (bf16[96,4480]{1,0:T(8,128)(2,1)}, bf16[96,4480]{1,0:T(8,128)(2,1)}, u32[]{:S(2)}, u32[]{:S(2)}) collective-permute-start(bf16[96,4480]{1,0:T(8,128)(2,1)} %get-tuple-element.404), channel_id=1, source_target_pairs={{0,16},{8,24},{16,0},{24,8},{1,17},{9,25},{17,1},{25,9},{2,18},{10... | collective-permute-start | bytes 2580488 | tf_op jit(solution)/shard_map/ppermute | solution.py:813
  233.8 20.6 %collective-permute-start.30 = (bf16[96,4480]{1,0:T(8,128)(2,1)}, bf16[96,4480]{1,0:T(8,128)(2,1)}, u32[]{:S(2)}, u32[]{:S(2)}) collective-permute-start(bf16[96,4480]{1,0:T(8,128)(2,1)} %collective-permute-done.26.refs_15_.refs_3_), channel_id=1, source_target_pairs={{0,8},{8,0},{16,24},{24,16},{1,9},{9,1},{17,25},{25,17},{2,10},{10... | collective-permute-start | bytes 2580488 | tf_op jit(solution)/shard_map/ppermute | solution.py:813
  234.0 20.4 %collective-permute-start.31 = (bf16[96,4480]{1,0:T(8,128)(2,1)}, bf16[96,4480]{1,0:T(8,128)(2,1)}, u32[]{:S(2)}, u32[]{:S(2)}) collective-permute-start(bf16[96,4480]{1,0:T(8,128)(2,1)} %collective-permute-done.27.refs_16_.refs_4_), channel_id=1, source_target_pairs={{0,8},{8,0},{16,24},{24,16},{1,9},{9,1},{17,25},{25,17},{2,10},{10... | collective-permute-start | bytes 2580488 | tf_op jit(solution)/shard_map/ppermute | solution.py:813
  254.4 357.3 %all-gather.5.cloned.1.call-start = ((), (), s32[]{:S(2)}) async-start(), calls=%async_computation.3 | async-start | bytes 4300800 | tf_op jit(solution)/shard_map/all_gather | solution.py:1187
  320.6 20.7 %collective-permute-start.34 = (bf16[1024,384]{1,0:T(8,128)(2,1)}, bf16[1024,384]{1,0:T(8,128)(2,1)S(1)}, u32[]{:S(2)}, u32[]{:S(2)}) collective-permute-start(bf16[1024,384]{1,0:T(8,128)(2,1)} %get-tuple-element.424.refs_0_), channel_id=1, source_target_pairs={{0,1},{1,0},{2,3},{3,2},{4,5},{5,4},{6,7},{7,6},{8,9},{9,8},{10,11... | collective-permute-start | bytes 2359304 | tf_op jit(solution)/shard_map/ppermute | solution.py:1078
  341.2 20.9 %collective-permute-start.35 = (bf16[768,4480]{1,0:T(8,128)(2,1)}, bf16[768,4480]{1,0:T(8,128)(2,1)S(1)}, u32[]{:S(2)}, u32[]{:S(2)}) collective-permute-start(bf16[768,4480]{1,0:T(8,128)(2,1)} %get-tuple-element.429), channel_id=1, source_target_pairs={{0,8},{8,0},{16,24},{24,16},{1,9},{9,1},{17,25},{25,17},{2,10},{10... | collective-permute-start | bytes 20643848 | tf_op jit(solution)/shard_map/ppermute | solution.py:813
  341.3 20.0 %collective-permute-start.36 = (bf16[1024,384]{1,0:T(8,128)(2,1)S(1)}, bf16[1024,384]{1,0:T(8,128)(2,1)S(1)}, u32[]{:S(2)}, u32[]{:S(2)}) collective-permute-start(bf16[1024,384]{1,0:T(8,128)(2,1)S(1)} %copy-done.60), channel_id=1, source_target_pairs={{0,1},{1,0},{2,3},{3,2},{4,5},{5,4},{6,7},{7,6},{8,9},{9,8},{10,11... | collective-permute-start | bytes 2359304 | tf_op jit(solution)/shard_map/ppermute | solution.py:1078
  365.1 37.1 %collective-permute-start.37 = (bf16[768,4480]{1,0:T(8,128)(2,1)}, bf16[768,4480]{1,0:T(8,128)(2,1)S(1)}, u32[]{:S(2)}, u32[]{:S(2)}) collective-permute-start(bf16[768,4480]{1,0:T(8,128)(2,1)} %get-tuple-element.436), channel_id=1, source_target_pairs={{0,8},{8,0},{16,24},{24,16},{1,9},{9,1},{17,25},{25,17},{2,10},{10... | collective-permute-start | bytes 20643848 | tf_op jit(solution)/shard_map/ppermute | solution.py:813
  365.2 37.0 %collective-permute-start.38 = (bf16[1024,768]{1,0:T(8,128)(2,1)}, bf16[1024,768]{1,0:T(8,128)(2,1)}, u32[]{:S(2)}, u32[]{:S(2)}) collective-permute-start(bf16[1024,768]{1,0:T(8,128)(2,1)} %get-tuple-element.437.refs_2_), channel_id=1, source_target_pairs={{0,1},{1,0},{2,3},{3,2},{4,5},{5,4},{6,7},{7,6},{8,9},{9,8},{10,11... | collective-permute-start | bytes 4718600 | tf_op jit(solution)/shard_map/ppermute | solution.py:1078
  375.0 63.5 %collective-permute-start.39 = (bf16[192,4480]{1,0:T(8,128)(2,1)}, bf16[192,4480]{1,0:T(8,128)(2,1)}, u32[]{:S(2)}, u32[]{:S(2)}) collective-permute-start(bf16[192,4480]{1,0:T(8,128)(2,1)} %add_rows.11), channel_id=1, source_target_pairs={{0,16},{8,24},{16,0},{24,8},{1,17},{9,25},{17,1},{25,9},{2,18},{10... | collective-permute-start | bytes 5160968 | tf_op jit(solution)/shard_map/ppermute | solution.py:813
  406.2 110.6 %collective-permute-start.43 = (bf16[1024,1536]{1,0:T(8,128)(2,1)}, bf16[1024,1536]{1,0:T(8,128)(2,1)}, u32[]{:S(2)}, u32[]{:S(2)}) collective-permute-start(bf16[1024,1536]{1,0:T(8,128)(2,1)} %down_project.1), channel_id=1, source_target_pairs={{0,1},{1,0},{2,3},{3,2},{4,5},{5,4},{6,7},{7,6},{8,9},{9,8},{10,11... | collective-permute-start | bytes 9437192 | tf_op jit(solution)/shard_map/ppermute | solution.py:1078
  407.6 63.2 %collective-permute-start.41 = (bf16[192,4480]{1,0:T(8,128)(2,1)S(1)}, bf16[192,4480]{1,0:T(8,128)(2,1)}, u32[]{:S(2)}, u32[]{:S(2)}) collective-permute-start(bf16[192,4480]{1,0:T(8,128)(2,1)S(1)} %add_rows.12), channel_id=1, source_target_pairs={{0,16},{8,24},{16,0},{24,8},{1,17},{9,25},{17,1},{25,9},{2,18},{10... | collective-permute-start | bytes 5160968 | tf_op jit(solution)/shard_map/ppermute | solution.py:813
  445.4 71.4 %collective-permute-start.40 = (bf16[192,4480]{1,0:T(8,128)(2,1)S(1)}, bf16[192,4480]{1,0:T(8,128)(2,1)}, u32[]{:S(2)}, u32[]{:S(2)}) collective-permute-start(bf16[192,4480]{1,0:T(8,128)(2,1)S(1)} %add_rows.15), channel_id=1, source_target_pairs={{0,2},{6,4},{1,3},{7,5},{8,10},{14,12},{9,11},{15,13},{16,18},{22,... | collective-permute-start | bytes 5160968 | tf_op jit(solution)/shard_map/ppermute | solution.py:959
  449.0 21.9 %collective-permute-start.42 = (bf16[768,768]{1,0:T(8,128)(2,1)}, bf16[768,768]{1,0:T(8,128)(2,1)S(1)}, u32[]{:S(2)}, u32[]{:S(2)}) collective-permute-start(bf16[768,768]{1,0:T(8,128)(2,1)} %get-tuple-element.463), channel_id=1, source_target_pairs={{0,8},{8,0},{16,24},{24,16},{1,9},{9,1},{17,25},{25,17},{2,10},{10... | collective-permute-start | bytes 3538952 | tf_op jit(solution)/shard_map/ppermute | solution.py:813
  525.7 28.7 %collective-permute-start.45 = (bf16[192,4480]{1,0:T(8,128)(2,1)}, bf16[192,4480]{1,0:T(8,128)(2,1)}, u32[]{:S(2)}, u32[]{:S(2)}) collective-permute-start(bf16[192,4480]{1,0:T(8,128)(2,1)} %add.247), channel_id=1, source_target_pairs={{2,4},{4,2},{3,5},{5,3},{10,12},{12,10},{11,13},{13,11},{18,20},{2... | collective-permute-start | bytes 5160968 | tf_op jit(solution)/shard_map/ppermute | solution.py:966
  527.5 43.6 %collective-permute-start.46 = (bf16[192,4480]{1,0:T(8,128)(2,1)S(1)}, bf16[192,4480]{1,0:T(8,128)(2,1)}, u32[]{:S(2)}, u32[]{:S(2)}) collective-permute-start(bf16[192,4480]{1,0:T(8,128)(2,1)S(1)} %add_rows.16), channel_id=1, source_target_pairs={{0,2},{6,4},{1,3},{7,5},{8,10},{14,12},{9,11},{15,13},{16,18},{22,... | collective-permute-start | bytes 5160968 | tf_op jit(solution)/shard_map/ppermute | solution.py:959
  536.1 40.8 %collective-permute-start.48 = (bf16[192,4480]{1,0:T(8,128)(2,1)}, bf16[192,4480]{1,0:T(8,128)(2,1)}, u32[]{:S(2)}, u32[]{:S(2)}) collective-permute-start(bf16[192,4480]{1,0:T(8,128)(2,1)} %add_rows.13), channel_id=1, source_target_pairs={{0,16},{8,24},{16,0},{24,8},{1,17},{9,25},{17,1},{25,9},{2,18},{10... | collective-permute-start | bytes 5160968 | tf_op jit(solution)/shard_map/ppermute | solution.py:813
  537.6 74.1 %collective-permute-start.50 = (bf16[192,4480]{1,0:T(8,128)(2,1)}, bf16[192,4480]{1,0:T(8,128)(2,1)}, u32[]{:S(2)}, u32[]{:S(2)}) collective-permute-start(bf16[192,4480]{1,0:T(8,128)(2,1)} %add_rows.14), channel_id=1, source_target_pairs={{0,16},{8,24},{16,0},{24,8},{1,17},{9,25},{17,1},{25,9},{2,18},{10... | collective-permute-start | bytes 5160968 | tf_op jit(solution)/shard_map/ppermute | solution.py:813
  572.2 23.6 %collective-permute-start.47 = (bf16[1024,256]{1,0:T(8,128)(2,1)S(1)}, bf16[1024,256]{1,0:T(8,128)(2,1)S(1)}, u32[]{:S(2)}, u32[]{:S(2)}) collective-permute-start(bf16[1024,256]{1,0:T(8,128)(2,1)S(1)} %slice_add_fusion.2), channel_id=1, source_target_pairs={{2,0},{4,2},{6,4},{3,1},{5,3},{7,5},{10,8},{12,10},{14,12},{11,9},... | collective-permute-start | bytes 1572872 | tf_op jit(solution)/shard_map/ppermute | solution.py:1215
  596.9 15.3 %collective-permute-start.49 = (bf16[1024,256]{1,0:T(8,128)(2,1)S(1)}, bf16[1024,256]{1,0:T(8,128)(2,1)S(1)}, u32[]{:S(2)}, u32[]{:S(2)}) collective-permute-start(bf16[1024,256]{1,0:T(8,128)(2,1)S(1)} %slice_add_fusion.1), channel_id=1, source_target_pairs={{2,0},{4,2},{6,4},{3,1},{5,3},{7,5},{10,8},{12,10},{14,12},{11,9},... | collective-permute-start | bytes 1572872 | tf_op jit(solution)/shard_map/ppermute | solution.py:1215
  630.0 37.5 %collective-permute-start.51 = (bf16[1024,384]{1,0:T(8,128)(2,1)}, bf16[1024,384]{1,0:T(8,128)(2,1)S(1)}, u32[]{:S(2)}, u32[]{:S(2)}) collective-permute-start(bf16[1024,384]{1,0:T(8,128)(2,1)} %copy-done.55), channel_id=1, source_target_pairs={{0,1},{1,0},{2,3},{3,2},{4,5},{5,4},{6,7},{7,6},{8,9},{9,8},{10,11... | collective-permute-start | bytes 2359304 | tf_op jit(solution)/shard_map/ppermute | solution.py:1078
  635.4 39.8 %collective-permute-start.56 = (bf16[192,4480]{1,0:T(8,128)(2,1)}, bf16[192,4480]{1,0:T(8,128)(2,1)}, u32[]{:S(2)}, u32[]{:S(2)}) collective-permute-start(bf16[192,4480]{1,0:T(8,128)(2,1)} %add.254), channel_id=1, source_target_pairs={{2,0},{4,6},{3,1},{5,7},{10,8},{12,14},{11,9},{13,15},{18,16},{20,... | collective-permute-start | bytes 5160968 | tf_op jit(solution)/shard_map/ppermute | solution.py:973
  639.8 35.5 %collective-permute-start.53 = (bf16[192,4480]{1,0:T(8,128)(2,1)}, bf16[192,4480]{1,0:T(8,128)(2,1)}, u32[]{:S(2)}, u32[]{:S(2)}) collective-permute-start(bf16[192,4480]{1,0:T(8,128)(2,1)} %add.252), channel_id=1, source_target_pairs={{2,4},{4,2},{3,5},{5,3},{10,12},{12,10},{11,13},{13,11},{18,20},{2... | collective-permute-start | bytes 5160968 | tf_op jit(solution)/shard_map/ppermute | solution.py:966
  641.6 47.6 %collective-permute-start.54 = (bf16[192,4480]{1,0:T(8,128)(2,1)}, bf16[192,4480]{1,0:T(8,128)(2,1)}, u32[]{:S(2)}, u32[]{:S(2)}) collective-permute-start(bf16[192,4480]{1,0:T(8,128)(2,1)} %add_rows.17), channel_id=1, source_target_pairs={{0,2},{6,4},{1,3},{7,5},{8,10},{14,12},{9,11},{15,13},{16,18},{22,... | collective-permute-start | bytes 5160968 | tf_op jit(solution)/shard_map/ppermute | solution.py:959
  668.5 20.7 %collective-permute-start.52 = (bf16[768,1024]{1,0:T(8,128)(2,1)}, bf16[768,1024]{1,0:T(8,128)(2,1)}, u32[]{:S(2)}, u32[]{:S(2)}) collective-permute-start(bf16[768,1024]{1,0:T(8,128)(2,1)} %get-tuple-element.505), channel_id=1, source_target_pairs={{0,8},{8,0},{16,24},{24,16},{1,9},{9,1},{17,25},{25,17},{2,10},{10... | collective-permute-start | bytes 4718600 | tf_op jit(solution)/shard_map/ppermute | solution.py:813
  671.5 51.1 %collective-permute-start.59 = (bf16[192,4480]{1,0:T(8,128)(2,1)S(1)}, bf16[192,4480]{1,0:T(8,128)(2,1)}, u32[]{:S(2)}, u32[]{:S(2)}) collective-permute-start(bf16[192,4480]{1,0:T(8,128)(2,1)S(1)} %copy-done.22), channel_id=1, source_target_pairs={{0,2},{6,4},{1,3},{7,5},{8,10},{14,12},{9,11},{15,13},{16,18},{22,... | collective-permute-start | bytes 5160968 | tf_op jit(solution)/shard_map/ppermute | solution.py:959
  696.4 33.5 %collective-permute-start.58 = (bf16[192,4480]{1,0:T(8,128)(2,1)}, bf16[192,4480]{1,0:T(8,128)(2,1)}, u32[]{:S(2)}, u32[]{:S(2)}) collective-permute-start(bf16[192,4480]{1,0:T(8,128)(2,1)} %add.256), channel_id=1, source_target_pairs={{2,4},{4,2},{3,5},{5,3},{10,12},{12,10},{11,13},{13,11},{18,20},{2... | collective-permute-start | bytes 5160968 | tf_op jit(solution)/shard_map/ppermute | solution.py:966
  698.3 34.2 %collective-permute-start.63 = (bf16[192,4480]{1,0:T(8,128)(2,1)}, bf16[192,4480]{1,0:T(8,128)(2,1)}, u32[]{:S(2)}, u32[]{:S(2)}) collective-permute-start(bf16[192,4480]{1,0:T(8,128)(2,1)} %add.258), channel_id=1, source_target_pairs={{2,0},{4,6},{3,1},{5,7},{10,8},{12,14},{11,9},{13,15},{18,16},{20,... | collective-permute-start | bytes 5160968 | tf_op jit(solution)/shard_map/ppermute | solution.py:973
  705.5 24.4 %collective-permute-start.61 = (bf16[384,1792]{1,0:T(8,128)(2,1)}, bf16[384,1792]{1,0:T(8,128)(2,1)}, u32[]{:S(2)}, u32[]{:S(2)}) collective-permute-start(bf16[384,1792]{1,0:T(8,128)(2,1)} %add_rows.19), channel_id=1, source_target_pairs={{0,16},{8,24},{16,0},{24,8},{1,17},{9,25},{17,1},{25,9},{2,18},{10... | collective-permute-start | bytes 4128776 | tf_op jit(solution)/shard_map/ppermute | solution.py:813
  742.6 24.7 %collective-permute-start.65 = (bf16[384,1792]{1,0:T(8,128)(2,1)S(1)}, bf16[384,1792]{1,0:T(8,128)(2,1)}, u32[]{:S(2)}, u32[]{:S(2)}) collective-permute-start(bf16[384,1792]{1,0:T(8,128)(2,1)S(1)} %add_rows.21), channel_id=1, source_target_pairs={{0,2},{6,4},{1,3},{7,5},{8,10},{14,12},{9,11},{15,13},{16,18},{22,... | collective-permute-start | bytes 4128776 | tf_op jit(solution)/shard_map/ppermute | solution.py:959
  747.0 27.4 %collective-permute-start.67 = (bf16[1024,768]{1,0:T(8,128)(2,1)S(1)}, bf16[1024,768]{1,0:T(8,128)(2,1)}, u32[]{:S(2)}, u32[]{:S(2)}) collective-permute-start(bf16[1024,768]{1,0:T(8,128)(2,1)S(1)} %copy-done.52), channel_id=1, source_target_pairs={{0,1},{1,0},{2,3},{3,2},{4,5},{5,4},{6,7},{7,6},{8,9},{9,8},{10,11... | collective-permute-start | bytes 4718600 | tf_op jit(solution)/shard_map/ppermute | solution.py:1078
  747.0 27.3 %collective-permute-start.64 = (bf16[192,4480]{1,0:T(8,128)(2,1)}, bf16[192,4480]{1,0:T(8,128)(2,1)}, u32[]{:S(2)}, u32[]{:S(2)}) collective-permute-start(bf16[192,4480]{1,0:T(8,128)(2,1)} %add.259), channel_id=1, source_target_pairs={{2,4},{4,2},{3,5},{5,3},{10,12},{12,10},{11,13},{13,11},{18,20},{2... | collective-permute-start | bytes 5160968 | tf_op jit(solution)/shard_map/ppermute | solution.py:966
  748.9 35.3 %collective-permute-start.68 = (bf16[192,4480]{1,0:T(8,128)(2,1)}, bf16[192,4480]{1,0:T(8,128)(2,1)}, u32[]{:S(2)}, u32[]{:S(2)}) collective-permute-start(bf16[192,4480]{1,0:T(8,128)(2,1)} %add.260), channel_id=1, source_target_pairs={{2,0},{4,6},{3,1},{5,7},{10,8},{12,14},{11,9},{13,15},{18,16},{20,... | collective-permute-start | bytes 5160968 | tf_op jit(solution)/shard_map/ppermute | solution.py:973
  786.7 37.5 %collective-permute-start.71 = (bf16[192,4480]{1,0:T(8,128)(2,1)S(1)}, bf16[192,4480]{1,0:T(8,128)(2,1)S(1)}, u32[]{:S(2)}, u32[]{:S(2)}) collective-permute-start(bf16[192,4480]{1,0:T(8,128)(2,1)S(1)} %add.263), channel_id=1, source_target_pairs={{2,0},{4,6},{3,1},{5,7},{10,8},{12,14},{11,9},{13,15},{18,16},{20,... | collective-permute-start | bytes 5160968 | tf_op jit(solution)/shard_map/ppermute | solution.py:973
  824.5 25.6 %collective-permute-start.73 = (bf16[384,1792]{1,0:T(8,128)(2,1)S(1)}, bf16[384,1792]{1,0:T(8,128)(2,1)S(1)}, u32[]{:S(2)}, u32[]{:S(2)}) collective-permute-start(bf16[384,1792]{1,0:T(8,128)(2,1)S(1)} %add.265), channel_id=1, source_target_pairs={{2,0},{4,6},{3,1},{5,7},{10,8},{12,14},{11,9},{13,15},{18,16},{20,... | collective-permute-start | bytes 4128776 | tf_op jit(solution)/shard_map/ppermute | solution.py:973
  826.0 22.2 %collective-permute-start.72 = (f32[5312]{0:T(1024)S(1)}, f32[5312]{0:T(1024)S(1)}, u32[]{:S(2)}, u32[]{:S(2)}) collective-permute-start(f32[5312]{0:T(1024)S(1)} %add.264), channel_id=1, source_target_pairs={{2,0},{4,6},{3,1},{5,7},{10,8},{12,14},{11,9},{13,15},{18,16},{20,... | collective-permute-start | bytes 63752 | tf_op jit(solution)/shard_map/ppermute | solution.py:973
  (118 other events, 1261.6 us)
Sparse Core Ops, SparseCore 0:
  96.7 69.5 all-gather.2
  254.6 151.5 reduce-scatter.1
  408.6 104.0 all-gather.4
